TPU v7x, 32 devices: a whole 2x2x4 slice. The times are simulated.
32 devices in a mesh: tm: 8 (over y, x, core), head: 4 (over z).
Axes of the slice: x: 2, y: 2, z: 4, core: 2. Of those that a mesh axis runs over, the one named last changes fastest.
Arguments:
- query_rows: bfloat16 [2048, 4096], P('tm', 'head'), may hold values from -6 to 6
- key_rows: bfloat16 [2048, 4096], P('tm', 'head'), may hold values from -6 to 6
- value_rows: bfloat16 [2048, 4096], P('tm', 'head'), may hold values from -12 to 12
- frame_counts: int32 [8], replicated, may hold values from 1 to 4, 24 in all
- history: bfloat16 [16, 4096], P('tm', 'head'), may hold values from -3 to 3
- offsets: int32 [8, 8], P('tm'), may hold values from 0 to 7, each once within a row
- cotangent: bfloat16 [2176, 2048], P('tm'), may hold values from -0.1875 to 0.1875
Outputs:
- attended: bfloat16 [2048, 4096], P('tm', 'head')
- disc_grad: float32 [2048, 4096], P('tm', 'head')
Inputs may be any that keep to these rules, and one draw needn't show every extreme that they name: Each row of offsets names every number below 8 once.
All inputs are finite; a program needn't handle non-finite values.
Results may differ from a plain program's by a relative error of at most 0.0049.
Values may be sent and summed in bfloat16 or wider, within the bound.
No kernel may reach another device: no remote copies, remote signals or barrier semaphores. Data moves between devices by JAX's collectives and lax.ppermute only.
A program may use at most 64 MiB of HBM per device.

v0:
```python
import math

import jax
import jax.numpy as jnp
from jax import lax
from jax.experimental import pallas as pl
from jax.experimental.pallas import tpu as pltpu
from jax.sharding import PartitionSpec as P

HD = 128
TPF = 64
WINB = 4
VMEM_LIMIT = 32 * 1024 * 1024
PACK_LIMIT = 63 * 1024 * 1024


def from_behind(x, axis, by):
    devices = lax.axis_size(axis)
    pairs = [(i, i + by) for i in range(devices) if 0 <= i + by < devices]
    return lax.ppermute(x, axis, pairs)


def window_body(query_rows, key_rows, value_rows, frame_counts, history, offsets, cotangent):
    tok_rows, feat_width = query_rows.shape
    local_heads = feat_width // HD
    block_total = lax.axis_size("tm")
    own_block = lax.axis_index("tm")
    score_scale = 1.0 / math.sqrt(HD)
    key_value = jnp.stack([key_rows, value_rows])
    pieces = []
    for distance in range(WINB - 1, 0, -1):
        pieces.append(from_behind(key_value, "tm", distance))
    window = jnp.concatenate(pieces + [key_value], axis=1)
    source_block = own_block - (WINB - 1) + jnp.arange(WINB, dtype=jnp.int32)
    block_match = jnp.arange(block_total, dtype=jnp.int32)[None, :] == source_block[:, None]
    block_count = jnp.sum(jnp.where(block_match, frame_counts[None, :], 0), axis=1)
    frame_index = jnp.arange(tok_rows, dtype=jnp.int32) // TPF
    kept_mask = (
        (source_block[:, None] >= 0) & (frame_index[None, :] < block_count[:, None])
    ).reshape(WINB * tok_rows)
    key_window = window[0].reshape(WINB * tok_rows, local_heads, HD)
    value_window = window[1].reshape(WINB * tok_rows, local_heads, HD)
    query_heads = query_rows.reshape(tok_rows, local_heads, HD)
    scores = (
        jnp.einsum("qhd,khd->hqk", query_heads, key_window, preferred_element_type=jnp.float32)
        * score_scale
    )
    scores = jnp.where(kept_mask[None, None, :], scores, -jnp.inf)
    row_max = jnp.max(scores, axis=-1, keepdims=True)
    weights = jnp.exp(scores - row_max)
    probs = (weights / jnp.sum(weights, axis=-1, keepdims=True)).astype(jnp.bfloat16)
    mixed = jnp.einsum("hqk,khd->qhd", probs, value_window, preferred_element_type=jnp.float32)
    attended = mixed.astype(jnp.bfloat16).reshape(tok_rows, feat_width)
    tile_rows = history.shape[0]
    source_tile = (own_block - offsets[0]) % block_total
    source_row = (
        source_tile[:, None] * tile_rows + jnp.arange(tile_rows, dtype=jnp.int32)[None, :]
    ).reshape(-1)
    incoming = lax.all_gather(history, "tm", axis=0, tiled=True)
    piece_rows = incoming.shape[0]
    selector = (source_row[:, None] == jnp.arange(piece_rows, dtype=jnp.int32)[None, :]).astype(
        jnp.bfloat16
    )
    clip_hist = jnp.dot(selector, incoming, preferred_element_type=jnp.float32).astype(jnp.bfloat16)
    disc_clip = jnp.concatenate([clip_hist, attended], axis=0)
    disc_grad = lax.psum_scatter(
        lax.dot_general(
            cotangent, disc_clip, (((0,), (0,)), ((), ())), preferred_element_type=jnp.float32
        ),
        "tm",
        scatter_dimension=0,
        tiled=True,
    )
    return (attended, disc_grad)


def pack_kernel(n, lo, off_hbm, q_hbm, k_hbm, v_hbm, hist_hbm, cot_hbm, out_hbm, off, hist, q, k, v, cot, out, sems):
    own = lax.axis_index("tm")
    plane = lax.rem(lax.axis_index("head"), 2)
    tok = q.shape[0]
    tile = hist.shape[0]
    clip_rows = n * tile
    part, all_cols = cot.shape
    cols = all_cols // n
    base = 3 * tok + clip_rows
    low = pl.multiple_of(plane * lo, 16)
    fetched = [
        (q_hbm, q),
        (k_hbm, k),
        (v_hbm, v),
        (cot_hbm.at[pl.ds(low, part), :], cot),
        (hist_hbm, hist),
        (off_hbm, off),
    ]
    fetches = [pltpu.make_async_copy(a, b, sems.at[i]) for i, (a, b) in enumerate(fetched)]
    cuts = [0, tok, 2 * tok, base, out.shape[1]]
    stores = []
    for i in range(4):
        rows = pl.ds(cuts[i], cuts[i + 1] - cuts[i])
        at = len(fetches) + i
        stores.append(
            pltpu.make_async_copy(out.at[:, rows, :], out_hbm.at[:, rows, :], sems.at[at])
        )
    for fetch in fetches:
        fetch.start()
    fetches[4].wait()
    fetches[5].wait()
    tiles = hist[...].astype(jnp.float32)
    row = lax.broadcasted_iota(jnp.int32, (clip_rows, n * HD), 0)
    placed = jnp.zeros((clip_rows, n * HD), jnp.float32)
    for t in range(tile):
        placed = jnp.where(row == own * tile + t, tiles[t : t + 1, :], placed)
    placed = placed.astype(jnp.bfloat16)
    for h in range(n):
        out[h, 3 * tok : base, :] = placed[:, h * HD : (h + 1) * HD]
    for i, x in enumerate((q, k, v)):
        fetches[i].wait()
        for h in range(n):
            out[h, i * tok : (i + 1) * tok, :] = x[:, h * HD : (h + 1) * HD]
        stores[i].start()
    r = lax.broadcasted_iota(jnp.int32, (clip_rows, clip_rows), 0)
    c = lax.broadcasted_iota(jnp.int32, (clip_rows, clip_rows), 1)
    select = jnp.where((r == c) & (plane != 0), 1.0, 0.0)
    for j in range(n):
        src = lax.rem(own - off[0, j] + 2 * n, n)
        for t in range(tile):
            hit = (c == j * tile + t) & (r == src * tile + t) & (plane == 0)
            select = jnp.where(hit, 1.0, select)
    fetches[3].wait()
    by_row = jnp.dot(
        select.astype(jnp.bfloat16), cot[0:clip_rows, :], preferred_element_type=jnp.float32
    ).astype(jnp.bfloat16)
    for h in range(n):
        for u in range(cols // HD):
            at = base + u * part
            lanes = slice(h * cols + u * HD, h * cols + (u + 1) * HD)
            out[h, at : at + clip_rows, :] = by_row[:, lanes]
            out[h, at + clip_rows : at + part, :] = cot[clip_rows:part, lanes]
    stores[3].start()
    for store in stores:
        store.wait()


def attend_blocks(n, tok, parity, counts, x_ref, out_ref):
    rate = math.log2(math.e) / math.sqrt(HD)
    token = lax.broadcasted_iota(jnp.int32, (1, tok), 1)
    for i in range(n // 2):
        block = 2 * i + parity
        keys = min(WINB, 2 * i + 2)
        sources = [block - (keys - 1) + k for k in range(keys)]
        q = x_ref[block, 0:tok, :]
        scores = []
        for s in sources:
            at = jnp.maximum(s, 0)
            kept = jnp.where(s >= 0, counts[at], 0) * TPF
            scores.append(
                lax.dot_general(
                    q,
                    x_ref[at, tok : 2 * tok, :],
                    (((1,), (1,)), ((), ())),
                    preferred_element_type=jnp.float32,
                )
                + jnp.where(token < kept, 0.0, -jnp.inf).astype(jnp.float32)
            )
        top = jnp.max(scores[0], axis=1, keepdims=True)
        for s in scores[1:]:
            top = jnp.maximum(top, jnp.max(s, axis=1, keepdims=True))
        weights = [jnp.exp2((s - top) * rate) for s in scores]
        total = jnp.sum(weights[0], axis=1, keepdims=True)
        for w in weights[1:]:
            total = total + jnp.sum(w, axis=1, keepdims=True)
        share = 1.0 / total
        mixed = jnp.zeros((tok, HD), jnp.float32)
        for s, w in zip(sources, weights):
            mixed = mixed + jnp.dot(
                (w * share).astype(jnp.bfloat16),
                x_ref[jnp.maximum(s, 0), 2 * tok : 3 * tok, :],
                preferred_element_type=jnp.float32,
            )
        out_ref[i * tok : (i + 1) * tok, :] = mixed.astype(jnp.bfloat16)
    rows = n // 2 * tok
    clip_rows = out_ref.shape[0] - rows
    hist = jnp.zeros((clip_rows, HD), jnp.float32)
    for s in range(n):
        hist = hist + x_ref[s, 3 * tok : 3 * tok + clip_rows, :].astype(jnp.float32)
    out_ref[rows:, :] = hist.astype(jnp.bfloat16)


def attend_kernel(n, tok, counts_hbm, x_ref, same_ref, cross_ref, cot_ref, counts, sem):
    copy = pltpu.make_async_copy(counts_hbm, counts, sem)
    copy.start()
    side = lax.rem(lax.axis_index("tm"), 2)
    length = x_ref.shape[1]
    part = cot_ref.shape[1]
    for s in range(n):
        cot_ref[s] = x_ref[s, length - part : length, :]
    copy.wait()
    attend_blocks(n, tok, side, counts, x_ref, same_ref)
    attend_blocks(n, tok, 1 - side, counts, x_ref, cross_ref)


def whole_cot(lo, part, plane, mine, swapped):
    pieces = []
    for u in range(mine.shape[0] // part):
        a = mine[u * part : (u + 1) * part, :]
        b = swapped[u * part : (u + 1) * part, :]
        low = jnp.where(plane == 0, a, b)
        high = jnp.where(plane == 0, b, a)
        pieces.append(jnp.concatenate([low[:lo], high], axis=0))
    return jnp.concatenate(pieces, axis=1)


def turn(wholes, clip_rows):
    pieces = [x[clip_rows:] for x in wholes] + [x[:clip_rows] for x in wholes]
    return jnp.concatenate(pieces, axis=0).T


def turn_kernel(lo, clip_rows, cot_rows, mine_ref, swapped_ref, *refs):
    own_ref, give_ref = refs[-2:]
    plane = lax.rem(lax.axis_index("head"), 2)
    side = lax.rem(lax.axis_index("tm"), 2)
    half = mine_ref.shape[0] // 2
    part = cot_rows - lo
    filled = half * cot_rows
    for out_ref, first in ((own_ref, side), (give_ref, 1 - side)):
        wholes = []
        for c in range(half):
            s = 2 * c + first
            wholes.append(whole_cot(lo, part, plane, mine_ref[s], swapped_ref[s]))
        out_ref[:, 0:filled] = turn(wholes, clip_rows)
        if filled < out_ref.shape[1]:
            out_ref[:, filled:] = jnp.zeros_like(out_ref[:, filled:])


def grad_part(turned_ref, head_refs, rows, copies):
    right = jnp.concatenate([x[0:rows, :] for x in head_refs], axis=1)
    hist = jnp.concatenate([x[rows:, :] for x in head_refs], axis=1)
    clip = copies * hist.shape[0]
    out = jnp.dot(turned_ref[:, 0:rows], right, preferred_element_type=jnp.float32)
    return out + jnp.dot(
        turned_ref[:, rows : rows + clip],
        jnp.concatenate([hist] * copies, axis=0),
        preferred_element_type=jnp.float32,
    )


def grad_kernel(rows, copies, turned_ref, *refs):
    out_ref = refs[-1]
    out_ref[...] = grad_part(turned_ref, refs[:-1], rows, copies).astype(out_ref.dtype)


def finish_kernel(n, tok, own_near, own_far, got_near, got_far, *refs):
    heads, att_ref, out_ref = refs[:n], refs[n], refs[n + 1]
    own = lax.axis_index("tm")
    at = pl.multiple_of(own // 2 * tok, tok)
    near = own_near.shape[1] // HD
    for k in range(n):
        lanes = pl.ds(pl.multiple_of((own ^ k) * HD, HD), HD)
        att_ref[:, lanes] = heads[k][pl.ds(at, tok), :]
        mine, got, a = (own_near, got_near, k) if k < near else (own_far, got_far, k - near)
        b = a ^ 1
        out_ref[:, lanes] = mine[:, a * HD : (a + 1) * HD] + got[:, b * HD : (b + 1) * HD].astype(
            jnp.float32
        )


def head_body(query_rows, key_rows, value_rows, frame_counts, history, offsets, cotangent):
    n = lax.axis_size("tm")
    planes = lax.axis_size("head")
    half = n // 2
    tok, width = query_rows.shape
    tile = history.shape[0]
    clip_rows = n * tile
    cot_rows, all_cols = cotangent.shape
    cols = all_cols // n
    units = cols // HD
    lo = cot_rows // 32 * 16
    part = cot_rows - lo
    base = 3 * tok + clip_rows
    length = base + units * part
    rows = half * tok
    vmem = pl.BlockSpec(memory_space=pltpu.VMEM)
    hbm = pl.BlockSpec(memory_space=pl.ANY)
    bf16 = jnp.bfloat16

    def swap(x, bit):
        return lax.ppermute(x, "tm", [(i, i ^ bit) for i in range(n)])

    def swap_plane(x, bit):
        pairs = [
            (i * planes + p, (i ^ bit) * planes + (p ^ 1)) for i in range(n) for p in range(planes)
        ]
        return lax.ppermute(x, ("tm", "head"), pairs)

    def call(
        kernel, name, outs, specs, flops, scratch=(), exps=0, out_spec=vmem, limit=VMEM_LIMIT
    ):
        shapes = [jax.ShapeDtypeStruct(s, d) for s, d in outs]
        moved = 2 * sum(math.prod(s.shape) * s.dtype.itemsize for s in shapes)
        return pl.pallas_call(
            kernel,
            out_shape=tuple(shapes),
            in_specs=specs,
            out_specs=tuple([out_spec] * len(shapes)),
            scratch_shapes=scratch,
            compiler_params=pltpu.CompilerParams(vmem_limit_bytes=limit),
            cost_estimate=pl.CostEstimate(flops=flops, bytes_accessed=moved, transcendentals=exps),
            name=name,
        )

    (packed,) = call(
        lambda *refs: pack_kernel(n, lo, *refs),
        "pack",
        [((n, length, HD), bf16)],
        [hbm] * 6,
        0,
        (
            pltpu.SMEM(offsets.shape, jnp.int32),
            pltpu.VMEM(history.shape, bf16),
            pltpu.VMEM((tok, width), bf16),
            pltpu.VMEM((tok, width), bf16),
            pltpu.VMEM((tok, width), bf16),
            pltpu.VMEM((part, all_cols), bf16),
            pltpu.VMEM((n, length, HD), bf16),
            pltpu.SemaphoreType.DMA((10,)),
        ),
        out_spec=hbm,
        limit=PACK_LIMIT,
    )(offsets, query_rows, key_rows, value_rows, history, cotangent)
    by_head = lax.all_to_all(packed, "tm", 0, 0)

    counts = (pltpu.SMEM(frame_counts.shape, jnp.int32), pltpu.SemaphoreType.DMA)
    pairs = half * tok * WINB * tok
    head_shape = ((rows + clip_rows, HD), bf16)
    same, cross, cot_mine = call(
        lambda *refs: attend_kernel(n, tok, *refs),
        "attend",
        [head_shape, head_shape, ((n, units * part, HD), bf16)],
        [hbm, vmem],
        8 * pairs * HD,
        counts,
        2 * pairs,
    )(frame_counts, by_head)
    cot_swapped = swap_plane(cot_mine, 0)
    x_same, y_cross = swap(same, 2), swap(cross, 4 ^ 1)
    y_same, x_cross, c_cross = swap(same, 4), swap(cross, 2 ^ 1), swap(cross, 1)
    far_same, far_cross = swap(x_same, 4), swap(y_cross, 2)

    turned_shape = ((cols, -(-half * cot_rows // HD) * HD), bf16)
    turned_own, turned_give = call(
        lambda *refs: turn_kernel(lo, clip_rows, cot_rows, *refs),
        "turn",
        [turned_shape] * 2,
        [vmem] * 2 + [hbm] * 4,
        0,
    )(cot_mine, cot_swapped, x_same, y_cross, x_cross, y_same)
    turned_other = swap(turned_give, 1)

    def grad(turned, heads, dtype, name):
        (out,) = call(
            lambda *refs: grad_kernel(rows, half, *refs),
            name,
            [((cols, len(heads) * HD), dtype)],
            [vmem] * (1 + len(heads)),
            2 * cols * half * cot_rows * len(heads) * HD,
        )(turned, *heads)
        return out

    near = [same, c_cross, x_same, x_cross, y_same, y_cross]
    far = [far_same, far_cross]
    got_near = swap(grad(turned_other, near, bf16, "grad_other_near"), 1)
    own_near = grad(turned_own, near, jnp.float32, "grad_own_near")
    got_far = swap(grad(turned_other, far, bf16, "grad_other_far"), 1)
    own_far = grad(turned_own, far, jnp.float32, "grad_own_far")
    return call(
        lambda *refs: finish_kernel(n, tok, *refs),
        "finish",
        [((tok, width), bf16), ((cols, width), jnp.float32)],
        [vmem] * (4 + n),
        0,
    )(own_near, own_far, got_near, got_far, *near, *far)


def body(query_rows, key_rows, value_rows, frame_counts, history, offsets, cotangent):
    n = lax.axis_size("tm")
    tok, width = query_rows.shape
    by_heads = (
        n == 8
        and lax.axis_size("head") % 2 == 0
        and width == n * HD
        and offsets.shape[1] == n
        and cotangent.shape[0] == tok + n * history.shape[0]
        and cotangent.shape[1] % (n * HD) == 0
        and tok % 16 == 0
        and (n * history.shape[0]) % 16 == 0
    )
    plan = head_body if by_heads else window_body
    return plan(query_rows, key_rows, value_rows, frame_counts, history, offsets, cotangent)


def solution(mesh):
    in_specs = (
        P("tm", "head"),
        P("tm", "head"),
        P("tm", "head"),
        P(),
        P("tm", "head"),
        P("tm", None),
        P("tm", None),
    )
    out_specs = (P("tm", "head"), P("tm", "head"))
    return jax.shard_map(body, mesh=mesh, in_specs=in_specs, out_specs=out_specs, check_vma=False)
```

profile of v0, /device:TPU:0, one launch (start us, length us, event | category | flops | bytes accessed | tf_op | source)
XLA Modules:
  0.0 70.8 jit_solution(11342673020894672935)
XLA Ops:
  0.6 2.9 %pack.1 = bf16[8,1072,128]{2,1,0:T(8,128)(2,1)} custom-call(s32[1,8]{1,0:T(1,128)} %refs_0_.2, bf16[256,1024]{1,0:T(8,128)(2,1)} %refs_1_.1, bf16[256,1024]{1,0:T(8,128)(2,1)} %refs_2_.1, bf16[256,1024]{1,0:T(8,128)(2,1)} %refs_3_.1, bf16[2,1024]{1,0:T(2,128)(2,1)} %refs_4_.1, bf16[272,2048]{1,0:T(8,128)(2,1)} %refs_5_.1), custom_call_target="tpu_custom_call" | custom-call | bytes 4390912 | tf_op jit(solution)/shard_map/pack/pallas_call | solution.py:311
  3.6 0.0 copy-start
  3.6 32.8 %all_to_all.5.refs_1_ = bf16[8,1072,128]{2,1,0:T(8,128)(2,1)S(1)} all-to-all(bf16[8,1072,128]{2,1,0:T(8,128)(2,1)} %pack.1), channel_id=1, replica_groups=mesh['tm'=8,'head'=4] {'tm'}, dimensions={0} | all-to-all | bytes 4390912 | tf_op jit(solution)/shard_map/all_to_all | solution.py:330
  36.4 5.1 %attend.1 = (bf16[1040,128]{1,0:T(8,128)(2,1)S(1)}, bf16[1040,128]{1,0:T(8,128)(2,1)S(1)}, bf16[8,288,128]{2,1,0:T(8,128)(2,1)S(1)}) custom-call(s32[8]{0:T(128)S(1)} %copy-done, bf16[8,1072,128]{2,1,0:T(8,128)(2,1)S(1)} %all_to_all.5.refs_1_), custom_call_target="tpu_custom_call" | custom-call | flops 1073741824 | bytes 2244608 | tf_op jit(solution)/shard_map/attend/pallas_call | solution.py:335
  41.5 1.6 %collective-permute-start = (bf16[8,288,128]{2,1,0:T(8,128)(2,1)S(1)}, bf16[8,288,128]{2,1,0:T(8,128)(2,1)S(1)}, u32[]{:S(2)}, u32[]{:S(2)}) collective-permute-start(bf16[8,288,128]{2,1,0:T(8,128)(2,1)S(1)} %get-tuple-element.7.refs_0_), channel_id=1, source_target_pairs={{0,1},{1,0},{2,3},{3,2},{4,5},{5,4},{6,7},{7,6},{8,9},{9,8},{10,11... | collective-permute-start | bytes 1769480 | tf_op jit(solution)/shard_map/ppermute | solution.py:293
  43.2 0.0 collective-permute-start.3
  43.2 0.8 %collective-permute-start.2 = (bf16[1040,128]{1,0:T(8,128)(2,1)S(1)}, bf16[1040,128]{1,0:T(8,128)(2,1)S(1)}, u32[]{:S(2)}, u32[]{:S(2)}) collective-permute-start(bf16[1040,128]{1,0:T(8,128)(2,1)S(1)} %get-tuple-element.9), channel_id=1, source_target_pairs={{0,20},{4,16},{8,28},{12,24},{16,4},{20,0},{24,12},{28,8},{1,21},{... | collective-permute-start | bytes 798728 | tf_op jit(solution)/shard_map/ppermute | solution.py:287
  44.0 1.5 %collective-permute-start.4 = (bf16[1040,128]{1,0:T(8,128)(2,1)S(1)}, bf16[1040,128]{1,0:T(8,128)(2,1)S(1)}, u32[]{:S(2)}, u32[]{:S(2)}) collective-permute-start(bf16[1040,128]{1,0:T(8,128)(2,1)S(1)} %get-tuple-element.8.refs_1_.refs_4_), channel_id=1, source_target_pairs={{0,16},{4,20},{8,24},{12,28},{16,0},{20,4},{24,8},{28,12},{1,17},{... | collective-permute-start | bytes 798728 | tf_op jit(solution)/shard_map/ppermute | solution.py:287
  45.5 1.5 %collective-permute-start.1 = (bf16[1040,128]{1,0:T(8,128)(2,1)S(1)}, bf16[1040,128]{1,0:T(8,128)(2,1)S(1)}, u32[]{:S(2)}, u32[]{:S(2)}) collective-permute-start(bf16[1040,128]{1,0:T(8,128)(2,1)S(1)} %get-tuple-element.8.refs_1_.refs_4_), channel_id=1, source_target_pairs={{0,8},{4,12},{8,0},{12,4},{16,24},{20,28},{24,16},{28,20},{1,9},{5... | collective-permute-start | bytes 798728 | tf_op jit(solution)/shard_map/ppermute | solution.py:287
  47.0 4.8 %collective-permute-done.3.refs_4_.refs_7_ = bf16[1040,128]{1,0:T(8,128)(2,1)S(1)} collective-permute-done((bf16[1040,128]{1,0:T(8,128)(2,1)S(1)}, bf16[1040,128]{1,0:T(8,128)(2,1)S(1)}, u32[]{:S(2)}, u32[]{:S(2)}) %collective-permute-start.3) | collective-permute-done | bytes 266272 | tf_op jit(solution)/shard_map/ppermute | solution.py:287
  51.8 0.0 collective-permute-done.2.refs_3_.refs_6_.refs_9_
  51.8 5.8 %collective-permute-done.4.refs_5_.refs_8_ = bf16[1040,128]{1,0:T(8,128)(2,1)S(1)} collective-permute-done((bf16[1040,128]{1,0:T(8,128)(2,1)S(1)}, bf16[1040,128]{1,0:T(8,128)(2,1)S(1)}, u32[]{:S(2)}, u32[]{:S(2)}) %collective-permute-start.4) | collective-permute-done | bytes 266272 | tf_op jit(solution)/shard_map/ppermute | solution.py:287
  57.6 0.0 collective-permute-done.1.refs_2_.refs_3_.refs_6_
  57.6 0.0 collective-permute-done.refs_1_
  57.6 0.4 turn.1
  58.0 0.1 collective-permute-start.8
  58.1 0.5 collective-permute-start.5
  58.6 1.0 %collective-permute-start.7 = (bf16[1040,128]{1,0:T(8,128)(2,1)S(1)}, bf16[1040,128]{1,0:T(8,128)(2,1)S(1)}, u32[]{:S(2)}, u32[]{:S(2)}) collective-permute-start(bf16[1040,128]{1,0:T(8,128)(2,1)S(1)} %collective-permute-done.2.refs_3_.refs_6_.refs_9_), channel_id=1, source_target_pairs={{0,8},{4,12},{8,0},{12,4},{16,24},{20,28},{24,16},{28,20},{1,9},{5... | collective-permute-start | bytes 798728 | tf_op jit(solution)/shard_map/ppermute | solution.py:287
  59.5 1.0 %collective-permute-start.6 = (bf16[1040,128]{1,0:T(8,128)(2,1)S(1)}, bf16[1040,128]{1,0:T(8,128)(2,1)S(1)}, u32[]{:S(2)}, u32[]{:S(2)}) collective-permute-start(bf16[1040,128]{1,0:T(8,128)(2,1)S(1)} %collective-permute-done.1.refs_2_.refs_3_.refs_6_), channel_id=1, source_target_pairs={{0,16},{4,20},{8,24},{12,28},{16,0},{20,4},{24,8},{28,12},{1,17},{... | collective-permute-start | bytes 798728 | tf_op jit(solution)/shard_map/ppermute | solution.py:287
  60.6 0.0 collective-permute-done.5.refs_2_.refs_5_
  60.6 0.0 collective-permute-done.8.refs_0_
  60.6 0.7 grad_other_near.1
  61.3 0.1 collective-permute-start.9
  61.4 5.6 %collective-permute-done.7.refs_2_.refs_11_ = bf16[1040,128]{1,0:T(8,128)(2,1)S(1)} collective-permute-done((bf16[1040,128]{1,0:T(8,128)(2,1)S(1)}, bf16[1040,128]{1,0:T(8,128)(2,1)S(1)}, u32[]{:S(2)}, u32[]{:S(2)}) %collective-permute-start.7) | collective-permute-done | bytes 266272 | tf_op jit(solution)/shard_map/ppermute | solution.py:287
  66.9 0.7 collective-permute-done.6.refs_1_.refs_10_
  67.6 0.3 grad_other_far.1
  68.0 0.1 collective-permute-start.10
  68.0 0.3 grad_own_far.1.refs_1_
  68.4 0.7 grad_own_near.1.refs_0_
  69.1 0.3 collective-permute-done.10.refs_3_
  69.4 0.0 collective-permute-done.9.refs_2_
  69.4 1.4 %finish.1 = (bf16[256,1024]{1,0:T(8,128)(2,1)}, f32[256,1024]{1,0:T(8,128)}) custom-call(f32[256,768]{1,0:T(8,128)S(1)} %grad_own_near.1.refs_0_, f32[256,256]{1,0:T(8,128)S(1)} %grad_own_far.1.refs_1_, bf16[256,768]{1,0:T(8,128)(2,1)S(1)} %collective-permute-done.9.refs_2_, bf16[256,256]{1,0:T(8,128)(2,1)S(1)} %collective-permute-done.10.refs_3_, ...), custom_call_target="tpu_custom_call" | custom-call | bytes 3145728 | tf_op jit(solution)/shard_map/finish/pallas_call | solution.py:375
  (1 shorter events, 0.0 us)
Async XLA Ops:
  3.6 32.8 %copy-start = (s32[8]{0:T(128)S(1)}, s32[8]{0:T(128)}, u32[]{:S(2)}) copy-start(s32[8]{0:T(128)} %refs_0_.3) | copy-start | bytes 100
  41.5 16.1 %collective-permute-start = (bf16[8,288,128]{2,1,0:T(8,128)(2,1)S(1)}, bf16[8,288,128]{2,1,0:T(8,128)(2,1)S(1)}, u32[]{:S(2)}, u32[]{:S(2)}) collective-permute-start(bf16[8,288,128]{2,1,0:T(8,128)(2,1)S(1)} %get-tuple-element.7.refs_0_), channel_id=1, source_target_pairs={{0,1},{1,0},{2,3},{3,2},{4,5},{5,4},{6,7},{7,6},{8,9},{9,8},{10,11... | collective-permute-start | bytes 1769480 | tf_op jit(solution)/shard_map/ppermute | solution.py:293
  43.2 8.6 %collective-permute-start.3 = (bf16[1040,128]{1,0:T(8,128)(2,1)S(1)}, bf16[1040,128]{1,0:T(8,128)(2,1)S(1)}, u32[]{:S(2)}, u32[]{:S(2)}) collective-permute-start(bf16[1040,128]{1,0:T(8,128)(2,1)S(1)} %get-tuple-element.9), channel_id=1, source_target_pairs={{0,12},{4,8},{8,4},{12,0},{16,28},{20,24},{24,20},{28,16},{1,13},{... | collective-permute-start | bytes 798728 | tf_op jit(solution)/shard_map/ppermute | solution.py:287
  43.2 8.6 %collective-permute-start.2 = (bf16[1040,128]{1,0:T(8,128)(2,1)S(1)}, bf16[1040,128]{1,0:T(8,128)(2,1)S(1)}, u32[]{:S(2)}, u32[]{:S(2)}) collective-permute-start(bf16[1040,128]{1,0:T(8,128)(2,1)S(1)} %get-tuple-element.9), channel_id=1, source_target_pairs={{0,20},{4,16},{8,28},{12,24},{16,4},{20,0},{24,12},{28,8},{1,21},{... | collective-permute-start | bytes 798728 | tf_op jit(solution)/shard_map/ppermute | solution.py:287
  44.0 13.6 %collective-permute-start.4 = (bf16[1040,128]{1,0:T(8,128)(2,1)S(1)}, bf16[1040,128]{1,0:T(8,128)(2,1)S(1)}, u32[]{:S(2)}, u32[]{:S(2)}) collective-permute-start(bf16[1040,128]{1,0:T(8,128)(2,1)S(1)} %get-tuple-element.8.refs_1_.refs_4_), channel_id=1, source_target_pairs={{0,16},{4,20},{8,24},{12,28},{16,0},{20,4},{24,8},{28,12},{1,17},{... | collective-permute-start | bytes 798728 | tf_op jit(solution)/shard_map/ppermute | solution.py:287
  45.5 12.1 %collective-permute-start.1 = (bf16[1040,128]{1,0:T(8,128)(2,1)S(1)}, bf16[1040,128]{1,0:T(8,128)(2,1)S(1)}, u32[]{:S(2)}, u32[]{:S(2)}) collective-permute-start(bf16[1040,128]{1,0:T(8,128)(2,1)S(1)} %get-tuple-element.8.refs_1_.refs_4_), channel_id=1, source_target_pairs={{0,8},{4,12},{8,0},{12,4},{16,24},{20,28},{24,16},{28,20},{1,9},{5... | collective-permute-start | bytes 798728 | tf_op jit(solution)/shard_map/ppermute | solution.py:287
  58.0 2.6 %collective-permute-start.8 = (bf16[256,1152]{1,0:T(8,128)(2,1)S(1)}, bf16[256,1152]{1,0:T(8,128)(2,1)S(1)}, u32[]{:S(2)}, u32[]{:S(2)}) collective-permute-start(bf16[256,1152]{1,0:T(8,128)(2,1)S(1)} %get-tuple-element.11), channel_id=1, source_target_pairs={{0,4},{4,0},{8,12},{12,8},{16,20},{20,16},{24,28},{28,24},{1,5},{5... | collective-permute-start | bytes 1769480 | tf_op jit(solution)/shard_map/ppermute | solution.py:287
  58.1 2.5 %collective-permute-start.5 = (bf16[1040,128]{1,0:T(8,128)(2,1)S(1)}, bf16[1040,128]{1,0:T(8,128)(2,1)S(1)}, u32[]{:S(2)}, u32[]{:S(2)}) collective-permute-start(bf16[1040,128]{1,0:T(8,128)(2,1)S(1)} %get-tuple-element.9), channel_id=1, source_target_pairs={{0,4},{4,0},{8,12},{12,8},{16,20},{20,16},{24,28},{28,24},{1,5},{5... | collective-permute-start | bytes 798728 | tf_op jit(solution)/shard_map/ppermute | solution.py:287
  58.6 8.4 %collective-permute-start.7 = (bf16[1040,128]{1,0:T(8,128)(2,1)S(1)}, bf16[1040,128]{1,0:T(8,128)(2,1)S(1)}, u32[]{:S(2)}, u32[]{:S(2)}) collective-permute-start(bf16[1040,128]{1,0:T(8,128)(2,1)S(1)} %collective-permute-done.2.refs_3_.refs_6_.refs_9_), channel_id=1, source_target_pairs={{0,8},{4,12},{8,0},{12,4},{16,24},{20,28},{24,16},{28,20},{1,9},{5... | collective-permute-start | bytes 798728 | tf_op jit(solution)/shard_map/ppermute | solution.py:287
  59.5 8.1 %collective-permute-start.6 = (bf16[1040,128]{1,0:T(8,128)(2,1)S(1)}, bf16[1040,128]{1,0:T(8,128)(2,1)S(1)}, u32[]{:S(2)}, u32[]{:S(2)}) collective-permute-start(bf16[1040,128]{1,0:T(8,128)(2,1)S(1)} %collective-permute-done.1.refs_2_.refs_3_.refs_6_), channel_id=1, source_target_pairs={{0,16},{4,20},{8,24},{12,28},{16,0},{20,4},{24,8},{28,12},{1,17},{... | collective-permute-start | bytes 798728 | tf_op jit(solution)/shard_map/ppermute | solution.py:287
  61.3 8.1 %collective-permute-start.9 = (bf16[256,768]{1,0:T(8,128)(2,1)S(1)}, bf16[256,768]{1,0:T(8,128)(2,1)S(1)}, u32[]{:S(2)}, u32[]{:S(2)}) collective-permute-start(bf16[256,768]{1,0:T(8,128)(2,1)S(1)} %grad_other_near.1), channel_id=1, source_target_pairs={{0,4},{4,0},{8,12},{12,8},{16,20},{20,16},{24,28},{28,24},{1,5},{5... | collective-permute-start | bytes 1179656 | tf_op jit(solution)/shard_map/ppermute | solution.py:287
  68.0 1.4 %collective-permute-start.10 = (bf16[256,256]{1,0:T(8,128)(2,1)S(1)}, bf16[256,256]{1,0:T(8,128)(2,1)S(1)}, u32[]{:S(2)}, u32[]{:S(2)}) collective-permute-start(bf16[256,256]{1,0:T(8,128)(2,1)S(1)} %grad_other_far.1), channel_id=1, source_target_pairs={{0,4},{4,0},{8,12},{12,8},{16,20},{20,16},{24,28},{28,24},{1,5},{5... | collective-permute-start | bytes 393224 | tf_op jit(solution)/shard_map/ppermute | solution.py:287
where the time goes:
time: 71 us; the launch traced here: 70.8 us
  blocking collectives  32.8 us (46%)
  waiting for transfers between devices  17.3 us (24%)
  Pallas kernels  11.9 us (17%)
  starting transfers between devices  8.15 us (11%)
  between operations  0.73 us (1%)
    all_to_all x1, blocking collectives, head_body(): by_head = lax.all_to_all(packed, 'tm', 0, 0)  32.8 us
    ppermute x10, waiting for transfers between devices, swap(): return lax.ppermute(x, 'tm', [(i, i ^ bit) for i in range(n)])  17.3 us
    ppermute x10, starting transfers between devices, swap(): return lax.ppermute(x, 'tm', [(i, i ^ bit) for i in range(n)])  6.51 us
    pallas_call x1, Pallas kernels, head_body(): call(lambda *refs: attend_kernel(n, tok, *refs), 'attend', [head_shape, h...  5.13 us
    pallas_call x1, Pallas kernels, head_body(): call(lambda *refs: pack_kernel(n, lo, *refs), 'pack', [((n, length, HD),...  2.92 us
    pallas_call x4, Pallas kernels, grad(): call(lambda *refs: grad_kernel(rows, half, *refs), name, [((cols, len(hea...  1.98 us
    ppermute x1, starting transfers between devices, swap_plane(): return lax.ppermute(x, ('tm', 'head'), pairs)  1.64 us
    pallas_call x1, Pallas kernels, head_body(): call(lambda *refs: finish_kernel(n, tok, *refs), 'finish', [((tok, width)...  1.44 us
  transfers between devices with their start and end apart: 11, of which 5 were waited for; matrix products, arithmetic and copies ran while one was open for 0% of the time, Pallas kernels for 3%

commit v1 on v0

--- a/solution.py
+++ b/solution.py
@@ -74,50 +74,20 @@
     return (attended, disc_grad)
 
 
-def pack_kernel(n, lo, off_hbm, q_hbm, k_hbm, v_hbm, hist_hbm, cot_hbm, out_hbm, off, hist, q, k, v, cot, out, sems):
+def cot_kernel(n, tile, lo, off_hbm, cot_hbm, *refs):
+    outs, (off, cot, sems) = refs[:-3], refs[-3:]
     own = lax.axis_index("tm")
+    chip, side = own // 2, lax.rem(own, 2)
     plane = lax.rem(lax.axis_index("head"), 2)
-    tok = q.shape[0]
-    tile = hist.shape[0]
     clip_rows = n * tile
     part, all_cols = cot.shape
     cols = all_cols // n
-    base = 3 * tok + clip_rows
     low = pl.multiple_of(plane * lo, 16)
-    fetched = [
-        (q_hbm, q),
-        (k_hbm, k),
-        (v_hbm, v),
-        (cot_hbm.at[pl.ds(low, part), :], cot),
-        (hist_hbm, hist),
-        (off_hbm, off),
-    ]
-    fetches = [pltpu.make_async_copy(a, b, sems.at[i]) for i, (a, b) in enumerate(fetched)]
-    cuts = [0, tok, 2 * tok, base, out.shape[1]]
-    stores = []
-    for i in range(4):
-        rows = pl.ds(cuts[i], cuts[i + 1] - cuts[i])
-        at = len(fetches) + i
-        stores.append(
-            pltpu.make_async_copy(out.at[:, rows, :], out_hbm.at[:, rows, :], sems.at[at])
-        )
-    for fetch in fetches:
-        fetch.start()
-    fetches[4].wait()
-    fetches[5].wait()
-    tiles = hist[...].astype(jnp.float32)
-    row = lax.broadcasted_iota(jnp.int32, (clip_rows, n * HD), 0)
-    placed = jnp.zeros((clip_rows, n * HD), jnp.float32)
-    for t in range(tile):
-        placed = jnp.where(row == own * tile + t, tiles[t : t + 1, :], placed)
-    placed = placed.astype(jnp.bfloat16)
-    for h in range(n):
-        out[h, 3 * tok : base, :] = placed[:, h * HD : (h + 1) * HD]
-    for i, x in enumerate((q, k, v)):
-        fetches[i].wait()
-        for h in range(n):
-            out[h, i * tok : (i + 1) * tok, :] = x[:, h * HD : (h + 1) * HD]
-        stores[i].start()
+    fetch_off = pltpu.make_async_copy(off_hbm, off, sems.at[0])
+    fetch_cot = pltpu.make_async_copy(cot_hbm.at[pl.ds(low, part), :], cot, sems.at[1])
+    fetch_off.start()
+    fetch_cot.start()
+    fetch_off.wait()
     r = lax.broadcasted_iota(jnp.int32, (clip_rows, clip_rows), 0)
     c = lax.broadcasted_iota(jnp.int32, (clip_rows, clip_rows), 1)
     select = jnp.where((r == c) & (plane != 0), 1.0, 0.0)
@@ -126,19 +96,43 @@
         for t in range(tile):
             hit = (c == j * tile + t) & (r == src * tile + t) & (plane == 0)
             select = jnp.where(hit, 1.0, select)
-    fetches[3].wait()
-    by_row = jnp.dot(
+    fetch_cot.wait()
+    cot[0:clip_rows, :] = jnp.dot(
         select.astype(jnp.bfloat16), cot[0:clip_rows, :], preferred_element_type=jnp.float32
     ).astype(jnp.bfloat16)
-    for h in range(n):
-        for u in range(cols // HD):
-            at = base + u * part
-            lanes = slice(h * cols + u * HD, h * cols + (u + 1) * HD)
-            out[h, at : at + clip_rows, :] = by_row[:, lanes]
-            out[h, at + clip_rows : at + part, :] = cot[clip_rows:part, lanes]
-    stores[3].start()
-    for store in stores:
-        store.wait()
+    units = cols // HD
+    for m, out_ref in enumerate(outs):
+        for i, block in enumerate((2 * (chip ^ m) + side, 2 * (chip ^ m) + 1 - side)):
+            for u in range(units):
+                at = (i * units + u) * part
+                lanes = pl.ds(pl.multiple_of(block * cols + u * HD, HD), HD)
+                out_ref[at : at + part, :] = cot[:, lanes]
+
+
+def pack_kernel(n, q_hbm, k_hbm, v_hbm, hist_hbm, *refs):
+    outs, (q, k, v, hist, sems) = refs[:n], refs[n:]
+    own = lax.axis_index("tm")
+    tok = q.shape[0]
+    tile = hist.shape[0]
+    clip_rows = n * tile
+    pairs = [(hist_hbm, hist), (q_hbm, q), (k_hbm, k), (v_hbm, v)]
+    copies = [pltpu.make_async_copy(a, b, sems.at[i]) for i, (a, b) in enumerate(pairs)]
+    for copy in copies:
+        copy.start()
+    copies[0].wait()
+    for d, out_ref in enumerate(outs):
+        lanes = pl.ds(pl.multiple_of((own ^ d) * HD, HD), HD)
+        tiles = hist[:, lanes].astype(jnp.float32)
+        row = lax.broadcasted_iota(jnp.int32, (clip_rows, HD), 0)
+        placed = jnp.zeros((clip_rows, HD), jnp.float32)
+        for t in range(tile):
+            placed = jnp.where(row == own * tile + t, tiles[t : t + 1, :], placed)
+        out_ref[3 * tok : 3 * tok + clip_rows, :] = placed.astype(jnp.bfloat16)
+    for i, x in enumerate((q, k, v)):
+        copies[1 + i].wait()
+        for d, out_ref in enumerate(outs):
+            lanes = pl.ds(pl.multiple_of((own ^ d) * HD, HD), HD)
+            out_ref[i * tok : (i + 1) * tok, :] = x[:, lanes]
 
 
 def attend_blocks(n, tok, parity, counts, x_ref, out_ref):
@@ -186,17 +180,23 @@
     out_ref[rows:, :] = hist.astype(jnp.bfloat16)
 
 
-def attend_kernel(n, tok, counts_hbm, x_ref, same_ref, cross_ref, cot_ref, counts, sem):
+def attend_kernel(n, tok, counts_hbm, *refs):
+    parts, (same_ref, cross_ref, x_ref, counts, sem) = refs[:n], refs[n:]
     copy = pltpu.make_async_copy(counts_hbm, counts, sem)
     copy.start()
-    side = lax.rem(lax.axis_index("tm"), 2)
-    length = x_ref.shape[1]
-    part = cot_ref.shape[1]
-    for s in range(n):
-        cot_ref[s] = x_ref[s, length - part : length, :]
+    own = lax.axis_index("tm")
+    side = lax.rem(own, 2)
+    for k, part in enumerate(parts):
+        x_ref[own ^ k] = part[...]
     copy.wait()
     attend_blocks(n, tok, side, counts, x_ref, same_ref)
     attend_blocks(n, tok, 1 - side, counts, x_ref, cross_ref)
+
+
+def stack_kernel(*refs):
+    out_ref = refs[-1]
+    for i, x in enumerate(refs[:-1]):
+        out_ref[i] = x[...]
 
 
 def whole_cot(lo, part, plane, mine, swapped):
@@ -215,21 +215,19 @@
     return jnp.concatenate(pieces, axis=0).T
 
 
-def turn_kernel(lo, clip_rows, cot_rows, mine_ref, swapped_ref, *refs):
-    own_ref, give_ref = refs[-2:]
+def turn_kernel(lo, clip_rows, cot_rows, mine_ref, swapped_ref, own_ref, other_ref):
     plane = lax.rem(lax.axis_index("head"), 2)
-    side = lax.rem(lax.axis_index("tm"), 2)
-    half = mine_ref.shape[0] // 2
-    part = cot_rows - lo
-    filled = half * cot_rows
-    for out_ref, first in ((own_ref, side), (give_ref, 1 - side)):
-        wholes = []
-        for c in range(half):
-            s = 2 * c + first
-            wholes.append(whole_cot(lo, part, plane, mine_ref[s], swapped_ref[s]))
-        out_ref[:, 0:filled] = turn(wholes, clip_rows)
-        if filled < out_ref.shape[1]:
-            out_ref[:, filled:] = jnp.zeros_like(out_ref[:, filled:])
+    chip = lax.axis_index("tm") // 2
+    chips, length, _ = mine_ref.shape
+    for i, out_ref in enumerate((own_ref, other_ref)):
+        rows = slice(i * length // 2, (i + 1) * length // 2)
+        wholes = [
+            whole_cot(
+                lo, cot_rows - lo, plane, mine_ref[chip ^ c, rows], swapped_ref[chip ^ c, rows]
+            )
+            for c in range(chips)
+        ]
+        out_ref[...] = turn(wholes, clip_rows)
 
 
 def grad_part(turned_ref, head_refs, rows, copies):
@@ -277,7 +275,7 @@
     lo = cot_rows // 32 * 16
     part = cot_rows - lo
     base = 3 * tok + clip_rows
-    length = base + units * part
+    length = base
     rows = half * tok
     vmem = pl.BlockSpec(memory_space=pltpu.VMEM)
     hbm = pl.BlockSpec(memory_space=pl.ANY)
@@ -308,53 +306,69 @@
             name=name,
         )
 
-    (packed,) = call(
-        lambda *refs: pack_kernel(n, lo, *refs),
-        "pack",
-        [((n, length, HD), bf16)],
-        [hbm] * 6,
+    chips = range(half)
+    cots = call(
+        lambda *refs: cot_kernel(n, tile, lo, *refs),
+        "cot",
+        [((2 * units * part, HD), bf16)] * half,
+        [hbm] * 2,
         0,
         (
             pltpu.SMEM(offsets.shape, jnp.int32),
-            pltpu.VMEM(history.shape, bf16),
+            pltpu.VMEM((part, all_cols), bf16),
+            pltpu.SemaphoreType.DMA((2,)),
+        ),
+        limit=PACK_LIMIT,
+    )(offsets, cotangent)
+    cots = [cots[0]] + [swap(cots[m], 2 * m) for m in chips[1:]]
+    packed = call(
+        lambda *refs: pack_kernel(n, *refs),
+        "pack",
+        [((length, HD), bf16)] * n,
+        [hbm] * 4,
+        0,
+        (
             pltpu.VMEM((tok, width), bf16),
             pltpu.VMEM((tok, width), bf16),
             pltpu.VMEM((tok, width), bf16),
-            pltpu.VMEM((part, all_cols), bf16),
-            pltpu.VMEM((n, length, HD), bf16),
-            pltpu.SemaphoreType.DMA((10,)),
+            pltpu.VMEM(history.shape, bf16),
+            pltpu.SemaphoreType.DMA((4,)),
         ),
-        out_spec=hbm,
         limit=PACK_LIMIT,
-    )(offsets, query_rows, key_rows, value_rows, history, cotangent)
-    by_head = lax.all_to_all(packed, "tm", 0, 0)
-
-    counts = (pltpu.SMEM(frame_counts.shape, jnp.int32), pltpu.SemaphoreType.DMA)
+    )(query_rows, key_rows, value_rows, history)
+    by_head = [packed[0]] + [swap(packed[k], k) for k in range(1, n)]
+    (cot_mine,) = call(
+        stack_kernel, "stack", [((half, 2 * units * part, HD), bf16)], [vmem] * half, 0
+    )(*cots)
+    cot_swapped = swap_plane(cot_mine, 0)
+
+    counts = (
+        pltpu.VMEM((n, length, HD), bf16),
+        pltpu.SMEM(frame_counts.shape, jnp.int32),
+        pltpu.SemaphoreType.DMA,
+    )
     pairs = half * tok * WINB * tok
     head_shape = ((rows + clip_rows, HD), bf16)
-    same, cross, cot_mine = call(
+    same, cross = call(
         lambda *refs: attend_kernel(n, tok, *refs),
         "attend",
-        [head_shape, head_shape, ((n, units * part, HD), bf16)],
-        [hbm, vmem],
+        [head_shape, head_shape],
+        [hbm] + [vmem] * n,
         8 * pairs * HD,
         counts,
         2 * pairs,
-    )(frame_counts, by_head)
-    cot_swapped = swap_plane(cot_mine, 0)
+    )(frame_counts, *by_head)
     x_same, y_cross = swap(same, 2), swap(cross, 4 ^ 1)
     y_same, x_cross, c_cross = swap(same, 4), swap(cross, 2 ^ 1), swap(cross, 1)
     far_same, far_cross = swap(x_same, 4), swap(y_cross, 2)
 
-    turned_shape = ((cols, -(-half * cot_rows // HD) * HD), bf16)
-    turned_own, turned_give = call(
+    turned_own, turned_other = call(
         lambda *refs: turn_kernel(lo, clip_rows, cot_rows, *refs),
         "turn",
-        [turned_shape] * 2,
-        [vmem] * 2 + [hbm] * 4,
+        [((cols, half * cot_rows), bf16)] * 2,
+        [vmem] * 2,
         0,
-    )(cot_mine, cot_swapped, x_same, y_cross, x_cross, y_same)
-    turned_other = swap(turned_give, 1)
+    )(cot_mine, cot_swapped)
 
     def grad(turned, heads, dtype, name):
         (out,) = call(

time: 71 us -> 68.8 us (0.969)
  blocking collectives: 32.8 us -> 0 us
  waiting for transfers between devices: 17.3 us -> 33 us
  starting transfers between devices: 8.15 us -> 20.2 us
  Pallas kernels: 11.9 us -> 13.7 us
  local copies, waits for them, and re-layouts: 0.01 us -> 0.92 us
    all_to_all x1 -> x0, blocking collectives: 32.8 us -> none  [head_body(): by_head = lax.all_to_all(packed, 'tm', 0, 0)]
    ppermute x10 -> x19, waiting for transfers between devices: 17.3 us -> 33 us  [swap(): return lax.ppermute(x, 'tm', [(i, i ^ bit) for i in range(n)])]
    ppermute x10 -> x19, starting transfers between devices: 6.51 us -> 18.4 us  [swap(): return lax.ppermute(x, 'tm', [(i, i ^ bit) for i in range(n)])]
    pallas_call x1 -> x3, Pallas kernels: 2.92 us -> 4.82 us  [the longest x1 2.68 us: head_body(): call(lambda *refs: pack_kernel(n, *refs), 'pack', [((length, HD), bf16)]...]
    unnamed x2 -> x8, local copies, waits for them, and re-layouts: 0.01 us -> 0.92 us
  transfers between devices with their start and end apart: 11 -> 20, of which waited for: 5 -> 9; matrix products, arithmetic and copies ran while one was open for 0% -> 0% of each run, Pallas kernels for 3% -> 14%
where the time goes in v1:
time: 68.8 us; the launch traced here: 68.6 us
  waiting for transfers between devices  33 us (48%)
  starting transfers between devices  20.2 us (29%)
  Pallas kernels  13.7 us (20%)
  local copies, waits for them, and re-layouts  0.92 us (1%)
  between operations  0.76 us (1%)
    ppermute x19, waiting for transfers between devices, swap(): return lax.ppermute(x, 'tm', [(i, i ^ bit) for i in range(n)])  33 us
    ppermute x19, starting transfers between devices, swap(): return lax.ppermute(x, 'tm', [(i, i ^ bit) for i in range(n)])  18.4 us
    pallas_call x1, Pallas kernels, head_body(): call(lambda *refs: attend_kernel(n, tok, *refs), 'attend', [head_shape, h...  5.11 us
    pallas_call x1, Pallas kernels, head_body(): call(lambda *refs: pack_kernel(n, *refs), 'pack', [((length, HD), bf16)]...  2.68 us
    pallas_call x1, Pallas kernels, head_body(): call(lambda *refs: cot_kernel(n, tile, lo, *refs), 'cot', [((2 * units *...  2.1 us
    pallas_call x4, Pallas kernels, grad(): call(lambda *refs: grad_kernel(rows, half, *refs), name, [((cols, len(hea...  1.99 us
    ppermute x1, starting transfers between devices, swap_plane(): return lax.ppermute(x, ('tm', 'head'), pairs)  1.72 us
    pallas_call x1, Pallas kernels, head_body(): call(lambda *refs: finish_kernel(n, tok, *refs), 'finish', [((tok, width)...  1.43 us
  transfers between devices with their start and end apart: 20, of which 9 were waited for; matrix products, arithmetic and copies ran while one was open for 0% of the time, Pallas kernels for 14%

profile of v1, /device:TPU:0, one launch (start us, length us, event | category | flops | bytes accessed | tf_op | source)
XLA Modules:
  0.0 68.6 jit_solution(10907210456978373503)
XLA Ops:
  0.6 2.7 %pack.1 = (bf16[784,128]{1,0:T(8,128)(2,1)}, bf16[784,128]{1,0:T(8,128)(2,1)}, bf16[784,128]{1,0:T(8,128)(2,1)}, bf16[784,128]{1,0:T(8,128)(2,1)}, bf16[784,128]...) custom-call(bf16[256,1024]{1,0:T(8,128)(2,1)} %refs_0_.4, ...), custom_call_target="tpu_custom_call" | custom-call | bytes 3211264 | tf_op jit(solution)/shard_map/pack/pallas_call | solution.py:324
  3.3 0.5 collective-permute-start.4
  3.9 2.6 %collective-permute-start.5 = (bf16[784,128]{1,0:T(8,128)(2,1)}, bf16[784,128]{1,0:T(8,128)(2,1)S(1)}, u32[]{:S(2)}, u32[]{:S(2)}) collective-permute-start(bf16[784,128]{1,0:T(8,128)(2,1)} %get-tuple-element.25), channel_id=1, source_target_pairs={{0,8},{4,12},{8,0},{12,4},{16,24},{20,28},{24,16},{28,20},{1,9},{5... | collective-permute-start | bytes 602120 | tf_op jit(solution)/shard_map/ppermute | solution.py:285
  6.4 2.1 %cot.1 = (bf16[576,128]{1,0:T(8,128)(2,1)}, bf16[576,128]{1,0:T(8,128)(2,1)}, bf16[576,128]{1,0:T(8,128)(2,1)}, bf16[576,128]{1,0:T(8,128)(2,1)}) custom-call(s32[1,8]{1,0:T(1,128)} %refs_0_.3, bf16[272,2048]{1,0:T(8,128)(2,1)} %refs_1_.2), custom_call_target="tpu_custom_call" | custom-call | bytes 1179648 | tf_op jit(solution)/shard_map/cot/pallas_call | solution.py:310
  8.6 2.0 %collective-permute-start.1 = (bf16[576,128]{1,0:T(8,128)(2,1)}, bf16[576,128]{1,0:T(8,128)(2,1)S(1)}, u32[]{:S(2)}, u32[]{:S(2)}) collective-permute-start(bf16[576,128]{1,0:T(8,128)(2,1)} %get-tuple-element.20), channel_id=1, source_target_pairs={{0,16},{4,20},{8,24},{12,28},{16,0},{20,4},{24,8},{28,12},{1,17},{... | collective-permute-start | bytes 442376 | tf_op jit(solution)/shard_map/ppermute | solution.py:285
  10.7 1.4 %collective-permute-start.2 = (bf16[576,128]{1,0:T(8,128)(2,1)}, bf16[576,128]{1,0:T(8,128)(2,1)S(1)}, u32[]{:S(2)}, u32[]{:S(2)}) collective-permute-start(bf16[576,128]{1,0:T(8,128)(2,1)} %get-tuple-element.21), channel_id=1, source_target_pairs={{0,24},{4,28},{8,16},{12,20},{16,8},{20,12},{24,0},{28,4},{1,25},{... | collective-permute-start | bytes 442376 | tf_op jit(solution)/shard_map/ppermute | solution.py:285
  12.1 3.6 %collective-permute-done.refs_1_ = bf16[576,128]{1,0:T(8,128)(2,1)S(1)} collective-permute-done((bf16[576,128]{1,0:T(8,128)(2,1)}, bf16[576,128]{1,0:T(8,128)(2,1)S(1)}, u32[]{:S(2)}, u32[]{:S(2)}) %collective-permute-start) | collective-permute-done | bytes 147488 | tf_op jit(solution)/shard_map/ppermute | solution.py:285
  15.7 0.7 %collective-permute-start.6 = (bf16[784,128]{1,0:T(8,128)(2,1)}, bf16[784,128]{1,0:T(8,128)(2,1)S(1)}, u32[]{:S(2)}, u32[]{:S(2)}) collective-permute-start(bf16[784,128]{1,0:T(8,128)(2,1)} %get-tuple-element.26), channel_id=1, source_target_pairs={{0,12},{4,8},{8,4},{12,0},{16,28},{20,24},{24,20},{28,16},{1,13},{... | collective-permute-start | bytes 602120 | tf_op jit(solution)/shard_map/ppermute | solution.py:285
  16.4 1.5 %collective-permute-start.7 = (bf16[784,128]{1,0:T(8,128)(2,1)}, bf16[784,128]{1,0:T(8,128)(2,1)S(1)}, u32[]{:S(2)}, u32[]{:S(2)}) collective-permute-start(bf16[784,128]{1,0:T(8,128)(2,1)} %get-tuple-element.27), channel_id=1, source_target_pairs={{0,16},{4,20},{8,24},{12,28},{16,0},{20,4},{24,8},{28,12},{1,17},{... | collective-permute-start | bytes 602120 | tf_op jit(solution)/shard_map/ppermute | solution.py:285
  17.9 1.9 %collective-permute-done.2.refs_3_ = bf16[576,128]{1,0:T(8,128)(2,1)S(1)} collective-permute-done((bf16[576,128]{1,0:T(8,128)(2,1)}, bf16[576,128]{1,0:T(8,128)(2,1)S(1)}, u32[]{:S(2)}, u32[]{:S(2)}) %collective-permute-start.2) | collective-permute-done | bytes 147488 | tf_op jit(solution)/shard_map/ppermute | solution.py:285
  19.8 2.2 %collective-permute-start.9 = (bf16[784,128]{1,0:T(8,128)(2,1)}, bf16[784,128]{1,0:T(8,128)(2,1)S(1)}, u32[]{:S(2)}, u32[]{:S(2)}) collective-permute-start(bf16[784,128]{1,0:T(8,128)(2,1)} %get-tuple-element.29), channel_id=1, source_target_pairs={{0,24},{4,28},{8,16},{12,20},{16,8},{20,12},{24,0},{28,4},{1,25},{... | collective-permute-start | bytes 602120 | tf_op jit(solution)/shard_map/ppermute | solution.py:285
  22.0 0.6 collective-permute-start.10
  22.6 0.9 %copy-done = bf16[576,128]{1,0:T(8,128)(2,1)S(1)} copy-done((bf16[576,128]{1,0:T(8,128)(2,1)S(1)}, bf16[576,128]{1,0:T(8,128)(2,1)}, u32[]{:S(2)}) %copy-start) | copy-done | bytes 147480
  23.5 1.7 %collective-permute-start.3 = (bf16[4,576,128]{2,1,0:T(8,128)(2,1)S(1)}, bf16[4,576,128]{2,1,0:T(8,128)(2,1)S(1)}, u32[]{:S(2)}, u32[]{:S(2)}) collective-permute-start(bf16[4,576,128]{2,1,0:T(8,128)(2,1)S(1)} %stack.1.refs_0_), channel_id=1, source_target_pairs={{0,1},{1,0},{2,3},{3,2},{4,5},{5,4},{6,7},{7,6},{8,9},{9,8},{10,11... | collective-permute-start | bytes 1769480 | tf_op jit(solution)/shard_map/ppermute | solution.py:291
  25.2 12.1 %collective-permute-done.8.refs_6_ = bf16[784,128]{1,0:T(8,128)(2,1)S(1)} collective-permute-done((bf16[784,128]{1,0:T(8,128)(2,1)}, bf16[784,128]{1,0:T(8,128)(2,1)S(1)}, u32[]{:S(2)}, u32[]{:S(2)}) %collective-permute-start.8) | collective-permute-done | bytes 200736 | tf_op jit(solution)/shard_map/ppermute | solution.py:285
  37.4 5.1 %attend.1 = (bf16[1040,128]{1,0:T(8,128)(2,1)S(1)}, bf16[1040,128]{1,0:T(8,128)(2,1)S(1)}) custom-call(s32[8]{0:T(128)S(1)} %copy-done.2, bf16[784,128]{1,0:T(8,128)(2,1)S(1)} %copy-done.1, bf16[784,128]{1,0:T(8,128)(2,1)S(1)} %collective-permute-done.4.refs_2_, bf16[784,128]{1,0:T(8,128)(2,1)S(1)} %collective-permute-done.5.refs_3_, ...), custom_call_target="tpu_custom_call" | custom-call | flops 1073741824 | bytes 1064960 | tf_op jit(solution)/shard_map/attend/pallas_call | solution.py:352
  42.5 1.0 %collective-permute-start.15 = (bf16[1040,128]{1,0:T(8,128)(2,1)S(1)}, bf16[1040,128]{1,0:T(8,128)(2,1)S(1)}, u32[]{:S(2)}, u32[]{:S(2)}) collective-permute-start(bf16[1040,128]{1,0:T(8,128)(2,1)S(1)} %get-tuple-element.32), channel_id=1, source_target_pairs={{0,20},{4,16},{8,28},{12,24},{16,4},{20,0},{24,12},{28,8},{1,21},{... | collective-permute-start | bytes 798728 | tf_op jit(solution)/shard_map/ppermute | solution.py:285
  43.5 1.2 %collective-permute-start.12 = (bf16[1040,128]{1,0:T(8,128)(2,1)S(1)}, bf16[1040,128]{1,0:T(8,128)(2,1)S(1)}, u32[]{:S(2)}, u32[]{:S(2)}) collective-permute-start(bf16[1040,128]{1,0:T(8,128)(2,1)S(1)} %get-tuple-element.31.refs_1_.refs_4_), channel_id=1, source_target_pairs={{0,8},{4,12},{8,0},{12,4},{16,24},{20,28},{24,16},{28,20},{1,9},{5... | collective-permute-start | bytes 798728 | tf_op jit(solution)/shard_map/ppermute | solution.py:285
  44.7 0.8 %collective-permute-start.13 = (bf16[1040,128]{1,0:T(8,128)(2,1)S(1)}, bf16[1040,128]{1,0:T(8,128)(2,1)S(1)}, u32[]{:S(2)}, u32[]{:S(2)}) collective-permute-start(bf16[1040,128]{1,0:T(8,128)(2,1)S(1)} %get-tuple-element.32), channel_id=1, source_target_pairs={{0,12},{4,8},{8,4},{12,0},{16,28},{20,24},{24,20},{28,16},{1,13},{... | collective-permute-start | bytes 798728 | tf_op jit(solution)/shard_map/ppermute | solution.py:285
  45.7 5.5 %collective-permute-done.15.refs_6_.refs_9_ = bf16[1040,128]{1,0:T(8,128)(2,1)S(1)} collective-permute-done((bf16[1040,128]{1,0:T(8,128)(2,1)S(1)}, bf16[1040,128]{1,0:T(8,128)(2,1)S(1)}, u32[]{:S(2)}, u32[]{:S(2)}) %collective-permute-start.15) | collective-permute-done | bytes 266272 | tf_op jit(solution)/shard_map/ppermute | solution.py:285
  51.2 1.6 %collective-permute-start.14 = (bf16[1040,128]{1,0:T(8,128)(2,1)S(1)}, bf16[1040,128]{1,0:T(8,128)(2,1)S(1)}, u32[]{:S(2)}, u32[]{:S(2)}) collective-permute-start(bf16[1040,128]{1,0:T(8,128)(2,1)S(1)} %get-tuple-element.31.refs_1_.refs_4_), channel_id=1, source_target_pairs={{0,16},{4,20},{8,24},{12,28},{16,0},{20,4},{24,8},{28,12},{1,17},{... | collective-permute-start | bytes 798728 | tf_op jit(solution)/shard_map/ppermute | solution.py:285
  52.8 1.2 %collective-permute-start.17 = (bf16[1040,128]{1,0:T(8,128)(2,1)S(1)}, bf16[1040,128]{1,0:T(8,128)(2,1)S(1)}, u32[]{:S(2)}, u32[]{:S(2)}) collective-permute-start(bf16[1040,128]{1,0:T(8,128)(2,1)S(1)} %collective-permute-done.15.refs_6_.refs_9_), channel_id=1, source_target_pairs={{0,8},{4,12},{8,0},{12,4},{16,24},{20,28},{24,16},{28,20},{1,9},{5... | collective-permute-start | bytes 798728 | tf_op jit(solution)/shard_map/ppermute | solution.py:285
  54.0 0.7 collective-permute-start.16
  54.6 0.4 turn.1
  55.0 2.9 %collective-permute-done.13.refs_4_.refs_7_ = bf16[1040,128]{1,0:T(8,128)(2,1)S(1)} collective-permute-done((bf16[1040,128]{1,0:T(8,128)(2,1)S(1)}, bf16[1040,128]{1,0:T(8,128)(2,1)S(1)}, u32[]{:S(2)}, u32[]{:S(2)}) %collective-permute-start.13) | collective-permute-done | bytes 266272 | tf_op jit(solution)/shard_map/ppermute | solution.py:285
  57.9 2.5 %collective-permute-done.14.refs_5_.refs_8_ = bf16[1040,128]{1,0:T(8,128)(2,1)S(1)} collective-permute-done((bf16[1040,128]{1,0:T(8,128)(2,1)S(1)}, bf16[1040,128]{1,0:T(8,128)(2,1)S(1)}, u32[]{:S(2)}, u32[]{:S(2)}) %collective-permute-start.14) | collective-permute-done | bytes 266272 | tf_op jit(solution)/shard_map/ppermute | solution.py:285
  60.4 0.7 grad_other_near.1
  61.2 2.8 %collective-permute-done.17.refs_2_.refs_11_ = bf16[1040,128]{1,0:T(8,128)(2,1)S(1)} collective-permute-done((bf16[1040,128]{1,0:T(8,128)(2,1)S(1)}, bf16[1040,128]{1,0:T(8,128)(2,1)S(1)}, u32[]{:S(2)}, u32[]{:S(2)}) %collective-permute-start.17) | collective-permute-done | bytes 266272 | tf_op jit(solution)/shard_map/ppermute | solution.py:285
  63.9 1.5 %collective-permute-done.16.refs_1_.refs_10_ = bf16[1040,128]{1,0:T(8,128)(2,1)S(1)} collective-permute-done((bf16[1040,128]{1,0:T(8,128)(2,1)S(1)}, bf16[1040,128]{1,0:T(8,128)(2,1)S(1)}, u32[]{:S(2)}, u32[]{:S(2)}) %collective-permute-start.16) | collective-permute-done | bytes 266272 | tf_op jit(solution)/shard_map/ppermute | solution.py:285
  65.8 0.3 grad_own_far.1.refs_1_
  66.1 0.7 grad_own_near.1.refs_0_
  67.1 1.4 %finish.1 = (bf16[256,1024]{1,0:T(8,128)(2,1)}, f32[256,1024]{1,0:T(8,128)}) custom-call(f32[256,768]{1,0:T(8,128)S(1)} %grad_own_near.1.refs_0_, f32[256,256]{1,0:T(8,128)S(1)} %grad_own_far.1.refs_1_, bf16[256,768]{1,0:T(8,128)(2,1)S(1)} %collective-permute-done.18.refs_2_, bf16[256,256]{1,0:T(8,128)(2,1)S(1)} %collective-permute-done.19.refs_3_, ...), custom_call_target="tpu_custom_call" | custom-call | bytes 3145728 | tf_op jit(solution)/shard_map/finish/pallas_call | solution.py:389
  (26 shorter events, 1.1 us)
Async XLA Ops:
  3.3 18.6 %copy-start.3 = (bf16[784,128]{1,0:T(8,128)(2,1)S(1)}, bf16[784,128]{1,0:T(8,128)(2,1)}, u32[]{:S(2)}) copy-start(bf16[784,128]{1,0:T(8,128)(2,1)} %get-tuple-element.30) | copy-start | bytes 602116
  3.3 16.4 %collective-permute-start.4 = (bf16[784,128]{1,0:T(8,128)(2,1)}, bf16[784,128]{1,0:T(8,128)(2,1)S(1)}, u32[]{:S(2)}, u32[]{:S(2)}) collective-permute-start(bf16[784,128]{1,0:T(8,128)(2,1)} %get-tuple-element.24), channel_id=1, source_target_pairs={{0,4},{4,0},{8,12},{12,8},{16,20},{20,16},{24,28},{28,24},{1,5},{5... | collective-permute-start | bytes 602120 | tf_op jit(solution)/shard_map/ppermute | solution.py:285
  3.9 33.5 %copy-start.1 = (bf16[784,128]{1,0:T(8,128)(2,1)S(1)}, bf16[784,128]{1,0:T(8,128)(2,1)}, u32[]{:S(2)}) copy-start(bf16[784,128]{1,0:T(8,128)(2,1)} %get-tuple-element.23.refs_1_) | copy-start | bytes 602116
  3.9 33.5 %copy-start.2 = (s32[8]{0:T(128)S(1)}, s32[8]{0:T(128)}, u32[]{:S(2)}) copy-start(s32[8]{0:T(128)} %refs_0_.5) | copy-start | bytes 100
  3.9 18.1 %collective-permute-start.5 = (bf16[784,128]{1,0:T(8,128)(2,1)}, bf16[784,128]{1,0:T(8,128)(2,1)S(1)}, u32[]{:S(2)}, u32[]{:S(2)}) collective-permute-start(bf16[784,128]{1,0:T(8,128)(2,1)} %get-tuple-element.25), channel_id=1, source_target_pairs={{0,8},{4,12},{8,0},{12,4},{16,24},{20,28},{24,16},{28,20},{1,9},{5... | collective-permute-start | bytes 602120 | tf_op jit(solution)/shard_map/ppermute | solution.py:285
  8.5 7.1 %collective-permute-start = (bf16[576,128]{1,0:T(8,128)(2,1)}, bf16[576,128]{1,0:T(8,128)(2,1)S(1)}, u32[]{:S(2)}, u32[]{:S(2)}) collective-permute-start(bf16[576,128]{1,0:T(8,128)(2,1)} %get-tuple-element.19), channel_id=1, source_target_pairs={{0,8},{4,12},{8,0},{12,4},{16,24},{20,28},{24,16},{28,20},{1,9},{5... | collective-permute-start | bytes 442376 | tf_op jit(solution)/shard_map/ppermute | solution.py:285
  8.6 7.7 %collective-permute-start.1 = (bf16[576,128]{1,0:T(8,128)(2,1)}, bf16[576,128]{1,0:T(8,128)(2,1)S(1)}, u32[]{:S(2)}, u32[]{:S(2)}) collective-permute-start(bf16[576,128]{1,0:T(8,128)(2,1)} %get-tuple-element.20), channel_id=1, source_target_pairs={{0,16},{4,20},{8,24},{12,28},{16,0},{20,4},{24,8},{28,12},{1,17},{... | collective-permute-start | bytes 442376 | tf_op jit(solution)/shard_map/ppermute | solution.py:285
  10.7 9.1 %collective-permute-start.2 = (bf16[576,128]{1,0:T(8,128)(2,1)}, bf16[576,128]{1,0:T(8,128)(2,1)S(1)}, u32[]{:S(2)}, u32[]{:S(2)}) collective-permute-start(bf16[576,128]{1,0:T(8,128)(2,1)} %get-tuple-element.21), channel_id=1, source_target_pairs={{0,24},{4,28},{8,16},{12,20},{16,8},{20,12},{24,0},{28,4},{1,25},{... | collective-permute-start | bytes 442376 | tf_op jit(solution)/shard_map/ppermute | solution.py:285
  15.7 7.9 %collective-permute-start.6 = (bf16[784,128]{1,0:T(8,128)(2,1)}, bf16[784,128]{1,0:T(8,128)(2,1)S(1)}, u32[]{:S(2)}, u32[]{:S(2)}) collective-permute-start(bf16[784,128]{1,0:T(8,128)(2,1)} %get-tuple-element.26), channel_id=1, source_target_pairs={{0,12},{4,8},{8,4},{12,0},{16,28},{20,24},{24,20},{28,16},{1,13},{... | collective-permute-start | bytes 602120 | tf_op jit(solution)/shard_map/ppermute | solution.py:285
  16.4 8.9 %collective-permute-start.7 = (bf16[784,128]{1,0:T(8,128)(2,1)}, bf16[784,128]{1,0:T(8,128)(2,1)S(1)}, u32[]{:S(2)}, u32[]{:S(2)}) collective-permute-start(bf16[784,128]{1,0:T(8,128)(2,1)} %get-tuple-element.27), channel_id=1, source_target_pairs={{0,16},{4,20},{8,24},{12,28},{16,0},{20,4},{24,8},{28,12},{1,17},{... | collective-permute-start | bytes 602120 | tf_op jit(solution)/shard_map/ppermute | solution.py:285
  19.8 17.6 %collective-permute-start.8 = (bf16[784,128]{1,0:T(8,128)(2,1)}, bf16[784,128]{1,0:T(8,128)(2,1)S(1)}, u32[]{:S(2)}, u32[]{:S(2)}) collective-permute-start(bf16[784,128]{1,0:T(8,128)(2,1)} %get-tuple-element.28), channel_id=1, source_target_pairs={{0,20},{4,16},{8,28},{12,24},{16,4},{20,0},{24,12},{28,8},{1,21},{... | collective-permute-start | bytes 602120 | tf_op jit(solution)/shard_map/ppermute | solution.py:285
  19.8 17.6 %collective-permute-start.9 = (bf16[784,128]{1,0:T(8,128)(2,1)}, bf16[784,128]{1,0:T(8,128)(2,1)S(1)}, u32[]{:S(2)}, u32[]{:S(2)}) collective-permute-start(bf16[784,128]{1,0:T(8,128)(2,1)} %get-tuple-element.29), channel_id=1, source_target_pairs={{0,24},{4,28},{8,16},{12,20},{16,8},{20,12},{24,0},{28,4},{1,25},{... | collective-permute-start | bytes 602120 | tf_op jit(solution)/shard_map/ppermute | solution.py:285
  22.0 15.4 %collective-permute-start.10 = (bf16[784,128]{1,0:T(8,128)(2,1)S(1)}, bf16[784,128]{1,0:T(8,128)(2,1)S(1)}, u32[]{:S(2)}, u32[]{:S(2)}) collective-permute-start(bf16[784,128]{1,0:T(8,128)(2,1)S(1)} %copy-done.3), channel_id=1, source_target_pairs={{0,28},{4,24},{8,20},{12,16},{16,12},{20,8},{24,4},{28,0},{1,29},{... | collective-permute-start | bytes 602120 | tf_op jit(solution)/shard_map/ppermute | solution.py:285
  22.6 0.9 %copy-start = (bf16[576,128]{1,0:T(8,128)(2,1)S(1)}, bf16[576,128]{1,0:T(8,128)(2,1)}, u32[]{:S(2)}) copy-start(bf16[576,128]{1,0:T(8,128)(2,1)} %get-tuple-element.18.refs_0_) | copy-start | bytes 442372
  23.5 30.5 %collective-permute-start.3 = (bf16[4,576,128]{2,1,0:T(8,128)(2,1)S(1)}, bf16[4,576,128]{2,1,0:T(8,128)(2,1)S(1)}, u32[]{:S(2)}, u32[]{:S(2)}) collective-permute-start(bf16[4,576,128]{2,1,0:T(8,128)(2,1)S(1)} %stack.1.refs_0_), channel_id=1, source_target_pairs={{0,1},{1,0},{2,3},{3,2},{4,5},{5,4},{6,7},{7,6},{8,9},{9,8},{10,11... | collective-permute-start | bytes 1769480 | tf_op jit(solution)/shard_map/ppermute | solution.py:291
  42.5 8.7 %collective-permute-start.15 = (bf16[1040,128]{1,0:T(8,128)(2,1)S(1)}, bf16[1040,128]{1,0:T(8,128)(2,1)S(1)}, u32[]{:S(2)}, u32[]{:S(2)}) collective-permute-start(bf16[1040,128]{1,0:T(8,128)(2,1)S(1)} %get-tuple-element.32), channel_id=1, source_target_pairs={{0,20},{4,16},{8,28},{12,24},{16,4},{20,0},{24,12},{28,8},{1,21},{... | collective-permute-start | bytes 798728 | tf_op jit(solution)/shard_map/ppermute | solution.py:285
  43.5 9.3 %collective-permute-start.12 = (bf16[1040,128]{1,0:T(8,128)(2,1)S(1)}, bf16[1040,128]{1,0:T(8,128)(2,1)S(1)}, u32[]{:S(2)}, u32[]{:S(2)}) collective-permute-start(bf16[1040,128]{1,0:T(8,128)(2,1)S(1)} %get-tuple-element.31.refs_1_.refs_4_), channel_id=1, source_target_pairs={{0,8},{4,12},{8,0},{12,4},{16,24},{20,28},{24,16},{28,20},{1,9},{5... | collective-permute-start | bytes 798728 | tf_op jit(solution)/shard_map/ppermute | solution.py:285
  44.7 13.2 %collective-permute-start.13 = (bf16[1040,128]{1,0:T(8,128)(2,1)S(1)}, bf16[1040,128]{1,0:T(8,128)(2,1)S(1)}, u32[]{:S(2)}, u32[]{:S(2)}) collective-permute-start(bf16[1040,128]{1,0:T(8,128)(2,1)S(1)} %get-tuple-element.32), channel_id=1, source_target_pairs={{0,12},{4,8},{8,4},{12,0},{16,28},{20,24},{24,20},{28,16},{1,13},{... | collective-permute-start | bytes 798728 | tf_op jit(solution)/shard_map/ppermute | solution.py:285
  45.6 12.4 %collective-permute-start.11 = (bf16[1040,128]{1,0:T(8,128)(2,1)S(1)}, bf16[1040,128]{1,0:T(8,128)(2,1)S(1)}, u32[]{:S(2)}, u32[]{:S(2)}) collective-permute-start(bf16[1040,128]{1,0:T(8,128)(2,1)S(1)} %get-tuple-element.32), channel_id=1, source_target_pairs={{0,4},{4,0},{8,12},{12,8},{16,20},{20,16},{24,28},{28,24},{1,5},{5... | collective-permute-start | bytes 798728 | tf_op jit(solution)/shard_map/ppermute | solution.py:285
  51.2 9.2 %collective-permute-start.14 = (bf16[1040,128]{1,0:T(8,128)(2,1)S(1)}, bf16[1040,128]{1,0:T(8,128)(2,1)S(1)}, u32[]{:S(2)}, u32[]{:S(2)}) collective-permute-start(bf16[1040,128]{1,0:T(8,128)(2,1)S(1)} %get-tuple-element.31.refs_1_.refs_4_), channel_id=1, source_target_pairs={{0,16},{4,20},{8,24},{12,28},{16,0},{20,4},{24,8},{28,12},{1,17},{... | collective-permute-start | bytes 798728 | tf_op jit(solution)/shard_map/ppermute | solution.py:285
  52.8 11.1 %collective-permute-start.17 = (bf16[1040,128]{1,0:T(8,128)(2,1)S(1)}, bf16[1040,128]{1,0:T(8,128)(2,1)S(1)}, u32[]{:S(2)}, u32[]{:S(2)}) collective-permute-start(bf16[1040,128]{1,0:T(8,128)(2,1)S(1)} %collective-permute-done.15.refs_6_.refs_9_), channel_id=1, source_target_pairs={{0,8},{4,12},{8,0},{12,4},{16,24},{20,28},{24,16},{28,20},{1,9},{5... | collective-permute-start | bytes 798728 | tf_op jit(solution)/shard_map/ppermute | solution.py:285
  54.0 11.4 %collective-permute-start.16 = (bf16[1040,128]{1,0:T(8,128)(2,1)S(1)}, bf16[1040,128]{1,0:T(8,128)(2,1)S(1)}, u32[]{:S(2)}, u32[]{:S(2)}) collective-permute-start(bf16[1040,128]{1,0:T(8,128)(2,1)S(1)} %collective-permute-done.12.refs_3_.refs_6_), channel_id=1, source_target_pairs={{0,16},{4,20},{8,24},{12,28},{16,0},{20,4},{24,8},{28,12},{1,17},{... | collective-permute-start | bytes 798728 | tf_op jit(solution)/shard_map/ppermute | solution.py:285
  61.1 6.0 %collective-permute-start.18 = (bf16[256,768]{1,0:T(8,128)(2,1)S(1)}, bf16[256,768]{1,0:T(8,128)(2,1)S(1)}, u32[]{:S(2)}, u32[]{:S(2)}) collective-permute-start(bf16[256,768]{1,0:T(8,128)(2,1)S(1)} %grad_other_near.1), channel_id=1, source_target_pairs={{0,4},{4,0},{8,12},{12,8},{16,20},{20,16},{24,28},{28,24},{1,5},{5... | collective-permute-start | bytes 1179656 | tf_op jit(solution)/shard_map/ppermute | solution.py:285
  65.7 1.4 %collective-permute-start.19 = (bf16[256,256]{1,0:T(8,128)(2,1)S(1)}, bf16[256,256]{1,0:T(8,128)(2,1)S(1)}, u32[]{:S(2)}, u32[]{:S(2)}) collective-permute-start(bf16[256,256]{1,0:T(8,128)(2,1)S(1)} %grad_other_far.1), channel_id=1, source_target_pairs={{0,4},{4,0},{8,12},{12,8},{16,20},{20,16},{24,28},{28,24},{1,5},{5... | collective-permute-start | bytes 393224 | tf_op jit(solution)/shard_map/ppermute | solution.py:285

commit v2 on v1

--- a/solution.py
+++ b/solution.py
@@ -10,7 +10,7 @@
 HD = 128
 TPF = 64
 WINB = 4
-VMEM_LIMIT = 32 * 1024 * 1024
+VMEM_LIMIT = 24 * 1024 * 1024
 PACK_LIMIT = 63 * 1024 * 1024
 
 
@@ -74,7 +74,7 @@
     return (attended, disc_grad)
 
 
-def cot_kernel(n, tile, lo, off_hbm, cot_hbm, *refs):
+def cot_kernel(n, tile, lo, off_hbm, cot_hbm, behind_a, behind_b, *refs):
     outs, (off, cot, sems) = refs[:-3], refs[-3:]
     own = lax.axis_index("tm")
     chip, side = own // 2, lax.rem(own, 2)
@@ -180,13 +180,13 @@
     out_ref[rows:, :] = hist.astype(jnp.bfloat16)
 
 
-def attend_kernel(n, tok, counts_hbm, *refs):
+def attend_kernel(n, tok, order, counts_hbm, *refs):
     parts, (same_ref, cross_ref, x_ref, counts, sem) = refs[:n], refs[n:]
     copy = pltpu.make_async_copy(counts_hbm, counts, sem)
     copy.start()
     own = lax.axis_index("tm")
     side = lax.rem(own, 2)
-    for k, part in enumerate(parts):
+    for k, part in zip(order, parts):
         x_ref[own ^ k] = part[...]
     copy.wait()
     attend_blocks(n, tok, side, counts, x_ref, same_ref)
@@ -195,8 +195,12 @@
 
 def stack_kernel(*refs):
     out_ref = refs[-1]
-    for i, x in enumerate(refs[:-1]):
+    for i, x in enumerate(refs[:-2]):
         out_ref[i] = x[...]
+
+
+def late_kernel(x_ref, behind, out_ref):
+    out_ref[...] = x_ref[...]
 
 
 def whole_cot(lo, part, plane, mine, swapped):
@@ -247,19 +251,22 @@
     out_ref[...] = grad_part(turned_ref, refs[:-1], rows, copies).astype(out_ref.dtype)
 
 
-def finish_kernel(n, tok, own_near, own_far, got_near, got_far, *refs):
+def finish_kernel(order, tok, own_near, own_far, got_near, got_far, *refs):
+    n = len(order)
     heads, att_ref, out_ref = refs[:n], refs[n], refs[n + 1]
     own = lax.axis_index("tm")
     at = pl.multiple_of(own // 2 * tok, tok)
     near = own_near.shape[1] // HD
-    for k in range(n):
+
+    def column(near_ref, far_ref, i):
+        ref, i = (near_ref, i) if i < near else (far_ref, i - near)
+        return ref[:, i * HD : (i + 1) * HD]
+
+    for i, k in enumerate(order):
         lanes = pl.ds(pl.multiple_of((own ^ k) * HD, HD), HD)
-        att_ref[:, lanes] = heads[k][pl.ds(at, tok), :]
-        mine, got, a = (own_near, got_near, k) if k < near else (own_far, got_far, k - near)
-        b = a ^ 1
-        out_ref[:, lanes] = mine[:, a * HD : (a + 1) * HD] + got[:, b * HD : (b + 1) * HD].astype(
-            jnp.float32
-        )
+        att_ref[:, lanes] = heads[i][pl.ds(at, tok), :]
+        got = column(got_near, got_far, order.index(k ^ 1))
+        out_ref[:, lanes] = column(own_near, own_far, i) + got.astype(jnp.float32)
 
 
 def head_body(query_rows, key_rows, value_rows, frame_counts, history, offsets, cotangent):
@@ -306,21 +313,6 @@
             name=name,
         )
 
-    chips = range(half)
-    cots = call(
-        lambda *refs: cot_kernel(n, tile, lo, *refs),
-        "cot",
-        [((2 * units * part, HD), bf16)] * half,
-        [hbm] * 2,
-        0,
-        (
-            pltpu.SMEM(offsets.shape, jnp.int32),
-            pltpu.VMEM((part, all_cols), bf16),
-            pltpu.SemaphoreType.DMA((2,)),
-        ),
-        limit=PACK_LIMIT,
-    )(offsets, cotangent)
-    cots = [cots[0]] + [swap(cots[m], 2 * m) for m in chips[1:]]
     packed = call(
         lambda *refs: pack_kernel(n, *refs),
         "pack",
@@ -336,12 +328,23 @@
         ),
         limit=PACK_LIMIT,
     )(query_rows, key_rows, value_rows, history)
-    by_head = [packed[0]] + [swap(packed[k], k) for k in range(1, n)]
-    (cot_mine,) = call(
-        stack_kernel, "stack", [((half, 2 * units * part, HD), bf16)], [vmem] * half, 0
-    )(*cots)
-    cot_swapped = swap_plane(cot_mine, 0)
-
+    order = [6, 7, 2, 4, 3, 5, 1]
+    arrived = {k: swap(packed[k], k) for k in order}
+    by_head = [packed[0]] + [arrived[k] for k in order]
+    chips = range(half)
+    cots = call(
+        lambda *refs: cot_kernel(n, tile, lo, *refs),
+        "cot",
+        [((2 * units * part, HD), bf16)] * half,
+        [hbm] * 4,
+        0,
+        (
+            pltpu.SMEM(offsets.shape, jnp.int32),
+            pltpu.VMEM((part, all_cols), bf16),
+            pltpu.SemaphoreType.DMA((2,)),
+        ),
+    )(offsets, cotangent, arrived[6], arrived[7])
+    cots = [cots[0]] + [swap(cots[m], 2 * m) for m in chips[1:]]
     counts = (
         pltpu.VMEM((n, length, HD), bf16),
         pltpu.SMEM(frame_counts.shape, jnp.int32),
@@ -350,7 +353,7 @@
     pairs = half * tok * WINB * tok
     head_shape = ((rows + clip_rows, HD), bf16)
     same, cross = call(
-        lambda *refs: attend_kernel(n, tok, *refs),
+        lambda *refs: attend_kernel(n, tok, [0] + order, *refs),
         "attend",
         [head_shape, head_shape],
         [hbm] + [vmem] * n,
@@ -358,9 +361,16 @@
         counts,
         2 * pairs,
     )(frame_counts, *by_head)
+    (cot_mine,) = call(
+        stack_kernel, "stack", [((half, 2 * units * part, HD), bf16)], [vmem] * half + [hbm], 0
+    )(*cots, same)
+    cot_swapped = swap_plane(cot_mine, 0)
+
     x_same, y_cross = swap(same, 2), swap(cross, 4 ^ 1)
-    y_same, x_cross, c_cross = swap(same, 4), swap(cross, 2 ^ 1), swap(cross, 1)
+    y_same, x_cross = swap(same, 4), swap(cross, 2 ^ 1)
     far_same, far_cross = swap(x_same, 4), swap(y_cross, 2)
+    (late_cross,) = call(late_kernel, "late", [head_shape], [vmem, hbm], 0)(cross, x_same)
+    c_cross = swap(late_cross, 1)
 
     turned_own, turned_other = call(
         lambda *refs: turn_kernel(lo, clip_rows, cot_rows, *refs),
@@ -380,14 +390,15 @@
         )(turned, *heads)
         return out
 
-    near = [same, c_cross, x_same, x_cross, y_same, y_cross]
+    near = [same, c_cross, x_cross, y_same, x_same, y_cross]
+    heads = [0, 1, 3, 4, 2, 5, 6, 7]
     far = [far_same, far_cross]
     got_near = swap(grad(turned_other, near, bf16, "grad_other_near"), 1)
     own_near = grad(turned_own, near, jnp.float32, "grad_own_near")
     got_far = swap(grad(turned_other, far, bf16, "grad_other_far"), 1)
     own_far = grad(turned_own, far, jnp.float32, "grad_own_far")
     return call(
-        lambda *refs: finish_kernel(n, tok, *refs),
+        lambda *refs: finish_kernel(heads, tok, *refs),
         "finish",
         [((tok, width), bf16), ((cols, width), jnp.float32)],
         [vmem] * (4 + n),

time: 68.8 us -> 59.4 us (0.86)
  waiting for transfers between devices: 33 us -> 28.5 us
  starting transfers between devices: 20.2 us -> 16.2 us
  Pallas kernels: 13.7 us -> 12.5 us
    ppermute x19, waiting for transfers between devices: 33 us -> 24.8 us  [swap(): return lax.ppermute(x, 'tm', [(i, i ^ bit) for i in range(n)])]
    ppermute x19, starting transfers between devices: 18.4 us -> 14.6 us  [swap(): return lax.ppermute(x, 'tm', [(i, i ^ bit) for i in range(n)])]
    ppermute x1, waiting for transfers between devices: 0.01 us -> 3.68 us  [swap_plane(): return lax.ppermute(x, ('tm', 'head'), pairs)]
    pallas_call x1, Pallas kernels: 2.1 us -> 0.88 us  [head_body(): call(lambda *refs: cot_kernel(n, tile, lo, *refs), 'cot', [((2 * units *...]
    pallas_call x2 -> x3, Pallas kernels: 6.55 us -> 6.58 us  [the longest x1 5.12 us: head_body(): call(lambda *refs: attend_kernel(n, tok, [0] + order, *refs), 'attend', [...]
where the time goes in v2:
time: 59.4 us; the launch traced here: 59.3 us
  waiting for transfers between devices  28.5 us (48%)
  starting transfers between devices  16.2 us (27%)
  Pallas kernels  12.5 us (21%)
  local copies, waits for them, and re-layouts  1.26 us (2%)
  between operations  0.82 us (1%)
    ppermute x19, waiting for transfers between devices, swap(): return lax.ppermute(x, 'tm', [(i, i ^ bit) for i in range(n)])  24.8 us
    ppermute x19, starting transfers between devices, swap(): return lax.ppermute(x, 'tm', [(i, i ^ bit) for i in range(n)])  14.6 us
    pallas_call x1, Pallas kernels, head_body(): call(lambda *refs: attend_kernel(n, tok, [0] + order, *refs), 'attend', [...  5.12 us
    ppermute x1, waiting for transfers between devices, swap_plane(): return lax.ppermute(x, ('tm', 'head'), pairs)  3.68 us
    pallas_call x1, Pallas kernels, head_body(): call(lambda *refs: pack_kernel(n, *refs), 'pack', [((length, HD), bf16)]...  2.69 us
    pallas_call x4, Pallas kernels, grad(): call(lambda *refs: grad_kernel(rows, half, *refs), name, [((cols, len(hea...  1.98 us
    ppermute x1, starting transfers between devices, swap_plane(): return lax.ppermute(x, ('tm', 'head'), pairs)  1.64 us
    pallas_call x1, Pallas kernels, head_body(): call(lambda *refs: finish_kernel(heads, tok, *refs), 'finish', [((tok, wi...  1.45 us
  transfers between devices with their start and end apart: 20, of which 9 were waited for; matrix products, arithmetic and copies ran while one was open for 0% of the time, Pallas kernels for 14%

profile of v2, /device:TPU:0, one launch (start us, length us, event | category | flops | bytes accessed | tf_op | source)
XLA Modules:
  0.0 59.3 jit_solution(3394769291986545078)
XLA Ops:
  0.6 2.7 %pack.1 = (bf16[784,128]{1,0:T(8,128)(2,1)}, bf16[784,128]{1,0:T(8,128)(2,1)}, bf16[784,128]{1,0:T(8,128)(2,1)}, bf16[784,128]{1,0:T(8,128)(2,1)}, bf16[784,128]...) custom-call(bf16[256,1024]{1,0:T(8,128)(2,1)} %refs_0_.3, ...), custom_call_target="tpu_custom_call" | custom-call | bytes 3211264 | tf_op jit(solution)/shard_map/pack/pallas_call | solution.py:316
  3.3 4.0 %collective-permute-start = (bf16[784,128]{1,0:T(8,128)(2,1)}, bf16[784,128]{1,0:T(8,128)(2,1)S(1)}, u32[]{:S(2)}, u32[]{:S(2)}) collective-permute-start(bf16[784,128]{1,0:T(8,128)(2,1)} %get-tuple-element.18), channel_id=1, source_target_pairs={{0,24},{4,28},{8,16},{12,20},{16,8},{20,12},{24,0},{28,4},{1,25},{... | collective-permute-start | bytes 602120 | tf_op jit(solution)/shard_map/ppermute | solution.py:292
  7.3 1.1 %collective-permute-start.5 = (bf16[784,128]{1,0:T(8,128)(2,1)}, bf16[784,128]{1,0:T(8,128)(2,1)S(1)}, u32[]{:S(2)}, u32[]{:S(2)}) collective-permute-start(bf16[784,128]{1,0:T(8,128)(2,1)} %get-tuple-element.25), channel_id=1, source_target_pairs={{0,8},{4,12},{8,0},{12,4},{16,24},{20,28},{24,16},{28,20},{1,9},{5... | collective-permute-start | bytes 602120 | tf_op jit(solution)/shard_map/ppermute | solution.py:292
  8.4 1.5 %collective-permute-start.6 = (bf16[784,128]{1,0:T(8,128)(2,1)}, bf16[784,128]{1,0:T(8,128)(2,1)S(1)}, u32[]{:S(2)}, u32[]{:S(2)}) collective-permute-start(bf16[784,128]{1,0:T(8,128)(2,1)} %get-tuple-element.26), channel_id=1, source_target_pairs={{0,16},{4,20},{8,24},{12,28},{16,0},{20,4},{24,8},{28,12},{1,17},{... | collective-permute-start | bytes 602120 | tf_op jit(solution)/shard_map/ppermute | solution.py:292
  10.0 0.6 collective-permute-start.7
  10.5 2.9 %collective-permute-done.refs_2_ = bf16[784,128]{1,0:T(8,128)(2,1)S(1)} collective-permute-done((bf16[784,128]{1,0:T(8,128)(2,1)}, bf16[784,128]{1,0:T(8,128)(2,1)S(1)}, u32[]{:S(2)}, u32[]{:S(2)}) %collective-permute-start) | collective-permute-done | bytes 200736 | tf_op jit(solution)/shard_map/ppermute | solution.py:292
  13.4 3.9 %collective-permute-done.1.refs_3_ = bf16[784,128]{1,0:T(8,128)(2,1)S(1)} collective-permute-done((bf16[784,128]{1,0:T(8,128)(2,1)}, bf16[784,128]{1,0:T(8,128)(2,1)S(1)}, u32[]{:S(2)}, u32[]{:S(2)}) %collective-permute-start.1) | collective-permute-done | bytes 200736 | tf_op jit(solution)/shard_map/ppermute | solution.py:292
  17.4 0.1 collective-permute-start.9
  17.5 1.2 %copy-done = bf16[272,2048]{1,0:T(8,128)(2,1)S(1)} copy-done((bf16[272,2048]{1,0:T(8,128)(2,1)S(1)}, bf16[272,2048]{1,0:T(8,128)(2,1)}, u32[]{:S(2)}) %copy-start) | copy-done | bytes 1114136
  18.8 0.9 %cot.1 = (bf16[576,128]{1,0:T(8,128)(2,1)S(1)}, bf16[576,128]{1,0:T(8,128)(2,1)S(1)}, bf16[576,128]{1,0:T(8,128)(2,1)S(1)}, bf16[576,128]{1,0:T(8,128)(2,1)S(1)}) custom-call(s32[1,8]{1,0:T(1,128)S(1)} %copy-done.1, bf16[272,2048]{1,0:T(8,128)(2,1)S(1)} %copy-done, bf16[784,128]{1,0:T(8,128)(2,1)S(1)} %collective-permute-done.refs_2_, ...), custom_call_target="tpu_custom_call" | custom-call | bytes 1179648 | tf_op jit(solution)/shard_map/cot/pallas_call | solution.py:335
  19.6 2.9 %collective-permute-done.5.refs_4_ = bf16[784,128]{1,0:T(8,128)(2,1)S(1)} collective-permute-done((bf16[784,128]{1,0:T(8,128)(2,1)}, bf16[784,128]{1,0:T(8,128)(2,1)S(1)}, u32[]{:S(2)}, u32[]{:S(2)}) %collective-permute-start.5) | collective-permute-done | bytes 200736 | tf_op jit(solution)/shard_map/ppermute | solution.py:292
  22.5 1.5 %collective-permute-start.2 = (bf16[576,128]{1,0:T(8,128)(2,1)S(1)}, bf16[576,128]{1,0:T(8,128)(2,1)S(1)}, u32[]{:S(2)}, u32[]{:S(2)}) collective-permute-start(bf16[576,128]{1,0:T(8,128)(2,1)S(1)} %get-tuple-element.21), channel_id=1, source_target_pairs={{0,8},{4,12},{8,0},{12,4},{16,24},{20,28},{24,16},{28,20},{1,9},{5... | collective-permute-start | bytes 442376 | tf_op jit(solution)/shard_map/ppermute | solution.py:292
  24.0 0.5 collective-permute-start.3
  24.5 1.4 %collective-permute-done.7.refs_6_ = bf16[784,128]{1,0:T(8,128)(2,1)S(1)} collective-permute-done((bf16[784,128]{1,0:T(8,128)(2,1)}, bf16[784,128]{1,0:T(8,128)(2,1)S(1)}, u32[]{:S(2)}, u32[]{:S(2)}) %collective-permute-start.7) | collective-permute-done | bytes 200736 | tf_op jit(solution)/shard_map/ppermute | solution.py:292
  26.1 5.1 %attend.1 = (bf16[1040,128]{1,0:T(8,128)(2,1)S(1)}, bf16[1040,128]{1,0:T(8,128)(2,1)S(1)}) custom-call(s32[8]{0:T(128)S(1)} %copy-done.3, bf16[784,128]{1,0:T(8,128)(2,1)S(1)} %copy-done.2, bf16[784,128]{1,0:T(8,128)(2,1)S(1)} %collective-permute-done.refs_2_, bf16[784,128]{1,0:T(8,128)(2,1)S(1)} %collective-permute-done.1.refs_3_, ...), custom_call_target="tpu_custom_call" | custom-call | flops 1073741824 | bytes 1064960 | tf_op jit(solution)/shard_map/attend/pallas_call | solution.py:355
  31.2 2.1 %collective-permute-done.4.refs_3_ = bf16[576,128]{1,0:T(8,128)(2,1)S(1)} collective-permute-done((bf16[576,128]{1,0:T(8,128)(2,1)S(1)}, bf16[576,128]{1,0:T(8,128)(2,1)S(1)}, u32[]{:S(2)}, u32[]{:S(2)}) %collective-permute-start.4) | collective-permute-done | bytes 147488 | tf_op jit(solution)/shard_map/ppermute | solution.py:292
  33.4 1.6 %collective-permute-start.10 = (bf16[4,576,128]{2,1,0:T(8,128)(2,1)S(1)}, bf16[4,576,128]{2,1,0:T(8,128)(2,1)S(1)}, u32[]{:S(2)}, u32[]{:S(2)}) collective-permute-start(bf16[4,576,128]{2,1,0:T(8,128)(2,1)S(1)} %stack.1.refs_0_), channel_id=1, source_target_pairs={{0,1},{1,0},{2,3},{3,2},{4,5},{5,4},{6,7},{7,6},{8,9},{9,8},{10,11... | collective-permute-start | bytes 1769480 | tf_op jit(solution)/shard_map/ppermute | solution.py:298
  35.0 0.8 %collective-permute-start.15 = (bf16[1040,128]{1,0:T(8,128)(2,1)S(1)}, bf16[1040,128]{1,0:T(8,128)(2,1)S(1)}, u32[]{:S(2)}, u32[]{:S(2)}) collective-permute-start(bf16[1040,128]{1,0:T(8,128)(2,1)S(1)} %get-tuple-element.32.x_ref), channel_id=1, source_target_pairs={{0,20},{4,16},{8,28},{12,24},{16,4},{20,0},{24,12},{28,8},{1,21},{... | collective-permute-start | bytes 798728 | tf_op jit(solution)/shard_map/ppermute | solution.py:292
  35.8 1.5 %collective-permute-start.13 = (bf16[1040,128]{1,0:T(8,128)(2,1)S(1)}, bf16[1040,128]{1,0:T(8,128)(2,1)S(1)}, u32[]{:S(2)}, u32[]{:S(2)}) collective-permute-start(bf16[1040,128]{1,0:T(8,128)(2,1)S(1)} %get-tuple-element.32.x_ref), channel_id=1, source_target_pairs={{0,12},{4,8},{8,4},{12,0},{16,28},{20,24},{24,20},{28,16},{1,13},{... | collective-permute-start | bytes 798728 | tf_op jit(solution)/shard_map/ppermute | solution.py:292
  37.4 1.4 %collective-permute-start.14 = (bf16[1040,128]{1,0:T(8,128)(2,1)S(1)}, bf16[1040,128]{1,0:T(8,128)(2,1)S(1)}, u32[]{:S(2)}, u32[]{:S(2)}) collective-permute-start(bf16[1040,128]{1,0:T(8,128)(2,1)S(1)} %get-tuple-element.30.refs_4_.refs_1_), channel_id=1, source_target_pairs={{0,16},{4,20},{8,24},{12,28},{16,0},{20,4},{24,8},{28,12},{1,17},{... | collective-permute-start | bytes 798728 | tf_op jit(solution)/shard_map/ppermute | solution.py:292
  38.8 5.5 %collective-permute-done.11.behind.refs_5_.refs_8_ = bf16[1040,128]{1,0:T(8,128)(2,1)S(1)} collective-permute-done((bf16[1040,128]{1,0:T(8,128)(2,1)S(1)}, bf16[1040,128]{1,0:T(8,128)(2,1)S(1)}, u32[]{:S(2)}, u32[]{:S(2)}) %collective-permute-start.11) | collective-permute-done | bytes 266272 | tf_op jit(solution)/shard_map/ppermute | solution.py:292
  44.4 0.5 collective-permute-start.16
  45.0 3.7 %collective-permute-done.10.refs_1_ = bf16[4,576,128]{2,1,0:T(8,128)(2,1)S(1)} collective-permute-done((bf16[4,576,128]{2,1,0:T(8,128)(2,1)S(1)}, bf16[4,576,128]{2,1,0:T(8,128)(2,1)S(1)}, u32[]{:S(2)}, u32[]{:S(2)}) %collective-permute-start.10) | collective-permute-done | bytes 589856 | tf_op jit(solution)/shard_map/ppermute | solution.py:298
  48.6 0.6 %collective-permute-start.17 = (bf16[1040,128]{1,0:T(8,128)(2,1)S(1)}, bf16[1040,128]{1,0:T(8,128)(2,1)S(1)}, u32[]{:S(2)}, u32[]{:S(2)}) collective-permute-start(bf16[1040,128]{1,0:T(8,128)(2,1)S(1)} %collective-permute-done.15.refs_6_.refs_9_), channel_id=1, source_target_pairs={{0,8},{4,12},{8,0},{12,4},{16,24},{20,28},{24,16},{28,20},{1,9},{5... | collective-permute-start | bytes 798728 | tf_op jit(solution)/shard_map/ppermute | solution.py:292
  49.3 0.4 turn.1
  49.7 0.7 %grad_other_near.1 = bf16[256,768]{1,0:T(8,128)(2,1)S(1)} custom-call(bf16[256,1088]{1,0:T(8,128)(2,1)S(1)} %get-tuple-element.33.refs_0_, bf16[1040,128]{1,0:T(8,128)(2,1)S(1)} %get-tuple-element.30.refs_4_.refs_1_, bf16[1040,128]{1,0:T(8,128)(2,1)S(1)} %collective-permute-done.12.refs_2_.refs_5_, ...), custom_call_target="tpu_custom_call" | custom-call | flops 427819008 | bytes 786432 | tf_op jit(solution)/shard_map/grad_other_near/pallas_call | solution.py:384
  50.4 5.6 %collective-permute-done.17.refs_2_.refs_11_ = bf16[1040,128]{1,0:T(8,128)(2,1)S(1)} collective-permute-done((bf16[1040,128]{1,0:T(8,128)(2,1)S(1)}, bf16[1040,128]{1,0:T(8,128)(2,1)S(1)}, u32[]{:S(2)}, u32[]{:S(2)}) %collective-permute-start.17) | collective-permute-done | bytes 266272 | tf_op jit(solution)/shard_map/ppermute | solution.py:292
  56.1 0.3 grad_other_far.1
  56.5 0.3 grad_own_far.1.refs_1_
  56.8 0.7 %grad_own_near.1.refs_0_ = f32[256,768]{1,0:T(8,128)S(1)} custom-call(bf16[256,1088]{1,0:T(8,128)(2,1)S(1)} %get-tuple-element.31.refs_0_, bf16[1040,128]{1,0:T(8,128)(2,1)S(1)} %get-tuple-element.30.refs_4_.refs_1_, bf16[1040,128]{1,0:T(8,128)(2,1)S(1)} %collective-permute-done.12.refs_2_.refs_5_, ...), custom_call_target="tpu_custom_call" | custom-call | flops 427819008 | bytes 1572864 | tf_op jit(solution)/shard_map/grad_own_near/pallas_call | solution.py:384
  57.5 0.3 collective-permute-done.19.refs_3_
  57.8 1.4 %finish.1 = (bf16[256,1024]{1,0:T(8,128)(2,1)}, f32[256,1024]{1,0:T(8,128)}) custom-call(f32[256,768]{1,0:T(8,128)S(1)} %grad_own_near.1.refs_0_, f32[256,256]{1,0:T(8,128)S(1)} %grad_own_far.1.refs_1_, bf16[256,768]{1,0:T(8,128)(2,1)S(1)} %collective-permute-done.18.refs_2_, bf16[256,256]{1,0:T(8,128)(2,1)S(1)} %collective-permute-done.19.refs_3_, ...), custom_call_target="tpu_custom_call" | custom-call | bytes 3145728 | tf_op jit(solution)/shard_map/finish/pallas_call | solution.py:400
  (27 shorter events, 0.4 us)
Async XLA Ops:
  0.6 16.9 %copy-start.1 = (s32[1,8]{1,0:T(1,128)S(1)}, s32[1,8]{1,0:T(1,128)}, u32[]{:S(2)}) copy-start(s32[1,8]{1,0:T(1,128)} %refs_0_.4) | copy-start | bytes 100
  3.3 22.7 %copy-start.3 = (s32[8]{0:T(128)S(1)}, s32[8]{0:T(128)}, u32[]{:S(2)}) copy-start(s32[8]{0:T(128)} %refs_0_.5) | copy-start | bytes 100
  3.3 10.1 %collective-permute-start = (bf16[784,128]{1,0:T(8,128)(2,1)}, bf16[784,128]{1,0:T(8,128)(2,1)S(1)}, u32[]{:S(2)}, u32[]{:S(2)}) collective-permute-start(bf16[784,128]{1,0:T(8,128)(2,1)} %get-tuple-element.18), channel_id=1, source_target_pairs={{0,24},{4,28},{8,16},{12,20},{16,8},{20,12},{24,0},{28,4},{1,25},{... | collective-permute-start | bytes 602120 | tf_op jit(solution)/shard_map/ppermute | solution.py:292
  7.3 10.1 %collective-permute-start.1 = (bf16[784,128]{1,0:T(8,128)(2,1)}, bf16[784,128]{1,0:T(8,128)(2,1)S(1)}, u32[]{:S(2)}, u32[]{:S(2)}) collective-permute-start(bf16[784,128]{1,0:T(8,128)(2,1)} %get-tuple-element.19), channel_id=1, source_target_pairs={{0,28},{4,24},{8,20},{12,16},{16,12},{20,8},{24,4},{28,0},{1,29},{... | collective-permute-start | bytes 602120 | tf_op jit(solution)/shard_map/ppermute | solution.py:292
  7.3 15.2 %collective-permute-start.5 = (bf16[784,128]{1,0:T(8,128)(2,1)}, bf16[784,128]{1,0:T(8,128)(2,1)S(1)}, u32[]{:S(2)}, u32[]{:S(2)}) collective-permute-start(bf16[784,128]{1,0:T(8,128)(2,1)} %get-tuple-element.25), channel_id=1, source_target_pairs={{0,8},{4,12},{8,0},{12,4},{16,24},{20,28},{24,16},{28,20},{1,9},{5... | collective-permute-start | bytes 602120 | tf_op jit(solution)/shard_map/ppermute | solution.py:292
  8.4 15.6 %collective-permute-start.6 = (bf16[784,128]{1,0:T(8,128)(2,1)}, bf16[784,128]{1,0:T(8,128)(2,1)S(1)}, u32[]{:S(2)}, u32[]{:S(2)}) collective-permute-start(bf16[784,128]{1,0:T(8,128)(2,1)} %get-tuple-element.26), channel_id=1, source_target_pairs={{0,16},{4,20},{8,24},{12,28},{16,0},{20,4},{24,8},{28,12},{1,17},{... | collective-permute-start | bytes 602120 | tf_op jit(solution)/shard_map/ppermute | solution.py:292
  10.0 16.0 %collective-permute-start.7 = (bf16[784,128]{1,0:T(8,128)(2,1)}, bf16[784,128]{1,0:T(8,128)(2,1)S(1)}, u32[]{:S(2)}, u32[]{:S(2)}) collective-permute-start(bf16[784,128]{1,0:T(8,128)(2,1)} %get-tuple-element.27), channel_id=1, source_target_pairs={{0,12},{4,8},{8,4},{12,0},{16,28},{20,24},{24,20},{28,16},{1,13},{... | collective-permute-start | bytes 602120 | tf_op jit(solution)/shard_map/ppermute | solution.py:292
  13.4 12.6 %collective-permute-start.8 = (bf16[784,128]{1,0:T(8,128)(2,1)}, bf16[784,128]{1,0:T(8,128)(2,1)S(1)}, u32[]{:S(2)}, u32[]{:S(2)}) collective-permute-start(bf16[784,128]{1,0:T(8,128)(2,1)} %get-tuple-element.28), channel_id=1, source_target_pairs={{0,20},{4,16},{8,28},{12,24},{16,4},{20,0},{24,12},{28,8},{1,21},{... | collective-permute-start | bytes 602120 | tf_op jit(solution)/shard_map/ppermute | solution.py:292
  17.4 8.7 %collective-permute-start.9 = (bf16[784,128]{1,0:T(8,128)(2,1)}, bf16[784,128]{1,0:T(8,128)(2,1)S(1)}, u32[]{:S(2)}, u32[]{:S(2)}) collective-permute-start(bf16[784,128]{1,0:T(8,128)(2,1)} %get-tuple-element.29), channel_id=1, source_target_pairs={{0,4},{4,0},{8,12},{12,8},{16,20},{20,16},{24,28},{28,24},{1,5},{5... | collective-permute-start | bytes 602120 | tf_op jit(solution)/shard_map/ppermute | solution.py:292
  17.5 1.2 %copy-start = (bf16[272,2048]{1,0:T(8,128)(2,1)S(1)}, bf16[272,2048]{1,0:T(8,128)(2,1)}, u32[]{:S(2)}) copy-start(bf16[272,2048]{1,0:T(8,128)(2,1)} %refs_1_.3) | copy-start | bytes 3342340
  18.8 7.3 %copy-start.2 = (bf16[784,128]{1,0:T(8,128)(2,1)S(1)}, bf16[784,128]{1,0:T(8,128)(2,1)}, u32[]{:S(2)}) copy-start(bf16[784,128]{1,0:T(8,128)(2,1)} %get-tuple-element.24.refs_1_) | copy-start | bytes 602116
  22.5 8.6 %collective-permute-start.2 = (bf16[576,128]{1,0:T(8,128)(2,1)S(1)}, bf16[576,128]{1,0:T(8,128)(2,1)S(1)}, u32[]{:S(2)}, u32[]{:S(2)}) collective-permute-start(bf16[576,128]{1,0:T(8,128)(2,1)S(1)} %get-tuple-element.21), channel_id=1, source_target_pairs={{0,8},{4,12},{8,0},{12,4},{16,24},{20,28},{24,16},{28,20},{1,9},{5... | collective-permute-start | bytes 442376 | tf_op jit(solution)/shard_map/ppermute | solution.py:292
  24.0 7.2 %collective-permute-start.3 = (bf16[576,128]{1,0:T(8,128)(2,1)S(1)}, bf16[576,128]{1,0:T(8,128)(2,1)S(1)}, u32[]{:S(2)}, u32[]{:S(2)}) collective-permute-start(bf16[576,128]{1,0:T(8,128)(2,1)S(1)} %get-tuple-element.22), channel_id=1, source_target_pairs={{0,16},{4,20},{8,24},{12,28},{16,0},{20,4},{24,8},{28,12},{1,17},{... | collective-permute-start | bytes 442376 | tf_op jit(solution)/shard_map/ppermute | solution.py:292
  26.0 7.4 %collective-permute-start.4 = (bf16[576,128]{1,0:T(8,128)(2,1)S(1)}, bf16[576,128]{1,0:T(8,128)(2,1)S(1)}, u32[]{:S(2)}, u32[]{:S(2)}) collective-permute-start(bf16[576,128]{1,0:T(8,128)(2,1)S(1)} %get-tuple-element.23), channel_id=1, source_target_pairs={{0,24},{4,28},{8,16},{12,20},{16,8},{20,12},{24,0},{28,4},{1,25},{... | collective-permute-start | bytes 442376 | tf_op jit(solution)/shard_map/ppermute | solution.py:292
  33.4 15.3 %collective-permute-start.10 = (bf16[4,576,128]{2,1,0:T(8,128)(2,1)S(1)}, bf16[4,576,128]{2,1,0:T(8,128)(2,1)S(1)}, u32[]{:S(2)}, u32[]{:S(2)}) collective-permute-start(bf16[4,576,128]{2,1,0:T(8,128)(2,1)S(1)} %stack.1.refs_0_), channel_id=1, source_target_pairs={{0,1},{1,0},{2,3},{3,2},{4,5},{5,4},{6,7},{7,6},{8,9},{9,8},{10,11... | collective-permute-start | bytes 1769480 | tf_op jit(solution)/shard_map/ppermute | solution.py:298
  35.0 9.3 %collective-permute-start.11 = (bf16[1040,128]{1,0:T(8,128)(2,1)S(1)}, bf16[1040,128]{1,0:T(8,128)(2,1)S(1)}, u32[]{:S(2)}, u32[]{:S(2)}) collective-permute-start(bf16[1040,128]{1,0:T(8,128)(2,1)S(1)} %get-tuple-element.30.refs_4_.refs_1_), channel_id=1, source_target_pairs={{0,8},{4,12},{8,0},{12,4},{16,24},{20,28},{24,16},{28,20},{1,9},{5... | collective-permute-start | bytes 798728 | tf_op jit(solution)/shard_map/ppermute | solution.py:292
  35.0 9.4 %collective-permute-start.15 = (bf16[1040,128]{1,0:T(8,128)(2,1)S(1)}, bf16[1040,128]{1,0:T(8,128)(2,1)S(1)}, u32[]{:S(2)}, u32[]{:S(2)}) collective-permute-start(bf16[1040,128]{1,0:T(8,128)(2,1)S(1)} %get-tuple-element.32.x_ref), channel_id=1, source_target_pairs={{0,20},{4,16},{8,28},{12,24},{16,4},{20,0},{24,12},{28,8},{1,21},{... | collective-permute-start | bytes 798728 | tf_op jit(solution)/shard_map/ppermute | solution.py:292
  35.8 13.8 %collective-permute-start.13 = (bf16[1040,128]{1,0:T(8,128)(2,1)S(1)}, bf16[1040,128]{1,0:T(8,128)(2,1)S(1)}, u32[]{:S(2)}, u32[]{:S(2)}) collective-permute-start(bf16[1040,128]{1,0:T(8,128)(2,1)S(1)} %get-tuple-element.32.x_ref), channel_id=1, source_target_pairs={{0,12},{4,8},{8,4},{12,0},{16,28},{20,24},{24,20},{28,16},{1,13},{... | collective-permute-start | bytes 798728 | tf_op jit(solution)/shard_map/ppermute | solution.py:292
  37.4 12.3 %collective-permute-start.14 = (bf16[1040,128]{1,0:T(8,128)(2,1)S(1)}, bf16[1040,128]{1,0:T(8,128)(2,1)S(1)}, u32[]{:S(2)}, u32[]{:S(2)}) collective-permute-start(bf16[1040,128]{1,0:T(8,128)(2,1)S(1)} %get-tuple-element.30.refs_4_.refs_1_), channel_id=1, source_target_pairs={{0,16},{4,20},{8,24},{12,28},{16,0},{20,4},{24,8},{28,12},{1,17},{... | collective-permute-start | bytes 798728 | tf_op jit(solution)/shard_map/ppermute | solution.py:292
  44.3 5.4 %collective-permute-start.12 = (bf16[1040,128]{1,0:T(8,128)(2,1)S(1)}, bf16[1040,128]{1,0:T(8,128)(2,1)S(1)}, u32[]{:S(2)}, u32[]{:S(2)}) collective-permute-start(bf16[1040,128]{1,0:T(8,128)(2,1)S(1)} %late.1), channel_id=1, source_target_pairs={{0,4},{4,0},{8,12},{12,8},{16,20},{20,16},{24,28},{28,24},{1,5},{5... | collective-permute-start | bytes 798728 | tf_op jit(solution)/shard_map/ppermute | solution.py:292
  44.4 11.7 %collective-permute-start.16 = (bf16[1040,128]{1,0:T(8,128)(2,1)S(1)}, bf16[1040,128]{1,0:T(8,128)(2,1)S(1)}, u32[]{:S(2)}, u32[]{:S(2)}) collective-permute-start(bf16[1040,128]{1,0:T(8,128)(2,1)S(1)} %collective-permute-done.11.behind.refs_5_.refs_8_), channel_id=1, source_target_pairs={{0,16},{4,20},{8,24},{12,28},{16,0},{20,4},{24,8},{28,12},{1,17},{... | collective-permute-start | bytes 798728 | tf_op jit(solution)/shard_map/ppermute | solution.py:292
  48.6 7.4 %collective-permute-start.17 = (bf16[1040,128]{1,0:T(8,128)(2,1)S(1)}, bf16[1040,128]{1,0:T(8,128)(2,1)S(1)}, u32[]{:S(2)}, u32[]{:S(2)}) collective-permute-start(bf16[1040,128]{1,0:T(8,128)(2,1)S(1)} %collective-permute-done.15.refs_6_.refs_9_), channel_id=1, source_target_pairs={{0,8},{4,12},{8,0},{12,4},{16,24},{20,28},{24,16},{28,20},{1,9},{5... | collective-permute-start | bytes 798728 | tf_op jit(solution)/shard_map/ppermute | solution.py:292
  50.4 7.5 %collective-permute-start.18 = (bf16[256,768]{1,0:T(8,128)(2,1)S(1)}, bf16[256,768]{1,0:T(8,128)(2,1)S(1)}, u32[]{:S(2)}, u32[]{:S(2)}) collective-permute-start(bf16[256,768]{1,0:T(8,128)(2,1)S(1)} %grad_other_near.1), channel_id=1, source_target_pairs={{0,4},{4,0},{8,12},{12,8},{16,20},{20,16},{24,28},{28,24},{1,5},{5... | collective-permute-start | bytes 1179656 | tf_op jit(solution)/shard_map/ppermute | solution.py:292
  56.4 1.4 %collective-permute-start.19 = (bf16[256,256]{1,0:T(8,128)(2,1)S(1)}, bf16[256,256]{1,0:T(8,128)(2,1)S(1)}, u32[]{:S(2)}, u32[]{:S(2)}) collective-permute-start(bf16[256,256]{1,0:T(8,128)(2,1)S(1)} %grad_other_far.1), channel_id=1, source_target_pairs={{0,4},{4,0},{8,12},{12,8},{16,20},{20,16},{24,28},{28,24},{1,5},{5... | collective-permute-start | bytes 393224 | tf_op jit(solution)/shard_map/ppermute | solution.py:292

commit v3 on v2

--- a/solution.py
+++ b/solution.py
@@ -109,18 +109,21 @@
                 out_ref[at : at + part, :] = cot[:, lanes]
 
 
-def pack_kernel(n, q_hbm, k_hbm, v_hbm, hist_hbm, *refs):
-    outs, (q, k, v, hist, sems) = refs[:n], refs[n:]
+def pack_kernel(n, heads, q_hbm, k_hbm, v_hbm, hist_hbm, *refs):
+    outs, (q, k, v, hist, sems) = refs[:-5], refs[-5:]
     own = lax.axis_index("tm")
-    tok = q.shape[0]
+    tok, width = q.shape
     tile = hist.shape[0]
     clip_rows = n * tile
-    pairs = [(hist_hbm, hist), (q_hbm, q), (k_hbm, k), (v_hbm, v)]
+    start = 0 if width == n * HD else pl.multiple_of(((own ^ heads[0]) // 2) * width, width)
+    pairs = [(hist_hbm, hist)] + [
+        (x.at[:, pl.ds(start, width)], y) for x, y in ((q_hbm, q), (k_hbm, k), (v_hbm, v))
+    ]
     copies = [pltpu.make_async_copy(a, b, sems.at[i]) for i, (a, b) in enumerate(pairs)]
     for copy in copies:
         copy.start()
     copies[0].wait()
-    for d, out_ref in enumerate(outs):
+    for d, out_ref in zip(heads, outs):
         lanes = pl.ds(pl.multiple_of((own ^ d) * HD, HD), HD)
         tiles = hist[:, lanes].astype(jnp.float32)
         row = lax.broadcasted_iota(jnp.int32, (clip_rows, HD), 0)
@@ -130,8 +133,8 @@
         out_ref[3 * tok : 3 * tok + clip_rows, :] = placed.astype(jnp.bfloat16)
     for i, x in enumerate((q, k, v)):
         copies[1 + i].wait()
-        for d, out_ref in enumerate(outs):
-            lanes = pl.ds(pl.multiple_of((own ^ d) * HD, HD), HD)
+        for d, out_ref in zip(heads, outs):
+            lanes = pl.ds(pl.multiple_of((own ^ d) * HD - start, HD), HD)
             out_ref[i * tok : (i + 1) * tok, :] = x[:, lanes]
 
 
@@ -313,21 +316,26 @@
             name=name,
         )
 
-    packed = call(
-        lambda *refs: pack_kernel(n, *refs),
-        "pack",
-        [((length, HD), bf16)] * n,
-        [hbm] * 4,
-        0,
-        (
-            pltpu.VMEM((tok, width), bf16),
-            pltpu.VMEM((tok, width), bf16),
-            pltpu.VMEM((tok, width), bf16),
-            pltpu.VMEM(history.shape, bf16),
-            pltpu.SemaphoreType.DMA((4,)),
-        ),
-        limit=PACK_LIMIT,
-    )(query_rows, key_rows, value_rows, history)
+    def pack(heads, lanes, name):
+        return call(
+            lambda *refs: pack_kernel(n, heads, *refs),
+            name,
+            [((length, HD), bf16)] * len(heads),
+            [hbm] * 4,
+            0,
+            (
+                pltpu.VMEM((tok, lanes), bf16),
+                pltpu.VMEM((tok, lanes), bf16),
+                pltpu.VMEM((tok, lanes), bf16),
+                pltpu.VMEM(history.shape, bf16),
+                pltpu.SemaphoreType.DMA((4,)),
+            ),
+            limit=PACK_LIMIT,
+        )(query_rows, key_rows, value_rows, history)
+
+    first, rest = [6, 7], [0, 1, 2, 3, 4, 5]
+    packed = dict(zip(first, pack(first, 2 * HD, "pack_first")))
+    packed.update(zip(rest, pack(rest, width, "pack_rest")))
     order = [6, 7, 2, 4, 3, 5, 1]
     arrived = {k: swap(packed[k], k) for k in order}
     by_head = [packed[0]] + [arrived[k] for k in order]
@@ -369,7 +377,7 @@
     x_same, y_cross = swap(same, 2), swap(cross, 4 ^ 1)
     y_same, x_cross = swap(same, 4), swap(cross, 2 ^ 1)
     far_same, far_cross = swap(x_same, 4), swap(y_cross, 2)
-    (late_cross,) = call(late_kernel, "late", [head_shape], [vmem, hbm], 0)(cross, x_same)
+    (late_cross,) = call(late_kernel, "late", [head_shape], [vmem, hbm], 0)(cross, x_cross)
     c_cross = swap(late_cross, 1)
 
     turned_own, turned_other = call(

time: 59.4 us -> 60.3 us (1.015)
  waiting for transfers between devices: 28.5 us -> 26.2 us
  Pallas kernels: 12.5 us -> 14.3 us
  starting transfers between devices: 16.2 us -> 17.6 us
    ppermute x1, waiting for transfers between devices: 3.68 us -> 0.01 us  [swap_plane(): return lax.ppermute(x, ('tm', 'head'), pairs)]
    pallas_call x2 -> x3, Pallas kernels: 2.7 us -> 4.42 us  [the longest x2 4.4 us: pack(): call(lambda *refs: pack_kernel(n, heads, *refs), name, [((length, HD), bf...]
    ppermute x19, starting transfers between devices: 14.6 us -> 16 us  [swap(): return lax.ppermute(x, 'tm', [(i, i ^ bit) for i in range(n)])]
    ppermute x19, waiting for transfers between devices: 24.8 us -> 26.2 us  [swap(): return lax.ppermute(x, 'tm', [(i, i ^ bit) for i in range(n)])]
  transfers between devices with their start and end apart: 20 -> 20, of which waited for: 9 -> 10; matrix products, arithmetic and copies ran while one was open for 0% -> 0% of each run, Pallas kernels for 14% -> 18%
where the time goes in v3:
time: 60.3 us; the launch traced here: 60.1 us
  waiting for transfers between devices  26.2 us (43%)
  starting transfers between devices  17.6 us (29%)
  Pallas kernels  14.3 us (24%)
  local copies, waits for them, and re-layouts  1.26 us (2%)
  between operations  0.81 us (1%)
    ppermute x19, waiting for transfers between devices, swap(): return lax.ppermute(x, 'tm', [(i, i ^ bit) for i in range(n)])  26.2 us
    ppermute x19, starting transfers between devices, swap(): return lax.ppermute(x, 'tm', [(i, i ^ bit) for i in range(n)])  16 us
    pallas_call x1, Pallas kernels, head_body(): call(lambda *refs: attend_kernel(n, tok, [0] + order, *refs), 'attend', [...  5.12 us
    pallas_call x2, Pallas kernels, pack(): call(lambda *refs: pack_kernel(n, heads, *refs), name, [((length, HD), bf...  4.4 us
    pallas_call x4, Pallas kernels, grad(): call(lambda *refs: grad_kernel(rows, half, *refs), name, [((cols, len(hea...  1.98 us
    ppermute x1, starting transfers between devices, swap_plane(): return lax.ppermute(x, ('tm', 'head'), pairs)  1.64 us
    pallas_call x1, Pallas kernels, head_body(): call(lambda *refs: finish_kernel(heads, tok, *refs), 'finish', [((tok, wi...  1.44 us
    unnamed x8, local copies, waits for them, and re-layouts  1.26 us
  transfers between devices with their start and end apart: 20, of which 10 were waited for; matrix products, arithmetic and copies ran while one was open for 0% of the time, Pallas kernels for 18%

profile of v3, /device:TPU:0, one launch (start us, length us, event | category | flops | bytes accessed | tf_op | source)
XLA Modules:
  0.0 60.1 jit_solution(18285686991163105522)
XLA Ops:
  0.6 1.9 %pack_first.1 = (bf16[784,128]{1,0:T(8,128)(2,1)}, bf16[784,128]{1,0:T(8,128)(2,1)}) custom-call(bf16[256,1024]{1,0:T(8,128)(2,1)} %refs_0_.6, bf16[256,1024]{1,0:T(8,128)(2,1)} %refs_1_.5, bf16[256,1024]{1,0:T(8,128)(2,1)} %refs_2_.3, bf16[2,1024]{1,0:T(2,128)(2,1)} %refs_3_.3), custom_call_target="tpu_custom_call" | custom-call | bytes 802816 | tf_op jit(solution)/shard_map/pack_first/pallas_call | solution.py:320
  2.5 4.0 %collective-permute-start = (bf16[784,128]{1,0:T(8,128)(2,1)}, bf16[784,128]{1,0:T(8,128)(2,1)S(1)}, u32[]{:S(2)}, u32[]{:S(2)}) collective-permute-start(bf16[784,128]{1,0:T(8,128)(2,1)} %get-tuple-element.18), channel_id=1, source_target_pairs={{0,24},{4,28},{8,16},{12,20},{16,8},{20,12},{24,0},{28,4},{1,25},{... | collective-permute-start | bytes 602120 | tf_op jit(solution)/shard_map/ppermute | solution.py:295
  6.5 2.5 %pack_rest.1 = (bf16[784,128]{1,0:T(8,128)(2,1)}, bf16[784,128]{1,0:T(8,128)(2,1)}, bf16[784,128]{1,0:T(8,128)(2,1)}, bf16[784,128]{1,0:T(8,128)(2,1)}, bf16[784...) custom-call(bf16[256,1024]{1,0:T(8,128)(2,1)} %refs_0_.6, bf16[256,1024]{1,0:T(8,128)(2,1)} %refs_1_.5, ...), custom_call_target="tpu_custom_call" | custom-call | bytes 2408448 | tf_op jit(solution)/shard_map/pack_rest/pallas_call | solution.py:320
  9.0 1.2 %collective-permute-start.5 = (bf16[784,128]{1,0:T(8,128)(2,1)}, bf16[784,128]{1,0:T(8,128)(2,1)S(1)}, u32[]{:S(2)}, u32[]{:S(2)}) collective-permute-start(bf16[784,128]{1,0:T(8,128)(2,1)} %get-tuple-element.25), channel_id=1, source_target_pairs={{0,8},{4,12},{8,0},{12,4},{16,24},{20,28},{24,16},{28,20},{1,9},{5... | collective-permute-start | bytes 602120 | tf_op jit(solution)/shard_map/ppermute | solution.py:295
  10.2 1.5 %collective-permute-start.6 = (bf16[784,128]{1,0:T(8,128)(2,1)}, bf16[784,128]{1,0:T(8,128)(2,1)S(1)}, u32[]{:S(2)}, u32[]{:S(2)}) collective-permute-start(bf16[784,128]{1,0:T(8,128)(2,1)} %get-tuple-element.26), channel_id=1, source_target_pairs={{0,16},{4,20},{8,24},{12,28},{16,0},{20,4},{24,8},{28,12},{1,17},{... | collective-permute-start | bytes 602120 | tf_op jit(solution)/shard_map/ppermute | solution.py:295
  11.7 0.6 collective-permute-start.7
  12.5 0.4 collective-permute-start.8
  12.9 3.6 %collective-permute-done.1.refs_3_ = bf16[784,128]{1,0:T(8,128)(2,1)S(1)} collective-permute-done((bf16[784,128]{1,0:T(8,128)(2,1)}, bf16[784,128]{1,0:T(8,128)(2,1)S(1)}, u32[]{:S(2)}, u32[]{:S(2)}) %collective-permute-start.1) | collective-permute-done | bytes 200736 | tf_op jit(solution)/shard_map/ppermute | solution.py:295
  16.6 1.2 %copy-done = bf16[272,2048]{1,0:T(8,128)(2,1)S(1)} copy-done((bf16[272,2048]{1,0:T(8,128)(2,1)S(1)}, bf16[272,2048]{1,0:T(8,128)(2,1)}, u32[]{:S(2)}) %copy-start) | copy-done | bytes 1114136
  17.9 0.9 %cot.1 = (bf16[576,128]{1,0:T(8,128)(2,1)S(1)}, bf16[576,128]{1,0:T(8,128)(2,1)S(1)}, bf16[576,128]{1,0:T(8,128)(2,1)S(1)}, bf16[576,128]{1,0:T(8,128)(2,1)S(1)}) custom-call(s32[1,8]{1,0:T(1,128)S(1)} %copy-done.1, bf16[272,2048]{1,0:T(8,128)(2,1)S(1)} %copy-done, bf16[784,128]{1,0:T(8,128)(2,1)S(1)} %collective-permute-done.refs_2_, ...), custom_call_target="tpu_custom_call" | custom-call | bytes 1179648 | tf_op jit(solution)/shard_map/cot/pallas_call | solution.py:343
  18.8 2.9 %collective-permute-done.5.refs_4_ = bf16[784,128]{1,0:T(8,128)(2,1)S(1)} collective-permute-done((bf16[784,128]{1,0:T(8,128)(2,1)}, bf16[784,128]{1,0:T(8,128)(2,1)S(1)}, u32[]{:S(2)}, u32[]{:S(2)}) %collective-permute-start.5) | collective-permute-done | bytes 200736 | tf_op jit(solution)/shard_map/ppermute | solution.py:295
  21.7 1.5 %collective-permute-start.2 = (bf16[576,128]{1,0:T(8,128)(2,1)S(1)}, bf16[576,128]{1,0:T(8,128)(2,1)S(1)}, u32[]{:S(2)}, u32[]{:S(2)}) collective-permute-start(bf16[576,128]{1,0:T(8,128)(2,1)S(1)} %get-tuple-element.21), channel_id=1, source_target_pairs={{0,8},{4,12},{8,0},{12,4},{16,24},{20,28},{24,16},{28,20},{1,9},{5... | collective-permute-start | bytes 442376 | tf_op jit(solution)/shard_map/ppermute | solution.py:295
  23.2 0.5 collective-permute-start.3
  23.7 1.4 %collective-permute-done.7.refs_6_ = bf16[784,128]{1,0:T(8,128)(2,1)S(1)} collective-permute-done((bf16[784,128]{1,0:T(8,128)(2,1)}, bf16[784,128]{1,0:T(8,128)(2,1)S(1)}, u32[]{:S(2)}, u32[]{:S(2)}) %collective-permute-start.7) | collective-permute-done | bytes 200736 | tf_op jit(solution)/shard_map/ppermute | solution.py:295
  25.2 5.1 %attend.1 = (bf16[1040,128]{1,0:T(8,128)(2,1)S(1)}, bf16[1040,128]{1,0:T(8,128)(2,1)S(1)}) custom-call(s32[8]{0:T(128)S(1)} %copy-done.3, bf16[784,128]{1,0:T(8,128)(2,1)S(1)} %copy-done.2, bf16[784,128]{1,0:T(8,128)(2,1)S(1)} %collective-permute-done.refs_2_, bf16[784,128]{1,0:T(8,128)(2,1)S(1)} %collective-permute-done.1.refs_3_, ...), custom_call_target="tpu_custom_call" | custom-call | flops 1073741824 | bytes 1064960 | tf_op jit(solution)/shard_map/attend/pallas_call | solution.py:363
  30.3 2.1 %collective-permute-done.4.refs_3_ = bf16[576,128]{1,0:T(8,128)(2,1)S(1)} collective-permute-done((bf16[576,128]{1,0:T(8,128)(2,1)S(1)}, bf16[576,128]{1,0:T(8,128)(2,1)S(1)}, u32[]{:S(2)}, u32[]{:S(2)}) %collective-permute-start.4) | collective-permute-done | bytes 147488 | tf_op jit(solution)/shard_map/ppermute | solution.py:295
  32.5 1.6 %collective-permute-start.10 = (bf16[4,576,128]{2,1,0:T(8,128)(2,1)S(1)}, bf16[4,576,128]{2,1,0:T(8,128)(2,1)S(1)}, u32[]{:S(2)}, u32[]{:S(2)}) collective-permute-start(bf16[4,576,128]{2,1,0:T(8,128)(2,1)S(1)} %stack.1.refs_0_), channel_id=1, source_target_pairs={{0,1},{1,0},{2,3},{3,2},{4,5},{5,4},{6,7},{7,6},{8,9},{9,8},{10,11... | collective-permute-start | bytes 1769480 | tf_op jit(solution)/shard_map/ppermute | solution.py:301
  34.1 1.1 %collective-permute-start.15 = (bf16[1040,128]{1,0:T(8,128)(2,1)S(1)}, bf16[1040,128]{1,0:T(8,128)(2,1)S(1)}, u32[]{:S(2)}, u32[]{:S(2)}) collective-permute-start(bf16[1040,128]{1,0:T(8,128)(2,1)S(1)} %get-tuple-element.32.x_ref), channel_id=1, source_target_pairs={{0,20},{4,16},{8,28},{12,24},{16,4},{20,0},{24,12},{28,8},{1,21},{... | collective-permute-start | bytes 798728 | tf_op jit(solution)/shard_map/ppermute | solution.py:295
  35.2 1.3 %collective-permute-start.14 = (bf16[1040,128]{1,0:T(8,128)(2,1)S(1)}, bf16[1040,128]{1,0:T(8,128)(2,1)S(1)}, u32[]{:S(2)}, u32[]{:S(2)}) collective-permute-start(bf16[1040,128]{1,0:T(8,128)(2,1)S(1)} %get-tuple-element.30.refs_4_.refs_1_), channel_id=1, source_target_pairs={{0,8},{4,12},{8,0},{12,4},{16,24},{20,28},{24,16},{28,20},{1,9},{5... | collective-permute-start | bytes 798728 | tf_op jit(solution)/shard_map/ppermute | solution.py:295
  36.5 1.4 %collective-permute-start.13 = (bf16[1040,128]{1,0:T(8,128)(2,1)S(1)}, bf16[1040,128]{1,0:T(8,128)(2,1)S(1)}, u32[]{:S(2)}, u32[]{:S(2)}) collective-permute-start(bf16[1040,128]{1,0:T(8,128)(2,1)S(1)} %get-tuple-element.30.refs_4_.refs_1_), channel_id=1, source_target_pairs={{0,16},{4,20},{8,24},{12,28},{16,0},{20,4},{24,8},{28,12},{1,17},{... | collective-permute-start | bytes 798728 | tf_op jit(solution)/shard_map/ppermute | solution.py:295
  37.9 4.9 %collective-permute-done.11.behind.refs_3_.refs_6_ = bf16[1040,128]{1,0:T(8,128)(2,1)S(1)} collective-permute-done((bf16[1040,128]{1,0:T(8,128)(2,1)S(1)}, bf16[1040,128]{1,0:T(8,128)(2,1)S(1)}, u32[]{:S(2)}, u32[]{:S(2)}) %collective-permute-start.11) | collective-permute-done | bytes 266272 | tf_op jit(solution)/shard_map/ppermute | solution.py:295
  42.9 0.6 %collective-permute-start.17 = (bf16[1040,128]{1,0:T(8,128)(2,1)S(1)}, bf16[1040,128]{1,0:T(8,128)(2,1)S(1)}, u32[]{:S(2)}, u32[]{:S(2)}) collective-permute-start(bf16[1040,128]{1,0:T(8,128)(2,1)S(1)} %collective-permute-done.15.refs_6_.refs_9_), channel_id=1, source_target_pairs={{0,8},{4,12},{8,0},{12,4},{16,24},{20,28},{24,16},{28,20},{1,9},{5... | collective-permute-start | bytes 798728 | tf_op jit(solution)/shard_map/ppermute | solution.py:295
  43.6 4.8 %collective-permute-done.14.refs_5_.refs_8_ = bf16[1040,128]{1,0:T(8,128)(2,1)S(1)} collective-permute-done((bf16[1040,128]{1,0:T(8,128)(2,1)S(1)}, bf16[1040,128]{1,0:T(8,128)(2,1)S(1)}, u32[]{:S(2)}, u32[]{:S(2)}) %collective-permute-start.14) | collective-permute-done | bytes 266272 | tf_op jit(solution)/shard_map/ppermute | solution.py:295
  48.4 1.6 %collective-permute-start.16 = (bf16[1040,128]{1,0:T(8,128)(2,1)S(1)}, bf16[1040,128]{1,0:T(8,128)(2,1)S(1)}, u32[]{:S(2)}, u32[]{:S(2)}) collective-permute-start(bf16[1040,128]{1,0:T(8,128)(2,1)S(1)} %collective-permute-done.14.refs_5_.refs_8_), channel_id=1, source_target_pairs={{0,16},{4,20},{8,24},{12,28},{16,0},{20,4},{24,8},{28,12},{1,17},{... | collective-permute-start | bytes 798728 | tf_op jit(solution)/shard_map/ppermute | solution.py:295
  49.9 0.4 turn.1
  50.3 0.7 %grad_other_near.1 = bf16[256,768]{1,0:T(8,128)(2,1)S(1)} custom-call(bf16[256,1088]{1,0:T(8,128)(2,1)S(1)} %get-tuple-element.33.refs_0_, bf16[1040,128]{1,0:T(8,128)(2,1)S(1)} %get-tuple-element.30.refs_4_.refs_1_, bf16[1040,128]{1,0:T(8,128)(2,1)S(1)} %collective-permute-done.12.refs_2_.refs_5_, ...), custom_call_target="tpu_custom_call" | custom-call | flops 427819008 | bytes 786432 | tf_op jit(solution)/shard_map/grad_other_near/pallas_call | solution.py:392
  51.1 3.0 %collective-permute-done.17.refs_2_.refs_11_ = bf16[1040,128]{1,0:T(8,128)(2,1)S(1)} collective-permute-done((bf16[1040,128]{1,0:T(8,128)(2,1)S(1)}, bf16[1040,128]{1,0:T(8,128)(2,1)S(1)}, u32[]{:S(2)}, u32[]{:S(2)}) %collective-permute-start.17) | collective-permute-done | bytes 266272 | tf_op jit(solution)/shard_map/ppermute | solution.py:295
  54.1 2.9 %collective-permute-done.16.refs_1_.refs_10_ = bf16[1040,128]{1,0:T(8,128)(2,1)S(1)} collective-permute-done((bf16[1040,128]{1,0:T(8,128)(2,1)S(1)}, bf16[1040,128]{1,0:T(8,128)(2,1)S(1)}, u32[]{:S(2)}, u32[]{:S(2)}) %collective-permute-start.16) | collective-permute-done | bytes 266272 | tf_op jit(solution)/shard_map/ppermute | solution.py:295
  56.9 0.3 grad_other_far.1
  57.7 0.7 %grad_own_near.1.refs_0_ = f32[256,768]{1,0:T(8,128)S(1)} custom-call(bf16[256,1088]{1,0:T(8,128)(2,1)S(1)} %get-tuple-element.31.refs_0_, bf16[1040,128]{1,0:T(8,128)(2,1)S(1)} %get-tuple-element.30.refs_4_.refs_1_, bf16[1040,128]{1,0:T(8,128)(2,1)S(1)} %collective-permute-done.12.refs_2_.refs_5_, ...), custom_call_target="tpu_custom_call" | custom-call | flops 427819008 | bytes 1572864 | tf_op jit(solution)/shard_map/grad_own_near/pallas_call | solution.py:392
  58.3 0.3 collective-permute-done.19.refs_3_
  58.7 1.4 %finish.1 = (bf16[256,1024]{1,0:T(8,128)(2,1)}, f32[256,1024]{1,0:T(8,128)}) custom-call(f32[256,768]{1,0:T(8,128)S(1)} %grad_own_near.1.refs_0_, f32[256,256]{1,0:T(8,128)S(1)} %grad_own_far.1.refs_1_, bf16[256,768]{1,0:T(8,128)(2,1)S(1)} %collective-permute-done.18.refs_2_, bf16[256,256]{1,0:T(8,128)(2,1)S(1)} %collective-permute-done.19.refs_3_, ...), custom_call_target="tpu_custom_call" | custom-call | bytes 3145728 | tf_op jit(solution)/shard_map/finish/pallas_call | solution.py:408
  (28 shorter events, 1.0 us)
Async XLA Ops:
  2.5 14.1 %copy-start.1 = (s32[1,8]{1,0:T(1,128)S(1)}, s32[1,8]{1,0:T(1,128)}, u32[]{:S(2)}) copy-start(s32[1,8]{1,0:T(1,128)} %refs_0_.5) | copy-start | bytes 100
  2.5 10.0 %collective-permute-start = (bf16[784,128]{1,0:T(8,128)(2,1)}, bf16[784,128]{1,0:T(8,128)(2,1)S(1)}, u32[]{:S(2)}, u32[]{:S(2)}) collective-permute-start(bf16[784,128]{1,0:T(8,128)(2,1)} %get-tuple-element.18), channel_id=1, source_target_pairs={{0,24},{4,28},{8,16},{12,20},{16,8},{20,12},{24,0},{28,4},{1,25},{... | collective-permute-start | bytes 602120 | tf_op jit(solution)/shard_map/ppermute | solution.py:295
  6.5 10.1 %collective-permute-start.1 = (bf16[784,128]{1,0:T(8,128)(2,1)}, bf16[784,128]{1,0:T(8,128)(2,1)S(1)}, u32[]{:S(2)}, u32[]{:S(2)}) collective-permute-start(bf16[784,128]{1,0:T(8,128)(2,1)} %get-tuple-element.19), channel_id=1, source_target_pairs={{0,28},{4,24},{8,20},{12,16},{16,12},{20,8},{24,4},{28,0},{1,29},{... | collective-permute-start | bytes 602120 | tf_op jit(solution)/shard_map/ppermute | solution.py:295
  9.0 16.1 %copy-start.3 = (s32[8]{0:T(128)S(1)}, s32[8]{0:T(128)}, u32[]{:S(2)}) copy-start(s32[8]{0:T(128)} %refs_0_.7) | copy-start | bytes 100
  9.0 12.6 %collective-permute-start.5 = (bf16[784,128]{1,0:T(8,128)(2,1)}, bf16[784,128]{1,0:T(8,128)(2,1)S(1)}, u32[]{:S(2)}, u32[]{:S(2)}) collective-permute-start(bf16[784,128]{1,0:T(8,128)(2,1)} %get-tuple-element.25), channel_id=1, source_target_pairs={{0,8},{4,12},{8,0},{12,4},{16,24},{20,28},{24,16},{28,20},{1,9},{5... | collective-permute-start | bytes 602120 | tf_op jit(solution)/shard_map/ppermute | solution.py:295
  10.2 13.0 %collective-permute-start.6 = (bf16[784,128]{1,0:T(8,128)(2,1)}, bf16[784,128]{1,0:T(8,128)(2,1)S(1)}, u32[]{:S(2)}, u32[]{:S(2)}) collective-permute-start(bf16[784,128]{1,0:T(8,128)(2,1)} %get-tuple-element.26), channel_id=1, source_target_pairs={{0,16},{4,20},{8,24},{12,28},{16,0},{20,4},{24,8},{28,12},{1,17},{... | collective-permute-start | bytes 602120 | tf_op jit(solution)/shard_map/ppermute | solution.py:295
  11.7 13.4 %collective-permute-start.7 = (bf16[784,128]{1,0:T(8,128)(2,1)}, bf16[784,128]{1,0:T(8,128)(2,1)S(1)}, u32[]{:S(2)}, u32[]{:S(2)}) collective-permute-start(bf16[784,128]{1,0:T(8,128)(2,1)} %get-tuple-element.27), channel_id=1, source_target_pairs={{0,12},{4,8},{8,4},{12,0},{16,28},{20,24},{24,20},{28,16},{1,13},{... | collective-permute-start | bytes 602120 | tf_op jit(solution)/shard_map/ppermute | solution.py:295
  12.5 12.7 %collective-permute-start.8 = (bf16[784,128]{1,0:T(8,128)(2,1)}, bf16[784,128]{1,0:T(8,128)(2,1)S(1)}, u32[]{:S(2)}, u32[]{:S(2)}) collective-permute-start(bf16[784,128]{1,0:T(8,128)(2,1)} %get-tuple-element.28), channel_id=1, source_target_pairs={{0,20},{4,16},{8,28},{12,24},{16,4},{20,0},{24,12},{28,8},{1,21},{... | collective-permute-start | bytes 602120 | tf_op jit(solution)/shard_map/ppermute | solution.py:295
  16.5 8.6 %collective-permute-start.9 = (bf16[784,128]{1,0:T(8,128)(2,1)}, bf16[784,128]{1,0:T(8,128)(2,1)S(1)}, u32[]{:S(2)}, u32[]{:S(2)}) collective-permute-start(bf16[784,128]{1,0:T(8,128)(2,1)} %get-tuple-element.29), channel_id=1, source_target_pairs={{0,4},{4,0},{8,12},{12,8},{16,20},{20,16},{24,28},{28,24},{1,5},{5... | collective-permute-start | bytes 602120 | tf_op jit(solution)/shard_map/ppermute | solution.py:295
  16.6 1.2 %copy-start = (bf16[272,2048]{1,0:T(8,128)(2,1)S(1)}, bf16[272,2048]{1,0:T(8,128)(2,1)}, u32[]{:S(2)}) copy-start(bf16[272,2048]{1,0:T(8,128)(2,1)} %refs_1_.4) | copy-start | bytes 3342340
  17.9 7.3 %copy-start.2 = (bf16[784,128]{1,0:T(8,128)(2,1)S(1)}, bf16[784,128]{1,0:T(8,128)(2,1)}, u32[]{:S(2)}) copy-start(bf16[784,128]{1,0:T(8,128)(2,1)} %get-tuple-element.24.refs_1_) | copy-start | bytes 602116
  21.7 8.6 %collective-permute-start.2 = (bf16[576,128]{1,0:T(8,128)(2,1)S(1)}, bf16[576,128]{1,0:T(8,128)(2,1)S(1)}, u32[]{:S(2)}, u32[]{:S(2)}) collective-permute-start(bf16[576,128]{1,0:T(8,128)(2,1)S(1)} %get-tuple-element.21), channel_id=1, source_target_pairs={{0,8},{4,12},{8,0},{12,4},{16,24},{20,28},{24,16},{28,20},{1,9},{5... | collective-permute-start | bytes 442376 | tf_op jit(solution)/shard_map/ppermute | solution.py:295
  23.2 7.1 %collective-permute-start.3 = (bf16[576,128]{1,0:T(8,128)(2,1)S(1)}, bf16[576,128]{1,0:T(8,128)(2,1)S(1)}, u32[]{:S(2)}, u32[]{:S(2)}) collective-permute-start(bf16[576,128]{1,0:T(8,128)(2,1)S(1)} %get-tuple-element.22), channel_id=1, source_target_pairs={{0,16},{4,20},{8,24},{12,28},{16,0},{20,4},{24,8},{28,12},{1,17},{... | collective-permute-start | bytes 442376 | tf_op jit(solution)/shard_map/ppermute | solution.py:295
  25.1 7.3 %collective-permute-start.4 = (bf16[576,128]{1,0:T(8,128)(2,1)S(1)}, bf16[576,128]{1,0:T(8,128)(2,1)S(1)}, u32[]{:S(2)}, u32[]{:S(2)}) collective-permute-start(bf16[576,128]{1,0:T(8,128)(2,1)S(1)} %get-tuple-element.23), channel_id=1, source_target_pairs={{0,24},{4,28},{8,16},{12,20},{16,8},{20,12},{24,0},{28,4},{1,25},{... | collective-permute-start | bytes 442376 | tf_op jit(solution)/shard_map/ppermute | solution.py:295
  32.5 17.4 %collective-permute-start.10 = (bf16[4,576,128]{2,1,0:T(8,128)(2,1)S(1)}, bf16[4,576,128]{2,1,0:T(8,128)(2,1)S(1)}, u32[]{:S(2)}, u32[]{:S(2)}) collective-permute-start(bf16[4,576,128]{2,1,0:T(8,128)(2,1)S(1)} %stack.1.refs_0_), channel_id=1, source_target_pairs={{0,1},{1,0},{2,3},{3,2},{4,5},{5,4},{6,7},{7,6},{8,9},{9,8},{10,11... | collective-permute-start | bytes 1769480 | tf_op jit(solution)/shard_map/ppermute | solution.py:301
  34.1 8.7 %collective-permute-start.11 = (bf16[1040,128]{1,0:T(8,128)(2,1)S(1)}, bf16[1040,128]{1,0:T(8,128)(2,1)S(1)}, u32[]{:S(2)}, u32[]{:S(2)}) collective-permute-start(bf16[1040,128]{1,0:T(8,128)(2,1)S(1)} %get-tuple-element.32.x_ref), channel_id=1, source_target_pairs={{0,12},{4,8},{8,4},{12,0},{16,28},{20,24},{24,20},{28,16},{1,13},{... | collective-permute-start | bytes 798728 | tf_op jit(solution)/shard_map/ppermute | solution.py:295
  34.1 8.8 %collective-permute-start.15 = (bf16[1040,128]{1,0:T(8,128)(2,1)S(1)}, bf16[1040,128]{1,0:T(8,128)(2,1)S(1)}, u32[]{:S(2)}, u32[]{:S(2)}) collective-permute-start(bf16[1040,128]{1,0:T(8,128)(2,1)S(1)} %get-tuple-element.32.x_ref), channel_id=1, source_target_pairs={{0,20},{4,16},{8,28},{12,24},{16,4},{20,0},{24,12},{28,8},{1,21},{... | collective-permute-start | bytes 798728 | tf_op jit(solution)/shard_map/ppermute | solution.py:295
  35.2 13.1 %collective-permute-start.14 = (bf16[1040,128]{1,0:T(8,128)(2,1)S(1)}, bf16[1040,128]{1,0:T(8,128)(2,1)S(1)}, u32[]{:S(2)}, u32[]{:S(2)}) collective-permute-start(bf16[1040,128]{1,0:T(8,128)(2,1)S(1)} %get-tuple-element.30.refs_4_.refs_1_), channel_id=1, source_target_pairs={{0,8},{4,12},{8,0},{12,4},{16,24},{20,28},{24,16},{28,20},{1,9},{5... | collective-permute-start | bytes 798728 | tf_op jit(solution)/shard_map/ppermute | solution.py:295
  36.5 13.8 %collective-permute-start.13 = (bf16[1040,128]{1,0:T(8,128)(2,1)S(1)}, bf16[1040,128]{1,0:T(8,128)(2,1)S(1)}, u32[]{:S(2)}, u32[]{:S(2)}) collective-permute-start(bf16[1040,128]{1,0:T(8,128)(2,1)S(1)} %get-tuple-element.30.refs_4_.refs_1_), channel_id=1, source_target_pairs={{0,16},{4,20},{8,24},{12,28},{16,0},{20,4},{24,8},{28,12},{1,17},{... | collective-permute-start | bytes 798728 | tf_op jit(solution)/shard_map/ppermute | solution.py:295
  42.8 7.5 %collective-permute-start.12 = (bf16[1040,128]{1,0:T(8,128)(2,1)S(1)}, bf16[1040,128]{1,0:T(8,128)(2,1)S(1)}, u32[]{:S(2)}, u32[]{:S(2)}) collective-permute-start(bf16[1040,128]{1,0:T(8,128)(2,1)S(1)} %late.1), channel_id=1, source_target_pairs={{0,4},{4,0},{8,12},{12,8},{16,20},{20,16},{24,28},{28,24},{1,5},{5... | collective-permute-start | bytes 798728 | tf_op jit(solution)/shard_map/ppermute | solution.py:295
  42.9 11.1 %collective-permute-start.17 = (bf16[1040,128]{1,0:T(8,128)(2,1)S(1)}, bf16[1040,128]{1,0:T(8,128)(2,1)S(1)}, u32[]{:S(2)}, u32[]{:S(2)}) collective-permute-start(bf16[1040,128]{1,0:T(8,128)(2,1)S(1)} %collective-permute-done.15.refs_6_.refs_9_), channel_id=1, source_target_pairs={{0,8},{4,12},{8,0},{12,4},{16,24},{20,28},{24,16},{28,20},{1,9},{5... | collective-permute-start | bytes 798728 | tf_op jit(solution)/shard_map/ppermute | solution.py:295
  48.4 8.6 %collective-permute-start.16 = (bf16[1040,128]{1,0:T(8,128)(2,1)S(1)}, bf16[1040,128]{1,0:T(8,128)(2,1)S(1)}, u32[]{:S(2)}, u32[]{:S(2)}) collective-permute-start(bf16[1040,128]{1,0:T(8,128)(2,1)S(1)} %collective-permute-done.14.refs_5_.refs_8_), channel_id=1, source_target_pairs={{0,16},{4,20},{8,24},{12,28},{16,0},{20,4},{24,8},{28,12},{1,17},{... | collective-permute-start | bytes 798728 | tf_op jit(solution)/shard_map/ppermute | solution.py:295
  51.0 7.7 %collective-permute-start.18 = (bf16[256,768]{1,0:T(8,128)(2,1)S(1)}, bf16[256,768]{1,0:T(8,128)(2,1)S(1)}, u32[]{:S(2)}, u32[]{:S(2)}) collective-permute-start(bf16[256,768]{1,0:T(8,128)(2,1)S(1)} %grad_other_near.1), channel_id=1, source_target_pairs={{0,4},{4,0},{8,12},{12,8},{16,20},{20,16},{24,28},{28,24},{1,5},{5... | collective-permute-start | bytes 1179656 | tf_op jit(solution)/shard_map/ppermute | solution.py:295
  57.3 1.4 %collective-permute-start.19 = (bf16[256,256]{1,0:T(8,128)(2,1)S(1)}, bf16[256,256]{1,0:T(8,128)(2,1)S(1)}, u32[]{:S(2)}, u32[]{:S(2)}) collective-permute-start(bf16[256,256]{1,0:T(8,128)(2,1)S(1)} %grad_other_far.1), channel_id=1, source_target_pairs={{0,4},{4,0},{8,12},{12,8},{16,20},{20,16},{24,28},{28,24},{1,5},{5... | collective-permute-start | bytes 393224 | tf_op jit(solution)/shard_map/ppermute | solution.py:295

commit v4 on v3

--- a/solution.py
+++ b/solution.py
@@ -196,14 +196,14 @@
     attend_blocks(n, tok, 1 - side, counts, x_ref, cross_ref)
 
 
-def stack_kernel(*refs):
+def stack_kernel(order, *refs):
     out_ref = refs[-1]
-    for i, x in enumerate(refs[:-2]):
+    for i, x in zip(order, refs):
         out_ref[i] = x[...]
 
 
-def late_kernel(x_ref, behind, out_ref):
-    out_ref[...] = x_ref[...]
+def late_kernel(x_ref, *refs):
+    refs[-1][...] = x_ref[...]
 
 
 def whole_cot(lo, part, plane, mine, swapped):
@@ -256,7 +256,7 @@
 
 def finish_kernel(order, tok, own_near, own_far, got_near, got_far, *refs):
     n = len(order)
-    heads, att_ref, out_ref = refs[:n], refs[n], refs[n + 1]
+    heads, (att_hbm, out_hbm, total, sems) = refs[:n], refs[n:]
     own = lax.axis_index("tm")
     at = pl.multiple_of(own // 2 * tok, tok)
     near = own_near.shape[1] // HD
@@ -265,11 +265,21 @@
         ref, i = (near_ref, i) if i < near else (far_ref, i - near)
         return ref[:, i * HD : (i + 1) * HD]
 
+    moves = []
+
+    def move(a, b):
+        moves.append(pltpu.make_async_copy(a, b, sems.at[len(moves)]))
+        moves[-1].start()
+
+    lanes = [pl.ds(pl.multiple_of((own ^ k) * HD, HD), HD) for k in order]
+    for i in range(n):
+        move(heads[i].at[pl.ds(at, tok), :], att_hbm.at[:, lanes[i]])
     for i, k in enumerate(order):
-        lanes = pl.ds(pl.multiple_of((own ^ k) * HD, HD), HD)
-        att_ref[:, lanes] = heads[i][pl.ds(at, tok), :]
         got = column(got_near, got_far, order.index(k ^ 1))
-        out_ref[:, lanes] = column(own_near, own_far, i) + got.astype(jnp.float32)
+        total[i] = column(own_near, own_far, i) + got.astype(jnp.float32)
+        move(total.at[i], out_hbm.at[:, lanes[i]])
+    for x in moves:
+        x.wait()
 
 
 def head_body(query_rows, key_rows, value_rows, frame_counts, history, offsets, cotangent):
@@ -352,7 +362,8 @@
             pltpu.SemaphoreType.DMA((2,)),
         ),
     )(offsets, cotangent, arrived[6], arrived[7])
-    cots = [cots[0]] + [swap(cots[m], 2 * m) for m in chips[1:]]
+    moved = {m: swap(cots[m], 2 * m) for m in reversed(chips[1:])}
+    cots = [cots[0]] + [moved[m] for m in chips[1:]]
     counts = (
         pltpu.VMEM((n, length, HD), bf16),
         pltpu.SMEM(frame_counts.shape, jnp.int32),
@@ -369,15 +380,20 @@
         counts,
         2 * pairs,
     )(frame_counts, *by_head)
+    stack_order = [3, 1, 2, 0]
     (cot_mine,) = call(
-        stack_kernel, "stack", [((half, 2 * units * part, HD), bf16)], [vmem] * half + [hbm], 0
-    )(*cots, same)
+        lambda *refs: stack_kernel(stack_order, *refs),
+        "stack",
+        [((half, 2 * units * part, HD), bf16)],
+        [vmem] * half + [hbm],
+        0,
+    )(*[cots[m] for m in stack_order], same)
     cot_swapped = swap_plane(cot_mine, 0)
 
     x_same, y_cross = swap(same, 2), swap(cross, 4 ^ 1)
     y_same, x_cross = swap(same, 4), swap(cross, 2 ^ 1)
     far_same, far_cross = swap(x_same, 4), swap(y_cross, 2)
-    (late_cross,) = call(late_kernel, "late", [head_shape], [vmem, hbm], 0)(cross, x_cross)
+    (late_cross,) = call(late_kernel, "late", [head_shape], [vmem] + [hbm] * 2, 0)(cross, x_cross, y_same)
     c_cross = swap(late_cross, 1)
 
     turned_own, turned_other = call(
@@ -398,9 +414,9 @@
         )(turned, *heads)
         return out
 
-    near = [same, c_cross, x_cross, y_same, x_same, y_cross]
-    heads = [0, 1, 3, 4, 2, 5, 6, 7]
-    far = [far_same, far_cross]
+    near = [same, x_cross, y_same, x_same, y_cross]
+    far = [c_cross, far_same, far_cross]
+    heads = [0, 3, 4, 2, 5, 1, 6, 7]
     got_near = swap(grad(turned_other, near, bf16, "grad_other_near"), 1)
     own_near = grad(turned_own, near, jnp.float32, "grad_own_near")
     got_far = swap(grad(turned_other, far, bf16, "grad_other_far"), 1)
@@ -411,6 +427,8 @@
         [((tok, width), bf16), ((cols, width), jnp.float32)],
         [vmem] * (4 + n),
         0,
+        (pltpu.VMEM((n, cols, HD), jnp.float32), pltpu.SemaphoreType.DMA((2 * n,))),
+        out_spec=hbm,
     )(own_near, own_far, got_near, got_far, *near, *far)
 
 

time: 60.3 us -> 58 us (0.962)
  waiting for transfers between devices: 26.2 us -> 23.8 us
    ppermute x19, waiting for transfers between devices: 26.2 us -> 23.8 us  [swap(): return lax.ppermute(x, 'tm', [(i, i ^ bit) for i in range(n)])]
  transfers between devices with their start and end apart: 20 -> 20, of which waited for: 10 -> 11; matrix products, arithmetic and copies ran while one was open for 0% -> 0% of each run, Pallas kernels for 18% -> 19%
where the time goes in v4:
time: 58 us; the launch traced here: 57.8 us
  waiting for transfers between devices  23.8 us (41%)
  starting transfers between devices  17.6 us (30%)
  Pallas kernels  14.3 us (25%)
  local copies, waits for them, and re-layouts  1.26 us (2%)
  between operations  0.76 us (1%)
    ppermute x19, waiting for transfers between devices, swap(): return lax.ppermute(x, 'tm', [(i, i ^ bit) for i in range(n)])  23.8 us
    ppermute x19, starting transfers between devices, swap(): return lax.ppermute(x, 'tm', [(i, i ^ bit) for i in range(n)])  15.9 us
    pallas_call x1, Pallas kernels, head_body(): call(lambda *refs: attend_kernel(n, tok, [0] + order, *refs), 'attend', [...  5.11 us
    pallas_call x2, Pallas kernels, pack(): call(lambda *refs: pack_kernel(n, heads, *refs), name, [((length, HD), bf...  4.4 us
    pallas_call x4, Pallas kernels, grad(): call(lambda *refs: grad_kernel(rows, half, *refs), name, [((cols, len(hea...  2.24 us
    ppermute x1, starting transfers between devices, swap_plane(): return lax.ppermute(x, ('tm', 'head'), pairs)  1.73 us
    pallas_call x1, Pallas kernels, head_body(): call(lambda *refs: finish_kernel(heads, tok, *refs), 'finish', [((tok, wi...  1.29 us
    unnamed x8, local copies, waits for them, and re-layouts  1.26 us
  transfers between devices with their start and end apart: 20, of which 11 were waited for; matrix products, arithmetic and copies ran while one was open for 0% of the time, Pallas kernels for 19%

profile of v4, /device:TPU:0, one launch (start us, length us, event | category | flops | bytes accessed | tf_op | source)
XLA Modules:
  0.0 57.8 jit_solution(18317987729368005175)
XLA Ops:
  0.6 1.9 %pack_first.1 = (bf16[784,128]{1,0:T(8,128)(2,1)}, bf16[784,128]{1,0:T(8,128)(2,1)}) custom-call(bf16[256,1024]{1,0:T(8,128)(2,1)} %refs_0_.6, bf16[256,1024]{1,0:T(8,128)(2,1)} %refs_1_.5, bf16[256,1024]{1,0:T(8,128)(2,1)} %refs_2_.3, bf16[2,1024]{1,0:T(2,128)(2,1)} %refs_3_.3), custom_call_target="tpu_custom_call" | custom-call | bytes 802816 | tf_op jit(solution)/shard_map/pack_first/pallas_call | solution.py:330
  2.5 4.0 %collective-permute-start = (bf16[784,128]{1,0:T(8,128)(2,1)}, bf16[784,128]{1,0:T(8,128)(2,1)S(1)}, u32[]{:S(2)}, u32[]{:S(2)}) collective-permute-start(bf16[784,128]{1,0:T(8,128)(2,1)} %get-tuple-element.18), channel_id=1, source_target_pairs={{0,24},{4,28},{8,16},{12,20},{16,8},{20,12},{24,0},{28,4},{1,25},{... | collective-permute-start | bytes 602120 | tf_op jit(solution)/shard_map/ppermute | solution.py:305
  6.5 2.5 %pack_rest.1 = (bf16[784,128]{1,0:T(8,128)(2,1)}, bf16[784,128]{1,0:T(8,128)(2,1)}, bf16[784,128]{1,0:T(8,128)(2,1)}, bf16[784,128]{1,0:T(8,128)(2,1)}, bf16[784...) custom-call(bf16[256,1024]{1,0:T(8,128)(2,1)} %refs_0_.6, bf16[256,1024]{1,0:T(8,128)(2,1)} %refs_1_.5, ...), custom_call_target="tpu_custom_call" | custom-call | bytes 2408448 | tf_op jit(solution)/shard_map/pack_rest/pallas_call | solution.py:330
  9.0 1.2 %collective-permute-start.5 = (bf16[784,128]{1,0:T(8,128)(2,1)}, bf16[784,128]{1,0:T(8,128)(2,1)S(1)}, u32[]{:S(2)}, u32[]{:S(2)}) collective-permute-start(bf16[784,128]{1,0:T(8,128)(2,1)} %get-tuple-element.25), channel_id=1, source_target_pairs={{0,8},{4,12},{8,0},{12,4},{16,24},{20,28},{24,16},{28,20},{1,9},{5... | collective-permute-start | bytes 602120 | tf_op jit(solution)/shard_map/ppermute | solution.py:305
  10.2 1.5 %collective-permute-start.6 = (bf16[784,128]{1,0:T(8,128)(2,1)}, bf16[784,128]{1,0:T(8,128)(2,1)S(1)}, u32[]{:S(2)}, u32[]{:S(2)}) collective-permute-start(bf16[784,128]{1,0:T(8,128)(2,1)} %get-tuple-element.26), channel_id=1, source_target_pairs={{0,16},{4,20},{8,24},{12,28},{16,0},{20,4},{24,8},{28,12},{1,17},{... | collective-permute-start | bytes 602120 | tf_op jit(solution)/shard_map/ppermute | solution.py:305
  11.7 0.6 collective-permute-start.7
  12.5 0.4 collective-permute-start.8
  12.9 3.6 %collective-permute-done.1.refs_3_ = bf16[784,128]{1,0:T(8,128)(2,1)S(1)} collective-permute-done((bf16[784,128]{1,0:T(8,128)(2,1)}, bf16[784,128]{1,0:T(8,128)(2,1)S(1)}, u32[]{:S(2)}, u32[]{:S(2)}) %collective-permute-start.1) | collective-permute-done | bytes 200736 | tf_op jit(solution)/shard_map/ppermute | solution.py:305
  16.6 1.2 %copy-done = bf16[272,2048]{1,0:T(8,128)(2,1)S(1)} copy-done((bf16[272,2048]{1,0:T(8,128)(2,1)S(1)}, bf16[272,2048]{1,0:T(8,128)(2,1)}, u32[]{:S(2)}) %copy-start) | copy-done | bytes 1114136
  17.9 0.9 %cot.1 = (bf16[576,128]{1,0:T(8,128)(2,1)S(1)}, bf16[576,128]{1,0:T(8,128)(2,1)S(1)}, bf16[576,128]{1,0:T(8,128)(2,1)S(1)}, bf16[576,128]{1,0:T(8,128)(2,1)S(1)}) custom-call(s32[1,8]{1,0:T(1,128)S(1)} %copy-done.1, bf16[272,2048]{1,0:T(8,128)(2,1)S(1)} %copy-done, bf16[784,128]{1,0:T(8,128)(2,1)S(1)} %collective-permute-done.refs_2_, ...), custom_call_target="tpu_custom_call" | custom-call | bytes 1179648 | tf_op jit(solution)/shard_map/cot/pallas_call | solution.py:353
  18.8 2.9 %collective-permute-done.5.refs_4_ = bf16[784,128]{1,0:T(8,128)(2,1)S(1)} collective-permute-done((bf16[784,128]{1,0:T(8,128)(2,1)}, bf16[784,128]{1,0:T(8,128)(2,1)S(1)}, u32[]{:S(2)}, u32[]{:S(2)}) %collective-permute-start.5) | collective-permute-done | bytes 200736 | tf_op jit(solution)/shard_map/ppermute | solution.py:305
  21.7 1.5 %collective-permute-start.2 = (bf16[576,128]{1,0:T(8,128)(2,1)S(1)}, bf16[576,128]{1,0:T(8,128)(2,1)S(1)}, u32[]{:S(2)}, u32[]{:S(2)}) collective-permute-start(bf16[576,128]{1,0:T(8,128)(2,1)S(1)} %get-tuple-element.20), channel_id=1, source_target_pairs={{0,24},{4,28},{8,16},{12,20},{16,8},{20,12},{24,0},{28,4},{1,25},{... | collective-permute-start | bytes 442376 | tf_op jit(solution)/shard_map/ppermute | solution.py:305
  23.2 1.9 %collective-permute-done.7.refs_6_ = bf16[784,128]{1,0:T(8,128)(2,1)S(1)} collective-permute-done((bf16[784,128]{1,0:T(8,128)(2,1)}, bf16[784,128]{1,0:T(8,128)(2,1)S(1)}, u32[]{:S(2)}, u32[]{:S(2)}) %collective-permute-start.7) | collective-permute-done | bytes 200736 | tf_op jit(solution)/shard_map/ppermute | solution.py:305
  25.1 0.5 collective-permute-start.4
  25.6 5.1 %attend.1 = (bf16[1040,128]{1,0:T(8,128)(2,1)S(1)}, bf16[1040,128]{1,0:T(8,128)(2,1)S(1)}) custom-call(s32[8]{0:T(128)S(1)} %copy-done.3, bf16[784,128]{1,0:T(8,128)(2,1)S(1)} %copy-done.2, bf16[784,128]{1,0:T(8,128)(2,1)S(1)} %collective-permute-done.refs_2_, bf16[784,128]{1,0:T(8,128)(2,1)S(1)} %collective-permute-done.1.refs_3_, ...), custom_call_target="tpu_custom_call" | custom-call | flops 1073741824 | bytes 1064960 | tf_op jit(solution)/shard_map/attend/pallas_call | solution.py:374
  31.1 0.9 %collective-permute-done.4.refs_2_ = bf16[576,128]{1,0:T(8,128)(2,1)S(1)} collective-permute-done((bf16[576,128]{1,0:T(8,128)(2,1)S(1)}, bf16[576,128]{1,0:T(8,128)(2,1)S(1)}, u32[]{:S(2)}, u32[]{:S(2)}) %collective-permute-start.4) | collective-permute-done | bytes 147488 | tf_op jit(solution)/shard_map/ppermute | solution.py:305
  32.1 1.7 %collective-permute-start.10 = (bf16[4,576,128]{2,1,0:T(8,128)(2,1)S(1)}, bf16[4,576,128]{2,1,0:T(8,128)(2,1)S(1)}, u32[]{:S(2)}, u32[]{:S(2)}) collective-permute-start(bf16[4,576,128]{2,1,0:T(8,128)(2,1)S(1)} %stack.1.refs_0_), channel_id=1, source_target_pairs={{0,1},{1,0},{2,3},{3,2},{4,5},{5,4},{6,7},{7,6},{8,9},{9,8},{10,11... | collective-permute-start | bytes 1769480 | tf_op jit(solution)/shard_map/ppermute | solution.py:311
  34.2 1.1 %collective-permute-start.13 = (bf16[1040,128]{1,0:T(8,128)(2,1)S(1)}, bf16[1040,128]{1,0:T(8,128)(2,1)S(1)}, u32[]{:S(2)}, u32[]{:S(2)}) collective-permute-start(bf16[1040,128]{1,0:T(8,128)(2,1)S(1)} %get-tuple-element.30.refs_4_.refs_1_), channel_id=1, source_target_pairs={{0,8},{4,12},{8,0},{12,4},{16,24},{20,28},{24,16},{28,20},{1,9},{5... | collective-permute-start | bytes 798728 | tf_op jit(solution)/shard_map/ppermute | solution.py:305
  35.3 0.9 %collective-permute-start.11 = (bf16[1040,128]{1,0:T(8,128)(2,1)S(1)}, bf16[1040,128]{1,0:T(8,128)(2,1)S(1)}, u32[]{:S(2)}, u32[]{:S(2)}) collective-permute-start(bf16[1040,128]{1,0:T(8,128)(2,1)S(1)} %get-tuple-element.32.x_ref), channel_id=1, source_target_pairs={{0,12},{4,8},{8,4},{12,0},{16,28},{20,24},{24,20},{28,16},{1,13},{... | collective-permute-start | bytes 798728 | tf_op jit(solution)/shard_map/ppermute | solution.py:305
  36.2 1.1 %collective-permute-start.12 = (bf16[1040,128]{1,0:T(8,128)(2,1)S(1)}, bf16[1040,128]{1,0:T(8,128)(2,1)S(1)}, u32[]{:S(2)}, u32[]{:S(2)}) collective-permute-start(bf16[1040,128]{1,0:T(8,128)(2,1)S(1)} %get-tuple-element.30.refs_4_.refs_1_), channel_id=1, source_target_pairs={{0,16},{4,20},{8,24},{12,28},{16,0},{20,4},{24,8},{28,12},{1,17},{... | collective-permute-start | bytes 798728 | tf_op jit(solution)/shard_map/ppermute | solution.py:305
  37.3 5.2 %collective-permute-done.14.refs_5_.refs_8_ = bf16[1040,128]{1,0:T(8,128)(2,1)S(1)} collective-permute-done((bf16[1040,128]{1,0:T(8,128)(2,1)S(1)}, bf16[1040,128]{1,0:T(8,128)(2,1)S(1)}, u32[]{:S(2)}, u32[]{:S(2)}) %collective-permute-start.14) | collective-permute-done | bytes 266272 | tf_op jit(solution)/shard_map/ppermute | solution.py:305
  42.5 0.7 %collective-permute-start.17 = (bf16[1040,128]{1,0:T(8,128)(2,1)S(1)}, bf16[1040,128]{1,0:T(8,128)(2,1)S(1)}, u32[]{:S(2)}, u32[]{:S(2)}) collective-permute-start(bf16[1040,128]{1,0:T(8,128)(2,1)S(1)} %collective-permute-done.14.refs_5_.refs_8_), channel_id=1, source_target_pairs={{0,8},{4,12},{8,0},{12,4},{16,24},{20,28},{24,16},{28,20},{1,9},{5... | collective-permute-start | bytes 798728 | tf_op jit(solution)/shard_map/ppermute | solution.py:305
  43.4 1.0 %collective-permute-start.16 = (bf16[1040,128]{1,0:T(8,128)(2,1)S(1)}, bf16[1040,128]{1,0:T(8,128)(2,1)S(1)}, u32[]{:S(2)}, u32[]{:S(2)}) collective-permute-start(bf16[1040,128]{1,0:T(8,128)(2,1)S(1)} %collective-permute-done.13.refs_4_.refs_7_), channel_id=1, source_target_pairs={{0,16},{4,20},{8,24},{12,28},{16,0},{20,4},{24,8},{28,12},{1,17},{... | collective-permute-start | bytes 798728 | tf_op jit(solution)/shard_map/ppermute | solution.py:305
  44.5 4.1 %collective-permute-done.11.refs_2_.refs_0_.refs_5_ = bf16[1040,128]{1,0:T(8,128)(2,1)S(1)} collective-permute-done((bf16[1040,128]{1,0:T(8,128)(2,1)S(1)}, bf16[1040,128]{1,0:T(8,128)(2,1)S(1)}, u32[]{:S(2)}, u32[]{:S(2)}) %collective-permute-start.11) | collective-permute-done | bytes 266272 | tf_op jit(solution)/shard_map/ppermute | solution.py:305
  48.6 0.8 %collective-permute-start.15 = (bf16[1040,128]{1,0:T(8,128)(2,1)S(1)}, bf16[1040,128]{1,0:T(8,128)(2,1)S(1)}, u32[]{:S(2)}, u32[]{:S(2)}) collective-permute-start(bf16[1040,128]{1,0:T(8,128)(2,1)S(1)} %late.1), channel_id=1, source_target_pairs={{0,4},{4,0},{8,12},{12,8},{16,20},{20,16},{24,28},{28,24},{1,5},{5... | collective-permute-start | bytes 798728 | tf_op jit(solution)/shard_map/ppermute | solution.py:305
  49.3 0.4 turn.1
  49.7 0.6 %grad_other_near.1 = bf16[256,640]{1,0:T(8,128)(2,1)S(1)} custom-call(bf16[256,1088]{1,0:T(8,128)(2,1)S(1)} %get-tuple-element.33.refs_0_, bf16[1040,128]{1,0:T(8,128)(2,1)S(1)} %get-tuple-element.30.refs_4_.refs_1_, bf16[1040,128]{1,0:T(8,128)(2,1)S(1)} %collective-permute-done.11.refs_2_.refs_0_.refs_5_, ...), custom_call_target="tpu_custom_call" | custom-call | flops 356515840 | bytes 655360 | tf_op jit(solution)/shard_map/grad_other_near/pallas_call | solution.py:408
  50.5 4.1 %collective-permute-done.17.refs_3_.refs_11_ = bf16[1040,128]{1,0:T(8,128)(2,1)S(1)} collective-permute-done((bf16[1040,128]{1,0:T(8,128)(2,1)S(1)}, bf16[1040,128]{1,0:T(8,128)(2,1)S(1)}, u32[]{:S(2)}, u32[]{:S(2)}) %collective-permute-start.17) | collective-permute-done | bytes 266272 | tf_op jit(solution)/shard_map/ppermute | solution.py:305
  54.6 0.5 grad_other_far.1
  55.1 0.5 grad_own_far.1.refs_1_
  55.6 0.6 %grad_own_near.1.refs_0_ = f32[256,640]{1,0:T(8,128)S(1)} custom-call(bf16[256,1088]{1,0:T(8,128)(2,1)S(1)} %get-tuple-element.31.refs_0_, bf16[1040,128]{1,0:T(8,128)(2,1)S(1)} %get-tuple-element.30.refs_4_.refs_1_, bf16[1040,128]{1,0:T(8,128)(2,1)S(1)} %collective-permute-done.11.refs_2_.refs_0_.refs_5_, ...), custom_call_target="tpu_custom_call" | custom-call | flops 356515840 | bytes 1310720 | tf_op jit(solution)/shard_map/grad_own_near/pallas_call | solution.py:408
  56.6 1.3 %finish.1 = (bf16[256,1024]{1,0:T(8,128)(2,1)}, f32[256,1024]{1,0:T(8,128)}) custom-call(f32[256,640]{1,0:T(8,128)S(1)} %grad_own_near.1.refs_0_, f32[256,384]{1,0:T(8,128)S(1)} %grad_own_far.1.refs_1_, bf16[256,640]{1,0:T(8,128)(2,1)S(1)} %collective-permute-done.18.refs_2_, bf16[256,384]{1,0:T(8,128)(2,1)S(1)} %collective-permute-done.19.refs_3_, ...), custom_call_target="tpu_custom_call" | custom-call | bytes 3145728 | tf_op jit(solution)/shard_map/finish/pallas_call | solution.py:424
  (28 shorter events, 1.9 us)
Async XLA Ops:
  2.5 14.1 %copy-start.1 = (s32[1,8]{1,0:T(1,128)S(1)}, s32[1,8]{1,0:T(1,128)}, u32[]{:S(2)}) copy-start(s32[1,8]{1,0:T(1,128)} %refs_0_.5) | copy-start | bytes 100
  2.5 10.0 %collective-permute-start = (bf16[784,128]{1,0:T(8,128)(2,1)}, bf16[784,128]{1,0:T(8,128)(2,1)S(1)}, u32[]{:S(2)}, u32[]{:S(2)}) collective-permute-start(bf16[784,128]{1,0:T(8,128)(2,1)} %get-tuple-element.18), channel_id=1, source_target_pairs={{0,24},{4,28},{8,16},{12,20},{16,8},{20,12},{24,0},{28,4},{1,25},{... | collective-permute-start | bytes 602120 | tf_op jit(solution)/shard_map/ppermute | solution.py:305
  6.5 10.1 %collective-permute-start.1 = (bf16[784,128]{1,0:T(8,128)(2,1)}, bf16[784,128]{1,0:T(8,128)(2,1)S(1)}, u32[]{:S(2)}, u32[]{:S(2)}) collective-permute-start(bf16[784,128]{1,0:T(8,128)(2,1)} %get-tuple-element.19), channel_id=1, source_target_pairs={{0,28},{4,24},{8,20},{12,16},{16,12},{20,8},{24,4},{28,0},{1,29},{... | collective-permute-start | bytes 602120 | tf_op jit(solution)/shard_map/ppermute | solution.py:305
  9.0 16.6 %copy-start.3 = (s32[8]{0:T(128)S(1)}, s32[8]{0:T(128)}, u32[]{:S(2)}) copy-start(s32[8]{0:T(128)} %refs_0_.7) | copy-start | bytes 100
  9.0 12.6 %collective-permute-start.5 = (bf16[784,128]{1,0:T(8,128)(2,1)}, bf16[784,128]{1,0:T(8,128)(2,1)S(1)}, u32[]{:S(2)}, u32[]{:S(2)}) collective-permute-start(bf16[784,128]{1,0:T(8,128)(2,1)} %get-tuple-element.25), channel_id=1, source_target_pairs={{0,8},{4,12},{8,0},{12,4},{16,24},{20,28},{24,16},{28,20},{1,9},{5... | collective-permute-start | bytes 602120 | tf_op jit(solution)/shard_map/ppermute | solution.py:305
  10.2 12.9 %collective-permute-start.6 = (bf16[784,128]{1,0:T(8,128)(2,1)}, bf16[784,128]{1,0:T(8,128)(2,1)S(1)}, u32[]{:S(2)}, u32[]{:S(2)}) collective-permute-start(bf16[784,128]{1,0:T(8,128)(2,1)} %get-tuple-element.26), channel_id=1, source_target_pairs={{0,16},{4,20},{8,24},{12,28},{16,0},{20,4},{24,8},{28,12},{1,17},{... | collective-permute-start | bytes 602120 | tf_op jit(solution)/shard_map/ppermute | solution.py:305
  11.7 13.4 %collective-permute-start.7 = (bf16[784,128]{1,0:T(8,128)(2,1)}, bf16[784,128]{1,0:T(8,128)(2,1)S(1)}, u32[]{:S(2)}, u32[]{:S(2)}) collective-permute-start(bf16[784,128]{1,0:T(8,128)(2,1)} %get-tuple-element.27), channel_id=1, source_target_pairs={{0,12},{4,8},{8,4},{12,0},{16,28},{20,24},{24,20},{28,16},{1,13},{... | collective-permute-start | bytes 602120 | tf_op jit(solution)/shard_map/ppermute | solution.py:305
  12.5 13.1 %collective-permute-start.8 = (bf16[784,128]{1,0:T(8,128)(2,1)}, bf16[784,128]{1,0:T(8,128)(2,1)S(1)}, u32[]{:S(2)}, u32[]{:S(2)}) collective-permute-start(bf16[784,128]{1,0:T(8,128)(2,1)} %get-tuple-element.28), channel_id=1, source_target_pairs={{0,20},{4,16},{8,28},{12,24},{16,4},{20,0},{24,12},{28,8},{1,21},{... | collective-permute-start | bytes 602120 | tf_op jit(solution)/shard_map/ppermute | solution.py:305
  16.5 9.1 %collective-permute-start.9 = (bf16[784,128]{1,0:T(8,128)(2,1)}, bf16[784,128]{1,0:T(8,128)(2,1)S(1)}, u32[]{:S(2)}, u32[]{:S(2)}) collective-permute-start(bf16[784,128]{1,0:T(8,128)(2,1)} %get-tuple-element.29), channel_id=1, source_target_pairs={{0,4},{4,0},{8,12},{12,8},{16,20},{20,16},{24,28},{28,24},{1,5},{5... | collective-permute-start | bytes 602120 | tf_op jit(solution)/shard_map/ppermute | solution.py:305
  16.6 1.2 %copy-start = (bf16[272,2048]{1,0:T(8,128)(2,1)S(1)}, bf16[272,2048]{1,0:T(8,128)(2,1)}, u32[]{:S(2)}) copy-start(bf16[272,2048]{1,0:T(8,128)(2,1)} %refs_1_.4) | copy-start | bytes 3342340
  17.9 7.8 %copy-start.2 = (bf16[784,128]{1,0:T(8,128)(2,1)S(1)}, bf16[784,128]{1,0:T(8,128)(2,1)}, u32[]{:S(2)}) copy-start(bf16[784,128]{1,0:T(8,128)(2,1)} %get-tuple-element.24.refs_1_) | copy-start | bytes 602116
  21.7 9.1 %collective-permute-start.2 = (bf16[576,128]{1,0:T(8,128)(2,1)S(1)}, bf16[576,128]{1,0:T(8,128)(2,1)S(1)}, u32[]{:S(2)}, u32[]{:S(2)}) collective-permute-start(bf16[576,128]{1,0:T(8,128)(2,1)S(1)} %get-tuple-element.20), channel_id=1, source_target_pairs={{0,24},{4,28},{8,16},{12,20},{16,8},{20,12},{24,0},{28,4},{1,25},{... | collective-permute-start | bytes 442376 | tf_op jit(solution)/shard_map/ppermute | solution.py:305
  23.1 8.0 %collective-permute-start.3 = (bf16[576,128]{1,0:T(8,128)(2,1)S(1)}, bf16[576,128]{1,0:T(8,128)(2,1)S(1)}, u32[]{:S(2)}, u32[]{:S(2)}) collective-permute-start(bf16[576,128]{1,0:T(8,128)(2,1)S(1)} %get-tuple-element.21), channel_id=1, source_target_pairs={{0,8},{4,12},{8,0},{12,4},{16,24},{20,28},{24,16},{28,20},{1,9},{5... | collective-permute-start | bytes 442376 | tf_op jit(solution)/shard_map/ppermute | solution.py:305
  25.1 6.9 %collective-permute-start.4 = (bf16[576,128]{1,0:T(8,128)(2,1)S(1)}, bf16[576,128]{1,0:T(8,128)(2,1)S(1)}, u32[]{:S(2)}, u32[]{:S(2)}) collective-permute-start(bf16[576,128]{1,0:T(8,128)(2,1)S(1)} %get-tuple-element.22), channel_id=1, source_target_pairs={{0,16},{4,20},{8,24},{12,28},{16,0},{20,4},{24,8},{28,12},{1,17},{... | collective-permute-start | bytes 442376 | tf_op jit(solution)/shard_map/ppermute | solution.py:305
  32.1 17.3 %collective-permute-start.10 = (bf16[4,576,128]{2,1,0:T(8,128)(2,1)S(1)}, bf16[4,576,128]{2,1,0:T(8,128)(2,1)S(1)}, u32[]{:S(2)}, u32[]{:S(2)}) collective-permute-start(bf16[4,576,128]{2,1,0:T(8,128)(2,1)S(1)} %stack.1.refs_0_), channel_id=1, source_target_pairs={{0,1},{1,0},{2,3},{3,2},{4,5},{5,4},{6,7},{7,6},{8,9},{9,8},{10,11... | collective-permute-start | bytes 1769480 | tf_op jit(solution)/shard_map/ppermute | solution.py:311
  33.8 8.7 %collective-permute-start.14 = (bf16[1040,128]{1,0:T(8,128)(2,1)S(1)}, bf16[1040,128]{1,0:T(8,128)(2,1)S(1)}, u32[]{:S(2)}, u32[]{:S(2)}) collective-permute-start(bf16[1040,128]{1,0:T(8,128)(2,1)S(1)} %get-tuple-element.32.x_ref), channel_id=1, source_target_pairs={{0,20},{4,16},{8,28},{12,24},{16,4},{20,0},{24,12},{28,8},{1,21},{... | collective-permute-start | bytes 798728 | tf_op jit(solution)/shard_map/ppermute | solution.py:305
  34.2 9.3 %collective-permute-start.13 = (bf16[1040,128]{1,0:T(8,128)(2,1)S(1)}, bf16[1040,128]{1,0:T(8,128)(2,1)S(1)}, u32[]{:S(2)}, u32[]{:S(2)}) collective-permute-start(bf16[1040,128]{1,0:T(8,128)(2,1)S(1)} %get-tuple-element.30.refs_4_.refs_1_), channel_id=1, source_target_pairs={{0,8},{4,12},{8,0},{12,4},{16,24},{20,28},{24,16},{28,20},{1,9},{5... | collective-permute-start | bytes 798728 | tf_op jit(solution)/shard_map/ppermute | solution.py:305
  35.3 13.3 %collective-permute-start.11 = (bf16[1040,128]{1,0:T(8,128)(2,1)S(1)}, bf16[1040,128]{1,0:T(8,128)(2,1)S(1)}, u32[]{:S(2)}, u32[]{:S(2)}) collective-permute-start(bf16[1040,128]{1,0:T(8,128)(2,1)S(1)} %get-tuple-element.32.x_ref), channel_id=1, source_target_pairs={{0,12},{4,8},{8,4},{12,0},{16,28},{20,24},{24,20},{28,16},{1,13},{... | collective-permute-start | bytes 798728 | tf_op jit(solution)/shard_map/ppermute | solution.py:305
  36.2 12.3 %collective-permute-start.12 = (bf16[1040,128]{1,0:T(8,128)(2,1)S(1)}, bf16[1040,128]{1,0:T(8,128)(2,1)S(1)}, u32[]{:S(2)}, u32[]{:S(2)}) collective-permute-start(bf16[1040,128]{1,0:T(8,128)(2,1)S(1)} %get-tuple-element.30.refs_4_.refs_1_), channel_id=1, source_target_pairs={{0,16},{4,20},{8,24},{12,28},{16,0},{20,4},{24,8},{28,12},{1,17},{... | collective-permute-start | bytes 798728 | tf_op jit(solution)/shard_map/ppermute | solution.py:305
  42.5 12.1 %collective-permute-start.17 = (bf16[1040,128]{1,0:T(8,128)(2,1)S(1)}, bf16[1040,128]{1,0:T(8,128)(2,1)S(1)}, u32[]{:S(2)}, u32[]{:S(2)}) collective-permute-start(bf16[1040,128]{1,0:T(8,128)(2,1)S(1)} %collective-permute-done.14.refs_5_.refs_8_), channel_id=1, source_target_pairs={{0,8},{4,12},{8,0},{12,4},{16,24},{20,28},{24,16},{28,20},{1,9},{5... | collective-permute-start | bytes 798728 | tf_op jit(solution)/shard_map/ppermute | solution.py:305
  43.4 11.1 %collective-permute-start.16 = (bf16[1040,128]{1,0:T(8,128)(2,1)S(1)}, bf16[1040,128]{1,0:T(8,128)(2,1)S(1)}, u32[]{:S(2)}, u32[]{:S(2)}) collective-permute-start(bf16[1040,128]{1,0:T(8,128)(2,1)S(1)} %collective-permute-done.13.refs_4_.refs_7_), channel_id=1, source_target_pairs={{0,16},{4,20},{8,24},{12,28},{16,0},{20,4},{24,8},{28,12},{1,17},{... | collective-permute-start | bytes 798728 | tf_op jit(solution)/shard_map/ppermute | solution.py:305
  48.6 6.0 %collective-permute-start.15 = (bf16[1040,128]{1,0:T(8,128)(2,1)S(1)}, bf16[1040,128]{1,0:T(8,128)(2,1)S(1)}, u32[]{:S(2)}, u32[]{:S(2)}) collective-permute-start(bf16[1040,128]{1,0:T(8,128)(2,1)S(1)} %late.1), channel_id=1, source_target_pairs={{0,4},{4,0},{8,12},{12,8},{16,20},{20,16},{24,28},{28,24},{1,5},{5... | collective-permute-start | bytes 798728 | tf_op jit(solution)/shard_map/ppermute | solution.py:305
  50.4 6.2 %collective-permute-start.18 = (bf16[256,640]{1,0:T(8,128)(2,1)S(1)}, bf16[256,640]{1,0:T(8,128)(2,1)S(1)}, u32[]{:S(2)}, u32[]{:S(2)}) collective-permute-start(bf16[256,640]{1,0:T(8,128)(2,1)S(1)} %grad_other_near.1), channel_id=1, source_target_pairs={{0,4},{4,0},{8,12},{12,8},{16,20},{20,16},{24,28},{28,24},{1,5},{5... | collective-permute-start | bytes 983048 | tf_op jit(solution)/shard_map/ppermute | solution.py:305
  55.0 1.5 %collective-permute-start.19 = (bf16[256,384]{1,0:T(8,128)(2,1)S(1)}, bf16[256,384]{1,0:T(8,128)(2,1)S(1)}, u32[]{:S(2)}, u32[]{:S(2)}) collective-permute-start(bf16[256,384]{1,0:T(8,128)(2,1)S(1)} %grad_other_far.1), channel_id=1, source_target_pairs={{0,4},{4,0},{8,12},{12,8},{16,20},{20,16},{24,28},{28,24},{1,5},{5... | collective-permute-start | bytes 589832 | tf_op jit(solution)/shard_map/ppermute | solution.py:305

commit v5 on v4

--- a/solution.py
+++ b/solution.py
@@ -11,7 +11,7 @@
 TPF = 64
 WINB = 4
 VMEM_LIMIT = 24 * 1024 * 1024
-PACK_LIMIT = 63 * 1024 * 1024
+PACK_LIMIT = 58 * 1024 * 1024
 
 
 def from_behind(x, axis, by):
@@ -343,8 +343,20 @@
             limit=PACK_LIMIT,
         )(query_rows, key_rows, value_rows, history)
 
-    first, rest = [6, 7], [0, 1, 2, 3, 4, 5]
-    packed = dict(zip(first, pack(first, 2 * HD, "pack_first")))
+    own = lax.axis_index("tm")
+    row = lax.broadcasted_iota(jnp.int32, (clip_rows, 1), 0)
+    placed = jnp.zeros((clip_rows, width), jnp.bfloat16)
+    for t in range(tile):
+        placed = jnp.where(row == own * tile + t, history[t : t + 1], placed)
+
+    def cut(k):
+        pieces = (query_rows, key_rows, value_rows, placed)
+        return jnp.concatenate(
+            [lax.dynamic_slice(x, (0, (own ^ k) * HD), (x.shape[0], HD)) for x in pieces], axis=0
+        )
+
+    rest = [0, 1, 2, 3, 4, 5]
+    packed = {k: cut(k) for k in (6, 7)}
     packed.update(zip(rest, pack(rest, width, "pack_rest")))
     order = [6, 7, 2, 4, 3, 5, 1]
     arrived = {k: swap(packed[k], k) for k in order}
@@ -361,7 +373,7 @@
             pltpu.VMEM((part, all_cols), bf16),
             pltpu.SemaphoreType.DMA((2,)),
         ),
-    )(offsets, cotangent, arrived[6], arrived[7])
+    )(offsets, cotangent, arrived[6], arrived[1])
     moved = {m: swap(cots[m], 2 * m) for m in reversed(chips[1:])}
     cots = [cots[0]] + [moved[m] for m in chips[1:]]
     counts = (

time: 58 us -> 59 us (1.017)
  starting transfers between devices: 17.6 us -> 20.8 us
  waiting for transfers between devices: 23.8 us -> 21.8 us
  Pallas kernels: 14.3 us -> 12.5 us
  local copies, waits for them, and re-layouts: 1.26 us -> 2.69 us
    ppermute x19, starting transfers between devices: 15.9 us -> 19.1 us  [swap(): return lax.ppermute(x, 'tm', [(i, i ^ bit) for i in range(n)])]
    ppermute x19, waiting for transfers between devices: 23.8 us -> 21.8 us  [swap(): return lax.ppermute(x, 'tm', [(i, i ^ bit) for i in range(n)])]
    pallas_call x2 -> x1, Pallas kernels: 4.4 us -> 2.53 us  [pack(): call(lambda *refs: pack_kernel(n, heads, *refs), name, [((length, HD), bf...]
    dynamic_slice x0 -> x3, local copies, waits for them, and re-layouts: none -> 1.87 us  [cut(): lax.dynamic_slice(x, (0, (own ^ k) * HD), (x.shape[0], HD))]
    unnamed x8, local copies, waits for them, and re-layouts: 1.26 us -> 0.03 us
    slice x0 -> x1, local copies, waits for them, and re-layouts: none -> 0.8 us  [head_body(): placed = jnp.where(row == own * tile + t, history[t:t + 1], placed)]
  transfers between devices with their start and end apart: 20 -> 20, of which waited for: 11 -> 9; matrix products, arithmetic and copies ran while one was open for 0% -> 0% of each run, Pallas kernels for 19% -> 19%
where the time goes in v5:
time: 59 us; the launch traced here: 58.7 us
  waiting for transfers between devices  21.8 us (37%)
  starting transfers between devices  20.8 us (35%)
  Pallas kernels  12.5 us (21%)
  local copies, waits for them, and re-layouts  2.69 us (5%)
  between operations  0.83 us (1%)
    ppermute x19, waiting for transfers between devices, swap(): return lax.ppermute(x, 'tm', [(i, i ^ bit) for i in range(n)])  21.8 us
    ppermute x19, starting transfers between devices, swap(): return lax.ppermute(x, 'tm', [(i, i ^ bit) for i in range(n)])  19.1 us
    pallas_call x1, Pallas kernels, head_body(): call(lambda *refs: attend_kernel(n, tok, [0] + order, *refs), 'attend', [...  5.11 us
    pallas_call x1, Pallas kernels, pack(): call(lambda *refs: pack_kernel(n, heads, *refs), name, [((length, HD), bf...  2.53 us
    pallas_call x4, Pallas kernels, grad(): call(lambda *refs: grad_kernel(rows, half, *refs), name, [((cols, len(hea...  2.26 us
    dynamic_slice x3, local copies, waits for them, and re-layouts, cut(): lax.dynamic_slice(x, (0, (own ^ k) * HD), (x.shape[0], HD))  1.87 us
    ppermute x1, starting transfers between devices, swap_plane(): return lax.ppermute(x, ('tm', 'head'), pairs)  1.64 us
    pallas_call x1, Pallas kernels, head_body(): call(lambda *refs: finish_kernel(heads, tok, *refs), 'finish', [((tok, wi...  1.29 us
  transfers between devices with their start and end apart: 20, of which 9 were waited for; matrix products, arithmetic and copies ran while one was open for 0% of the time, Pallas kernels for 19%

profile of v5, /device:TPU:0, one launch (start us, length us, event | category | flops | bytes accessed | tf_op | source)
XLA Modules:
  0.0 58.7 jit_solution(848849693175141772)
XLA Ops:
  0.7 0.8 %slice_reduce_fusion.1 = (bf16[1024]{0:T(1024)(128)(2,1)S(1)}, bf16[1024]{0:T(1024)(128)(2,1)S(1)}) fusion(bf16[2,1024]{1,0:T(2,128)(2,1)} %refs_3_.1), kind=kLoop, calls=%fused_computation.4 | loop fusion | bytes 8192 | tf_op jit(solution)/shard_map/slice | solution.py:350
  1.5 0.9 %constant_dynamic-slice_fusion.3 = (bf16[256,128]{1,0:T(8,128)(2,1)S(1)}, bf16[256,128]{1,0:T(8,128)(2,1)S(1)}) fusion(bf16[256,1024]{1,0:T(8,128)(2,1)} %refs_0_.3, s32[]{:T(128)S(6)} %select_n.22, s32[]{:T(128)S(6)} %select_n.19), kind=kLoop, calls=%fused_computation.8 | loop fusion | bytes 262152 | tf_op jit(solution)/shard_map/dynamic_slice | solution.py:355
  2.4 1.0 %constant_dynamic-slice_fusion.1 = (bf16[256,128]{1,0:T(8,128)(2,1)S(1)}, bf16[256,128]{1,0:T(8,128)(2,1)S(1)}, bf16[256,128]{1,0:T(8,128)(2,1)S(1)}, bf16[256,128]{1,0:T(8,128)(2,1)S(1)}) fusion(bf16[256,1024]{1,0:T(8,128)(2,1)} %refs_2_.1, s32[]{:T(128)S(6)} %select_n.22, s32[]{:T(128)S(6)} %select_n.19, bf16[256,1024]{1,0:T(8,128)(2,1)} %refs_1_.2), kind=kLoop, calls=%fused_computation.6 | loop fusion | bytes 524296 | tf_op jit(solution)/shard_map/dynamic_slice | solution.py:355
  3.5 4.0 %collective-permute-start = (bf16[784,128]{1,0:T(8,128)(2,1)S(1)}, bf16[784,128]{1,0:T(8,128)(2,1)S(1)}, u32[]{:S(2)}, u32[]{:S(2)}) collective-permute-start(bf16[784,128]{1,0:T(8,128)(2,1)S(1)} %pad_maximum_fusion), channel_id=1, source_target_pairs={{0,24},{4,28},{8,16},{12,20},{16,8},{20,12},{24,0},{28,4},{1,25},{... | collective-permute-start | bytes 602120 | tf_op jit(solution)/shard_map/ppermute | solution.py:305
  7.4 2.5 %pack_rest.1 = (bf16[784,128]{1,0:T(8,128)(2,1)}, bf16[784,128]{1,0:T(8,128)(2,1)}, bf16[784,128]{1,0:T(8,128)(2,1)}, bf16[784,128]{1,0:T(8,128)(2,1)}, bf16[784...) custom-call(bf16[256,1024]{1,0:T(8,128)(2,1)} %refs_0_.3, bf16[256,1024]{1,0:T(8,128)(2,1)} %refs_1_.2, ...), custom_call_target="tpu_custom_call" | custom-call | bytes 2408448 | tf_op jit(solution)/shard_map/pack_rest/pallas_call | solution.py:330
  10.3 1.9 %collective-permute-start.6 = (bf16[784,128]{1,0:T(8,128)(2,1)}, bf16[784,128]{1,0:T(8,128)(2,1)S(1)}, u32[]{:S(2)}, u32[]{:S(2)}) collective-permute-start(bf16[784,128]{1,0:T(8,128)(2,1)} %get-tuple-element.22), channel_id=1, source_target_pairs={{0,8},{4,12},{8,0},{12,4},{16,24},{20,28},{24,16},{28,20},{1,9},{5... | collective-permute-start | bytes 602120 | tf_op jit(solution)/shard_map/ppermute | solution.py:305
  12.2 1.5 %collective-permute-start.7 = (bf16[784,128]{1,0:T(8,128)(2,1)}, bf16[784,128]{1,0:T(8,128)(2,1)S(1)}, u32[]{:S(2)}, u32[]{:S(2)}) collective-permute-start(bf16[784,128]{1,0:T(8,128)(2,1)} %get-tuple-element.23), channel_id=1, source_target_pairs={{0,16},{4,20},{8,24},{12,28},{16,0},{20,4},{24,8},{28,12},{1,17},{... | collective-permute-start | bytes 602120 | tf_op jit(solution)/shard_map/ppermute | solution.py:305
  13.7 2.2 %collective-permute-start.9 = (bf16[784,128]{1,0:T(8,128)(2,1)}, bf16[784,128]{1,0:T(8,128)(2,1)S(1)}, u32[]{:S(2)}, u32[]{:S(2)}) collective-permute-start(bf16[784,128]{1,0:T(8,128)(2,1)} %get-tuple-element.25), channel_id=1, source_target_pairs={{0,20},{4,16},{8,28},{12,24},{16,4},{20,0},{24,12},{28,8},{1,21},{... | collective-permute-start | bytes 602120 | tf_op jit(solution)/shard_map/ppermute | solution.py:305
  15.9 0.9 %cot.1 = (bf16[576,128]{1,0:T(8,128)(2,1)S(1)}, bf16[576,128]{1,0:T(8,128)(2,1)S(1)}, bf16[576,128]{1,0:T(8,128)(2,1)S(1)}, bf16[576,128]{1,0:T(8,128)(2,1)S(1)}) custom-call(s32[1,8]{1,0:T(1,128)S(1)} %copy-done.1, bf16[272,2048]{1,0:T(8,128)(2,1)S(1)} %copy-done, bf16[784,128]{1,0:T(8,128)(2,1)S(1)} %collective-permute-done.refs_2_, ...), custom_call_target="tpu_custom_call" | custom-call | bytes 1179648 | tf_op jit(solution)/shard_map/cot/pallas_call | solution.py:365
  16.8 1.0 %collective-permute-done.5.refs_3_ = bf16[784,128]{1,0:T(8,128)(2,1)S(1)} collective-permute-done((bf16[784,128]{1,0:T(8,128)(2,1)S(1)}, bf16[784,128]{1,0:T(8,128)(2,1)S(1)}, u32[]{:S(2)}, u32[]{:S(2)}) %collective-permute-start.5) | collective-permute-done | bytes 200736 | tf_op jit(solution)/shard_map/ppermute | solution.py:305
  17.8 1.1 %collective-permute-start.2 = (bf16[576,128]{1,0:T(8,128)(2,1)S(1)}, bf16[576,128]{1,0:T(8,128)(2,1)S(1)}, u32[]{:S(2)}, u32[]{:S(2)}) collective-permute-start(bf16[576,128]{1,0:T(8,128)(2,1)S(1)} %get-tuple-element.17), channel_id=1, source_target_pairs={{0,24},{4,28},{8,16},{12,20},{16,8},{20,12},{24,0},{28,4},{1,25},{... | collective-permute-start | bytes 442376 | tf_op jit(solution)/shard_map/ppermute | solution.py:305
  18.9 3.5 %collective-permute-done.6.refs_4_ = bf16[784,128]{1,0:T(8,128)(2,1)S(1)} collective-permute-done((bf16[784,128]{1,0:T(8,128)(2,1)}, bf16[784,128]{1,0:T(8,128)(2,1)S(1)}, u32[]{:S(2)}, u32[]{:S(2)}) %collective-permute-start.6) | collective-permute-done | bytes 200736 | tf_op jit(solution)/shard_map/ppermute | solution.py:305
  22.3 1.0 %collective-permute-start.3 = (bf16[576,128]{1,0:T(8,128)(2,1)S(1)}, bf16[576,128]{1,0:T(8,128)(2,1)S(1)}, u32[]{:S(2)}, u32[]{:S(2)}) collective-permute-start(bf16[576,128]{1,0:T(8,128)(2,1)S(1)} %get-tuple-element.18), channel_id=1, source_target_pairs={{0,8},{4,12},{8,0},{12,4},{16,24},{20,28},{24,16},{28,20},{1,9},{5... | collective-permute-start | bytes 442376 | tf_op jit(solution)/shard_map/ppermute | solution.py:305
  23.4 1.0 %collective-permute-start.4 = (bf16[576,128]{1,0:T(8,128)(2,1)S(1)}, bf16[576,128]{1,0:T(8,128)(2,1)S(1)}, u32[]{:S(2)}, u32[]{:S(2)}) collective-permute-start(bf16[576,128]{1,0:T(8,128)(2,1)S(1)} %get-tuple-element.19), channel_id=1, source_target_pairs={{0,16},{4,20},{8,24},{12,28},{16,0},{20,4},{24,8},{28,12},{1,17},{... | collective-permute-start | bytes 442376 | tf_op jit(solution)/shard_map/ppermute | solution.py:305
  24.4 1.0 %collective-permute-done.8.refs_6_ = bf16[784,128]{1,0:T(8,128)(2,1)S(1)} collective-permute-done((bf16[784,128]{1,0:T(8,128)(2,1)}, bf16[784,128]{1,0:T(8,128)(2,1)S(1)}, u32[]{:S(2)}, u32[]{:S(2)}) %collective-permute-start.8) | collective-permute-done | bytes 200736 | tf_op jit(solution)/shard_map/ppermute | solution.py:305
  25.4 1.9 %collective-permute-done.9.refs_7_ = bf16[784,128]{1,0:T(8,128)(2,1)S(1)} collective-permute-done((bf16[784,128]{1,0:T(8,128)(2,1)}, bf16[784,128]{1,0:T(8,128)(2,1)S(1)}, u32[]{:S(2)}, u32[]{:S(2)}) %collective-permute-start.9) | collective-permute-done | bytes 200736 | tf_op jit(solution)/shard_map/ppermute | solution.py:305
  27.3 5.1 %attend.1 = (bf16[1040,128]{1,0:T(8,128)(2,1)S(1)}, bf16[1040,128]{1,0:T(8,128)(2,1)S(1)}) custom-call(s32[8]{0:T(128)S(1)} %copy-done.3, bf16[784,128]{1,0:T(8,128)(2,1)S(1)} %copy-done.2, bf16[784,128]{1,0:T(8,128)(2,1)S(1)} %collective-permute-done.refs_2_, bf16[784,128]{1,0:T(8,128)(2,1)S(1)} %collective-permute-done.5.refs_3_, ...), custom_call_target="tpu_custom_call" | custom-call | flops 1073741824 | bytes 1064960 | tf_op jit(solution)/shard_map/attend/pallas_call | solution.py:386
  32.5 0.8 %collective-permute-done.4.refs_2_ = bf16[576,128]{1,0:T(8,128)(2,1)S(1)} collective-permute-done((bf16[576,128]{1,0:T(8,128)(2,1)S(1)}, bf16[576,128]{1,0:T(8,128)(2,1)S(1)}, u32[]{:S(2)}, u32[]{:S(2)}) %collective-permute-start.4) | collective-permute-done | bytes 147488 | tf_op jit(solution)/shard_map/ppermute | solution.py:305
  33.3 1.6 %collective-permute-start.10 = (bf16[4,576,128]{2,1,0:T(8,128)(2,1)S(1)}, bf16[4,576,128]{2,1,0:T(8,128)(2,1)S(1)}, u32[]{:S(2)}, u32[]{:S(2)}) collective-permute-start(bf16[4,576,128]{2,1,0:T(8,128)(2,1)S(1)} %stack.1.refs_0_), channel_id=1, source_target_pairs={{0,1},{1,0},{2,3},{3,2},{4,5},{5,4},{6,7},{7,6},{8,9},{9,8},{10,11... | collective-permute-start | bytes 1769480 | tf_op jit(solution)/shard_map/ppermute | solution.py:311
  34.9 0.8 %collective-permute-start.13 = (bf16[1040,128]{1,0:T(8,128)(2,1)S(1)}, bf16[1040,128]{1,0:T(8,128)(2,1)S(1)}, u32[]{:S(2)}, u32[]{:S(2)}) collective-permute-start(bf16[1040,128]{1,0:T(8,128)(2,1)S(1)} %get-tuple-element.26.refs_4_.refs_1_), channel_id=1, source_target_pairs={{0,8},{4,12},{8,0},{12,4},{16,24},{20,28},{24,16},{28,20},{1,9},{5... | collective-permute-start | bytes 798728 | tf_op jit(solution)/shard_map/ppermute | solution.py:305
  35.8 1.3 %collective-permute-start.11 = (bf16[1040,128]{1,0:T(8,128)(2,1)S(1)}, bf16[1040,128]{1,0:T(8,128)(2,1)S(1)}, u32[]{:S(2)}, u32[]{:S(2)}) collective-permute-start(bf16[1040,128]{1,0:T(8,128)(2,1)S(1)} %get-tuple-element.28.x_ref), channel_id=1, source_target_pairs={{0,12},{4,8},{8,4},{12,0},{16,28},{20,24},{24,20},{28,16},{1,13},{... | collective-permute-start | bytes 798728 | tf_op jit(solution)/shard_map/ppermute | solution.py:305
  37.1 1.4 %collective-permute-start.12 = (bf16[1040,128]{1,0:T(8,128)(2,1)S(1)}, bf16[1040,128]{1,0:T(8,128)(2,1)S(1)}, u32[]{:S(2)}, u32[]{:S(2)}) collective-permute-start(bf16[1040,128]{1,0:T(8,128)(2,1)S(1)} %get-tuple-element.26.refs_4_.refs_1_), channel_id=1, source_target_pairs={{0,16},{4,20},{8,24},{12,28},{16,0},{20,4},{24,8},{28,12},{1,17},{... | collective-permute-start | bytes 798728 | tf_op jit(solution)/shard_map/ppermute | solution.py:305
  38.4 5.2 %collective-permute-done.14.refs_5_.refs_8_ = bf16[1040,128]{1,0:T(8,128)(2,1)S(1)} collective-permute-done((bf16[1040,128]{1,0:T(8,128)(2,1)S(1)}, bf16[1040,128]{1,0:T(8,128)(2,1)S(1)}, u32[]{:S(2)}, u32[]{:S(2)}) %collective-permute-start.14) | collective-permute-done | bytes 266272 | tf_op jit(solution)/shard_map/ppermute | solution.py:305
  43.6 0.5 collective-permute-start.17
  44.2 1.4 %collective-permute-start.16 = (bf16[1040,128]{1,0:T(8,128)(2,1)S(1)}, bf16[1040,128]{1,0:T(8,128)(2,1)S(1)}, u32[]{:S(2)}, u32[]{:S(2)}) collective-permute-start(bf16[1040,128]{1,0:T(8,128)(2,1)S(1)} %collective-permute-done.13.refs_4_.refs_7_), channel_id=1, source_target_pairs={{0,16},{4,20},{8,24},{12,28},{16,0},{20,4},{24,8},{28,12},{1,17},{... | collective-permute-start | bytes 798728 | tf_op jit(solution)/shard_map/ppermute | solution.py:305
  45.6 3.9 %collective-permute-done.11.refs_2_.refs_0_.refs_5_ = bf16[1040,128]{1,0:T(8,128)(2,1)S(1)} collective-permute-done((bf16[1040,128]{1,0:T(8,128)(2,1)S(1)}, bf16[1040,128]{1,0:T(8,128)(2,1)S(1)}, u32[]{:S(2)}, u32[]{:S(2)}) %collective-permute-start.11) | collective-permute-done | bytes 266272 | tf_op jit(solution)/shard_map/ppermute | solution.py:305
  49.5 0.6 collective-permute-start.15
  50.5 0.6 %grad_other_near.1 = bf16[256,640]{1,0:T(8,128)(2,1)S(1)} custom-call(bf16[256,1088]{1,0:T(8,128)(2,1)S(1)} %get-tuple-element.29.refs_0_, bf16[1040,128]{1,0:T(8,128)(2,1)S(1)} %get-tuple-element.26.refs_4_.refs_1_, bf16[1040,128]{1,0:T(8,128)(2,1)S(1)} %collective-permute-done.11.refs_2_.refs_0_.refs_5_, ...), custom_call_target="tpu_custom_call" | custom-call | flops 356515840 | bytes 655360 | tf_op jit(solution)/shard_map/grad_other_near/pallas_call | solution.py:420
  51.3 4.2 %collective-permute-done.17.refs_3_.refs_11_ = bf16[1040,128]{1,0:T(8,128)(2,1)S(1)} collective-permute-done((bf16[1040,128]{1,0:T(8,128)(2,1)S(1)}, bf16[1040,128]{1,0:T(8,128)(2,1)S(1)}, u32[]{:S(2)}, u32[]{:S(2)}) %collective-permute-start.17) | collective-permute-done | bytes 266272 | tf_op jit(solution)/shard_map/ppermute | solution.py:305
  56.0 0.5 grad_own_far.1.refs_1_
  56.5 0.6 %grad_own_near.1.refs_0_ = f32[256,640]{1,0:T(8,128)S(1)} custom-call(bf16[256,1088]{1,0:T(8,128)(2,1)S(1)} %get-tuple-element.27.refs_0_, bf16[1040,128]{1,0:T(8,128)(2,1)S(1)} %get-tuple-element.26.refs_4_.refs_1_, bf16[1040,128]{1,0:T(8,128)(2,1)S(1)} %collective-permute-done.11.refs_2_.refs_0_.refs_5_, ...), custom_call_target="tpu_custom_call" | custom-call | flops 356515840 | bytes 1310720 | tf_op jit(solution)/shard_map/grad_own_near/pallas_call | solution.py:420
  57.4 1.3 %finish.1 = (bf16[256,1024]{1,0:T(8,128)(2,1)}, f32[256,1024]{1,0:T(8,128)}) custom-call(f32[256,640]{1,0:T(8,128)S(1)} %grad_own_near.1.refs_0_, f32[256,384]{1,0:T(8,128)S(1)} %grad_own_far.1.refs_1_, bf16[256,640]{1,0:T(8,128)(2,1)S(1)} %collective-permute-done.18.refs_2_, bf16[256,384]{1,0:T(8,128)(2,1)S(1)} %collective-permute-done.19.refs_3_, ...), custom_call_target="tpu_custom_call" | custom-call | bytes 3145728 | tf_op jit(solution)/shard_map/finish/pallas_call | solution.py:436
  (35 shorter events, 1.9 us)
Async XLA Ops:
  3.4 12.5 %copy-start = (bf16[272,2048]{1,0:T(8,128)(2,1)S(1)}, bf16[272,2048]{1,0:T(8,128)(2,1)}, u32[]{:S(2)}) copy-start(bf16[272,2048]{1,0:T(8,128)(2,1)} %refs_1_.3) | copy-start | bytes 3342340
  3.4 12.5 %copy-start.1 = (s32[1,8]{1,0:T(1,128)S(1)}, s32[1,8]{1,0:T(1,128)}, u32[]{:S(2)}) copy-start(s32[1,8]{1,0:T(1,128)} %refs_0_.4) | copy-start | bytes 100
  3.5 10.3 %collective-permute-start = (bf16[784,128]{1,0:T(8,128)(2,1)S(1)}, bf16[784,128]{1,0:T(8,128)(2,1)S(1)}, u32[]{:S(2)}, u32[]{:S(2)}) collective-permute-start(bf16[784,128]{1,0:T(8,128)(2,1)S(1)} %pad_maximum_fusion), channel_id=1, source_target_pairs={{0,24},{4,28},{8,16},{12,20},{16,8},{20,12},{24,0},{28,4},{1,25},{... | collective-permute-start | bytes 602120 | tf_op jit(solution)/shard_map/ppermute | solution.py:305
  10.0 17.4 %copy-start.2 = (bf16[784,128]{1,0:T(8,128)(2,1)S(1)}, bf16[784,128]{1,0:T(8,128)(2,1)}, u32[]{:S(2)}) copy-start(bf16[784,128]{1,0:T(8,128)(2,1)} %get-tuple-element.21.refs_1_) | copy-start | bytes 602116
  10.0 17.4 %copy-start.3 = (s32[8]{0:T(128)S(1)}, s32[8]{0:T(128)}, u32[]{:S(2)}) copy-start(s32[8]{0:T(128)} %refs_0_.5) | copy-start | bytes 100
  10.0 3.8 %collective-permute-start.1 = (bf16[784,128]{1,0:T(8,128)(2,1)}, bf16[784,128]{1,0:T(8,128)(2,1)S(1)}, u32[]{:S(2)}, u32[]{:S(2)}) collective-permute-start(bf16[784,128]{1,0:T(8,128)(2,1)} %get-tuple-element.16), channel_id=1, source_target_pairs={{0,4},{4,0},{8,12},{12,8},{16,20},{20,16},{24,28},{28,24},{1,5},{5... | collective-permute-start | bytes 602120 | tf_op jit(solution)/shard_map/ppermute | solution.py:305
  10.1 7.7 %collective-permute-start.5 = (bf16[784,128]{1,0:T(8,128)(2,1)S(1)}, bf16[784,128]{1,0:T(8,128)(2,1)S(1)}, u32[]{:S(2)}, u32[]{:S(2)}) collective-permute-start(bf16[784,128]{1,0:T(8,128)(2,1)S(1)} %pad_maximum_fusion.1), channel_id=1, source_target_pairs={{0,28},{4,24},{8,20},{12,16},{16,12},{20,8},{24,4},{28,0},{1,29},{... | collective-permute-start | bytes 602120 | tf_op jit(solution)/shard_map/ppermute | solution.py:305
  10.3 12.0 %collective-permute-start.6 = (bf16[784,128]{1,0:T(8,128)(2,1)}, bf16[784,128]{1,0:T(8,128)(2,1)S(1)}, u32[]{:S(2)}, u32[]{:S(2)}) collective-permute-start(bf16[784,128]{1,0:T(8,128)(2,1)} %get-tuple-element.22), channel_id=1, source_target_pairs={{0,8},{4,12},{8,0},{12,4},{16,24},{20,28},{24,16},{28,20},{1,9},{5... | collective-permute-start | bytes 602120 | tf_op jit(solution)/shard_map/ppermute | solution.py:305
  12.2 11.2 %collective-permute-start.7 = (bf16[784,128]{1,0:T(8,128)(2,1)}, bf16[784,128]{1,0:T(8,128)(2,1)S(1)}, u32[]{:S(2)}, u32[]{:S(2)}) collective-permute-start(bf16[784,128]{1,0:T(8,128)(2,1)} %get-tuple-element.23), channel_id=1, source_target_pairs={{0,16},{4,20},{8,24},{12,28},{16,0},{20,4},{24,8},{28,12},{1,17},{... | collective-permute-start | bytes 602120 | tf_op jit(solution)/shard_map/ppermute | solution.py:305
  13.7 11.7 %collective-permute-start.8 = (bf16[784,128]{1,0:T(8,128)(2,1)}, bf16[784,128]{1,0:T(8,128)(2,1)S(1)}, u32[]{:S(2)}, u32[]{:S(2)}) collective-permute-start(bf16[784,128]{1,0:T(8,128)(2,1)} %get-tuple-element.24), channel_id=1, source_target_pairs={{0,12},{4,8},{8,4},{12,0},{16,28},{20,24},{24,20},{28,16},{1,13},{... | collective-permute-start | bytes 602120 | tf_op jit(solution)/shard_map/ppermute | solution.py:305
  13.7 13.6 %collective-permute-start.9 = (bf16[784,128]{1,0:T(8,128)(2,1)}, bf16[784,128]{1,0:T(8,128)(2,1)S(1)}, u32[]{:S(2)}, u32[]{:S(2)}) collective-permute-start(bf16[784,128]{1,0:T(8,128)(2,1)} %get-tuple-element.25), channel_id=1, source_target_pairs={{0,20},{4,16},{8,28},{12,24},{16,4},{20,0},{24,12},{28,8},{1,21},{... | collective-permute-start | bytes 602120 | tf_op jit(solution)/shard_map/ppermute | solution.py:305
  17.8 14.6 %collective-permute-start.2 = (bf16[576,128]{1,0:T(8,128)(2,1)S(1)}, bf16[576,128]{1,0:T(8,128)(2,1)S(1)}, u32[]{:S(2)}, u32[]{:S(2)}) collective-permute-start(bf16[576,128]{1,0:T(8,128)(2,1)S(1)} %get-tuple-element.17), channel_id=1, source_target_pairs={{0,24},{4,28},{8,16},{12,20},{16,8},{20,12},{24,0},{28,4},{1,25},{... | collective-permute-start | bytes 442376 | tf_op jit(solution)/shard_map/ppermute | solution.py:305
  22.3 10.1 %collective-permute-start.3 = (bf16[576,128]{1,0:T(8,128)(2,1)S(1)}, bf16[576,128]{1,0:T(8,128)(2,1)S(1)}, u32[]{:S(2)}, u32[]{:S(2)}) collective-permute-start(bf16[576,128]{1,0:T(8,128)(2,1)S(1)} %get-tuple-element.18), channel_id=1, source_target_pairs={{0,8},{4,12},{8,0},{12,4},{16,24},{20,28},{24,16},{28,20},{1,9},{5... | collective-permute-start | bytes 442376 | tf_op jit(solution)/shard_map/ppermute | solution.py:305
  23.4 9.9 %collective-permute-start.4 = (bf16[576,128]{1,0:T(8,128)(2,1)S(1)}, bf16[576,128]{1,0:T(8,128)(2,1)S(1)}, u32[]{:S(2)}, u32[]{:S(2)}) collective-permute-start(bf16[576,128]{1,0:T(8,128)(2,1)S(1)} %get-tuple-element.19), channel_id=1, source_target_pairs={{0,16},{4,20},{8,24},{12,28},{16,0},{20,4},{24,8},{28,12},{1,17},{... | collective-permute-start | bytes 442376 | tf_op jit(solution)/shard_map/ppermute | solution.py:305
  33.3 16.8 %collective-permute-start.10 = (bf16[4,576,128]{2,1,0:T(8,128)(2,1)S(1)}, bf16[4,576,128]{2,1,0:T(8,128)(2,1)S(1)}, u32[]{:S(2)}, u32[]{:S(2)}) collective-permute-start(bf16[4,576,128]{2,1,0:T(8,128)(2,1)S(1)} %stack.1.refs_0_), channel_id=1, source_target_pairs={{0,1},{1,0},{2,3},{3,2},{4,5},{5,4},{6,7},{7,6},{8,9},{9,8},{10,11... | collective-permute-start | bytes 1769480 | tf_op jit(solution)/shard_map/ppermute | solution.py:311
  34.9 8.7 %collective-permute-start.14 = (bf16[1040,128]{1,0:T(8,128)(2,1)S(1)}, bf16[1040,128]{1,0:T(8,128)(2,1)S(1)}, u32[]{:S(2)}, u32[]{:S(2)}) collective-permute-start(bf16[1040,128]{1,0:T(8,128)(2,1)S(1)} %get-tuple-element.28.x_ref), channel_id=1, source_target_pairs={{0,20},{4,16},{8,28},{12,24},{16,4},{20,0},{24,12},{28,8},{1,21},{... | collective-permute-start | bytes 798728 | tf_op jit(solution)/shard_map/ppermute | solution.py:305
  34.9 9.3 %collective-permute-start.13 = (bf16[1040,128]{1,0:T(8,128)(2,1)S(1)}, bf16[1040,128]{1,0:T(8,128)(2,1)S(1)}, u32[]{:S(2)}, u32[]{:S(2)}) collective-permute-start(bf16[1040,128]{1,0:T(8,128)(2,1)S(1)} %get-tuple-element.26.refs_4_.refs_1_), channel_id=1, source_target_pairs={{0,8},{4,12},{8,0},{12,4},{16,24},{20,28},{24,16},{28,20},{1,9},{5... | collective-permute-start | bytes 798728 | tf_op jit(solution)/shard_map/ppermute | solution.py:305
  35.8 13.8 %collective-permute-start.11 = (bf16[1040,128]{1,0:T(8,128)(2,1)S(1)}, bf16[1040,128]{1,0:T(8,128)(2,1)S(1)}, u32[]{:S(2)}, u32[]{:S(2)}) collective-permute-start(bf16[1040,128]{1,0:T(8,128)(2,1)S(1)} %get-tuple-element.28.x_ref), channel_id=1, source_target_pairs={{0,12},{4,8},{8,4},{12,0},{16,28},{20,24},{24,20},{28,16},{1,13},{... | collective-permute-start | bytes 798728 | tf_op jit(solution)/shard_map/ppermute | solution.py:305
  37.1 12.5 %collective-permute-start.12 = (bf16[1040,128]{1,0:T(8,128)(2,1)S(1)}, bf16[1040,128]{1,0:T(8,128)(2,1)S(1)}, u32[]{:S(2)}, u32[]{:S(2)}) collective-permute-start(bf16[1040,128]{1,0:T(8,128)(2,1)S(1)} %get-tuple-element.26.refs_4_.refs_1_), channel_id=1, source_target_pairs={{0,16},{4,20},{8,24},{12,28},{16,0},{20,4},{24,8},{28,12},{1,17},{... | collective-permute-start | bytes 798728 | tf_op jit(solution)/shard_map/ppermute | solution.py:305
  43.6 11.8 %collective-permute-start.17 = (bf16[1040,128]{1,0:T(8,128)(2,1)S(1)}, bf16[1040,128]{1,0:T(8,128)(2,1)S(1)}, u32[]{:S(2)}, u32[]{:S(2)}) collective-permute-start(bf16[1040,128]{1,0:T(8,128)(2,1)S(1)} %collective-permute-done.14.refs_5_.refs_8_), channel_id=1, source_target_pairs={{0,8},{4,12},{8,0},{12,4},{16,24},{20,28},{24,16},{28,20},{1,9},{5... | collective-permute-start | bytes 798728 | tf_op jit(solution)/shard_map/ppermute | solution.py:305
  44.2 11.2 %collective-permute-start.16 = (bf16[1040,128]{1,0:T(8,128)(2,1)S(1)}, bf16[1040,128]{1,0:T(8,128)(2,1)S(1)}, u32[]{:S(2)}, u32[]{:S(2)}) collective-permute-start(bf16[1040,128]{1,0:T(8,128)(2,1)S(1)} %collective-permute-done.13.refs_4_.refs_7_), channel_id=1, source_target_pairs={{0,16},{4,20},{8,24},{12,28},{16,0},{20,4},{24,8},{28,12},{1,17},{... | collective-permute-start | bytes 798728 | tf_op jit(solution)/shard_map/ppermute | solution.py:305
  49.5 5.9 %collective-permute-start.15 = (bf16[1040,128]{1,0:T(8,128)(2,1)S(1)}, bf16[1040,128]{1,0:T(8,128)(2,1)S(1)}, u32[]{:S(2)}, u32[]{:S(2)}) collective-permute-start(bf16[1040,128]{1,0:T(8,128)(2,1)S(1)} %late.1), channel_id=1, source_target_pairs={{0,4},{4,0},{8,12},{12,8},{16,20},{20,16},{24,28},{28,24},{1,5},{5... | collective-permute-start | bytes 798728 | tf_op jit(solution)/shard_map/ppermute | solution.py:305
  51.2 6.3 %collective-permute-start.18 = (bf16[256,640]{1,0:T(8,128)(2,1)S(1)}, bf16[256,640]{1,0:T(8,128)(2,1)S(1)}, u32[]{:S(2)}, u32[]{:S(2)}) collective-permute-start(bf16[256,640]{1,0:T(8,128)(2,1)S(1)} %grad_other_near.1), channel_id=1, source_target_pairs={{0,4},{4,0},{8,12},{12,8},{16,20},{20,16},{24,28},{28,24},{1,5},{5... | collective-permute-start | bytes 983048 | tf_op jit(solution)/shard_map/ppermute | solution.py:305
  55.9 1.5 %collective-permute-start.19 = (bf16[256,384]{1,0:T(8,128)(2,1)S(1)}, bf16[256,384]{1,0:T(8,128)(2,1)S(1)}, u32[]{:S(2)}, u32[]{:S(2)}) collective-permute-start(bf16[256,384]{1,0:T(8,128)(2,1)S(1)} %grad_other_far.1), channel_id=1, source_target_pairs={{0,4},{4,0},{8,12},{12,8},{16,20},{20,16},{24,28},{28,24},{1,5},{5... | collective-permute-start | bytes 589832 | tf_op jit(solution)/shard_map/ppermute | solution.py:305

commit v6 on v4

--- a/solution.py
+++ b/solution.py
@@ -11,7 +11,7 @@
 TPF = 64
 WINB = 4
 VMEM_LIMIT = 24 * 1024 * 1024
-PACK_LIMIT = 63 * 1024 * 1024
+PACK_LIMIT = 58 * 1024 * 1024
 
 
 def from_behind(x, axis, by):
@@ -74,39 +74,55 @@
     return (attended, disc_grad)
 
 
-def cot_kernel(n, tile, lo, off_hbm, cot_hbm, behind_a, behind_b, *refs):
-    outs, (off, cot, sems) = refs[:-3], refs[-3:]
+def mate_bit(i):
+    return 4 >> (i % 2)
+
+
+def sum_bit(i):
+    return 2 << (i % 2)
+
+
+def place():
     own = lax.axis_index("tm")
-    chip, side = own // 2, lax.rem(own, 2)
+    side = lax.rem(own, 2)
+    return own, side, jnp.where(side == 0, 4, 2), jnp.where(side == 0, 2, 4)
+
+
+def cot_kernel(n, tile, lo, off_hbm, cot_hbm, *refs):
+    outs, (off, cot, sems) = refs[-7:-3], refs[-3:]
+    own, side, mate, partner = place()
     plane = lax.rem(lax.axis_index("head"), 2)
     clip_rows = n * tile
-    part, all_cols = cot.shape
+    all_rows, all_cols = cot.shape
     cols = all_cols // n
+    part = all_rows - lo
     low = pl.multiple_of(plane * lo, 16)
     fetch_off = pltpu.make_async_copy(off_hbm, off, sems.at[0])
-    fetch_cot = pltpu.make_async_copy(cot_hbm.at[pl.ds(low, part), :], cot, sems.at[1])
+    fetch_cot = pltpu.make_async_copy(cot_hbm, cot, sems.at[1])
     fetch_off.start()
     fetch_cot.start()
     fetch_off.wait()
     r = lax.broadcasted_iota(jnp.int32, (clip_rows, clip_rows), 0)
     c = lax.broadcasted_iota(jnp.int32, (clip_rows, clip_rows), 1)
-    select = jnp.where((r == c) & (plane != 0), 1.0, 0.0)
+    select = jnp.zeros((clip_rows, clip_rows), jnp.float32)
     for j in range(n):
         src = lax.rem(own - off[0, j] + 2 * n, n)
         for t in range(tile):
-            hit = (c == j * tile + t) & (r == src * tile + t) & (plane == 0)
-            select = jnp.where(hit, 1.0, select)
+            select = jnp.where((c == j * tile + t) & (r == src * tile + t), 1.0, select)
     fetch_cot.wait()
     cot[0:clip_rows, :] = jnp.dot(
         select.astype(jnp.bfloat16), cot[0:clip_rows, :], preferred_element_type=jnp.float32
     ).astype(jnp.bfloat16)
+    devices = ((own, partner), (own ^ 1, mate), (own ^ mate, partner), (own ^ partner ^ 1, mate))
     units = cols // HD
-    for m, out_ref in enumerate(outs):
-        for i, block in enumerate((2 * (chip ^ m) + side, 2 * (chip ^ m) + 1 - side)):
+    for d, ((device, its_partner), out_ref) in enumerate(zip(devices, outs)):
+        rows, first = (all_rows, 0) if d < 2 else (part, low)
+        blocks = (device, device ^ 1, device ^ its_partner, device ^ its_partner ^ 1)
+        for i, block in enumerate(blocks):
             for u in range(units):
-                at = (i * units + u) * part
+                at = (i * units + u) * rows
                 lanes = pl.ds(pl.multiple_of(block * cols + u * HD, HD), HD)
-                out_ref[at : at + part, :] = cot[:, lanes]
+                out_ref[at : at + rows, :] = cot[pl.ds(first, rows), lanes]
 
 
 def pack_kernel(n, heads, q_hbm, k_hbm, v_hbm, hist_hbm, *refs):
@@ -138,27 +154,32 @@
             out_ref[i * tok : (i + 1) * tok, :] = x[:, lanes]
 
 
-def attend_blocks(n, tok, parity, counts, x_ref, out_ref):
+def attend_kernel(n, tok, order, counts_hbm, *refs):
+    parts, (mine_ref, other_ref, x_ref, mixed_ref, counts, sem) = refs[:n], refs[n:]
+    copy = pltpu.make_async_copy(counts_hbm, counts, sem)
+    copy.start()
+    own, side, mate, partner = place()
+    for k, part in zip(order, parts):
+        x_ref[own ^ k] = part[...]
+    copy.wait()
     rate = math.log2(math.e) / math.sqrt(HD)
     token = lax.broadcasted_iota(jnp.int32, (1, tok), 1)
-    for i in range(n // 2):
-        block = 2 * i + parity
-        keys = min(WINB, 2 * i + 2)
-        sources = [block - (keys - 1) + k for k in range(keys)]
+    bias = [
+        jnp.where(token < counts[s] * TPF, 0.0, -jnp.inf).astype(jnp.float32) for s in range(n)
+    ]
+    for block in range(n):
+        sources = range(max(0, block - (WINB - 1)), block + 1)
         q = x_ref[block, 0:tok, :]
-        scores = []
-        for s in sources:
-            at = jnp.maximum(s, 0)
-            kept = jnp.where(s >= 0, counts[at], 0) * TPF
-            scores.append(
-                lax.dot_general(
-                    q,
-                    x_ref[at, tok : 2 * tok, :],
-                    (((1,), (1,)), ((), ())),
-                    preferred_element_type=jnp.float32,
-                )
-                + jnp.where(token < kept, 0.0, -jnp.inf).astype(jnp.float32)
+        scores = [
+            lax.dot_general(
+                q,
+                x_ref[s, tok : 2 * tok, :],
+                (((1,), (1,)), ((), ())),
+                preferred_element_type=jnp.float32,
             )
+            + bias[s]
+            for s in sources
+        ]
         top = jnp.max(scores[0], axis=1, keepdims=True)
         for s in scores[1:]:
             top = jnp.maximum(top, jnp.max(s, axis=1, keepdims=True))
@@ -171,70 +192,57 @@
         for s, w in zip(sources, weights):
             mixed = mixed + jnp.dot(
                 (w * share).astype(jnp.bfloat16),
-                x_ref[jnp.maximum(s, 0), 2 * tok : 3 * tok, :],
+                x_ref[s, 2 * tok : 3 * tok, :],
                 preferred_element_type=jnp.float32,
             )
-        out_ref[i * tok : (i + 1) * tok, :] = mixed.astype(jnp.bfloat16)
+        mixed_ref[block] = mixed.astype(jnp.bfloat16)
     rows = n // 2 * tok
-    clip_rows = out_ref.shape[0] - rows
+    clip_rows = mine_ref.shape[0] - rows
     hist = jnp.zeros((clip_rows, HD), jnp.float32)
     for s in range(n):
         hist = hist + x_ref[s, 3 * tok : 3 * tok + clip_rows, :].astype(jnp.float32)
-    out_ref[rows:, :] = hist.astype(jnp.bfloat16)
-
-
-def attend_kernel(n, tok, order, counts_hbm, *refs):
-    parts, (same_ref, cross_ref, x_ref, counts, sem) = refs[:n], refs[n:]
-    copy = pltpu.make_async_copy(counts_hbm, counts, sem)
-    copy.start()
-    own = lax.axis_index("tm")
-    side = lax.rem(own, 2)
-    for k, part in zip(order, parts):
-        x_ref[own ^ k] = part[...]
-    copy.wait()
-    attend_blocks(n, tok, side, counts, x_ref, same_ref)
-    attend_blocks(n, tok, 1 - side, counts, x_ref, cross_ref)
-
-
-def stack_kernel(order, *refs):
-    out_ref = refs[-1]
-    for i, x in zip(order, refs):
-        out_ref[i] = x[...]
-
-
-def late_kernel(x_ref, *refs):
-    refs[-1][...] = x_ref[...]
-
-
-def whole_cot(lo, part, plane, mine, swapped):
-    pieces = []
-    for u in range(mine.shape[0] // part):
-        a = mine[u * part : (u + 1) * part, :]
-        b = swapped[u * part : (u + 1) * part, :]
-        low = jnp.where(plane == 0, a, b)
-        high = jnp.where(plane == 0, b, a)
-        pieces.append(jnp.concatenate([low[:lo], high], axis=0))
-    return jnp.concatenate(pieces, axis=1)
-
-
-def turn(wholes, clip_rows):
-    pieces = [x[clip_rows:] for x in wholes] + [x[:clip_rows] for x in wholes]
-    return jnp.concatenate(pieces, axis=0).T
-
-
-def turn_kernel(lo, clip_rows, cot_rows, mine_ref, swapped_ref, own_ref, other_ref):
+    hist = hist.astype(jnp.bfloat16)
+    x, y = lax.rem(own // 2, 2), own // 4
+    for flip, out_ref in ((0, mine_ref), (1, other_ref)):
+        for p in range(n // 2):
+            by_x = 4 * (p // 2) + 2 * (x ^ flip) + p % 2
+            by_y = 4 * (y ^ flip) + p
+            out_ref[p * tok : (p + 1) * tok, :] = mixed_ref[jnp.where(side == 0, by_x, by_y)]
+        out_ref[rows:, :] = hist
+
+
+def stack_kernel(a_ref, b_ref, behind, out_ref):
+    out_ref[0] = a_ref[...]
+    out_ref[1] = b_ref[...]
+
+
+def lay_out(rows, pieces):
+    return jnp.concatenate([x[:rows] for x in pieces], axis=1)
+
+
+def turn_kernel(lo, clip_rows, own_in, core_in, mine_ref, swapped_ref, own_ref, give_ref, whole):
+    own, side, mate, partner = place()
     plane = lax.rem(lax.axis_index("head"), 2)
-    chip = lax.axis_index("tm") // 2
-    chips, length, _ = mine_ref.shape
-    for i, out_ref in enumerate((own_ref, other_ref)):
-        rows = slice(i * length // 2, (i + 1) * length // 2)
-        wholes = [
-            whole_cot(
-                lo, cot_rows - lo, plane, mine_ref[chip ^ c, rows], swapped_ref[chip ^ c, rows]
-            )
-            for c in range(chips)
-        ]
-        out_ref[...] = turn(wholes, clip_rows)
+    _, all_rows, width = whole.shape
+    tiles = width // HD
+    part = all_rows - lo
+    for u in range(tiles):
+        lanes = slice(u * HD, (u + 1) * HD)
+        full = slice(u * all_rows, (u + 1) * all_rows)
+        whole[0, :, lanes] = own_in[full, :]
+        whole[1, :, lanes] = core_in[full, :]
+        for i in range(2):
+            a = mine_ref[i, u * part : (u + 1) * part, :]
+            b = swapped_ref[i, u * part : (u + 1) * part, :]
+            whole[2 + i, 0:lo, lanes] = jnp.where(plane == 0, a, b)[:lo]
+            whole[2 + i, lo:all_rows, lanes] = jnp.where(plane == 0, b, a)
+    at = lax.rem(own // mate, 2)
+    slots = [2 * ((p // 2) ^ at) + ((p % 2) ^ side) for p in range(4)]
+    for i, out_ref in enumerate((own_ref, give_ref)):
+        lanes = slice(i * width // 2, (i + 1) * width // 2)
+        pieces = [whole[s, clip_rows:all_rows, lanes] for s in slots]
+        pieces += [whole[s, 0:clip_rows, lanes] for s in slots]
+        out_ref[...] = jnp.concatenate(pieces, axis=0).T
 
 
 def grad_part(turned_ref, head_refs, rows, copies):
@@ -249,35 +257,63 @@
     )
 
 
-def grad_kernel(rows, copies, turned_ref, *refs):
-    out_ref = refs[-1]
-    out_ref[...] = grad_part(turned_ref, refs[:-1], rows, copies).astype(out_ref.dtype)
-
-
-def finish_kernel(order, tok, own_near, own_far, got_near, got_far, *refs):
-    n = len(order)
-    heads, (att_hbm, out_hbm, total, sems) = refs[:n], refs[n:]
-    own = lax.axis_index("tm")
-    at = pl.multiple_of(own // 2 * tok, tok)
-    near = own_near.shape[1] // HD
-
-    def column(near_ref, far_ref, i):
-        ref, i = (near_ref, i) if i < near else (far_ref, i - near)
-        return ref[:, i * HD : (i + 1) * HD]
-
+def send_kernel(rows, copies, heads, turned_ref, *refs):
+    same_ref, cross_ref = refs[-2:]
+    cols = same_ref.shape[0]
+    out = grad_part(turned_ref, refs[:heads], rows, copies).astype(jnp.bfloat16)
+    same_ref[...] = out[:cols]
+    cross_ref[...] = out[cols:]
+
+
+def keep_kernel(rows, copies, tok, turned_ref, *refs):
+    heads, (keep_ref, give_ref) = refs[:-2], refs[-2:]
+    own, side, mate, partner = place()
+    cols, width = keep_ref.shape
+    out = grad_part(turned_ref, heads, rows, copies)
+    keep_ref[...] = out[:cols]
+    give_ref[0:cols, :] = out[cols:].astype(jnp.bfloat16)
+    at = 2 * lax.rem(own // mate, 2) + 1 - side
+    for i, x in enumerate(heads):
+        give_ref[cols : cols + tok, i * HD : (i + 1) * HD] = x[
+            pl.ds(pl.multiple_of(at * tok, tok), tok), :
+        ]
+
+
+def finish_kernel(tok, keep_near, keep_far, same_near, same_far, cross_near, cross_far, core_near, core_far, *refs):
+    heads, (att_hbm, out_hbm, total, sems) = refs[:4], refs[4:]
+    own, side, mate, partner = place()
+    cols = keep_near.shape[0]
+    at = 2 * lax.rem(own // mate, 2) + side
     moves = []
 
     def move(a, b):
         moves.append(pltpu.make_async_copy(a, b, sems.at[len(moves)]))
         moves[-1].start()
 
-    lanes = [pl.ds(pl.multiple_of((own ^ k) * HD, HD), HD) for k in order]
-    for i in range(n):
-        move(heads[i].at[pl.ds(at, tok), :], att_hbm.at[:, lanes[i]])
-    for i, k in enumerate(order):
-        got = column(got_near, got_far, order.index(k ^ 1))
-        total[i] = column(own_near, own_far, i) + got.astype(jnp.float32)
-        move(total.at[i], out_hbm.at[:, lanes[i]])
+    def lanes(head):
+        return pl.ds(pl.multiple_of(head * HD, HD), HD)
+
+    def column(near, far, i):
+        ref, i = (near, i) if i < 3 else (far, 0)
+        return ref[0:cols, i * HD : (i + 1) * HD].astype(jnp.float32)
+
+    mine = [own, own ^ partner, own ^ mate, own ^ 6]
+    theirs = [own ^ 1, own ^ 1 ^ mate, own ^ 1 ^ partner, own ^ 7]
+    for i, head in enumerate(mine):
+        move(heads[i].at[pl.ds(pl.multiple_of(at * tok, tok), tok), :], att_hbm.at[:, lanes(head)])
+    for i, head in enumerate(theirs):
+        ref, k = (core_near, i) if i < 3 else (core_far, 0)
+        move(
+            ref.at[pl.ds(cols, tok), pl.ds(k * HD, HD)],
+            att_hbm.at[:, lanes(head)],
+        )
+    there = [1, 0, 3, 2]
+    for i, head in enumerate(mine):
+        total[i] = column(keep_near, keep_far, i) + column(same_near, same_far, there[i])
+        move(total.at[i], out_hbm.at[:, lanes(head)])
+    for i, head in enumerate(theirs):
+        total[4 + i] = column(core_near, core_far, i) + column(cross_near, cross_far, there[i])
+        move(total.at[4 + i], out_hbm.at[:, lanes(head)])
     for x in moves:
         x.wait()
 
@@ -302,13 +338,10 @@
     bf16 = jnp.bfloat16
 
     def swap(x, bit):
-        return lax.ppermute(x, "tm", [(i, i ^ bit) for i in range(n)])
-
-    def swap_plane(x, bit):
-        pairs = [
-            (i * planes + p, (i ^ bit) * planes + (p ^ 1)) for i in range(n) for p in range(planes)
-        ]
-        return lax.ppermute(x, ("tm", "head"), pairs)
+        return lax.ppermute(x, "tm", [(i, i ^ bit(i)) for i in range(n)])
+
+    def swap_plane(x):
+        return lax.ppermute(x, "head", [(p, p ^ 1) for p in range(planes)])
 
     def call(
         kernel, name, outs, specs, flops, scratch=(), exps=0, out_spec=vmem, limit=VMEM_LIMIT
@@ -347,89 +380,95 @@
     packed = dict(zip(first, pack(first, 2 * HD, "pack_first")))
     packed.update(zip(rest, pack(rest, width, "pack_rest")))
     order = [6, 7, 2, 4, 3, 5, 1]
-    arrived = {k: swap(packed[k], k) for k in order}
+    arrived = {k: swap(packed[k], lambda i: k) for k in order}
     by_head = [packed[0]] + [arrived[k] for k in order]
-    chips = range(half)
-    cots = call(
+    tiles = 4 * units
+    full, split = ((tiles * cot_rows, HD), bf16), ((tiles * part, HD), bf16)
+    cot_own, cot_core, cot_mate, cot_cross = call(
         lambda *refs: cot_kernel(n, tile, lo, *refs),
         "cot",
-        [((2 * units * part, HD), bf16)] * half,
+        [full, full, split, split],
         [hbm] * 4,
         0,
         (
             pltpu.SMEM(offsets.shape, jnp.int32),
-            pltpu.VMEM((part, all_cols), bf16),
+            pltpu.VMEM(cotangent.shape, bf16),
             pltpu.SemaphoreType.DMA((2,)),
         ),
     )(offsets, cotangent, arrived[6], arrived[7])
-    moved = {m: swap(cots[m], 2 * m) for m in reversed(chips[1:])}
-    cots = [cots[0]] + [moved[m] for m in chips[1:]]
-    counts = (
-        pltpu.VMEM((n, length, HD), bf16),
-        pltpu.SMEM(frame_counts.shape, jnp.int32),
-        pltpu.SemaphoreType.DMA,
-    )
+    cot_core = swap(cot_core, lambda i: 1)
+    cot_cross = swap(cot_cross, lambda i: sum_bit(i) ^ 1)
+    cot_mate = swap(cot_mate, mate_bit)
+
     pairs = half * tok * WINB * tok
     head_shape = ((rows + clip_rows, HD), bf16)
-    same, cross = call(
+    mine, others = call(
         lambda *refs: attend_kernel(n, tok, [0] + order, *refs),
         "attend",
         [head_shape, head_shape],
         [hbm] + [vmem] * n,
         8 * pairs * HD,
-        counts,
+        (
+            pltpu.VMEM((n, length, HD), bf16),
+            pltpu.VMEM((n, tok, HD), bf16),
+            pltpu.SMEM(frame_counts.shape, jnp.int32),
+            pltpu.SemaphoreType.DMA,
+        ),
         2 * pairs,
     )(frame_counts, *by_head)
-    stack_order = [3, 1, 2, 0]
+    sum_head, mate_head = swap(others, sum_bit), swap(mine, mate_bit)
+    far_head = swap(sum_head, mate_bit)
     (cot_mine,) = call(
-        lambda *refs: stack_kernel(stack_order, *refs),
+        stack_kernel,
         "stack",
-        [((half, 2 * units * part, HD), bf16)],
-        [vmem] * half + [hbm],
+        [((2, tiles * part, HD), bf16)],
+        [vmem] * 2 + [hbm],
         0,
-    )(*[cots[m] for m in stack_order], same)
-    cot_swapped = swap_plane(cot_mine, 0)
-
-    x_same, y_cross = swap(same, 2), swap(cross, 4 ^ 1)
-    y_same, x_cross = swap(same, 4), swap(cross, 2 ^ 1)
-    far_same, far_cross = swap(x_same, 4), swap(y_cross, 2)
-    (late_cross,) = call(late_kernel, "late", [head_shape], [vmem] + [hbm] * 2, 0)(cross, x_cross, y_same)
-    c_cross = swap(late_cross, 1)
-
-    turned_own, turned_other = call(
-        lambda *refs: turn_kernel(lo, clip_rows, cot_rows, *refs),
+    )(cot_mate, cot_cross, mine)
+    cot_swapped = swap_plane(cot_mine)
+
+    turned_own, turned_give = call(
+        lambda *refs: turn_kernel(lo, clip_rows, *refs),
         "turn",
-        [((cols, half * cot_rows), bf16)] * 2,
-        [vmem] * 2,
+        [((2 * cols, half * cot_rows), bf16)] * 2,
+        [vmem] * 4,
         0,
-    )(cot_mine, cot_swapped)
-
-    def grad(turned, heads, dtype, name):
-        (out,) = call(
-            lambda *refs: grad_kernel(rows, half, *refs),
-            name,
-            [((cols, len(heads) * HD), dtype)],
+        (pltpu.VMEM((4, cot_rows, tiles * HD), bf16),),
+    )(cot_own, cot_core, cot_mine, cot_swapped)
+
+    def share(heads, name, *behind):
+        lanes = len(heads) * HD
+        flops = 4 * cols * half * cot_rows * lanes
+        same, cross = call(
+            lambda *refs: send_kernel(rows, half, len(heads), *refs),
+            "send_" + name,
+            [((cols, lanes), bf16)] * 2,
+            [vmem] * (1 + len(heads)) + [hbm] * len(behind),
+            flops,
+        )(turned_give, *heads, *behind)
+        same, cross = swap(same, sum_bit), swap(cross, lambda i: sum_bit(i) ^ 1)
+        keep, give = call(
+            lambda *refs: keep_kernel(rows, half, tok, *refs),
+            "keep_" + name,
+            [((cols, lanes), jnp.float32), ((cols + tok, lanes), bf16)],
             [vmem] * (1 + len(heads)),
-            2 * cols * half * cot_rows * len(heads) * HD,
-        )(turned, *heads)
-        return out
-
-    near = [same, x_cross, y_same, x_same, y_cross]
-    far = [c_cross, far_same, far_cross]
-    heads = [0, 3, 4, 2, 5, 1, 6, 7]
-    got_near = swap(grad(turned_other, near, bf16, "grad_other_near"), 1)
-    own_near = grad(turned_own, near, jnp.float32, "grad_own_near")
-    got_far = swap(grad(turned_other, far, bf16, "grad_other_far"), 1)
-    own_far = grad(turned_own, far, jnp.float32, "grad_own_far")
+            flops,
+        )(turned_own, *heads)
+        return keep, same, cross, swap(give, lambda i: 1)
+
+    near, far = [mine, sum_head, mate_head], [far_head]
+    near_sums = share(near, "near")
+    far_sums = share(far, "far", near_sums[3])
+    sums = [x for pair in zip(near_sums, far_sums) for x in pair]
     return call(
-        lambda *refs: finish_kernel(heads, tok, *refs),
+        lambda *refs: finish_kernel(tok, *refs),
         "finish",
         [((tok, width), bf16), ((cols, width), jnp.float32)],
-        [vmem] * (4 + n),
+        [vmem] * 12,
         0,
         (pltpu.VMEM((n, cols, HD), jnp.float32), pltpu.SemaphoreType.DMA((2 * n,))),
         out_spec=hbm,
-    )(own_near, own_far, got_near, got_far, *near, *far)
+    )(*sums, *near, *far)
 
 
 def body(query_rows, key_rows, value_rows, frame_counts, history, offsets, cotangent):

time: 58 us -> 65.4 us (1.13)
  waiting for transfers between devices: 23.8 us -> 30.5 us
  Pallas kernels: 14.3 us -> 15.7 us
  local copies, waits for them, and re-layouts: 1.26 us -> 0.02 us
    ppermute x20, waiting for transfers between devices: 23.8 us -> 30.5 us  [the longest x19 19.8 us: swap(): return lax.ppermute(x, 'tm', [(i, i ^ bit(i)) for i in range(n)])]
    pallas_call x9 -> x8, Pallas kernels: 4.83 us -> 6.17 us  [the longest x1 1.31 us: head_body(): call(lambda *refs: finish_kernel(tok, *refs), 'finish', [((tok, width), b...]
    unnamed x8, local copies, waits for them, and re-layouts: 1.26 us -> 0.02 us
  transfers between devices with their start and end apart: 20 -> 20, of which waited for: 11 -> 9; matrix products, arithmetic and copies ran while one was open for 0% -> 0% of each run, Pallas kernels for 19% -> 18%
where the time goes in v6:
time: 65.4 us; the launch traced here: 65.2 us
  waiting for transfers between devices  30.5 us (47%)
  starting transfers between devices  18.2 us (28%)
  Pallas kernels  15.7 us (24%)
  between operations  0.8 us (1%)
    ppermute x19, waiting for transfers between devices, swap(): return lax.ppermute(x, 'tm', [(i, i ^ bit(i)) for i in range(n)])  19.8 us
    ppermute x19, starting transfers between devices, swap(): return lax.ppermute(x, 'tm', [(i, i ^ bit(i)) for i in range(n)])  16.1 us
    ppermute x1, waiting for transfers between devices, swap_plane(): return lax.ppermute(x, 'head', [(p, p ^ 1) for p in range(planes)])  10.8 us
    pallas_call x1, Pallas kernels, head_body(): call(lambda *refs: attend_kernel(n, tok, [0] + order, *refs), 'attend', [...  5.09 us
    pallas_call x2, Pallas kernels, pack(): call(lambda *refs: pack_kernel(n, heads, *refs), name, [((length, HD), bf...  4.42 us
    ppermute x1, starting transfers between devices, swap_plane(): return lax.ppermute(x, 'head', [(p, p ^ 1) for p in range(planes)])  2.12 us
    pallas_call x1, Pallas kernels, head_body(): call(lambda *refs: finish_kernel(tok, *refs), 'finish', [((tok, width), b...  1.31 us
  transfers between devices with their start and end apart: 20, of which 9 were waited for; matrix products, arithmetic and copies ran while one was open for 0% of the time, Pallas kernels for 18%

profile of v6, /device:TPU:0, one launch (start us, length us, event | category | flops | bytes accessed | tf_op | source)
XLA Modules:
  0.0 65.2 jit_solution(9376313636430501488)
XLA Ops:
  0.6 1.9 %pack_first.1 = (bf16[784,128]{1,0:T(8,128)(2,1)}, bf16[784,128]{1,0:T(8,128)(2,1)}) custom-call(bf16[256,1024]{1,0:T(8,128)(2,1)} %refs_0_.6, bf16[256,1024]{1,0:T(8,128)(2,1)} %refs_1_.5, bf16[256,1024]{1,0:T(8,128)(2,1)} %refs_2_.3, bf16[2,1024]{1,0:T(2,128)(2,1)} %refs_3_.3), custom_call_target="tpu_custom_call" | custom-call | bytes 802816 | tf_op jit(solution)/shard_map/pack_first/pallas_call | solution.py:363
  2.5 4.0 %collective-permute-start = (bf16[784,128]{1,0:T(8,128)(2,1)}, bf16[784,128]{1,0:T(8,128)(2,1)S(1)}, u32[]{:S(2)}, u32[]{:S(2)}) collective-permute-start(bf16[784,128]{1,0:T(8,128)(2,1)} %get-tuple-element.26), channel_id=1, source_target_pairs={{0,24},{4,28},{8,16},{12,20},{16,8},{20,12},{24,0},{28,4},{1,25},{... | collective-permute-start | bytes 602120 | tf_op jit(solution)/shard_map/ppermute | solution.py:341
  6.5 2.6 %pack_rest.1 = (bf16[784,128]{1,0:T(8,128)(2,1)}, bf16[784,128]{1,0:T(8,128)(2,1)}, bf16[784,128]{1,0:T(8,128)(2,1)}, bf16[784,128]{1,0:T(8,128)(2,1)}, bf16[784...) custom-call(bf16[256,1024]{1,0:T(8,128)(2,1)} %refs_0_.6, bf16[256,1024]{1,0:T(8,128)(2,1)} %refs_1_.5, ...), custom_call_target="tpu_custom_call" | custom-call | bytes 2408448 | tf_op jit(solution)/shard_map/pack_rest/pallas_call | solution.py:363
  9.1 1.2 %collective-permute-start.5 = (bf16[784,128]{1,0:T(8,128)(2,1)}, bf16[784,128]{1,0:T(8,128)(2,1)S(1)}, u32[]{:S(2)}, u32[]{:S(2)}) collective-permute-start(bf16[784,128]{1,0:T(8,128)(2,1)} %get-tuple-element.33), channel_id=1, source_target_pairs={{0,8},{4,12},{8,0},{12,4},{16,24},{20,28},{24,16},{28,20},{1,9},{5... | collective-permute-start | bytes 602120 | tf_op jit(solution)/shard_map/ppermute | solution.py:341
  10.2 1.5 %collective-permute-start.6 = (bf16[784,128]{1,0:T(8,128)(2,1)}, bf16[784,128]{1,0:T(8,128)(2,1)S(1)}, u32[]{:S(2)}, u32[]{:S(2)}) collective-permute-start(bf16[784,128]{1,0:T(8,128)(2,1)} %get-tuple-element.34), channel_id=1, source_target_pairs={{0,16},{4,20},{8,24},{12,28},{16,0},{20,4},{24,8},{28,12},{1,17},{... | collective-permute-start | bytes 602120 | tf_op jit(solution)/shard_map/ppermute | solution.py:341
  11.8 0.6 collective-permute-start.7
  12.3 0.2 collective-permute-done.refs_2_
  12.5 0.4 collective-permute-start.8
  12.9 3.6 %collective-permute-done.1.refs_3_ = bf16[784,128]{1,0:T(8,128)(2,1)S(1)} collective-permute-done((bf16[784,128]{1,0:T(8,128)(2,1)}, bf16[784,128]{1,0:T(8,128)(2,1)S(1)}, u32[]{:S(2)}, u32[]{:S(2)}) %collective-permute-start.1) | collective-permute-done | bytes 200736 | tf_op jit(solution)/shard_map/ppermute | solution.py:341
  16.5 0.1 collective-permute-start.9
  16.6 1.1 %cot.1 = (bf16[2176,128]{1,0:T(8,128)(2,1)S(1)}, bf16[2176,128]{1,0:T(8,128)(2,1)S(1)}, bf16[1152,128]{1,0:T(8,128)(2,1)S(1)}, bf16[1152,128]{1,0:T(8,128)(2,1)S(1)}) custom-call(s32[1,8]{1,0:T(1,128)S(1)} %copy-done.1, bf16[272,2048]{1,0:T(8,128)(2,1)S(1)} %copy-done, bf16[784,128]{1,0:T(8,128)(2,1)S(1)} %collective-permute-done.refs_2_, ...), custom_call_target="tpu_custom_call" | custom-call | bytes 3407872 | tf_op jit(solution)/shard_map/cot/pallas_call | solution.py:387
  17.8 3.9 %collective-permute-done.5.refs_4_ = bf16[784,128]{1,0:T(8,128)(2,1)S(1)} collective-permute-done((bf16[784,128]{1,0:T(8,128)(2,1)}, bf16[784,128]{1,0:T(8,128)(2,1)S(1)}, u32[]{:S(2)}, u32[]{:S(2)}) %collective-permute-start.5) | collective-permute-done | bytes 200736 | tf_op jit(solution)/shard_map/ppermute | solution.py:341
  21.7 3.4 %collective-permute-done.7.refs_6_ = bf16[784,128]{1,0:T(8,128)(2,1)S(1)} collective-permute-done((bf16[784,128]{1,0:T(8,128)(2,1)}, bf16[784,128]{1,0:T(8,128)(2,1)S(1)}, u32[]{:S(2)}, u32[]{:S(2)}) %collective-permute-start.7) | collective-permute-done | bytes 200736 | tf_op jit(solution)/shard_map/ppermute | solution.py:341
  25.2 5.1 %attend.1 = (bf16[1040,128]{1,0:T(8,128)(2,1)S(1)}, bf16[1040,128]{1,0:T(8,128)(2,1)S(1)}) custom-call(s32[8]{0:T(128)S(1)} %copy-done.3, bf16[784,128]{1,0:T(8,128)(2,1)S(1)} %copy-done.2, bf16[784,128]{1,0:T(8,128)(2,1)S(1)} %collective-permute-done.refs_2_, bf16[784,128]{1,0:T(8,128)(2,1)S(1)} %collective-permute-done.1.refs_3_, ...), custom_call_target="tpu_custom_call" | custom-call | flops 1073741824 | bytes 1064960 | tf_op jit(solution)/shard_map/attend/pallas_call | solution.py:405
  30.3 0.8 %collective-permute-done.3.a_ref = bf16[1152,128]{1,0:T(8,128)(2,1)S(1)} collective-permute-done((bf16[1152,128]{1,0:T(8,128)(2,1)S(1)}, bf16[1152,128]{1,0:T(8,128)(2,1)S(1)}, u32[]{:S(2)}, u32[]{:S(2)}) %collective-permute-start.3) | collective-permute-done | bytes 294944 | tf_op jit(solution)/shard_map/ppermute | solution.py:341
  31.1 2.1 %collective-permute-start.10 = (bf16[2,1152,128]{2,1,0:T(8,128)(2,1)S(1)}, bf16[2,1152,128]{2,1,0:T(8,128)(2,1)S(1)}, u32[]{:S(2)}, u32[]{:S(2)}) collective-permute-start(bf16[2,1152,128]{2,1,0:T(8,128)(2,1)S(1)} %stack.1.refs_2_), channel_id=1, source_target_pairs={{0,1},{1,0},{2,3},{3,2},{4,5},{5,4},{6,7},{7,6},{8,9},{9,8},{10,11... | collective-permute-start | bytes 1769480 | tf_op jit(solution)/shard_map/ppermute | solution.py:344
  33.2 1.1 %collective-permute-start.12 = (bf16[1040,128]{1,0:T(8,128)(2,1)S(1)}, bf16[1040,128]{1,0:T(8,128)(2,1)S(1)}, u32[]{:S(2)}, u32[]{:S(2)}) collective-permute-start(bf16[1040,128]{1,0:T(8,128)(2,1)S(1)} %get-tuple-element.38.behind.refs_1_.refs_8_), channel_id=1, source_target_pairs={{0,16},{4,12},{8,24},{12,4},{16,0},{20,28},{24,8},{28,20},{1,17},{... | collective-permute-start | bytes 798728 | tf_op jit(solution)/shard_map/ppermute | solution.py:341
  34.3 1.5 %collective-permute-start.11 = (bf16[1040,128]{1,0:T(8,128)(2,1)S(1)}, bf16[1040,128]{1,0:T(8,128)(2,1)S(1)}, u32[]{:S(2)}, u32[]{:S(2)}) collective-permute-start(bf16[1040,128]{1,0:T(8,128)(2,1)S(1)} %get-tuple-element.40), channel_id=1, source_target_pairs={{0,8},{4,20},{8,0},{12,28},{16,24},{20,4},{24,16},{28,12},{1,9},{5... | collective-permute-start | bytes 798728 | tf_op jit(solution)/shard_map/ppermute | solution.py:341
  35.8 10.8 %collective-permute-done.10.refs_3_ = bf16[2,1152,128]{2,1,0:T(8,128)(2,1)S(1)} collective-permute-done((bf16[2,1152,128]{2,1,0:T(8,128)(2,1)S(1)}, bf16[2,1152,128]{2,1,0:T(8,128)(2,1)S(1)}, u32[]{:S(2)}, u32[]{:S(2)}) %collective-permute-start.10) | collective-permute-done | bytes 589856 | tf_op jit(solution)/shard_map/ppermute | solution.py:344
  46.6 1.2 %turn.1 = (bf16[512,1088]{1,0:T(8,128)(2,1)S(1)}, bf16[512,1088]{1,0:T(8,128)(2,1)S(1)}) custom-call(bf16[2176,128]{1,0:T(8,128)(2,1)S(1)} %get-tuple-element.28.refs_0_, bf16[2176,128]{1,0:T(8,128)(2,1)S(1)} %collective-permute-done.2.refs_1_, bf16[2,1152,128]{2,1,0:T(8,128)(2,1)S(1)} %stack.1.refs_2_, bf16[2,1152,128]{2,1,0:T(8,128)(2,1)S(1)} %collective-permute-done.10.refs_3_), custom_call_target="tpu_custom_call" | custom-call | bytes 4456448 | tf_op jit(solution)/shard_map/turn/pallas_call | solution.py:430
  47.8 0.8 %keep_near.1 = (f32[256,384]{1,0:T(8,128)S(1)}, bf16[512,384]{1,0:T(8,128)(2,1)S(1)}) custom-call(bf16[512,1088]{1,0:T(8,128)(2,1)S(1)} %get-tuple-element.39.refs_0_, bf16[1040,128]{1,0:T(8,128)(2,1)S(1)} %get-tuple-element.38.behind.refs_1_.refs_8_, bf16[1040,128]{1,0:T(8,128)(2,1)S(1)} %collective-permute-done.11.refs_2_.refs_9_, ...), custom_call_target="tpu_custom_call" | custom-call | flops 427819008 | bytes 1572864 | tf_op jit(solution)/shard_map/keep_near/pallas_call | solution.py:450
  48.7 0.4 collective-permute-start.13
  49.1 0.8 %send_near.1 = (bf16[256,384]{1,0:T(8,128)(2,1)S(1)}, bf16[256,384]{1,0:T(8,128)(2,1)S(1)}) custom-call(bf16[512,1088]{1,0:T(8,128)(2,1)S(1)} %get-tuple-element.43.refs_0_, bf16[1040,128]{1,0:T(8,128)(2,1)S(1)} %get-tuple-element.38.behind.refs_1_.refs_8_, bf16[1040,128]{1,0:T(8,128)(2,1)S(1)} %collective-permute-done.11.refs_2_.refs_9_, ...), custom_call_target="tpu_custom_call" | custom-call | flops 427819008 | bytes 786432 | tf_op jit(solution)/shard_map/send_near/pallas_call | solution.py:442
  49.9 1.8 %collective-permute-start.14 = (bf16[256,384]{1,0:T(8,128)(2,1)S(1)}, bf16[256,384]{1,0:T(8,128)(2,1)S(1)}, u32[]{:S(2)}, u32[]{:S(2)}) collective-permute-start(bf16[256,384]{1,0:T(8,128)(2,1)S(1)} %get-tuple-element.44), channel_id=1, source_target_pairs={{0,8},{4,20},{8,0},{12,28},{16,24},{20,4},{24,16},{28,12},{1,9},{5... | collective-permute-start | bytes 589832 | tf_op jit(solution)/shard_map/ppermute | solution.py:341
  51.7 4.6 %collective-permute-done.13.refs_1_.refs_11_ = bf16[1040,128]{1,0:T(8,128)(2,1)S(1)} collective-permute-done((bf16[1040,128]{1,0:T(8,128)(2,1)S(1)}, bf16[1040,128]{1,0:T(8,128)(2,1)S(1)}, u32[]{:S(2)}, u32[]{:S(2)}) %collective-permute-start.13) | collective-permute-done | bytes 266272 | tf_op jit(solution)/shard_map/ppermute | solution.py:341
  56.3 0.5 keep_far.1
  56.9 0.5 send_far.1
  57.3 2.9 %collective-permute-start.16 = (bf16[256,128]{1,0:T(8,128)(2,1)S(1)}, bf16[256,128]{1,0:T(8,128)(2,1)S(1)}, u32[]{:S(2)}, u32[]{:S(2)}) collective-permute-start(bf16[256,128]{1,0:T(8,128)(2,1)S(1)} %get-tuple-element.46), channel_id=1, source_target_pairs={{0,8},{4,20},{8,0},{12,28},{16,24},{20,4},{24,16},{28,12},{1,9},{5... | collective-permute-start | bytes 196616 | tf_op jit(solution)/shard_map/ppermute | solution.py:341
  60.2 0.5 collective-permute-start.18
  60.7 1.8 %collective-permute-done.16.refs_3_ = bf16[256,128]{1,0:T(8,128)(2,1)S(1)} collective-permute-done((bf16[256,128]{1,0:T(8,128)(2,1)S(1)}, bf16[256,128]{1,0:T(8,128)(2,1)S(1)}, u32[]{:S(2)}, u32[]{:S(2)}) %collective-permute-start.16) | collective-permute-done | bytes 65568 | tf_op jit(solution)/shard_map/ppermute | solution.py:341
  62.5 1.4 %collective-permute-done.18.refs_5_ = bf16[256,128]{1,0:T(8,128)(2,1)S(1)} collective-permute-done((bf16[256,128]{1,0:T(8,128)(2,1)S(1)}, bf16[256,128]{1,0:T(8,128)(2,1)S(1)}, u32[]{:S(2)}, u32[]{:S(2)}) %collective-permute-start.18) | collective-permute-done | bytes 65568 | tf_op jit(solution)/shard_map/ppermute | solution.py:341
  63.9 1.3 %finish.1 = (bf16[256,1024]{1,0:T(8,128)(2,1)}, f32[256,1024]{1,0:T(8,128)}) custom-call(f32[256,384]{1,0:T(8,128)S(1)} %get-tuple-element.41.refs_0_, f32[256,128]{1,0:T(8,128)S(1)} %get-tuple-element.42.refs_1_, bf16[256,384]{1,0:T(8,128)(2,1)S(1)} %collective-permute-done.14.refs_2_, bf16[256,128]{1,0:T(8,128)(2,1)S(1)} %collective-permute-done.16.refs_3_, ...), custom_call_target="tpu_custom_call" | custom-call | bytes 3145728 | tf_op jit(solution)/shard_map/finish/pallas_call | solution.py:463
  (27 shorter events, 0.2 us)
Async XLA Ops:
  2.5 14.1 %copy-start = (bf16[272,2048]{1,0:T(8,128)(2,1)S(1)}, bf16[272,2048]{1,0:T(8,128)(2,1)}, u32[]{:S(2)}) copy-start(bf16[272,2048]{1,0:T(8,128)(2,1)} %refs_1_.4) | copy-start | bytes 3342340
  2.5 14.1 %copy-start.1 = (s32[1,8]{1,0:T(1,128)S(1)}, s32[1,8]{1,0:T(1,128)}, u32[]{:S(2)}) copy-start(s32[1,8]{1,0:T(1,128)} %refs_0_.5) | copy-start | bytes 100
  2.5 10.0 %collective-permute-start = (bf16[784,128]{1,0:T(8,128)(2,1)}, bf16[784,128]{1,0:T(8,128)(2,1)S(1)}, u32[]{:S(2)}, u32[]{:S(2)}) collective-permute-start(bf16[784,128]{1,0:T(8,128)(2,1)} %get-tuple-element.26), channel_id=1, source_target_pairs={{0,24},{4,28},{8,16},{12,20},{16,8},{20,12},{24,0},{28,4},{1,25},{... | collective-permute-start | bytes 602120 | tf_op jit(solution)/shard_map/ppermute | solution.py:341
  6.5 18.7 %copy-start.3 = (s32[8]{0:T(128)S(1)}, s32[8]{0:T(128)}, u32[]{:S(2)}) copy-start(s32[8]{0:T(128)} %refs_0_.7) | copy-start | bytes 100
  6.5 10.1 %collective-permute-start.1 = (bf16[784,128]{1,0:T(8,128)(2,1)}, bf16[784,128]{1,0:T(8,128)(2,1)S(1)}, u32[]{:S(2)}, u32[]{:S(2)}) collective-permute-start(bf16[784,128]{1,0:T(8,128)(2,1)} %get-tuple-element.27), channel_id=1, source_target_pairs={{0,28},{4,24},{8,20},{12,16},{16,12},{20,8},{24,4},{28,0},{1,29},{... | collective-permute-start | bytes 602120 | tf_op jit(solution)/shard_map/ppermute | solution.py:341
  9.1 16.1 %copy-start.2 = (bf16[784,128]{1,0:T(8,128)(2,1)S(1)}, bf16[784,128]{1,0:T(8,128)(2,1)}, u32[]{:S(2)}) copy-start(bf16[784,128]{1,0:T(8,128)(2,1)} %get-tuple-element.32.refs_1_) | copy-start | bytes 602116
  9.1 12.6 %collective-permute-start.5 = (bf16[784,128]{1,0:T(8,128)(2,1)}, bf16[784,128]{1,0:T(8,128)(2,1)S(1)}, u32[]{:S(2)}, u32[]{:S(2)}) collective-permute-start(bf16[784,128]{1,0:T(8,128)(2,1)} %get-tuple-element.33), channel_id=1, source_target_pairs={{0,8},{4,12},{8,0},{12,4},{16,24},{20,28},{24,16},{28,20},{1,9},{5... | collective-permute-start | bytes 602120 | tf_op jit(solution)/shard_map/ppermute | solution.py:341
  10.2 11.4 %collective-permute-start.6 = (bf16[784,128]{1,0:T(8,128)(2,1)}, bf16[784,128]{1,0:T(8,128)(2,1)S(1)}, u32[]{:S(2)}, u32[]{:S(2)}) collective-permute-start(bf16[784,128]{1,0:T(8,128)(2,1)} %get-tuple-element.34), channel_id=1, source_target_pairs={{0,16},{4,20},{8,24},{12,28},{16,0},{20,4},{24,8},{28,12},{1,17},{... | collective-permute-start | bytes 602120 | tf_op jit(solution)/shard_map/ppermute | solution.py:341
  11.8 13.4 %collective-permute-start.7 = (bf16[784,128]{1,0:T(8,128)(2,1)}, bf16[784,128]{1,0:T(8,128)(2,1)S(1)}, u32[]{:S(2)}, u32[]{:S(2)}) collective-permute-start(bf16[784,128]{1,0:T(8,128)(2,1)} %get-tuple-element.35), channel_id=1, source_target_pairs={{0,12},{4,8},{8,4},{12,0},{16,28},{20,24},{24,20},{28,16},{1,13},{... | collective-permute-start | bytes 602120 | tf_op jit(solution)/shard_map/ppermute | solution.py:341
  12.5 12.6 %collective-permute-start.8 = (bf16[784,128]{1,0:T(8,128)(2,1)}, bf16[784,128]{1,0:T(8,128)(2,1)S(1)}, u32[]{:S(2)}, u32[]{:S(2)}) collective-permute-start(bf16[784,128]{1,0:T(8,128)(2,1)} %get-tuple-element.36), channel_id=1, source_target_pairs={{0,20},{4,16},{8,28},{12,24},{16,4},{20,0},{24,12},{28,8},{1,21},{... | collective-permute-start | bytes 602120 | tf_op jit(solution)/shard_map/ppermute | solution.py:341
  16.5 8.6 %collective-permute-start.9 = (bf16[784,128]{1,0:T(8,128)(2,1)}, bf16[784,128]{1,0:T(8,128)(2,1)S(1)}, u32[]{:S(2)}, u32[]{:S(2)}) collective-permute-start(bf16[784,128]{1,0:T(8,128)(2,1)} %get-tuple-element.37), channel_id=1, source_target_pairs={{0,4},{4,0},{8,12},{12,8},{16,20},{20,16},{24,28},{28,24},{1,5},{5... | collective-permute-start | bytes 602120 | tf_op jit(solution)/shard_map/ppermute | solution.py:341
  21.7 9.3 %collective-permute-start.3 = (bf16[1152,128]{1,0:T(8,128)(2,1)S(1)}, bf16[1152,128]{1,0:T(8,128)(2,1)S(1)}, u32[]{:S(2)}, u32[]{:S(2)}) collective-permute-start(bf16[1152,128]{1,0:T(8,128)(2,1)S(1)} %get-tuple-element.30), channel_id=1, source_target_pairs={{0,16},{4,12},{8,24},{12,4},{16,0},{20,28},{24,8},{28,20},{1,17},{... | collective-permute-start | bytes 884744 | tf_op jit(solution)/shard_map/ppermute | solution.py:341
  21.7 9.3 %collective-permute-start.4 = (bf16[1152,128]{1,0:T(8,128)(2,1)S(1)}, bf16[1152,128]{1,0:T(8,128)(2,1)S(1)}, u32[]{:S(2)}, u32[]{:S(2)}) collective-permute-start(bf16[1152,128]{1,0:T(8,128)(2,1)S(1)} %get-tuple-element.31), channel_id=1, source_target_pairs={{0,12},{4,16},{8,4},{12,24},{16,28},{20,0},{24,20},{28,8},{1,13},{... | collective-permute-start | bytes 884744 | tf_op jit(solution)/shard_map/ppermute | solution.py:341
  31.1 15.5 %collective-permute-start.10 = (bf16[2,1152,128]{2,1,0:T(8,128)(2,1)S(1)}, bf16[2,1152,128]{2,1,0:T(8,128)(2,1)S(1)}, u32[]{:S(2)}, u32[]{:S(2)}) collective-permute-start(bf16[2,1152,128]{2,1,0:T(8,128)(2,1)S(1)} %stack.1.refs_2_), channel_id=1, source_target_pairs={{0,1},{1,0},{2,3},{3,2},{4,5},{5,4},{6,7},{7,6},{8,9},{9,8},{10,11... | collective-permute-start | bytes 1769480 | tf_op jit(solution)/shard_map/ppermute | solution.py:344
  33.2 2.6 %collective-permute-start.2 = (bf16[2176,128]{1,0:T(8,128)(2,1)S(1)}, bf16[2176,128]{1,0:T(8,128)(2,1)S(1)}, u32[]{:S(2)}, u32[]{:S(2)}) collective-permute-start(bf16[2176,128]{1,0:T(8,128)(2,1)S(1)} %get-tuple-element.29), channel_id=1, source_target_pairs={{0,4},{4,0},{8,12},{12,8},{16,20},{20,16},{24,28},{28,24},{1,5},{5... | collective-permute-start | bytes 1671176 | tf_op jit(solution)/shard_map/ppermute | solution.py:341
  33.2 14.6 %collective-permute-start.12 = (bf16[1040,128]{1,0:T(8,128)(2,1)S(1)}, bf16[1040,128]{1,0:T(8,128)(2,1)S(1)}, u32[]{:S(2)}, u32[]{:S(2)}) collective-permute-start(bf16[1040,128]{1,0:T(8,128)(2,1)S(1)} %get-tuple-element.38.behind.refs_1_.refs_8_), channel_id=1, source_target_pairs={{0,16},{4,12},{8,24},{12,4},{16,0},{20,28},{24,8},{28,20},{1,17},{... | collective-permute-start | bytes 798728 | tf_op jit(solution)/shard_map/ppermute | solution.py:341
  34.3 13.5 %collective-permute-start.11 = (bf16[1040,128]{1,0:T(8,128)(2,1)S(1)}, bf16[1040,128]{1,0:T(8,128)(2,1)S(1)}, u32[]{:S(2)}, u32[]{:S(2)}) collective-permute-start(bf16[1040,128]{1,0:T(8,128)(2,1)S(1)} %get-tuple-element.40), channel_id=1, source_target_pairs={{0,8},{4,20},{8,0},{12,28},{16,24},{20,4},{24,16},{28,12},{1,9},{5... | collective-permute-start | bytes 798728 | tf_op jit(solution)/shard_map/ppermute | solution.py:341
  48.6 8.3 %collective-permute-start.15 = (bf16[512,384]{1,0:T(8,128)(2,1)S(1)}, bf16[512,384]{1,0:T(8,128)(2,1)S(1)}, u32[]{:S(2)}, u32[]{:S(2)}) collective-permute-start(bf16[512,384]{1,0:T(8,128)(2,1)S(1)} %get-tuple-element.45), channel_id=1, source_target_pairs={{0,4},{4,0},{8,12},{12,8},{16,20},{20,16},{24,28},{28,24},{1,5},{5... | collective-permute-start | bytes 1179656 | tf_op jit(solution)/shard_map/ppermute | solution.py:341
  48.7 7.6 %collective-permute-start.13 = (bf16[1040,128]{1,0:T(8,128)(2,1)S(1)}, bf16[1040,128]{1,0:T(8,128)(2,1)S(1)}, u32[]{:S(2)}, u32[]{:S(2)}) collective-permute-start(bf16[1040,128]{1,0:T(8,128)(2,1)S(1)} %collective-permute-done.11.refs_2_.refs_9_), channel_id=1, source_target_pairs={{0,16},{4,12},{8,24},{12,4},{16,0},{20,28},{24,8},{28,20},{1,17},{... | collective-permute-start | bytes 798728 | tf_op jit(solution)/shard_map/ppermute | solution.py:341
  49.9 10.8 %collective-permute-start.14 = (bf16[256,384]{1,0:T(8,128)(2,1)S(1)}, bf16[256,384]{1,0:T(8,128)(2,1)S(1)}, u32[]{:S(2)}, u32[]{:S(2)}) collective-permute-start(bf16[256,384]{1,0:T(8,128)(2,1)S(1)} %get-tuple-element.44), channel_id=1, source_target_pairs={{0,8},{4,20},{8,0},{12,28},{16,24},{20,4},{24,16},{28,12},{1,9},{5... | collective-permute-start | bytes 589832 | tf_op jit(solution)/shard_map/ppermute | solution.py:341
  51.7 9.0 %collective-permute-start.17 = (bf16[256,384]{1,0:T(8,128)(2,1)S(1)}, bf16[256,384]{1,0:T(8,128)(2,1)S(1)}, u32[]{:S(2)}, u32[]{:S(2)}) collective-permute-start(bf16[256,384]{1,0:T(8,128)(2,1)S(1)} %get-tuple-element.47), channel_id=1, source_target_pairs={{0,12},{4,16},{8,4},{12,24},{16,28},{20,0},{24,20},{28,8},{1,13},{... | collective-permute-start | bytes 589832 | tf_op jit(solution)/shard_map/ppermute | solution.py:341
  56.8 3.9 %collective-permute-start.19 = (bf16[512,128]{1,0:T(8,128)(2,1)S(1)}, bf16[512,128]{1,0:T(8,128)(2,1)S(1)}, u32[]{:S(2)}, u32[]{:S(2)}) collective-permute-start(bf16[512,128]{1,0:T(8,128)(2,1)S(1)} %get-tuple-element.49), channel_id=1, source_target_pairs={{0,4},{4,0},{8,12},{12,8},{16,20},{20,16},{24,28},{28,24},{1,5},{5... | collective-permute-start | bytes 393224 | tf_op jit(solution)/shard_map/ppermute | solution.py:341
  57.3 5.1 %collective-permute-start.16 = (bf16[256,128]{1,0:T(8,128)(2,1)S(1)}, bf16[256,128]{1,0:T(8,128)(2,1)S(1)}, u32[]{:S(2)}, u32[]{:S(2)}) collective-permute-start(bf16[256,128]{1,0:T(8,128)(2,1)S(1)} %get-tuple-element.46), channel_id=1, source_target_pairs={{0,8},{4,20},{8,0},{12,28},{16,24},{20,4},{24,16},{28,12},{1,9},{5... | collective-permute-start | bytes 196616 | tf_op jit(solution)/shard_map/ppermute | solution.py:341
  60.2 3.7 %collective-permute-start.18 = (bf16[256,128]{1,0:T(8,128)(2,1)S(1)}, bf16[256,128]{1,0:T(8,128)(2,1)S(1)}, u32[]{:S(2)}, u32[]{:S(2)}) collective-permute-start(bf16[256,128]{1,0:T(8,128)(2,1)S(1)} %get-tuple-element.48), channel_id=1, source_target_pairs={{0,12},{4,16},{8,4},{12,24},{16,28},{20,0},{24,20},{28,8},{1,13},{... | collective-permute-start | bytes 196616 | tf_op jit(solution)/shard_map/ppermute | solution.py:341

commit v7 on v6

--- a/solution.py
+++ b/solution.py
@@ -211,16 +211,16 @@
         out_ref[rows:, :] = hist
 
 
-def stack_kernel(a_ref, b_ref, behind, out_ref):
-    out_ref[0] = a_ref[...]
-    out_ref[1] = b_ref[...]
-
-
-def lay_out(rows, pieces):
-    return jnp.concatenate([x[:rows] for x in pieces], axis=1)
-
-
-def turn_kernel(lo, clip_rows, own_in, core_in, mine_ref, swapped_ref, own_ref, give_ref, whole):
+def stack_kernel(tiles, lo, a_ref, b_ref, behind, out_ref):
+    plane = lax.rem(lax.axis_index("head"), 2)
+    part = a_ref.shape[0] // tiles
+    for i, ref in enumerate((a_ref, b_ref)):
+        for u in range(tiles):
+            first = pl.multiple_of(u * part + plane * (part - lo), 16)
+            out_ref[i, u * lo : (u + 1) * lo, :] = ref[pl.ds(first, lo), :]
+
+
+def turn_kernel(lo, clip_rows, own_in, core_in, mate_in, cross_in, swapped_ref, own_ref, give_ref, whole):
     own, side, mate, partner = place()
     plane = lax.rem(lax.axis_index("head"), 2)
     _, all_rows, width = whole.shape
@@ -231,11 +231,12 @@
         full = slice(u * all_rows, (u + 1) * all_rows)
         whole[0, :, lanes] = own_in[full, :]
         whole[1, :, lanes] = core_in[full, :]
-        for i in range(2):
-            a = mine_ref[i, u * part : (u + 1) * part, :]
-            b = swapped_ref[i, u * part : (u + 1) * part, :]
-            whole[2 + i, 0:lo, lanes] = jnp.where(plane == 0, a, b)[:lo]
-            whole[2 + i, lo:all_rows, lanes] = jnp.where(plane == 0, b, a)
+        for i, ref in enumerate((mate_in, cross_in)):
+            a = ref[u * part : (u + 1) * part, :]
+            b = swapped_ref[i, u * lo : (u + 1) * lo, :]
+            whole[2 + i, 0:lo, lanes] = jnp.where(plane == 0, a[:lo], b)
+            whole[2 + i, lo:part, lanes] = jnp.where(plane == 0, a[lo:], a[: part - lo])
+            whole[2 + i, part:all_rows, lanes] = jnp.where(plane == 0, b, a[part - lo :])
     at = lax.rem(own // mate, 2)
     slots = [2 * ((p // 2) ^ at) + ((p % 2) ^ side) for p in range(4)]
     for i, out_ref in enumerate((own_ref, give_ref)):
@@ -265,21 +266,24 @@
     cross_ref[...] = out[cols:]
 
 
-def keep_kernel(rows, copies, tok, turned_ref, *refs):
-    heads, (keep_ref, give_ref) = refs[:-2], refs[-2:]
+def keep_kernel(rows, copies, tok, before, n, turned_ref, *refs):
+    heads, (keep_ref, give_ref) = refs[before : before + n], refs[-2:]
     own, side, mate, partner = place()
     cols, width = keep_ref.shape
+    start = give_ref.shape[1] - width
+    if before:
+        give_ref[:, 0:start] = refs[0][...]
     out = grad_part(turned_ref, heads, rows, copies)
     keep_ref[...] = out[:cols]
-    give_ref[0:cols, :] = out[cols:].astype(jnp.bfloat16)
+    give_ref[0:cols, start:] = out[cols:].astype(jnp.bfloat16)
     at = 2 * lax.rem(own // mate, 2) + 1 - side
     for i, x in enumerate(heads):
-        give_ref[cols : cols + tok, i * HD : (i + 1) * HD] = x[
+        give_ref[cols : cols + tok, start + i * HD : start + (i + 1) * HD] = x[
             pl.ds(pl.multiple_of(at * tok, tok), tok), :
         ]
 
 
-def finish_kernel(tok, keep_near, keep_far, same_near, same_far, cross_near, cross_far, core_near, core_far, *refs):
+def finish_kernel(tok, keep_near, keep_far, same_near, same_far, cross_near, cross_far, core, *refs):
     heads, (att_hbm, out_hbm, total, sems) = refs[:4], refs[4:]
     own, side, mate, partner = place()
     cols = keep_near.shape[0]
@@ -294,7 +298,7 @@
         return pl.ds(pl.multiple_of(head * HD, HD), HD)
 
     def column(near, far, i):
-        ref, i = (near, i) if i < 3 else (far, 0)
+        ref, i = (far, 0) if i == 3 and far is not near else (near, i)
         return ref[0:cols, i * HD : (i + 1) * HD].astype(jnp.float32)
 
     mine = [own, own ^ partner, own ^ mate, own ^ 6]
@@ -302,17 +306,13 @@
     for i, head in enumerate(mine):
         move(heads[i].at[pl.ds(pl.multiple_of(at * tok, tok), tok), :], att_hbm.at[:, lanes(head)])
     for i, head in enumerate(theirs):
-        ref, k = (core_near, i) if i < 3 else (core_far, 0)
-        move(
-            ref.at[pl.ds(cols, tok), pl.ds(k * HD, HD)],
-            att_hbm.at[:, lanes(head)],
-        )
+        move(core.at[pl.ds(cols, tok), pl.ds(i * HD, HD)], att_hbm.at[:, lanes(head)])
     there = [1, 0, 3, 2]
     for i, head in enumerate(mine):
         total[i] = column(keep_near, keep_far, i) + column(same_near, same_far, there[i])
         move(total.at[i], out_hbm.at[:, lanes(head)])
     for i, head in enumerate(theirs):
-        total[4 + i] = column(core_near, core_far, i) + column(cross_near, cross_far, there[i])
+        total[4 + i] = column(core, core, i) + column(cross_near, cross_far, there[i])
         move(total.at[4 + i], out_hbm.at[:, lanes(head)])
     for x in moves:
         x.wait()
@@ -328,7 +328,7 @@
     cot_rows, all_cols = cotangent.shape
     cols = all_cols // n
     units = cols // HD
-    lo = cot_rows // 32 * 16
+    lo = cot_rows // 64 * 16
     part = cot_rows - lo
     base = 3 * tok + clip_rows
     length = base
@@ -355,7 +355,7 @@
             out_specs=tuple([out_spec] * len(shapes)),
             scratch_shapes=scratch,
             compiler_params=pltpu.CompilerParams(vmem_limit_bytes=limit),
-            cost_estimate=pl.CostEstimate(flops=flops, bytes_accessed=moved, transcendentals=exps),
+            cost_estimate=pl.CostEstimate(flops=flops, bytes_accessed=moved if flops else 0, transcendentals=exps),
             name=name,
         )
 
@@ -418,53 +418,58 @@
     )(frame_counts, *by_head)
     sum_head, mate_head = swap(others, sum_bit), swap(mine, mate_bit)
     far_head = swap(sum_head, mate_bit)
-    (cot_mine,) = call(
-        stack_kernel,
+    (cot_rest,) = call(
+        lambda *refs: stack_kernel(tiles, lo, *refs),
         "stack",
-        [((2, tiles * part, HD), bf16)],
+        [((2, tiles * lo, HD), bf16)],
         [vmem] * 2 + [hbm],
         0,
     )(cot_mate, cot_cross, mine)
-    cot_swapped = swap_plane(cot_mine)
+    cot_swapped = swap_plane(cot_rest)
 
     turned_own, turned_give = call(
         lambda *refs: turn_kernel(lo, clip_rows, *refs),
         "turn",
         [((2 * cols, half * cot_rows), bf16)] * 2,
-        [vmem] * 4,
+        [vmem] * 5,
         0,
         (pltpu.VMEM((4, cot_rows, tiles * HD), bf16),),
-    )(cot_own, cot_core, cot_mine, cot_swapped)
-
-    def share(heads, name, *behind):
+    )(cot_own, cot_core, cot_mate, cot_cross, cot_swapped)
+
+    def send(heads, name):
         lanes = len(heads) * HD
-        flops = 4 * cols * half * cot_rows * lanes
         same, cross = call(
             lambda *refs: send_kernel(rows, half, len(heads), *refs),
             "send_" + name,
             [((cols, lanes), bf16)] * 2,
-            [vmem] * (1 + len(heads)) + [hbm] * len(behind),
-            flops,
-        )(turned_give, *heads, *behind)
-        same, cross = swap(same, sum_bit), swap(cross, lambda i: sum_bit(i) ^ 1)
-        keep, give = call(
-            lambda *refs: keep_kernel(rows, half, tok, *refs),
+            [vmem] * (1 + len(heads)),
+            0,
+        )(turned_give, *heads)
+        return same, swap(same, sum_bit), swap(cross, lambda i: sum_bit(i) ^ 1)
+
+    def keep(heads, name, behind, *before):
+        lanes = len(heads) * HD
+        given = lanes + sum(x.shape[1] for x in before)
+        return call(
+            lambda *refs: keep_kernel(rows, half, tok, len(before), len(heads), *refs),
             "keep_" + name,
-            [((cols, lanes), jnp.float32), ((cols + tok, lanes), bf16)],
-            [vmem] * (1 + len(heads)),
-            flops,
-        )(turned_own, *heads)
-        return keep, same, cross, swap(give, lambda i: 1)
+            [((cols, lanes), jnp.float32), ((cols + tok, given), bf16)],
+            [vmem] * (1 + len(before) + len(heads)) + [hbm] * len(behind),
+            0,
+        )(turned_own, *before, *heads, *behind)
 
     near, far = [mine, sum_head, mate_head], [far_head]
-    near_sums = share(near, "near")
-    far_sums = share(far, "far", near_sums[3])
-    sums = [x for pair in zip(near_sums, far_sums) for x in pair]
+    sent, same_near, cross_near = send(near, "near")
+    keep_near, give_near = keep(near, "near", [sent])
+    sent, same_far, cross_far = send(far, "far")
+    keep_far, give = keep(far, "far", [same_near, cross_near], give_near)
+    core = swap(give, lambda i: 1)
+    sums = (keep_near, keep_far, same_near, same_far, cross_near, cross_far, core)
     return call(
         lambda *refs: finish_kernel(tok, *refs),
         "finish",
         [((tok, width), bf16), ((cols, width), jnp.float32)],
-        [vmem] * 12,
+        [vmem] * 11,
         0,
         (pltpu.VMEM((n, cols, HD), jnp.float32), pltpu.SemaphoreType.DMA((2 * n,))),
         out_spec=hbm,

time: 65.4 us -> 66.5 us (1.017)
  waiting for transfers between devices: 30.5 us -> 32.2 us
    ppermute x19 -> x18, waiting for transfers between devices: 19.8 us -> 31.8 us  [swap(): return lax.ppermute(x, 'tm', [(i, i ^ bit(i)) for i in range(n)])]
    ppermute x1, waiting for transfers between devices: 10.8 us -> 0.4 us  [swap_plane(): return lax.ppermute(x, 'head', [(p, p ^ 1) for p in range(planes)])]
    ppermute x19 -> x18, starting transfers between devices: 16.1 us -> 16 us  [swap(): return lax.ppermute(x, 'tm', [(i, i ^ bit(i)) for i in range(n)])]
  transfers between devices with their start and end apart: 20 -> 19, of which waited for: 9 -> 12; matrix products, arithmetic and copies ran while one was open for 0% -> 0% of each run, Pallas kernels for 18% -> 18%
where the time goes in v7:
time: 66.5 us; the launch traced here: 66.3 us
  waiting for transfers between devices  32.2 us (48%)
  starting transfers between devices  17.6 us (26%)
  Pallas kernels  15.7 us (24%)
  between operations  0.78 us (1%)
    ppermute x18, waiting for transfers between devices, swap(): return lax.ppermute(x, 'tm', [(i, i ^ bit(i)) for i in range(n)])  31.8 us
    ppermute x18, starting transfers between devices, swap(): return lax.ppermute(x, 'tm', [(i, i ^ bit(i)) for i in range(n)])  16 us
    pallas_call x1, Pallas kernels, head_body(): call(lambda *refs: attend_kernel(n, tok, [0] + order, *refs), 'attend', [...  5.08 us
    pallas_call x2, Pallas kernels, pack(): call(lambda *refs: pack_kernel(n, heads, *refs), name, [((length, HD), bf...  4.42 us
    ppermute x1, starting transfers between devices, swap_plane(): return lax.ppermute(x, 'head', [(p, p ^ 1) for p in range(planes)])  1.65 us
  transfers between devices with their start and end apart: 19, of which 12 were waited for; matrix products, arithmetic and copies ran while one was open for 0% of the time, Pallas kernels for 18%

profile of v7, /device:TPU:0, one launch (start us, length us, event | category | flops | bytes accessed | tf_op | source)
XLA Modules:
  0.0 66.3 jit_solution(7604509460388304851)
XLA Ops:
  0.6 1.9 %pack_first.1 = (bf16[784,128]{1,0:T(8,128)(2,1)}, bf16[784,128]{1,0:T(8,128)(2,1)}) custom-call(bf16[256,1024]{1,0:T(8,128)(2,1)} %refs_0_.6, bf16[256,1024]{1,0:T(8,128)(2,1)} %refs_1_.5, bf16[256,1024]{1,0:T(8,128)(2,1)} %refs_2_.3, bf16[2,1024]{1,0:T(2,128)(2,1)} %refs_3_.3), custom_call_target="tpu_custom_call" | custom-call | tf_op jit(solution)/shard_map/pack_first/pallas_call | solution.py:363
  2.5 4.0 %collective-permute-start = (bf16[784,128]{1,0:T(8,128)(2,1)}, bf16[784,128]{1,0:T(8,128)(2,1)S(1)}, u32[]{:S(2)}, u32[]{:S(2)}) collective-permute-start(bf16[784,128]{1,0:T(8,128)(2,1)} %get-tuple-element.26), channel_id=1, source_target_pairs={{0,24},{4,28},{8,16},{12,20},{16,8},{20,12},{24,0},{28,4},{1,25},{... | collective-permute-start | bytes 602120 | tf_op jit(solution)/shard_map/ppermute | solution.py:341
  6.5 2.6 %pack_rest.1 = (bf16[784,128]{1,0:T(8,128)(2,1)}, bf16[784,128]{1,0:T(8,128)(2,1)}, bf16[784,128]{1,0:T(8,128)(2,1)}, bf16[784,128]{1,0:T(8,128)(2,1)}, bf16[784...) custom-call(bf16[256,1024]{1,0:T(8,128)(2,1)} %refs_0_.6, bf16[256,1024]{1,0:T(8,128)(2,1)} %refs_1_.5, ...), custom_call_target="tpu_custom_call" | custom-call | tf_op jit(solution)/shard_map/pack_rest/pallas_call | solution.py:363
  9.1 1.2 %collective-permute-start.5 = (bf16[784,128]{1,0:T(8,128)(2,1)}, bf16[784,128]{1,0:T(8,128)(2,1)S(1)}, u32[]{:S(2)}, u32[]{:S(2)}) collective-permute-start(bf16[784,128]{1,0:T(8,128)(2,1)} %get-tuple-element.33), channel_id=1, source_target_pairs={{0,8},{4,12},{8,0},{12,4},{16,24},{20,28},{24,16},{28,20},{1,9},{5... | collective-permute-start | bytes 602120 | tf_op jit(solution)/shard_map/ppermute | solution.py:341
  10.3 1.5 %collective-permute-start.6 = (bf16[784,128]{1,0:T(8,128)(2,1)}, bf16[784,128]{1,0:T(8,128)(2,1)S(1)}, u32[]{:S(2)}, u32[]{:S(2)}) collective-permute-start(bf16[784,128]{1,0:T(8,128)(2,1)} %get-tuple-element.34), channel_id=1, source_target_pairs={{0,16},{4,20},{8,24},{12,28},{16,0},{20,4},{24,8},{28,12},{1,17},{... | collective-permute-start | bytes 602120 | tf_op jit(solution)/shard_map/ppermute | solution.py:341
  11.8 0.6 collective-permute-start.7
  12.5 4.0 %collective-permute-done.1.refs_3_ = bf16[784,128]{1,0:T(8,128)(2,1)S(1)} collective-permute-done((bf16[784,128]{1,0:T(8,128)(2,1)}, bf16[784,128]{1,0:T(8,128)(2,1)S(1)}, u32[]{:S(2)}, u32[]{:S(2)}) %collective-permute-start.1) | collective-permute-done | bytes 200736 | tf_op jit(solution)/shard_map/ppermute | solution.py:341
  16.5 1.2 %cot.1 = (bf16[2176,128]{1,0:T(8,128)(2,1)S(1)}, bf16[2176,128]{1,0:T(8,128)(2,1)S(1)}, bf16[1664,128]{1,0:T(8,128)(2,1)S(1)}, bf16[1664,128]{1,0:T(8,128)(2,1)S(1)}) custom-call(s32[1,8]{1,0:T(1,128)S(1)} %copy-done.1, bf16[272,2048]{1,0:T(8,128)(2,1)S(1)} %copy-done, bf16[784,128]{1,0:T(8,128)(2,1)S(1)} %collective-permute-done.refs_2_, ...), custom_call_target="tpu_custom_call" | custom-call | tf_op jit(solution)/shard_map/cot/pallas_call | solution.py:387
  17.7 0.6 collective-permute-start.3
  18.3 1.3 %collective-permute-start.4 = (bf16[1664,128]{1,0:T(8,128)(2,1)S(1)}, bf16[1664,128]{1,0:T(8,128)(2,1)S(1)}, u32[]{:S(2)}, u32[]{:S(2)}) collective-permute-start(bf16[1664,128]{1,0:T(8,128)(2,1)S(1)} %get-tuple-element.31), channel_id=1, source_target_pairs={{0,12},{4,16},{8,4},{12,24},{16,28},{20,0},{24,20},{28,8},{1,13},{... | collective-permute-start | bytes 1277960 | tf_op jit(solution)/shard_map/ppermute | solution.py:341
  19.6 2.1 %collective-permute-done.5.refs_4_ = bf16[784,128]{1,0:T(8,128)(2,1)S(1)} collective-permute-done((bf16[784,128]{1,0:T(8,128)(2,1)}, bf16[784,128]{1,0:T(8,128)(2,1)S(1)}, u32[]{:S(2)}, u32[]{:S(2)}) %collective-permute-start.5) | collective-permute-done | bytes 200736 | tf_op jit(solution)/shard_map/ppermute | solution.py:341
  21.8 3.3 %collective-permute-done.7.refs_6_ = bf16[784,128]{1,0:T(8,128)(2,1)S(1)} collective-permute-done((bf16[784,128]{1,0:T(8,128)(2,1)}, bf16[784,128]{1,0:T(8,128)(2,1)S(1)}, u32[]{:S(2)}, u32[]{:S(2)}) %collective-permute-start.7) | collective-permute-done | bytes 200736 | tf_op jit(solution)/shard_map/ppermute | solution.py:341
  25.1 1.0 %collective-permute-start.2 = (bf16[2176,128]{1,0:T(8,128)(2,1)S(1)}, bf16[2176,128]{1,0:T(8,128)(2,1)S(1)}, u32[]{:S(2)}, u32[]{:S(2)}) collective-permute-start(bf16[2176,128]{1,0:T(8,128)(2,1)S(1)} %get-tuple-element.29), channel_id=1, source_target_pairs={{0,4},{4,0},{8,12},{12,8},{16,20},{20,16},{24,28},{28,24},{1,5},{5... | collective-permute-start | bytes 1671176 | tf_op jit(solution)/shard_map/ppermute | solution.py:341
  26.1 8.7 %collective-permute-done.8.refs_7_ = bf16[784,128]{1,0:T(8,128)(2,1)S(1)} collective-permute-done((bf16[784,128]{1,0:T(8,128)(2,1)S(1)}, bf16[784,128]{1,0:T(8,128)(2,1)S(1)}, u32[]{:S(2)}, u32[]{:S(2)}) %collective-permute-start.8) | collective-permute-done | bytes 200736 | tf_op jit(solution)/shard_map/ppermute | solution.py:341
  34.8 5.1 %attend.1 = (bf16[1040,128]{1,0:T(8,128)(2,1)S(1)}, bf16[1040,128]{1,0:T(8,128)(2,1)S(1)}) custom-call(s32[8]{0:T(128)S(1)} %copy-done.3, bf16[784,128]{1,0:T(8,128)(2,1)S(1)} %copy-done.2, bf16[784,128]{1,0:T(8,128)(2,1)S(1)} %collective-permute-done.refs_2_, bf16[784,128]{1,0:T(8,128)(2,1)S(1)} %collective-permute-done.1.refs_3_, ...), custom_call_target="tpu_custom_call" | custom-call | flops 1073741824 | bytes 1064960 | tf_op jit(solution)/shard_map/attend/pallas_call | solution.py:405
  39.9 0.7 collective-permute-start.11
  40.6 1.5 %collective-permute-start.12 = (bf16[1040,128]{1,0:T(8,128)(2,1)S(1)}, bf16[1040,128]{1,0:T(8,128)(2,1)S(1)}, u32[]{:S(2)}, u32[]{:S(2)}) collective-permute-start(bf16[1040,128]{1,0:T(8,128)(2,1)S(1)} %get-tuple-element.38.refs_2_.refs_1_.refs_7_), channel_id=1, source_target_pairs={{0,16},{4,12},{8,24},{12,4},{16,0},{20,28},{24,8},{28,20},{1,17},{... | collective-permute-start | bytes 798728 | tf_op jit(solution)/shard_map/ppermute | solution.py:341
  42.1 1.7 %collective-permute-start.10 = (bf16[2,512,128]{2,1,0:T(8,128)(2,1)S(1)}, bf16[2,512,128]{2,1,0:T(8,128)(2,1)S(1)}, u32[]{:S(2)}, u32[]{:S(2)}) collective-permute-start(bf16[2,512,128]{2,1,0:T(8,128)(2,1)S(1)} %stack.1), channel_id=1, source_target_pairs={{0,1},{1,0},{2,3},{3,2},{4,5},{5,4},{6,7},{7,6},{8,9},{9,8},{10,11... | collective-permute-start | bytes 786440 | tf_op jit(solution)/shard_map/ppermute | solution.py:344
  43.7 4.7 %collective-permute-done.11.refs_2_.refs_8_ = bf16[1040,128]{1,0:T(8,128)(2,1)S(1)} collective-permute-done((bf16[1040,128]{1,0:T(8,128)(2,1)S(1)}, bf16[1040,128]{1,0:T(8,128)(2,1)S(1)}, u32[]{:S(2)}, u32[]{:S(2)}) %collective-permute-start.11) | collective-permute-done | bytes 266272 | tf_op jit(solution)/shard_map/ppermute | solution.py:341
  48.5 1.0 %collective-permute-start.13 = (bf16[1040,128]{1,0:T(8,128)(2,1)S(1)}, bf16[1040,128]{1,0:T(8,128)(2,1)S(1)}, u32[]{:S(2)}, u32[]{:S(2)}) collective-permute-start(bf16[1040,128]{1,0:T(8,128)(2,1)S(1)} %collective-permute-done.11.refs_2_.refs_8_), channel_id=1, source_target_pairs={{0,16},{4,12},{8,24},{12,4},{16,0},{20,28},{24,8},{28,20},{1,17},{... | collective-permute-start | bytes 798728 | tf_op jit(solution)/shard_map/ppermute | solution.py:341
  49.9 1.2 %turn.1 = (bf16[512,1088]{1,0:T(8,128)(2,1)S(1)}, bf16[512,1088]{1,0:T(8,128)(2,1)S(1)}) custom-call(bf16[2176,128]{1,0:T(8,128)(2,1)S(1)} %get-tuple-element.28.refs_0_, bf16[2176,128]{1,0:T(8,128)(2,1)S(1)} %collective-permute-done.2.refs_1_, bf16[1664,128]{1,0:T(8,128)(2,1)S(1)} %collective-permute-done.3.refs_0_.refs_2_, ...), custom_call_target="tpu_custom_call" | custom-call | tf_op jit(solution)/shard_map/turn/pallas_call | solution.py:430
  51.1 0.8 %send_near.1 = (bf16[256,384]{1,0:T(8,128)(2,1)S(1)}, bf16[256,384]{1,0:T(8,128)(2,1)S(1)}) custom-call(bf16[512,1088]{1,0:T(8,128)(2,1)S(1)} %get-tuple-element.41.refs_0_, bf16[1040,128]{1,0:T(8,128)(2,1)S(1)} %get-tuple-element.38.refs_2_.refs_1_.refs_7_, bf16[1040,128]{1,0:T(8,128)(2,1)S(1)} %collective-permute-done.11.refs_2_.refs_8_, ...), custom_call_target="tpu_custom_call" | custom-call | tf_op jit(solution)/shard_map/send_near/pallas_call | solution.py:441
  51.9 0.7 %collective-permute-start.14 = (bf16[256,384]{1,0:T(8,128)(2,1)S(1)}, bf16[256,384]{1,0:T(8,128)(2,1)S(1)}, u32[]{:S(2)}, u32[]{:S(2)}) collective-permute-start(bf16[256,384]{1,0:T(8,128)(2,1)S(1)} %get-tuple-element.42.refs_4_), channel_id=1, source_target_pairs={{0,8},{4,20},{8,0},{12,28},{16,24},{20,4},{24,16},{28,12},{1,9},{5... | collective-permute-start | bytes 589832 | tf_op jit(solution)/shard_map/ppermute | solution.py:341
  52.7 0.8 %keep_near.1 = (f32[256,384]{1,0:T(8,128)S(1)}, bf16[512,384]{1,0:T(8,128)(2,1)S(1)}) custom-call(bf16[512,1088]{1,0:T(8,128)(2,1)S(1)} %get-tuple-element.39.refs_0_, bf16[1040,128]{1,0:T(8,128)(2,1)S(1)} %get-tuple-element.38.refs_2_.refs_1_.refs_7_, bf16[1040,128]{1,0:T(8,128)(2,1)S(1)} %collective-permute-done.11.refs_2_.refs_8_, ...), custom_call_target="tpu_custom_call" | custom-call | tf_op jit(solution)/shard_map/keep_near/pallas_call | solution.py:453
  53.5 3.0 %collective-permute-done.13.refs_2_.refs_1_.refs_10_ = bf16[1040,128]{1,0:T(8,128)(2,1)S(1)} collective-permute-done((bf16[1040,128]{1,0:T(8,128)(2,1)S(1)}, bf16[1040,128]{1,0:T(8,128)(2,1)S(1)}, u32[]{:S(2)}, u32[]{:S(2)}) %collective-permute-start.13) | collective-permute-done | bytes 266272 | tf_op jit(solution)/shard_map/ppermute | solution.py:341
  56.5 1.2 %collective-permute-done.14.refs_3_.refs_2_ = bf16[256,384]{1,0:T(8,128)(2,1)S(1)} collective-permute-done((bf16[256,384]{1,0:T(8,128)(2,1)S(1)}, bf16[256,384]{1,0:T(8,128)(2,1)S(1)}, u32[]{:S(2)}, u32[]{:S(2)}) %collective-permute-start.14) | collective-permute-done | bytes 196640 | tf_op jit(solution)/shard_map/ppermute | solution.py:341
  57.7 1.4 %collective-permute-done.15.refs_4_ = bf16[256,384]{1,0:T(8,128)(2,1)S(1)} collective-permute-done((bf16[256,384]{1,0:T(8,128)(2,1)S(1)}, bf16[256,384]{1,0:T(8,128)(2,1)S(1)}, u32[]{:S(2)}, u32[]{:S(2)}) %collective-permute-start.15) | collective-permute-done | bytes 196640 | tf_op jit(solution)/shard_map/ppermute | solution.py:341
  59.6 0.6 collective-permute-start.18
  60.6 0.8 %collective-permute-start.16 = (bf16[256,128]{1,0:T(8,128)(2,1)S(1)}, bf16[256,128]{1,0:T(8,128)(2,1)S(1)}, u32[]{:S(2)}, u32[]{:S(2)}) collective-permute-start(bf16[256,128]{1,0:T(8,128)(2,1)S(1)} %get-tuple-element.47), channel_id=1, source_target_pairs={{0,8},{4,20},{8,0},{12,28},{16,24},{20,4},{24,16},{28,12},{1,9},{5... | collective-permute-start | bytes 196616 | tf_op jit(solution)/shard_map/ppermute | solution.py:341
  61.3 0.6 collective-permute-start.17
  61.9 3.0 %collective-permute-done.16.refs_3_ = bf16[256,128]{1,0:T(8,128)(2,1)S(1)} collective-permute-done((bf16[256,128]{1,0:T(8,128)(2,1)S(1)}, bf16[256,128]{1,0:T(8,128)(2,1)S(1)}, u32[]{:S(2)}, u32[]{:S(2)}) %collective-permute-start.16) | collective-permute-done | bytes 65568 | tf_op jit(solution)/shard_map/ppermute | solution.py:341
  65.0 1.3 %finish.1 = (bf16[256,1024]{1,0:T(8,128)(2,1)}, f32[256,1024]{1,0:T(8,128)}) custom-call(f32[256,384]{1,0:T(8,128)S(1)} %get-tuple-element.43.refs_0_, f32[256,128]{1,0:T(8,128)S(1)} %get-tuple-element.46.refs_1_, bf16[256,384]{1,0:T(8,128)(2,1)S(1)} %collective-permute-done.14.refs_3_.refs_2_, bf16[256,128]{1,0:T(8,128)(2,1)S(1)} %collective-permute-done.16.refs_3_, ...), custom_call_target="tpu_custom_call" | custom-call | tf_op jit(solution)/shard_map/finish/pallas_call | solution.py:468
  (29 shorter events, 1.7 us)
Async XLA Ops:
  2.5 14.0 %copy-start = (bf16[272,2048]{1,0:T(8,128)(2,1)S(1)}, bf16[272,2048]{1,0:T(8,128)(2,1)}, u32[]{:S(2)}) copy-start(bf16[272,2048]{1,0:T(8,128)(2,1)} %refs_1_.4) | copy-start | bytes 3342340
  2.5 14.0 %copy-start.1 = (s32[1,8]{1,0:T(1,128)S(1)}, s32[1,8]{1,0:T(1,128)}, u32[]{:S(2)}) copy-start(s32[1,8]{1,0:T(1,128)} %refs_0_.5) | copy-start | bytes 100
  2.5 10.0 %collective-permute-start = (bf16[784,128]{1,0:T(8,128)(2,1)}, bf16[784,128]{1,0:T(8,128)(2,1)S(1)}, u32[]{:S(2)}, u32[]{:S(2)}) collective-permute-start(bf16[784,128]{1,0:T(8,128)(2,1)} %get-tuple-element.26), channel_id=1, source_target_pairs={{0,24},{4,28},{8,16},{12,20},{16,8},{20,12},{24,0},{28,4},{1,25},{... | collective-permute-start | bytes 602120 | tf_op jit(solution)/shard_map/ppermute | solution.py:341
  6.5 28.3 %copy-start.3 = (s32[8]{0:T(128)S(1)}, s32[8]{0:T(128)}, u32[]{:S(2)}) copy-start(s32[8]{0:T(128)} %refs_0_.7) | copy-start | bytes 100
  6.5 10.1 %collective-permute-start.1 = (bf16[784,128]{1,0:T(8,128)(2,1)}, bf16[784,128]{1,0:T(8,128)(2,1)S(1)}, u32[]{:S(2)}, u32[]{:S(2)}) collective-permute-start(bf16[784,128]{1,0:T(8,128)(2,1)} %get-tuple-element.27), channel_id=1, source_target_pairs={{0,28},{4,24},{8,20},{12,16},{16,12},{20,8},{24,4},{28,0},{1,29},{... | collective-permute-start | bytes 602120 | tf_op jit(solution)/shard_map/ppermute | solution.py:341
  9.1 12.6 %copy-start.5 = (bf16[784,128]{1,0:T(8,128)(2,1)S(1)}, bf16[784,128]{1,0:T(8,128)(2,1)}, u32[]{:S(2)}) copy-start(bf16[784,128]{1,0:T(8,128)(2,1)} %get-tuple-element.36) | copy-start | bytes 602116
  9.1 12.6 %copy-start.4 = (bf16[784,128]{1,0:T(8,128)(2,1)S(1)}, bf16[784,128]{1,0:T(8,128)(2,1)}, u32[]{:S(2)}) copy-start(bf16[784,128]{1,0:T(8,128)(2,1)} %get-tuple-element.37) | copy-start | bytes 602116
  9.1 25.7 %copy-start.2 = (bf16[784,128]{1,0:T(8,128)(2,1)S(1)}, bf16[784,128]{1,0:T(8,128)(2,1)}, u32[]{:S(2)}) copy-start(bf16[784,128]{1,0:T(8,128)(2,1)} %get-tuple-element.32.refs_1_) | copy-start | bytes 602116
  9.1 12.6 %collective-permute-start.5 = (bf16[784,128]{1,0:T(8,128)(2,1)}, bf16[784,128]{1,0:T(8,128)(2,1)S(1)}, u32[]{:S(2)}, u32[]{:S(2)}) collective-permute-start(bf16[784,128]{1,0:T(8,128)(2,1)} %get-tuple-element.33), channel_id=1, source_target_pairs={{0,8},{4,12},{8,0},{12,4},{16,24},{20,28},{24,16},{28,20},{1,9},{5... | collective-permute-start | bytes 602120 | tf_op jit(solution)/shard_map/ppermute | solution.py:341
  10.3 11.4 %collective-permute-start.6 = (bf16[784,128]{1,0:T(8,128)(2,1)}, bf16[784,128]{1,0:T(8,128)(2,1)S(1)}, u32[]{:S(2)}, u32[]{:S(2)}) collective-permute-start(bf16[784,128]{1,0:T(8,128)(2,1)} %get-tuple-element.34), channel_id=1, source_target_pairs={{0,16},{4,20},{8,24},{12,28},{16,0},{20,4},{24,8},{28,12},{1,17},{... | collective-permute-start | bytes 602120 | tf_op jit(solution)/shard_map/ppermute | solution.py:341
  11.8 13.3 %collective-permute-start.7 = (bf16[784,128]{1,0:T(8,128)(2,1)}, bf16[784,128]{1,0:T(8,128)(2,1)S(1)}, u32[]{:S(2)}, u32[]{:S(2)}) collective-permute-start(bf16[784,128]{1,0:T(8,128)(2,1)} %get-tuple-element.35), channel_id=1, source_target_pairs={{0,12},{4,8},{8,4},{12,0},{16,28},{20,24},{24,20},{28,16},{1,13},{... | collective-permute-start | bytes 602120 | tf_op jit(solution)/shard_map/ppermute | solution.py:341
  17.7 24.3 %collective-permute-start.3 = (bf16[1664,128]{1,0:T(8,128)(2,1)S(1)}, bf16[1664,128]{1,0:T(8,128)(2,1)S(1)}, u32[]{:S(2)}, u32[]{:S(2)}) collective-permute-start(bf16[1664,128]{1,0:T(8,128)(2,1)S(1)} %get-tuple-element.30), channel_id=1, source_target_pairs={{0,16},{4,12},{8,24},{12,4},{16,0},{20,28},{24,8},{28,20},{1,17},{... | collective-permute-start | bytes 1277960 | tf_op jit(solution)/shard_map/ppermute | solution.py:341
  18.3 23.7 %collective-permute-start.4 = (bf16[1664,128]{1,0:T(8,128)(2,1)S(1)}, bf16[1664,128]{1,0:T(8,128)(2,1)S(1)}, u32[]{:S(2)}, u32[]{:S(2)}) collective-permute-start(bf16[1664,128]{1,0:T(8,128)(2,1)S(1)} %get-tuple-element.31), channel_id=1, source_target_pairs={{0,12},{4,16},{8,4},{12,24},{16,28},{20,0},{24,20},{28,8},{1,13},{... | collective-permute-start | bytes 1277960 | tf_op jit(solution)/shard_map/ppermute | solution.py:341
  21.7 13.1 %collective-permute-start.8 = (bf16[784,128]{1,0:T(8,128)(2,1)S(1)}, bf16[784,128]{1,0:T(8,128)(2,1)S(1)}, u32[]{:S(2)}, u32[]{:S(2)}) collective-permute-start(bf16[784,128]{1,0:T(8,128)(2,1)S(1)} %copy-done.5), channel_id=1, source_target_pairs={{0,20},{4,16},{8,28},{12,24},{16,4},{20,0},{24,12},{28,8},{1,21},{... | collective-permute-start | bytes 602120 | tf_op jit(solution)/shard_map/ppermute | solution.py:341
  21.7 13.1 %collective-permute-start.9 = (bf16[784,128]{1,0:T(8,128)(2,1)S(1)}, bf16[784,128]{1,0:T(8,128)(2,1)S(1)}, u32[]{:S(2)}, u32[]{:S(2)}) collective-permute-start(bf16[784,128]{1,0:T(8,128)(2,1)S(1)} %copy-done.4), channel_id=1, source_target_pairs={{0,4},{4,0},{8,12},{12,8},{16,20},{20,16},{24,28},{28,24},{1,5},{5... | collective-permute-start | bytes 602120 | tf_op jit(solution)/shard_map/ppermute | solution.py:341
  25.1 24.4 %collective-permute-start.2 = (bf16[2176,128]{1,0:T(8,128)(2,1)S(1)}, bf16[2176,128]{1,0:T(8,128)(2,1)S(1)}, u32[]{:S(2)}, u32[]{:S(2)}) collective-permute-start(bf16[2176,128]{1,0:T(8,128)(2,1)S(1)} %get-tuple-element.29), channel_id=1, source_target_pairs={{0,4},{4,0},{8,12},{12,8},{16,20},{20,16},{24,28},{28,24},{1,5},{5... | collective-permute-start | bytes 1671176 | tf_op jit(solution)/shard_map/ppermute | solution.py:341
  39.9 8.6 %collective-permute-start.11 = (bf16[1040,128]{1,0:T(8,128)(2,1)S(1)}, bf16[1040,128]{1,0:T(8,128)(2,1)S(1)}, u32[]{:S(2)}, u32[]{:S(2)}) collective-permute-start(bf16[1040,128]{1,0:T(8,128)(2,1)S(1)} %get-tuple-element.40), channel_id=1, source_target_pairs={{0,8},{4,20},{8,0},{12,28},{16,24},{20,4},{24,16},{28,12},{1,9},{5... | collective-permute-start | bytes 798728 | tf_op jit(solution)/shard_map/ppermute | solution.py:341
  40.6 10.6 %collective-permute-start.12 = (bf16[1040,128]{1,0:T(8,128)(2,1)S(1)}, bf16[1040,128]{1,0:T(8,128)(2,1)S(1)}, u32[]{:S(2)}, u32[]{:S(2)}) collective-permute-start(bf16[1040,128]{1,0:T(8,128)(2,1)S(1)} %get-tuple-element.38.refs_2_.refs_1_.refs_7_), channel_id=1, source_target_pairs={{0,16},{4,12},{8,24},{12,4},{16,0},{20,28},{24,8},{28,20},{1,17},{... | collective-permute-start | bytes 798728 | tf_op jit(solution)/shard_map/ppermute | solution.py:341
  42.1 7.8 %collective-permute-start.10 = (bf16[2,512,128]{2,1,0:T(8,128)(2,1)S(1)}, bf16[2,512,128]{2,1,0:T(8,128)(2,1)S(1)}, u32[]{:S(2)}, u32[]{:S(2)}) collective-permute-start(bf16[2,512,128]{2,1,0:T(8,128)(2,1)S(1)} %stack.1), channel_id=1, source_target_pairs={{0,1},{1,0},{2,3},{3,2},{4,5},{5,4},{6,7},{7,6},{8,9},{9,8},{10,11... | collective-permute-start | bytes 786440 | tf_op jit(solution)/shard_map/ppermute | solution.py:344
  48.5 8.0 %collective-permute-start.13 = (bf16[1040,128]{1,0:T(8,128)(2,1)S(1)}, bf16[1040,128]{1,0:T(8,128)(2,1)S(1)}, u32[]{:S(2)}, u32[]{:S(2)}) collective-permute-start(bf16[1040,128]{1,0:T(8,128)(2,1)S(1)} %collective-permute-done.11.refs_2_.refs_8_), channel_id=1, source_target_pairs={{0,16},{4,12},{8,24},{12,4},{16,0},{20,28},{24,8},{28,20},{1,17},{... | collective-permute-start | bytes 798728 | tf_op jit(solution)/shard_map/ppermute | solution.py:341
  51.9 5.7 %collective-permute-start.14 = (bf16[256,384]{1,0:T(8,128)(2,1)S(1)}, bf16[256,384]{1,0:T(8,128)(2,1)S(1)}, u32[]{:S(2)}, u32[]{:S(2)}) collective-permute-start(bf16[256,384]{1,0:T(8,128)(2,1)S(1)} %get-tuple-element.42.refs_4_), channel_id=1, source_target_pairs={{0,8},{4,20},{8,0},{12,28},{16,24},{20,4},{24,16},{28,12},{1,9},{5... | collective-permute-start | bytes 589832 | tf_op jit(solution)/shard_map/ppermute | solution.py:341
  52.7 6.5 %collective-permute-start.15 = (bf16[256,384]{1,0:T(8,128)(2,1)S(1)}, bf16[256,384]{1,0:T(8,128)(2,1)S(1)}, u32[]{:S(2)}, u32[]{:S(2)}) collective-permute-start(bf16[256,384]{1,0:T(8,128)(2,1)S(1)} %get-tuple-element.45), channel_id=1, source_target_pairs={{0,12},{4,16},{8,4},{12,24},{16,28},{20,0},{24,20},{28,8},{1,13},{... | collective-permute-start | bytes 589832 | tf_op jit(solution)/shard_map/ppermute | solution.py:341
  59.6 5.5 %collective-permute-start.18 = (bf16[512,512]{1,0:T(8,128)(2,1)S(1)}, bf16[512,512]{1,0:T(8,128)(2,1)S(1)}, u32[]{:S(2)}, u32[]{:S(2)}) collective-permute-start(bf16[512,512]{1,0:T(8,128)(2,1)S(1)} %get-tuple-element.49), channel_id=1, source_target_pairs={{0,4},{4,0},{8,12},{12,8},{16,20},{20,16},{24,28},{28,24},{1,5},{5... | collective-permute-start | bytes 1572872 | tf_op jit(solution)/shard_map/ppermute | solution.py:341
  60.6 4.3 %collective-permute-start.16 = (bf16[256,128]{1,0:T(8,128)(2,1)S(1)}, bf16[256,128]{1,0:T(8,128)(2,1)S(1)}, u32[]{:S(2)}, u32[]{:S(2)}) collective-permute-start(bf16[256,128]{1,0:T(8,128)(2,1)S(1)} %get-tuple-element.47), channel_id=1, source_target_pairs={{0,8},{4,20},{8,0},{12,28},{16,24},{20,4},{24,16},{28,12},{1,9},{5... | collective-permute-start | bytes 196616 | tf_op jit(solution)/shard_map/ppermute | solution.py:341
  61.3 3.7 %collective-permute-start.17 = (bf16[256,128]{1,0:T(8,128)(2,1)S(1)}, bf16[256,128]{1,0:T(8,128)(2,1)S(1)}, u32[]{:S(2)}, u32[]{:S(2)}) collective-permute-start(bf16[256,128]{1,0:T(8,128)(2,1)S(1)} %get-tuple-element.48), channel_id=1, source_target_pairs={{0,12},{4,16},{8,4},{12,24},{16,28},{20,0},{24,20},{28,8},{1,13},{... | collective-permute-start | bytes 196616 | tf_op jit(solution)/shard_map/ppermute | solution.py:341

commit v8 on v4

--- a/solution.py
+++ b/solution.py
@@ -11,7 +11,7 @@
 TPF = 64
 WINB = 4
 VMEM_LIMIT = 24 * 1024 * 1024
-PACK_LIMIT = 63 * 1024 * 1024
+PACK_LIMIT = 58 * 1024 * 1024
 
 
 def from_behind(x, axis, by):
@@ -74,39 +74,40 @@
     return (attended, disc_grad)
 
 
-def cot_kernel(n, tile, lo, off_hbm, cot_hbm, behind_a, behind_b, *refs):
-    outs, (off, cot, sems) = refs[:-3], refs[-3:]
+def cot_kernel(n, tile, lo, off_hbm, cot_hbm, *refs):
+    outs, (off, cot, sems) = refs[-3 - n // 2 : -3], refs[-3:]
     own = lax.axis_index("tm")
     chip, side = own // 2, lax.rem(own, 2)
     plane = lax.rem(lax.axis_index("head"), 2)
     clip_rows = n * tile
-    part, all_cols = cot.shape
+    all_rows, all_cols = cot.shape
     cols = all_cols // n
+    part = all_rows - lo
     low = pl.multiple_of(plane * lo, 16)
     fetch_off = pltpu.make_async_copy(off_hbm, off, sems.at[0])
-    fetch_cot = pltpu.make_async_copy(cot_hbm.at[pl.ds(low, part), :], cot, sems.at[1])
+    fetch_cot = pltpu.make_async_copy(cot_hbm, cot, sems.at[1])
     fetch_off.start()
     fetch_cot.start()
     fetch_off.wait()
     r = lax.broadcasted_iota(jnp.int32, (clip_rows, clip_rows), 0)
     c = lax.broadcasted_iota(jnp.int32, (clip_rows, clip_rows), 1)
-    select = jnp.where((r == c) & (plane != 0), 1.0, 0.0)
+    select = jnp.zeros((clip_rows, clip_rows), jnp.float32)
     for j in range(n):
         src = lax.rem(own - off[0, j] + 2 * n, n)
         for t in range(tile):
-            hit = (c == j * tile + t) & (r == src * tile + t) & (plane == 0)
-            select = jnp.where(hit, 1.0, select)
+            select = jnp.where((c == j * tile + t) & (r == src * tile + t), 1.0, select)
     fetch_cot.wait()
     cot[0:clip_rows, :] = jnp.dot(
         select.astype(jnp.bfloat16), cot[0:clip_rows, :], preferred_element_type=jnp.float32
     ).astype(jnp.bfloat16)
     units = cols // HD
     for m, out_ref in enumerate(outs):
+        rows, first = (part, low) if m else (all_rows, 0)
         for i, block in enumerate((2 * (chip ^ m) + side, 2 * (chip ^ m) + 1 - side)):
             for u in range(units):
-                at = (i * units + u) * part
+                at = (i * units + u) * rows
                 lanes = pl.ds(pl.multiple_of(block * cols + u * HD, HD), HD)
-                out_ref[at : at + part, :] = cot[:, lanes]
+                out_ref[at : at + rows, :] = cot[pl.ds(first, rows), lanes]
 
 
 def pack_kernel(n, heads, q_hbm, k_hbm, v_hbm, hist_hbm, *refs):
@@ -196,45 +197,40 @@
     attend_blocks(n, tok, 1 - side, counts, x_ref, cross_ref)
 
 
-def stack_kernel(order, *refs):
+def stack_kernel(order, lo, tiles, *refs):
     out_ref = refs[-1]
-    for i, x in zip(order, refs):
-        out_ref[i] = x[...]
+    plane = lax.rem(lax.axis_index("head"), 2)
+    for m, ref in zip(order, refs):
+        part = ref.shape[0] // tiles
+        for u in range(tiles):
+            first = pl.multiple_of(u * part + plane * (part - lo), 16)
+            out_ref[m - 1, u * lo : (u + 1) * lo, :] = ref[pl.ds(first, lo), :]
 
 
 def late_kernel(x_ref, *refs):
     refs[-1][...] = x_ref[...]
 
 
-def whole_cot(lo, part, plane, mine, swapped):
-    pieces = []
-    for u in range(mine.shape[0] // part):
-        a = mine[u * part : (u + 1) * part, :]
-        b = swapped[u * part : (u + 1) * part, :]
-        low = jnp.where(plane == 0, a, b)
-        high = jnp.where(plane == 0, b, a)
-        pieces.append(jnp.concatenate([low[:lo], high], axis=0))
-    return jnp.concatenate(pieces, axis=1)
-
-
-def turn(wholes, clip_rows):
-    pieces = [x[clip_rows:] for x in wholes] + [x[:clip_rows] for x in wholes]
-    return jnp.concatenate(pieces, axis=0).T
-
-
-def turn_kernel(lo, clip_rows, cot_rows, mine_ref, swapped_ref, own_ref, other_ref):
+def turn_kernel(lo, clip_rows, order, own_in, *refs):
+    pieces, (swapped_ref, own_ref, other_ref, whole) = refs[:-4], refs[-4:]
     plane = lax.rem(lax.axis_index("head"), 2)
     chip = lax.axis_index("tm") // 2
-    chips, length, _ = mine_ref.shape
+    chips, all_rows, width = whole.shape
+    part = all_rows - lo
+    for u in range(width // HD):
+        lanes = slice(u * HD, (u + 1) * HD)
+        whole[0, :, lanes] = own_in[u * all_rows : (u + 1) * all_rows, :]
+        for m, ref in zip(order, pieces):
+            a = ref[u * part : (u + 1) * part, :]
+            b = swapped_ref[m - 1, u * lo : (u + 1) * lo, :]
+            whole[m, 0:lo, lanes] = jnp.where(plane == 0, a[:lo], b)
+            whole[m, lo:part, lanes] = jnp.where(plane == 0, a[lo:], a[: part - lo])
+            whole[m, part:all_rows, lanes] = jnp.where(plane == 0, b, a[part - lo :])
     for i, out_ref in enumerate((own_ref, other_ref)):
-        rows = slice(i * length // 2, (i + 1) * length // 2)
-        wholes = [
-            whole_cot(
-                lo, cot_rows - lo, plane, mine_ref[chip ^ c, rows], swapped_ref[chip ^ c, rows]
-            )
-            for c in range(chips)
-        ]
-        out_ref[...] = turn(wholes, clip_rows)
+        lanes = slice(i * width // 2, (i + 1) * width // 2)
+        rows = [whole[chip ^ c, clip_rows:all_rows, lanes] for c in range(chips)]
+        rows += [whole[chip ^ c, 0:clip_rows, lanes] for c in range(chips)]
+        out_ref[...] = jnp.concatenate(rows, axis=0).T
 
 
 def grad_part(turned_ref, head_refs, rows, copies):
@@ -292,7 +288,7 @@
     cot_rows, all_cols = cotangent.shape
     cols = all_cols // n
     units = cols // HD
-    lo = cot_rows // 32 * 16
+    lo = cot_rows * 7 // 17 // 16 * 16
     part = cot_rows - lo
     base = 3 * tok + clip_rows
     length = base
@@ -353,12 +349,12 @@
     cots = call(
         lambda *refs: cot_kernel(n, tile, lo, *refs),
         "cot",
-        [((2 * units * part, HD), bf16)] * half,
+        [((2 * units * cot_rows, HD), bf16)] + [((2 * units * part, HD), bf16)] * (half - 1),
         [hbm] * 4,
         0,
         (
             pltpu.SMEM(offsets.shape, jnp.int32),
-            pltpu.VMEM((part, all_cols), bf16),
+            pltpu.VMEM(cotangent.shape, bf16),
             pltpu.SemaphoreType.DMA((2,)),
         ),
     )(offsets, cotangent, arrived[6], arrived[7])
@@ -380,16 +376,15 @@
         counts,
         2 * pairs,
     )(frame_counts, *by_head)
-    stack_order = [3, 1, 2, 0]
-    (cot_mine,) = call(
-        lambda *refs: stack_kernel(stack_order, *refs),
+    stack_order = [3, 1, 2]
+    (cot_rest,) = call(
+        lambda *refs: stack_kernel(stack_order, lo, 2 * units, *refs),
         "stack",
-        [((half, 2 * units * part, HD), bf16)],
-        [vmem] * half + [hbm],
+        [((half - 1, 2 * units * lo, HD), bf16)],
+        [vmem] * (half - 1) + [hbm],
         0,
     )(*[cots[m] for m in stack_order], same)
-    cot_swapped = swap_plane(cot_mine, 0)
-
+    cot_swapped = swap_plane(cot_rest, 0)
     x_same, y_cross = swap(same, 2), swap(cross, 4 ^ 1)
     y_same, x_cross = swap(same, 4), swap(cross, 2 ^ 1)
     far_same, far_cross = swap(x_same, 4), swap(y_cross, 2)
@@ -397,12 +392,13 @@
     c_cross = swap(late_cross, 1)
 
     turned_own, turned_other = call(
-        lambda *refs: turn_kernel(lo, clip_rows, cot_rows, *refs),
+        lambda *refs: turn_kernel(lo, clip_rows, stack_order, *refs),
         "turn",
         [((cols, half * cot_rows), bf16)] * 2,
-        [vmem] * 2,
+        [vmem] * (half + 1),
         0,
-    )(cot_mine, cot_swapped)
+        (pltpu.VMEM((half, cot_rows, 2 * cols), bf16),),
+    )(cots[0], *[cots[m] for m in stack_order], cot_swapped)
 
     def grad(turned, heads, dtype, name):
         (out,) = call(

time: 58 us -> 55.9 us (0.964)
  waiting for transfers between devices: 23.8 us -> 21.4 us
  starting transfers between devices: 17.6 us -> 18.9 us
  local copies, waits for them, and re-layouts: 1.26 us -> 0.02 us
    ppermute x19, waiting for transfers between devices: 23.8 us -> 21.4 us  [swap(): return lax.ppermute(x, 'tm', [(i, i ^ bit) for i in range(n)])]
    ppermute x19, starting transfers between devices: 15.9 us -> 17.2 us  [swap(): return lax.ppermute(x, 'tm', [(i, i ^ bit) for i in range(n)])]
    unnamed x8, local copies, waits for them, and re-layouts: 1.26 us -> 0.02 us
  transfers between devices with their start and end apart: 20 -> 20, of which waited for: 11 -> 9; matrix products, arithmetic and copies ran while one was open for 0% -> 0% of each run, Pallas kernels for 19% -> 21%
where the time goes in v8:
time: 55.9 us; the launch traced here: 55.7 us
  waiting for transfers between devices  21.4 us (38%)
  starting transfers between devices  18.9 us (34%)
  Pallas kernels  14.6 us (26%)
  between operations  0.77 us (1%)
    ppermute x19, waiting for transfers between devices, swap(): return lax.ppermute(x, 'tm', [(i, i ^ bit) for i in range(n)])  21.4 us
    ppermute x19, starting transfers between devices, swap(): return lax.ppermute(x, 'tm', [(i, i ^ bit) for i in range(n)])  17.2 us
    pallas_call x1, Pallas kernels, head_body(): call(lambda *refs: attend_kernel(n, tok, [0] + order, *refs), 'attend', [...  5.12 us
    pallas_call x2, Pallas kernels, pack(): call(lambda *refs: pack_kernel(n, heads, *refs), name, [((length, HD), bf...  4.4 us
    pallas_call x4, Pallas kernels, grad(): call(lambda *refs: grad_kernel(rows, half, *refs), name, [((cols, len(hea...  2.25 us
    ppermute x1, starting transfers between devices, swap_plane(): return lax.ppermute(x, ('tm', 'head'), pairs)  1.65 us
    pallas_call x1, Pallas kernels, head_body(): call(lambda *refs: finish_kernel(heads, tok, *refs), 'finish', [((tok, wi...  1.29 us
  transfers between devices with their start and end apart: 20, of which 9 were waited for; matrix products, arithmetic and copies ran while one was open for 0% of the time, Pallas kernels for 21%

profile of v8, /device:TPU:0, one launch (start us, length us, event | category | flops | bytes accessed | tf_op | source)
XLA Modules:
  0.0 55.7 jit_solution(15499848506418088982)
XLA Ops:
  0.6 1.9 %pack_first.1 = (bf16[784,128]{1,0:T(8,128)(2,1)}, bf16[784,128]{1,0:T(8,128)(2,1)}) custom-call(bf16[256,1024]{1,0:T(8,128)(2,1)} %refs_0_.6, bf16[256,1024]{1,0:T(8,128)(2,1)} %refs_1_.5, bf16[256,1024]{1,0:T(8,128)(2,1)} %refs_2_.3, bf16[2,1024]{1,0:T(2,128)(2,1)} %refs_3_.3), custom_call_target="tpu_custom_call" | custom-call | bytes 802816 | tf_op jit(solution)/shard_map/pack_first/pallas_call | solution.py:326
  2.5 4.0 %collective-permute-start = (bf16[784,128]{1,0:T(8,128)(2,1)}, bf16[784,128]{1,0:T(8,128)(2,1)S(1)}, u32[]{:S(2)}, u32[]{:S(2)}) collective-permute-start(bf16[784,128]{1,0:T(8,128)(2,1)} %get-tuple-element.18), channel_id=1, source_target_pairs={{0,24},{4,28},{8,16},{12,20},{16,8},{20,12},{24,0},{28,4},{1,25},{... | collective-permute-start | bytes 602120 | tf_op jit(solution)/shard_map/ppermute | solution.py:301
  6.5 2.5 %pack_rest.1 = (bf16[784,128]{1,0:T(8,128)(2,1)}, bf16[784,128]{1,0:T(8,128)(2,1)}, bf16[784,128]{1,0:T(8,128)(2,1)}, bf16[784,128]{1,0:T(8,128)(2,1)}, bf16[784...) custom-call(bf16[256,1024]{1,0:T(8,128)(2,1)} %refs_0_.6, bf16[256,1024]{1,0:T(8,128)(2,1)} %refs_1_.5, ...), custom_call_target="tpu_custom_call" | custom-call | bytes 2408448 | tf_op jit(solution)/shard_map/pack_rest/pallas_call | solution.py:326
  9.1 1.2 %collective-permute-start.5 = (bf16[784,128]{1,0:T(8,128)(2,1)}, bf16[784,128]{1,0:T(8,128)(2,1)S(1)}, u32[]{:S(2)}, u32[]{:S(2)}) collective-permute-start(bf16[784,128]{1,0:T(8,128)(2,1)} %get-tuple-element.25), channel_id=1, source_target_pairs={{0,8},{4,12},{8,0},{12,4},{16,24},{20,28},{24,16},{28,20},{1,9},{5... | collective-permute-start | bytes 602120 | tf_op jit(solution)/shard_map/ppermute | solution.py:301
  10.2 1.5 %collective-permute-start.6 = (bf16[784,128]{1,0:T(8,128)(2,1)}, bf16[784,128]{1,0:T(8,128)(2,1)S(1)}, u32[]{:S(2)}, u32[]{:S(2)}) collective-permute-start(bf16[784,128]{1,0:T(8,128)(2,1)} %get-tuple-element.26), channel_id=1, source_target_pairs={{0,16},{4,20},{8,24},{12,28},{16,0},{20,4},{24,8},{28,12},{1,17},{... | collective-permute-start | bytes 602120 | tf_op jit(solution)/shard_map/ppermute | solution.py:301
  11.8 0.6 %collective-permute-start.7 = (bf16[784,128]{1,0:T(8,128)(2,1)}, bf16[784,128]{1,0:T(8,128)(2,1)S(1)}, u32[]{:S(2)}, u32[]{:S(2)}) collective-permute-start(bf16[784,128]{1,0:T(8,128)(2,1)} %get-tuple-element.27), channel_id=1, source_target_pairs={{0,12},{4,8},{8,4},{12,0},{16,28},{20,24},{24,20},{28,16},{1,13},{... | collective-permute-start | bytes 602120 | tf_op jit(solution)/shard_map/ppermute | solution.py:301
  12.5 0.4 collective-permute-start.8
  12.9 3.6 %collective-permute-done.1.refs_3_ = bf16[784,128]{1,0:T(8,128)(2,1)S(1)} collective-permute-done((bf16[784,128]{1,0:T(8,128)(2,1)}, bf16[784,128]{1,0:T(8,128)(2,1)S(1)}, u32[]{:S(2)}, u32[]{:S(2)}) %collective-permute-start.1) | collective-permute-done | bytes 200736 | tf_op jit(solution)/shard_map/ppermute | solution.py:301
  16.6 0.9 %cot.1 = (bf16[1088,128]{1,0:T(8,128)(2,1)S(1)}, bf16[640,128]{1,0:T(8,128)(2,1)S(1)}, bf16[640,128]{1,0:T(8,128)(2,1)S(1)}, bf16[640,128]{1,0:T(8,128)(2,1)S(1)}) custom-call(s32[1,8]{1,0:T(1,128)S(1)} %copy-done.1, bf16[272,2048]{1,0:T(8,128)(2,1)S(1)} %copy-done, bf16[784,128]{1,0:T(8,128)(2,1)S(1)} %collective-permute-done.refs_2_, ...), custom_call_target="tpu_custom_call" | custom-call | bytes 1540096 | tf_op jit(solution)/shard_map/cot/pallas_call | solution.py:349
  17.6 4.1 %collective-permute-done.5.refs_4_ = bf16[784,128]{1,0:T(8,128)(2,1)S(1)} collective-permute-done((bf16[784,128]{1,0:T(8,128)(2,1)}, bf16[784,128]{1,0:T(8,128)(2,1)S(1)}, u32[]{:S(2)}, u32[]{:S(2)}) %collective-permute-start.5) | collective-permute-done | bytes 200736 | tf_op jit(solution)/shard_map/ppermute | solution.py:301
  21.7 1.5 %collective-permute-start.2 = (bf16[640,128]{1,0:T(8,128)(2,1)S(1)}, bf16[640,128]{1,0:T(8,128)(2,1)S(1)}, u32[]{:S(2)}, u32[]{:S(2)}) collective-permute-start(bf16[640,128]{1,0:T(8,128)(2,1)S(1)} %get-tuple-element.21), channel_id=1, source_target_pairs={{0,24},{4,28},{8,16},{12,20},{16,8},{20,12},{24,0},{28,4},{1,25},{... | collective-permute-start | bytes 491528 | tf_op jit(solution)/shard_map/ppermute | solution.py:301
  23.2 1.9 %collective-permute-done.7.refs_6_ = bf16[784,128]{1,0:T(8,128)(2,1)S(1)} collective-permute-done((bf16[784,128]{1,0:T(8,128)(2,1)}, bf16[784,128]{1,0:T(8,128)(2,1)S(1)}, u32[]{:S(2)}, u32[]{:S(2)}) %collective-permute-start.7) | collective-permute-done | bytes 200736 | tf_op jit(solution)/shard_map/ppermute | solution.py:301
  25.1 0.5 collective-permute-start.4
  25.7 5.1 %attend.1 = (bf16[1040,128]{1,0:T(8,128)(2,1)S(1)}, bf16[1040,128]{1,0:T(8,128)(2,1)S(1)}) custom-call(s32[8]{0:T(128)S(1)} %copy-done.3, bf16[784,128]{1,0:T(8,128)(2,1)S(1)} %copy-done.2, bf16[784,128]{1,0:T(8,128)(2,1)S(1)} %collective-permute-done.refs_2_, bf16[784,128]{1,0:T(8,128)(2,1)S(1)} %collective-permute-done.1.refs_3_, ...), custom_call_target="tpu_custom_call" | custom-call | flops 1073741824 | bytes 1064960 | tf_op jit(solution)/shard_map/attend/pallas_call | solution.py:370
  30.8 1.6 %collective-permute-start.14 = (bf16[1040,128]{1,0:T(8,128)(2,1)S(1)}, bf16[1040,128]{1,0:T(8,128)(2,1)S(1)}, u32[]{:S(2)}, u32[]{:S(2)}) collective-permute-start(bf16[1040,128]{1,0:T(8,128)(2,1)S(1)} %get-tuple-element.32.x_ref), channel_id=1, source_target_pairs={{0,20},{4,16},{8,28},{12,24},{16,4},{20,0},{24,12},{28,8},{1,21},{... | collective-permute-start | bytes 798728 | tf_op jit(solution)/shard_map/ppermute | solution.py:301
  32.4 1.5 %collective-permute-start.13 = (bf16[1040,128]{1,0:T(8,128)(2,1)S(1)}, bf16[1040,128]{1,0:T(8,128)(2,1)S(1)}, u32[]{:S(2)}, u32[]{:S(2)}) collective-permute-start(bf16[1040,128]{1,0:T(8,128)(2,1)S(1)} %get-tuple-element.30.refs_3_.refs_1_.refs_4_), channel_id=1, source_target_pairs={{0,8},{4,12},{8,0},{12,4},{16,24},{20,28},{24,16},{28,20},{1,9},{5... | collective-permute-start | bytes 798728 | tf_op jit(solution)/shard_map/ppermute | solution.py:301
  34.1 0.7 %collective-permute-start.12 = (bf16[1040,128]{1,0:T(8,128)(2,1)S(1)}, bf16[1040,128]{1,0:T(8,128)(2,1)S(1)}, u32[]{:S(2)}, u32[]{:S(2)}) collective-permute-start(bf16[1040,128]{1,0:T(8,128)(2,1)S(1)} %get-tuple-element.30.refs_3_.refs_1_.refs_4_), channel_id=1, source_target_pairs={{0,16},{4,20},{8,24},{12,28},{16,0},{20,4},{24,8},{28,12},{1,17},{... | collective-permute-start | bytes 798728 | tf_op jit(solution)/shard_map/ppermute | solution.py:301
  34.8 1.7 %collective-permute-start.10 = (bf16[3,448,128]{2,1,0:T(8,128)(2,1)S(1)}, bf16[3,448,128]{2,1,0:T(8,128)(2,1)S(1)}, u32[]{:S(2)}, u32[]{:S(2)}) collective-permute-start(bf16[3,448,128]{2,1,0:T(8,128)(2,1)S(1)} %stack.1), channel_id=1, source_target_pairs={{0,1},{1,0},{2,3},{3,2},{4,5},{5,4},{6,7},{7,6},{8,9},{9,8},{10,11... | collective-permute-start | bytes 1032200 | tf_op jit(solution)/shard_map/ppermute | solution.py:307
  36.5 2.8 %collective-permute-done.14.refs_5_.refs_8_ = bf16[1040,128]{1,0:T(8,128)(2,1)S(1)} collective-permute-done((bf16[1040,128]{1,0:T(8,128)(2,1)S(1)}, bf16[1040,128]{1,0:T(8,128)(2,1)S(1)}, u32[]{:S(2)}, u32[]{:S(2)}) %collective-permute-start.14) | collective-permute-done | bytes 266272 | tf_op jit(solution)/shard_map/ppermute | solution.py:301
  39.2 1.4 %collective-permute-start.17 = (bf16[1040,128]{1,0:T(8,128)(2,1)S(1)}, bf16[1040,128]{1,0:T(8,128)(2,1)S(1)}, u32[]{:S(2)}, u32[]{:S(2)}) collective-permute-start(bf16[1040,128]{1,0:T(8,128)(2,1)S(1)} %collective-permute-done.14.refs_5_.refs_8_), channel_id=1, source_target_pairs={{0,8},{4,12},{8,0},{12,4},{16,24},{20,28},{24,16},{28,20},{1,9},{5... | collective-permute-start | bytes 798728 | tf_op jit(solution)/shard_map/ppermute | solution.py:301
  40.6 1.0 %collective-permute-done.13.refs_4_.refs_7_ = bf16[1040,128]{1,0:T(8,128)(2,1)S(1)} collective-permute-done((bf16[1040,128]{1,0:T(8,128)(2,1)S(1)}, bf16[1040,128]{1,0:T(8,128)(2,1)S(1)}, u32[]{:S(2)}, u32[]{:S(2)}) %collective-permute-start.13) | collective-permute-done | bytes 266272 | tf_op jit(solution)/shard_map/ppermute | solution.py:301
  41.6 0.8 %collective-permute-start.16 = (bf16[1040,128]{1,0:T(8,128)(2,1)S(1)}, bf16[1040,128]{1,0:T(8,128)(2,1)S(1)}, u32[]{:S(2)}, u32[]{:S(2)}) collective-permute-start(bf16[1040,128]{1,0:T(8,128)(2,1)S(1)} %collective-permute-done.13.refs_4_.refs_7_), channel_id=1, source_target_pairs={{0,16},{4,20},{8,24},{12,28},{16,0},{20,4},{24,8},{28,12},{1,17},{... | collective-permute-start | bytes 798728 | tf_op jit(solution)/shard_map/ppermute | solution.py:301
  42.4 4.0 %collective-permute-done.11.refs_2_.refs_0_.refs_5_ = bf16[1040,128]{1,0:T(8,128)(2,1)S(1)} collective-permute-done((bf16[1040,128]{1,0:T(8,128)(2,1)S(1)}, bf16[1040,128]{1,0:T(8,128)(2,1)S(1)}, u32[]{:S(2)}, u32[]{:S(2)}) %collective-permute-start.11) | collective-permute-done | bytes 266272 | tf_op jit(solution)/shard_map/ppermute | solution.py:301
  46.4 1.1 %collective-permute-start.15 = (bf16[1040,128]{1,0:T(8,128)(2,1)S(1)}, bf16[1040,128]{1,0:T(8,128)(2,1)S(1)}, u32[]{:S(2)}, u32[]{:S(2)}) collective-permute-start(bf16[1040,128]{1,0:T(8,128)(2,1)S(1)} %late.1), channel_id=1, source_target_pairs={{0,4},{4,0},{8,12},{12,8},{16,20},{20,16},{24,28},{28,24},{1,5},{5... | collective-permute-start | bytes 798728 | tf_op jit(solution)/shard_map/ppermute | solution.py:301
  47.5 0.6 %turn.1 = (bf16[256,1088]{1,0:T(8,128)(2,1)S(1)}, bf16[256,1088]{1,0:T(8,128)(2,1)S(1)}) custom-call(bf16[1088,128]{1,0:T(8,128)(2,1)S(1)} %get-tuple-element.20.refs_0_, bf16[640,128]{1,0:T(8,128)(2,1)S(1)} %collective-permute-done.2.refs_0_.refs_1_, bf16[640,128]{1,0:T(8,128)(2,1)S(1)} %collective-permute-done.3.refs_1_.refs_2_, ...), custom_call_target="tpu_custom_call" | custom-call | bytes 2228224 | tf_op jit(solution)/shard_map/turn/pallas_call | solution.py:394
  48.1 0.6 %grad_other_near.1 = bf16[256,640]{1,0:T(8,128)(2,1)S(1)} custom-call(bf16[256,1088]{1,0:T(8,128)(2,1)S(1)} %get-tuple-element.33.refs_0_, bf16[1040,128]{1,0:T(8,128)(2,1)S(1)} %get-tuple-element.30.refs_3_.refs_1_.refs_4_, bf16[1040,128]{1,0:T(8,128)(2,1)S(1)} %collective-permute-done.11.refs_2_.refs_0_.refs_5_, ...), custom_call_target="tpu_custom_call" | custom-call | flops 356515840 | bytes 655360 | tf_op jit(solution)/shard_map/grad_other_near/pallas_call | solution.py:404
  48.8 3.6 %collective-permute-done.17.refs_3_.refs_11_ = bf16[1040,128]{1,0:T(8,128)(2,1)S(1)} collective-permute-done((bf16[1040,128]{1,0:T(8,128)(2,1)S(1)}, bf16[1040,128]{1,0:T(8,128)(2,1)S(1)}, u32[]{:S(2)}, u32[]{:S(2)}) %collective-permute-start.17) | collective-permute-done | bytes 266272 | tf_op jit(solution)/shard_map/ppermute | solution.py:301
  52.4 0.5 grad_other_far.1
  53.0 0.6 %grad_own_near.1.refs_0_ = f32[256,640]{1,0:T(8,128)S(1)} custom-call(bf16[256,1088]{1,0:T(8,128)(2,1)S(1)} %get-tuple-element.31.refs_0_, bf16[1040,128]{1,0:T(8,128)(2,1)S(1)} %get-tuple-element.30.refs_3_.refs_1_.refs_4_, bf16[1040,128]{1,0:T(8,128)(2,1)S(1)} %collective-permute-done.11.refs_2_.refs_0_.refs_5_, ...), custom_call_target="tpu_custom_call" | custom-call | flops 356515840 | bytes 1310720 | tf_op jit(solution)/shard_map/grad_own_near/pallas_call | solution.py:404
  53.6 0.5 grad_own_far.1.refs_1_
  54.1 0.3 collective-permute-done.19.refs_3_
  54.4 1.3 %finish.1 = (bf16[256,1024]{1,0:T(8,128)(2,1)}, f32[256,1024]{1,0:T(8,128)}) custom-call(f32[256,640]{1,0:T(8,128)S(1)} %grad_own_near.1.refs_0_, f32[256,384]{1,0:T(8,128)S(1)} %grad_own_far.1.refs_1_, bf16[256,640]{1,0:T(8,128)(2,1)S(1)} %collective-permute-done.18.refs_2_, bf16[256,384]{1,0:T(8,128)(2,1)S(1)} %collective-permute-done.19.refs_3_, ...), custom_call_target="tpu_custom_call" | custom-call | bytes 3145728 | tf_op jit(solution)/shard_map/finish/pallas_call | solution.py:420
  (28 shorter events, 0.8 us)
Async XLA Ops:
  2.5 14.1 %copy-start = (bf16[272,2048]{1,0:T(8,128)(2,1)S(1)}, bf16[272,2048]{1,0:T(8,128)(2,1)}, u32[]{:S(2)}) copy-start(bf16[272,2048]{1,0:T(8,128)(2,1)} %refs_1_.4) | copy-start | bytes 3342340
  2.5 14.1 %copy-start.1 = (s32[1,8]{1,0:T(1,128)S(1)}, s32[1,8]{1,0:T(1,128)}, u32[]{:S(2)}) copy-start(s32[1,8]{1,0:T(1,128)} %refs_0_.5) | copy-start | bytes 100
  2.5 10.0 %collective-permute-start = (bf16[784,128]{1,0:T(8,128)(2,1)}, bf16[784,128]{1,0:T(8,128)(2,1)S(1)}, u32[]{:S(2)}, u32[]{:S(2)}) collective-permute-start(bf16[784,128]{1,0:T(8,128)(2,1)} %get-tuple-element.18), channel_id=1, source_target_pairs={{0,24},{4,28},{8,16},{12,20},{16,8},{20,12},{24,0},{28,4},{1,25},{... | collective-permute-start | bytes 602120 | tf_op jit(solution)/shard_map/ppermute | solution.py:301
  6.5 10.1 %collective-permute-start.1 = (bf16[784,128]{1,0:T(8,128)(2,1)}, bf16[784,128]{1,0:T(8,128)(2,1)S(1)}, u32[]{:S(2)}, u32[]{:S(2)}) collective-permute-start(bf16[784,128]{1,0:T(8,128)(2,1)} %get-tuple-element.19), channel_id=1, source_target_pairs={{0,28},{4,24},{8,20},{12,16},{16,12},{20,8},{24,4},{28,0},{1,29},{... | collective-permute-start | bytes 602120 | tf_op jit(solution)/shard_map/ppermute | solution.py:301
  9.0 16.6 %copy-start.2 = (bf16[784,128]{1,0:T(8,128)(2,1)S(1)}, bf16[784,128]{1,0:T(8,128)(2,1)}, u32[]{:S(2)}) copy-start(bf16[784,128]{1,0:T(8,128)(2,1)} %get-tuple-element.24.refs_1_) | copy-start | bytes 602116
  9.0 16.6 %copy-start.3 = (s32[8]{0:T(128)S(1)}, s32[8]{0:T(128)}, u32[]{:S(2)}) copy-start(s32[8]{0:T(128)} %refs_0_.7) | copy-start | bytes 100
  9.1 12.6 %collective-permute-start.5 = (bf16[784,128]{1,0:T(8,128)(2,1)}, bf16[784,128]{1,0:T(8,128)(2,1)S(1)}, u32[]{:S(2)}, u32[]{:S(2)}) collective-permute-start(bf16[784,128]{1,0:T(8,128)(2,1)} %get-tuple-element.25), channel_id=1, source_target_pairs={{0,8},{4,12},{8,0},{12,4},{16,24},{20,28},{24,16},{28,20},{1,9},{5... | collective-permute-start | bytes 602120 | tf_op jit(solution)/shard_map/ppermute | solution.py:301
  10.2 12.9 %collective-permute-start.6 = (bf16[784,128]{1,0:T(8,128)(2,1)}, bf16[784,128]{1,0:T(8,128)(2,1)S(1)}, u32[]{:S(2)}, u32[]{:S(2)}) collective-permute-start(bf16[784,128]{1,0:T(8,128)(2,1)} %get-tuple-element.26), channel_id=1, source_target_pairs={{0,16},{4,20},{8,24},{12,28},{16,0},{20,4},{24,8},{28,12},{1,17},{... | collective-permute-start | bytes 602120 | tf_op jit(solution)/shard_map/ppermute | solution.py:301
  11.8 13.4 %collective-permute-start.7 = (bf16[784,128]{1,0:T(8,128)(2,1)}, bf16[784,128]{1,0:T(8,128)(2,1)S(1)}, u32[]{:S(2)}, u32[]{:S(2)}) collective-permute-start(bf16[784,128]{1,0:T(8,128)(2,1)} %get-tuple-element.27), channel_id=1, source_target_pairs={{0,12},{4,8},{8,4},{12,0},{16,28},{20,24},{24,20},{28,16},{1,13},{... | collective-permute-start | bytes 602120 | tf_op jit(solution)/shard_map/ppermute | solution.py:301
  12.5 13.1 %collective-permute-start.8 = (bf16[784,128]{1,0:T(8,128)(2,1)}, bf16[784,128]{1,0:T(8,128)(2,1)S(1)}, u32[]{:S(2)}, u32[]{:S(2)}) collective-permute-start(bf16[784,128]{1,0:T(8,128)(2,1)} %get-tuple-element.28), channel_id=1, source_target_pairs={{0,20},{4,16},{8,28},{12,24},{16,4},{20,0},{24,12},{28,8},{1,21},{... | collective-permute-start | bytes 602120 | tf_op jit(solution)/shard_map/ppermute | solution.py:301
  16.5 9.1 %collective-permute-start.9 = (bf16[784,128]{1,0:T(8,128)(2,1)}, bf16[784,128]{1,0:T(8,128)(2,1)S(1)}, u32[]{:S(2)}, u32[]{:S(2)}) collective-permute-start(bf16[784,128]{1,0:T(8,128)(2,1)} %get-tuple-element.29), channel_id=1, source_target_pairs={{0,4},{4,0},{8,12},{12,8},{16,20},{20,16},{24,28},{28,24},{1,5},{5... | collective-permute-start | bytes 602120 | tf_op jit(solution)/shard_map/ppermute | solution.py:301
  21.7 12.2 %collective-permute-start.2 = (bf16[640,128]{1,0:T(8,128)(2,1)S(1)}, bf16[640,128]{1,0:T(8,128)(2,1)S(1)}, u32[]{:S(2)}, u32[]{:S(2)}) collective-permute-start(bf16[640,128]{1,0:T(8,128)(2,1)S(1)} %get-tuple-element.21), channel_id=1, source_target_pairs={{0,24},{4,28},{8,16},{12,20},{16,8},{20,12},{24,0},{28,4},{1,25},{... | collective-permute-start | bytes 491528 | tf_op jit(solution)/shard_map/ppermute | solution.py:301
  23.2 10.9 %collective-permute-start.3 = (bf16[640,128]{1,0:T(8,128)(2,1)S(1)}, bf16[640,128]{1,0:T(8,128)(2,1)S(1)}, u32[]{:S(2)}, u32[]{:S(2)}) collective-permute-start(bf16[640,128]{1,0:T(8,128)(2,1)S(1)} %get-tuple-element.22), channel_id=1, source_target_pairs={{0,8},{4,12},{8,0},{12,4},{16,24},{20,28},{24,16},{28,20},{1,9},{5... | collective-permute-start | bytes 491528 | tf_op jit(solution)/shard_map/ppermute | solution.py:301
  25.1 9.6 %collective-permute-start.4 = (bf16[640,128]{1,0:T(8,128)(2,1)S(1)}, bf16[640,128]{1,0:T(8,128)(2,1)S(1)}, u32[]{:S(2)}, u32[]{:S(2)}) collective-permute-start(bf16[640,128]{1,0:T(8,128)(2,1)S(1)} %get-tuple-element.23), channel_id=1, source_target_pairs={{0,16},{4,20},{8,24},{12,28},{16,0},{20,4},{24,8},{28,12},{1,17},{... | collective-permute-start | bytes 491528 | tf_op jit(solution)/shard_map/ppermute | solution.py:301
  30.8 8.4 %collective-permute-start.14 = (bf16[1040,128]{1,0:T(8,128)(2,1)S(1)}, bf16[1040,128]{1,0:T(8,128)(2,1)S(1)}, u32[]{:S(2)}, u32[]{:S(2)}) collective-permute-start(bf16[1040,128]{1,0:T(8,128)(2,1)S(1)} %get-tuple-element.32.x_ref), channel_id=1, source_target_pairs={{0,20},{4,16},{8,28},{12,24},{16,4},{20,0},{24,12},{28,8},{1,21},{... | collective-permute-start | bytes 798728 | tf_op jit(solution)/shard_map/ppermute | solution.py:301
  32.4 9.2 %collective-permute-start.13 = (bf16[1040,128]{1,0:T(8,128)(2,1)S(1)}, bf16[1040,128]{1,0:T(8,128)(2,1)S(1)}, u32[]{:S(2)}, u32[]{:S(2)}) collective-permute-start(bf16[1040,128]{1,0:T(8,128)(2,1)S(1)} %get-tuple-element.30.refs_3_.refs_1_.refs_4_), channel_id=1, source_target_pairs={{0,8},{4,12},{8,0},{12,4},{16,24},{20,28},{24,16},{28,20},{1,9},{5... | collective-permute-start | bytes 798728 | tf_op jit(solution)/shard_map/ppermute | solution.py:301
  33.9 12.4 %collective-permute-start.11 = (bf16[1040,128]{1,0:T(8,128)(2,1)S(1)}, bf16[1040,128]{1,0:T(8,128)(2,1)S(1)}, u32[]{:S(2)}, u32[]{:S(2)}) collective-permute-start(bf16[1040,128]{1,0:T(8,128)(2,1)S(1)} %get-tuple-element.32.x_ref), channel_id=1, source_target_pairs={{0,12},{4,8},{8,4},{12,0},{16,28},{20,24},{24,20},{28,16},{1,13},{... | collective-permute-start | bytes 798728 | tf_op jit(solution)/shard_map/ppermute | solution.py:301
  34.1 12.3 %collective-permute-start.12 = (bf16[1040,128]{1,0:T(8,128)(2,1)S(1)}, bf16[1040,128]{1,0:T(8,128)(2,1)S(1)}, u32[]{:S(2)}, u32[]{:S(2)}) collective-permute-start(bf16[1040,128]{1,0:T(8,128)(2,1)S(1)} %get-tuple-element.30.refs_3_.refs_1_.refs_4_), channel_id=1, source_target_pairs={{0,16},{4,20},{8,24},{12,28},{16,0},{20,4},{24,8},{28,12},{1,17},{... | collective-permute-start | bytes 798728 | tf_op jit(solution)/shard_map/ppermute | solution.py:301
  34.8 12.7 %collective-permute-start.10 = (bf16[3,448,128]{2,1,0:T(8,128)(2,1)S(1)}, bf16[3,448,128]{2,1,0:T(8,128)(2,1)S(1)}, u32[]{:S(2)}, u32[]{:S(2)}) collective-permute-start(bf16[3,448,128]{2,1,0:T(8,128)(2,1)S(1)} %stack.1), channel_id=1, source_target_pairs={{0,1},{1,0},{2,3},{3,2},{4,5},{5,4},{6,7},{7,6},{8,9},{9,8},{10,11... | collective-permute-start | bytes 1032200 | tf_op jit(solution)/shard_map/ppermute | solution.py:307
  39.2 13.2 %collective-permute-start.17 = (bf16[1040,128]{1,0:T(8,128)(2,1)S(1)}, bf16[1040,128]{1,0:T(8,128)(2,1)S(1)}, u32[]{:S(2)}, u32[]{:S(2)}) collective-permute-start(bf16[1040,128]{1,0:T(8,128)(2,1)S(1)} %collective-permute-done.14.refs_5_.refs_8_), channel_id=1, source_target_pairs={{0,8},{4,12},{8,0},{12,4},{16,24},{20,28},{24,16},{28,20},{1,9},{5... | collective-permute-start | bytes 798728 | tf_op jit(solution)/shard_map/ppermute | solution.py:301
  41.6 10.8 %collective-permute-start.16 = (bf16[1040,128]{1,0:T(8,128)(2,1)S(1)}, bf16[1040,128]{1,0:T(8,128)(2,1)S(1)}, u32[]{:S(2)}, u32[]{:S(2)}) collective-permute-start(bf16[1040,128]{1,0:T(8,128)(2,1)S(1)} %collective-permute-done.13.refs_4_.refs_7_), channel_id=1, source_target_pairs={{0,16},{4,20},{8,24},{12,28},{16,0},{20,4},{24,8},{28,12},{1,17},{... | collective-permute-start | bytes 798728 | tf_op jit(solution)/shard_map/ppermute | solution.py:301
  46.4 6.1 %collective-permute-start.15 = (bf16[1040,128]{1,0:T(8,128)(2,1)S(1)}, bf16[1040,128]{1,0:T(8,128)(2,1)S(1)}, u32[]{:S(2)}, u32[]{:S(2)}) collective-permute-start(bf16[1040,128]{1,0:T(8,128)(2,1)S(1)} %late.1), channel_id=1, source_target_pairs={{0,4},{4,0},{8,12},{12,8},{16,20},{20,16},{24,28},{28,24},{1,5},{5... | collective-permute-start | bytes 798728 | tf_op jit(solution)/shard_map/ppermute | solution.py:301
  48.7 5.7 %collective-permute-start.18 = (bf16[256,640]{1,0:T(8,128)(2,1)S(1)}, bf16[256,640]{1,0:T(8,128)(2,1)S(1)}, u32[]{:S(2)}, u32[]{:S(2)}) collective-permute-start(bf16[256,640]{1,0:T(8,128)(2,1)S(1)} %grad_other_near.1), channel_id=1, source_target_pairs={{0,4},{4,0},{8,12},{12,8},{16,20},{20,16},{24,28},{28,24},{1,5},{5... | collective-permute-start | bytes 983048 | tf_op jit(solution)/shard_map/ppermute | solution.py:301
  52.9 1.5 %collective-permute-start.19 = (bf16[256,384]{1,0:T(8,128)(2,1)S(1)}, bf16[256,384]{1,0:T(8,128)(2,1)S(1)}, u32[]{:S(2)}, u32[]{:S(2)}) collective-permute-start(bf16[256,384]{1,0:T(8,128)(2,1)S(1)} %grad_other_far.1), channel_id=1, source_target_pairs={{0,4},{4,0},{8,12},{12,8},{16,20},{20,16},{24,28},{28,24},{1,5},{5... | collective-permute-start | bytes 589832 | tf_op jit(solution)/shard_map/ppermute | solution.py:301

commit v9 on v8

--- a/solution.py
+++ b/solution.py
@@ -139,53 +139,8 @@
             out_ref[i * tok : (i + 1) * tok, :] = x[:, lanes]
 
 
-def attend_blocks(n, tok, parity, counts, x_ref, out_ref):
-    rate = math.log2(math.e) / math.sqrt(HD)
-    token = lax.broadcasted_iota(jnp.int32, (1, tok), 1)
-    for i in range(n // 2):
-        block = 2 * i + parity
-        keys = min(WINB, 2 * i + 2)
-        sources = [block - (keys - 1) + k for k in range(keys)]
-        q = x_ref[block, 0:tok, :]
-        scores = []
-        for s in sources:
-            at = jnp.maximum(s, 0)
-            kept = jnp.where(s >= 0, counts[at], 0) * TPF
-            scores.append(
-                lax.dot_general(
-                    q,
-                    x_ref[at, tok : 2 * tok, :],
-                    (((1,), (1,)), ((), ())),
-                    preferred_element_type=jnp.float32,
-                )
-                + jnp.where(token < kept, 0.0, -jnp.inf).astype(jnp.float32)
-            )
-        top = jnp.max(scores[0], axis=1, keepdims=True)
-        for s in scores[1:]:
-            top = jnp.maximum(top, jnp.max(s, axis=1, keepdims=True))
-        weights = [jnp.exp2((s - top) * rate) for s in scores]
-        total = jnp.sum(weights[0], axis=1, keepdims=True)
-        for w in weights[1:]:
-            total = total + jnp.sum(w, axis=1, keepdims=True)
-        share = 1.0 / total
-        mixed = jnp.zeros((tok, HD), jnp.float32)
-        for s, w in zip(sources, weights):
-            mixed = mixed + jnp.dot(
-                (w * share).astype(jnp.bfloat16),
-                x_ref[jnp.maximum(s, 0), 2 * tok : 3 * tok, :],
-                preferred_element_type=jnp.float32,
-            )
-        out_ref[i * tok : (i + 1) * tok, :] = mixed.astype(jnp.bfloat16)
-    rows = n // 2 * tok
-    clip_rows = out_ref.shape[0] - rows
-    hist = jnp.zeros((clip_rows, HD), jnp.float32)
-    for s in range(n):
-        hist = hist + x_ref[s, 3 * tok : 3 * tok + clip_rows, :].astype(jnp.float32)
-    out_ref[rows:, :] = hist.astype(jnp.bfloat16)
-
-
 def attend_kernel(n, tok, order, counts_hbm, *refs):
-    parts, (same_ref, cross_ref, x_ref, counts, sem) = refs[:n], refs[n:]
+    parts, (same_ref, cross_ref, x_ref, mixed_ref, counts, sem) = refs[:n], refs[n:]
     copy = pltpu.make_async_copy(counts_hbm, counts, sem)
     copy.start()
     own = lax.axis_index("tm")
@@ -193,8 +148,49 @@
     for k, part in zip(order, parts):
         x_ref[own ^ k] = part[...]
     copy.wait()
-    attend_blocks(n, tok, side, counts, x_ref, same_ref)
-    attend_blocks(n, tok, 1 - side, counts, x_ref, cross_ref)
+    rate = math.log2(math.e) / math.sqrt(HD)
+    token = lax.broadcasted_iota(jnp.int32, (tok, 1), 0)
+    bias = [
+        jnp.where(token < counts[s] * TPF, 0.0, -jnp.inf).astype(jnp.float32) for s in range(n)
+    ]
+    values = [x_ref[s, 2 * tok : 3 * tok, :].T for s in range(n)]
+    for block in range(n):
+        sources = range(max(0, block - (WINB - 1)), block + 1)
+        q = x_ref[block, 0:tok, :]
+        scores = [
+            lax.dot_general(
+                x_ref[s, tok : 2 * tok, :],
+                q,
+                (((1,), (1,)), ((), ())),
+                preferred_element_type=jnp.float32,
+            )
+            + bias[s]
+            for s in sources
+        ]
+        top = jnp.max(scores[0], axis=0, keepdims=True)
+        for s in scores[1:]:
+            top = jnp.maximum(top, jnp.max(s, axis=0, keepdims=True))
+        weights = [jnp.exp2((s - top) * rate) for s in scores]
+        total = jnp.sum(weights[0], axis=0, keepdims=True)
+        for w in weights[1:]:
+            total = total + jnp.sum(w, axis=0, keepdims=True)
+        share = 1.0 / total
+        mixed = jnp.zeros((HD, tok), jnp.float32)
+        for s, w in zip(sources, weights):
+            mixed = mixed + jnp.dot(
+                values[s], (w * share).astype(jnp.bfloat16), preferred_element_type=jnp.float32
+            )
+        mixed_ref[block] = mixed.astype(jnp.bfloat16).T
+    rows = n // 2 * tok
+    clip_rows = same_ref.shape[0] - rows
+    hist = jnp.zeros((clip_rows, HD), jnp.float32)
+    for s in range(n):
+        hist = hist + x_ref[s, 3 * tok : 3 * tok + clip_rows, :].astype(jnp.float32)
+    hist = hist.astype(jnp.bfloat16)
+    for flip, out_ref in ((0, same_ref), (1, cross_ref)):
+        for i in range(n // 2):
+            out_ref[i * tok : (i + 1) * tok, :] = mixed_ref[2 * i + (side ^ flip)]
+        out_ref[rows:, :] = hist
 
 
 def stack_kernel(order, lo, tiles, *refs):
@@ -245,37 +241,54 @@
     )
 
 
-def grad_kernel(rows, copies, turned_ref, *refs):
+def grad_kernel(rows, copies, heads, turned_ref, *refs):
     out_ref = refs[-1]
-    out_ref[...] = grad_part(turned_ref, refs[:-1], rows, copies).astype(out_ref.dtype)
-
-
-def finish_kernel(order, tok, own_near, own_far, got_near, got_far, *refs):
-    n = len(order)
-    heads, (att_hbm, out_hbm, total, sems) = refs[:n], refs[n:]
+    out_ref[...] = grad_part(turned_ref, refs[:heads], rows, copies).astype(out_ref.dtype)
+
+
+def store_columns(tok, heads, sums, att_hbm, out_hbm, total, sems):
     own = lax.axis_index("tm")
     at = pl.multiple_of(own // 2 * tok, tok)
-    near = own_near.shape[1] // HD
-
-    def column(near_ref, far_ref, i):
-        ref, i = (near_ref, i) if i < near else (far_ref, i - near)
-        return ref[:, i * HD : (i + 1) * HD]
-
     moves = []
 
     def move(a, b):
         moves.append(pltpu.make_async_copy(a, b, sems.at[len(moves)]))
         moves[-1].start()
 
-    lanes = [pl.ds(pl.multiple_of((own ^ k) * HD, HD), HD) for k in order]
-    for i in range(n):
-        move(heads[i].at[pl.ds(at, tok), :], att_hbm.at[:, lanes[i]])
-    for i, k in enumerate(order):
-        got = column(got_near, got_far, order.index(k ^ 1))
-        total[i] = column(own_near, own_far, i) + got.astype(jnp.float32)
-        move(total.at[i], out_hbm.at[:, lanes[i]])
+    def lanes(k):
+        return pl.ds(pl.multiple_of((own ^ k) * HD, HD), HD)
+
+    for k, ref in heads:
+        move(ref.at[pl.ds(at, tok), :], att_hbm.at[:, lanes(k)])
+    for i, (k, (mine, m), (got, g)) in enumerate(sums):
+        columns = got[:, g * HD : (g + 1) * HD].astype(jnp.float32)
+        total[i] = mine[:, m * HD : (m + 1) * HD] + columns
+        move(total.at[i], out_hbm.at[:, lanes(k)])
     for x in moves:
         x.wait()
+
+
+def near_kernel(tok, near, own_near, got_near, *refs):
+    heads, outs = refs[: len(near)], refs[len(near) :]
+    sums = [
+        (k, (own_near, i), (got_near, near.index(k ^ 1)))
+        for i, k in enumerate(near)
+        if k ^ 1 in near
+    ]
+    store_columns(tok, zip(near, heads), sums, *outs)
+
+
+def last_kernel(tok, near, far, own_near, got_near, own_far, got_far, *refs):
+    heads, outs = refs[: len(far)], refs[len(far) + 2 :]
+    sums = [
+        (k, (own_near, i), (got_far, far.index(k ^ 1)))
+        for i, k in enumerate(near)
+        if k ^ 1 in far
+    ]
+    for i, k in enumerate(far):
+        got = (got_far, far.index(k ^ 1)) if k ^ 1 in far else (got_near, near.index(k ^ 1))
+        sums.append((k, (own_far, i), got))
+    store_columns(tok, zip(far, heads), sums, *outs)
 
 
 def head_body(query_rows, key_rows, value_rows, frame_counts, history, offsets, cotangent):
@@ -307,7 +320,7 @@
         return lax.ppermute(x, ("tm", "head"), pairs)
 
     def call(
-        kernel, name, outs, specs, flops, scratch=(), exps=0, out_spec=vmem, limit=VMEM_LIMIT
+        kernel, name, outs, specs, flops, scratch=(), exps=0, out_spec=vmem, limit=VMEM_LIMIT, aliases={}
     ):
         shapes = [jax.ShapeDtypeStruct(s, d) for s, d in outs]
         moved = 2 * sum(math.prod(s.shape) * s.dtype.itemsize for s in shapes)
@@ -317,6 +330,7 @@
             in_specs=specs,
             out_specs=tuple([out_spec] * len(shapes)),
             scratch_shapes=scratch,
+            input_output_aliases=aliases,
             compiler_params=pltpu.CompilerParams(vmem_limit_bytes=limit),
             cost_estimate=pl.CostEstimate(flops=flops, bytes_accessed=moved, transcendentals=exps),
             name=name,
@@ -362,6 +376,7 @@
     cots = [cots[0]] + [moved[m] for m in chips[1:]]
     counts = (
         pltpu.VMEM((n, length, HD), bf16),
+        pltpu.VMEM((n, tok, HD), bf16),
         pltpu.SMEM(frame_counts.shape, jnp.int32),
         pltpu.SemaphoreType.DMA,
     )
@@ -400,32 +415,42 @@
         (pltpu.VMEM((half, cot_rows, 2 * cols), bf16),),
     )(cots[0], *[cots[m] for m in stack_order], cot_swapped)
 
-    def grad(turned, heads, dtype, name):
+    def grad(turned, heads, dtype, name, behind=()):
         (out,) = call(
-            lambda *refs: grad_kernel(rows, half, *refs),
+            lambda *refs: grad_kernel(rows, half, len(heads), *refs),
             name,
             [((cols, len(heads) * HD), dtype)],
-            [vmem] * (1 + len(heads)),
+            [vmem] * (1 + len(heads)) + [hbm] * len(behind),
             2 * cols * half * cot_rows * len(heads) * HD,
-        )(turned, *heads)
+        )(turned, *heads, *behind)
         return out
 
-    near = [same, x_cross, y_same, x_same, y_cross]
-    far = [c_cross, far_same, far_cross]
-    heads = [0, 3, 4, 2, 5, 1, 6, 7]
+    near, near_bits = [same, x_cross, y_same, x_same, y_cross], [0, 3, 4, 2, 5]
+    far, far_bits = [c_cross, far_same, far_cross], [1, 6, 7]
+    whole = [((tok, width), bf16), ((cols, width), jnp.float32)]
     got_near = swap(grad(turned_other, near, bf16, "grad_other_near"), 1)
     own_near = grad(turned_own, near, jnp.float32, "grad_own_near")
-    got_far = swap(grad(turned_other, far, bf16, "grad_other_far"), 1)
+    got_far = swap(grad(turned_other, far, bf16, "grad_other_far", (own_near,)), 1)
     own_far = grad(turned_own, far, jnp.float32, "grad_own_far")
+    halfway = call(
+        lambda *refs: near_kernel(tok, near_bits, *refs),
+        "near",
+        whole,
+        [vmem] * (2 + len(near)),
+        0,
+        (pltpu.VMEM((4, cols, HD), jnp.float32), pltpu.SemaphoreType.DMA((9,))),
+        out_spec=hbm,
+    )(own_near, got_near, *near)
     return call(
-        lambda *refs: finish_kernel(heads, tok, *refs),
-        "finish",
-        [((tok, width), bf16), ((cols, width), jnp.float32)],
-        [vmem] * (4 + n),
+        lambda *refs: last_kernel(tok, near_bits, far_bits, *refs),
+        "last",
+        whole,
+        [vmem] * (4 + len(far)) + [hbm] * 2,
         0,
-        (pltpu.VMEM((n, cols, HD), jnp.float32), pltpu.SemaphoreType.DMA((2 * n,))),
+        (pltpu.VMEM((4, cols, HD), jnp.float32), pltpu.SemaphoreType.DMA((7,))),
         out_spec=hbm,
-    )(own_near, own_far, got_near, got_far, *near, *far)
+        aliases={4 + len(far): 0, 5 + len(far): 1},
+    )(own_near, got_near, own_far, got_far, *far, *halfway)
 
 
 def body(query_rows, key_rows, value_rows, frame_counts, history, offsets, cotangent):

time: 55.9 us -> 55.4 us (level)
  waiting for transfers between devices: 21.4 us -> 20.6 us
    ppermute x19, waiting for transfers between devices: 21.4 us -> 20.6 us  [swap(): return lax.ppermute(x, 'tm', [(i, i ^ bit) for i in range(n)])]
    pallas_call x5 -> x6, Pallas kernels: 3.53 us -> 4.18 us  [the longest x4 2.24 us: grad(): call(lambda *refs: grad_kernel(rows, half, len(heads), *refs), name, [((c...]
  transfers between devices with their start and end apart: 20 -> 20, of which waited for: 9 -> 8; matrix products, arithmetic and copies ran while one was open for 0% -> 0% of each run, Pallas kernels for 21% -> 22%
where the time goes in v9:
time: 55.4 us; the launch traced here: 55.1 us
  waiting for transfers between devices  20.6 us (37%)
  starting transfers between devices  18.8 us (34%)
  Pallas kernels  14.9 us (27%)
  between operations  0.79 us (1%)
    ppermute x19, waiting for transfers between devices, swap(): return lax.ppermute(x, 'tm', [(i, i ^ bit) for i in range(n)])  20.6 us
    ppermute x19, starting transfers between devices, swap(): return lax.ppermute(x, 'tm', [(i, i ^ bit) for i in range(n)])  17.1 us
    pallas_call x1, Pallas kernels, head_body(): call(lambda *refs: attend_kernel(n, tok, [0] + order, *refs), 'attend', [...  4.81 us
    pallas_call x2, Pallas kernels, pack(): call(lambda *refs: pack_kernel(n, heads, *refs), name, [((length, HD), bf...  4.42 us
    pallas_call x4, Pallas kernels, grad(): call(lambda *refs: grad_kernel(rows, half, len(heads), *refs), name, [((c...  2.24 us
    ppermute x1, starting transfers between devices, swap_plane(): return lax.ppermute(x, ('tm', 'head'), pairs)  1.64 us
  transfers between devices with their start and end apart: 20, of which 8 were waited for; matrix products, arithmetic and copies ran while one was open for 0% of the time, Pallas kernels for 22%

profile of v9, /device:TPU:0, one launch (start us, length us, event | category | flops | bytes accessed | tf_op | source)
XLA Modules:
  0.0 55.1 jit_solution(13371624374257435322)
XLA Ops:
  0.6 1.9 %pack_first.1 = (bf16[784,128]{1,0:T(8,128)(2,1)}, bf16[784,128]{1,0:T(8,128)(2,1)}) custom-call(bf16[256,1024]{1,0:T(8,128)(2,1)} %refs_0_.6, bf16[256,1024]{1,0:T(8,128)(2,1)} %refs_1_.5, bf16[256,1024]{1,0:T(8,128)(2,1)} %refs_2_.3, bf16[2,1024]{1,0:T(2,128)(2,1)} %refs_3_.3), custom_call_target="tpu_custom_call" | custom-call | bytes 802816 | tf_op jit(solution)/shard_map/pack_first/pallas_call | solution.py:340
  2.5 4.0 %collective-permute-start = (bf16[784,128]{1,0:T(8,128)(2,1)}, bf16[784,128]{1,0:T(8,128)(2,1)S(1)}, u32[]{:S(2)}, u32[]{:S(2)}) collective-permute-start(bf16[784,128]{1,0:T(8,128)(2,1)} %get-tuple-element.20), channel_id=1, source_target_pairs={{0,24},{4,28},{8,16},{12,20},{16,8},{20,12},{24,0},{28,4},{1,25},{... | collective-permute-start | bytes 602120 | tf_op jit(solution)/shard_map/ppermute | solution.py:314
  6.5 2.6 %pack_rest.1 = (bf16[784,128]{1,0:T(8,128)(2,1)}, bf16[784,128]{1,0:T(8,128)(2,1)}, bf16[784,128]{1,0:T(8,128)(2,1)}, bf16[784,128]{1,0:T(8,128)(2,1)}, bf16[784...) custom-call(bf16[256,1024]{1,0:T(8,128)(2,1)} %refs_0_.6, bf16[256,1024]{1,0:T(8,128)(2,1)} %refs_1_.5, ...), custom_call_target="tpu_custom_call" | custom-call | bytes 2408448 | tf_op jit(solution)/shard_map/pack_rest/pallas_call | solution.py:340
  9.1 1.2 %collective-permute-start.5 = (bf16[784,128]{1,0:T(8,128)(2,1)}, bf16[784,128]{1,0:T(8,128)(2,1)S(1)}, u32[]{:S(2)}, u32[]{:S(2)}) collective-permute-start(bf16[784,128]{1,0:T(8,128)(2,1)} %get-tuple-element.27), channel_id=1, source_target_pairs={{0,8},{4,12},{8,0},{12,4},{16,24},{20,28},{24,16},{28,20},{1,9},{5... | collective-permute-start | bytes 602120 | tf_op jit(solution)/shard_map/ppermute | solution.py:314
  10.3 1.5 %collective-permute-start.6 = (bf16[784,128]{1,0:T(8,128)(2,1)}, bf16[784,128]{1,0:T(8,128)(2,1)S(1)}, u32[]{:S(2)}, u32[]{:S(2)}) collective-permute-start(bf16[784,128]{1,0:T(8,128)(2,1)} %get-tuple-element.28), channel_id=1, source_target_pairs={{0,16},{4,20},{8,24},{12,28},{16,0},{20,4},{24,8},{28,12},{1,17},{... | collective-permute-start | bytes 602120 | tf_op jit(solution)/shard_map/ppermute | solution.py:314
  11.8 0.6 %collective-permute-start.7 = (bf16[784,128]{1,0:T(8,128)(2,1)}, bf16[784,128]{1,0:T(8,128)(2,1)S(1)}, u32[]{:S(2)}, u32[]{:S(2)}) collective-permute-start(bf16[784,128]{1,0:T(8,128)(2,1)} %get-tuple-element.29), channel_id=1, source_target_pairs={{0,12},{4,8},{8,4},{12,0},{16,28},{20,24},{24,20},{28,16},{1,13},{... | collective-permute-start | bytes 602120 | tf_op jit(solution)/shard_map/ppermute | solution.py:314
  12.5 0.4 collective-permute-start.8
  12.9 3.6 %collective-permute-done.1.refs_3_ = bf16[784,128]{1,0:T(8,128)(2,1)S(1)} collective-permute-done((bf16[784,128]{1,0:T(8,128)(2,1)}, bf16[784,128]{1,0:T(8,128)(2,1)S(1)}, u32[]{:S(2)}, u32[]{:S(2)}) %collective-permute-start.1) | collective-permute-done | bytes 200736 | tf_op jit(solution)/shard_map/ppermute | solution.py:314
  16.6 0.9 %cot.1 = (bf16[1088,128]{1,0:T(8,128)(2,1)S(1)}, bf16[640,128]{1,0:T(8,128)(2,1)S(1)}, bf16[640,128]{1,0:T(8,128)(2,1)S(1)}, bf16[640,128]{1,0:T(8,128)(2,1)S(1)}) custom-call(s32[1,8]{1,0:T(1,128)S(1)} %copy-done.1, bf16[272,2048]{1,0:T(8,128)(2,1)S(1)} %copy-done, bf16[784,128]{1,0:T(8,128)(2,1)S(1)} %collective-permute-done.refs_2_, ...), custom_call_target="tpu_custom_call" | custom-call | bytes 1540096 | tf_op jit(solution)/shard_map/cot/pallas_call | solution.py:363
  17.6 4.1 %collective-permute-done.5.refs_4_ = bf16[784,128]{1,0:T(8,128)(2,1)S(1)} collective-permute-done((bf16[784,128]{1,0:T(8,128)(2,1)}, bf16[784,128]{1,0:T(8,128)(2,1)S(1)}, u32[]{:S(2)}, u32[]{:S(2)}) %collective-permute-start.5) | collective-permute-done | bytes 200736 | tf_op jit(solution)/shard_map/ppermute | solution.py:314
  21.7 1.5 %collective-permute-start.2 = (bf16[640,128]{1,0:T(8,128)(2,1)S(1)}, bf16[640,128]{1,0:T(8,128)(2,1)S(1)}, u32[]{:S(2)}, u32[]{:S(2)}) collective-permute-start(bf16[640,128]{1,0:T(8,128)(2,1)S(1)} %get-tuple-element.23), channel_id=1, source_target_pairs={{0,24},{4,28},{8,16},{12,20},{16,8},{20,12},{24,0},{28,4},{1,25},{... | collective-permute-start | bytes 491528 | tf_op jit(solution)/shard_map/ppermute | solution.py:314
  23.2 1.9 %collective-permute-done.7.refs_6_ = bf16[784,128]{1,0:T(8,128)(2,1)S(1)} collective-permute-done((bf16[784,128]{1,0:T(8,128)(2,1)}, bf16[784,128]{1,0:T(8,128)(2,1)S(1)}, u32[]{:S(2)}, u32[]{:S(2)}) %collective-permute-start.7) | collective-permute-done | bytes 200736 | tf_op jit(solution)/shard_map/ppermute | solution.py:314
  25.1 0.5 collective-permute-start.4
  25.7 4.8 %attend.1 = (bf16[1040,128]{1,0:T(8,128)(2,1)S(1)}, bf16[1040,128]{1,0:T(8,128)(2,1)S(1)}) custom-call(s32[8]{0:T(128)S(1)} %copy-done.3, bf16[784,128]{1,0:T(8,128)(2,1)S(1)} %copy-done.2, bf16[784,128]{1,0:T(8,128)(2,1)S(1)} %collective-permute-done.refs_2_, bf16[784,128]{1,0:T(8,128)(2,1)S(1)} %collective-permute-done.1.refs_3_, ...), custom_call_target="tpu_custom_call" | custom-call | flops 1073741824 | bytes 1064960 | tf_op jit(solution)/shard_map/attend/pallas_call | solution.py:385
  30.5 1.6 %collective-permute-start.14 = (bf16[1040,128]{1,0:T(8,128)(2,1)S(1)}, bf16[1040,128]{1,0:T(8,128)(2,1)S(1)}, u32[]{:S(2)}, u32[]{:S(2)}) collective-permute-start(bf16[1040,128]{1,0:T(8,128)(2,1)S(1)} %get-tuple-element.34.x_ref), channel_id=1, source_target_pairs={{0,20},{4,16},{8,28},{12,24},{16,4},{20,0},{24,12},{28,8},{1,21},{... | collective-permute-start | bytes 798728 | tf_op jit(solution)/shard_map/ppermute | solution.py:314
  32.1 1.5 %collective-permute-start.13 = (bf16[1040,128]{1,0:T(8,128)(2,1)S(1)}, bf16[1040,128]{1,0:T(8,128)(2,1)S(1)}, u32[]{:S(2)}, u32[]{:S(2)}) collective-permute-start(bf16[1040,128]{1,0:T(8,128)(2,1)S(1)} %get-tuple-element.32.refs_3_.refs_1_.refs_2_), channel_id=1, source_target_pairs={{0,8},{4,12},{8,0},{12,4},{16,24},{20,28},{24,16},{28,20},{1,9},{5... | collective-permute-start | bytes 798728 | tf_op jit(solution)/shard_map/ppermute | solution.py:314
  33.7 0.7 %collective-permute-start.12 = (bf16[1040,128]{1,0:T(8,128)(2,1)S(1)}, bf16[1040,128]{1,0:T(8,128)(2,1)S(1)}, u32[]{:S(2)}, u32[]{:S(2)}) collective-permute-start(bf16[1040,128]{1,0:T(8,128)(2,1)S(1)} %get-tuple-element.32.refs_3_.refs_1_.refs_2_), channel_id=1, source_target_pairs={{0,16},{4,20},{8,24},{12,28},{16,0},{20,4},{24,8},{28,12},{1,17},{... | collective-permute-start | bytes 798728 | tf_op jit(solution)/shard_map/ppermute | solution.py:314
  34.5 1.6 %collective-permute-start.10 = (bf16[3,448,128]{2,1,0:T(8,128)(2,1)S(1)}, bf16[3,448,128]{2,1,0:T(8,128)(2,1)S(1)}, u32[]{:S(2)}, u32[]{:S(2)}) collective-permute-start(bf16[3,448,128]{2,1,0:T(8,128)(2,1)S(1)} %stack.1), channel_id=1, source_target_pairs={{0,1},{1,0},{2,3},{3,2},{4,5},{5,4},{6,7},{7,6},{8,9},{9,8},{10,11... | collective-permute-start | bytes 1032200 | tf_op jit(solution)/shard_map/ppermute | solution.py:320
  36.1 2.8 %collective-permute-done.14.refs_5_.refs_6_ = bf16[1040,128]{1,0:T(8,128)(2,1)S(1)} collective-permute-done((bf16[1040,128]{1,0:T(8,128)(2,1)S(1)}, bf16[1040,128]{1,0:T(8,128)(2,1)S(1)}, u32[]{:S(2)}, u32[]{:S(2)}) %collective-permute-start.14) | collective-permute-done | bytes 266272 | tf_op jit(solution)/shard_map/ppermute | solution.py:314
  39.0 1.3 %collective-permute-start.18 = (bf16[1040,128]{1,0:T(8,128)(2,1)S(1)}, bf16[1040,128]{1,0:T(8,128)(2,1)S(1)}, u32[]{:S(2)}, u32[]{:S(2)}) collective-permute-start(bf16[1040,128]{1,0:T(8,128)(2,1)S(1)} %collective-permute-done.14.refs_5_.refs_6_), channel_id=1, source_target_pairs={{0,8},{4,12},{8,0},{12,4},{16,24},{20,28},{24,16},{28,20},{1,9},{5... | collective-permute-start | bytes 798728 | tf_op jit(solution)/shard_map/ppermute | solution.py:314
  40.3 1.0 %collective-permute-done.13.refs_4_.refs_5_ = bf16[1040,128]{1,0:T(8,128)(2,1)S(1)} collective-permute-done((bf16[1040,128]{1,0:T(8,128)(2,1)S(1)}, bf16[1040,128]{1,0:T(8,128)(2,1)S(1)}, u32[]{:S(2)}, u32[]{:S(2)}) %collective-permute-start.13) | collective-permute-done | bytes 266272 | tf_op jit(solution)/shard_map/ppermute | solution.py:314
  41.3 0.8 %collective-permute-start.17 = (bf16[1040,128]{1,0:T(8,128)(2,1)S(1)}, bf16[1040,128]{1,0:T(8,128)(2,1)S(1)}, u32[]{:S(2)}, u32[]{:S(2)}) collective-permute-start(bf16[1040,128]{1,0:T(8,128)(2,1)S(1)} %collective-permute-done.13.refs_4_.refs_5_), channel_id=1, source_target_pairs={{0,16},{4,20},{8,24},{12,28},{16,0},{20,4},{24,8},{28,12},{1,17},{... | collective-permute-start | bytes 798728 | tf_op jit(solution)/shard_map/ppermute | solution.py:314
  42.1 4.0 %collective-permute-done.11.refs_2_.refs_0_.refs_3_ = bf16[1040,128]{1,0:T(8,128)(2,1)S(1)} collective-permute-done((bf16[1040,128]{1,0:T(8,128)(2,1)S(1)}, bf16[1040,128]{1,0:T(8,128)(2,1)S(1)}, u32[]{:S(2)}, u32[]{:S(2)}) %collective-permute-start.11) | collective-permute-done | bytes 266272 | tf_op jit(solution)/shard_map/ppermute | solution.py:314
  46.1 1.1 %collective-permute-start.16 = (bf16[1040,128]{1,0:T(8,128)(2,1)S(1)}, bf16[1040,128]{1,0:T(8,128)(2,1)S(1)}, u32[]{:S(2)}, u32[]{:S(2)}) collective-permute-start(bf16[1040,128]{1,0:T(8,128)(2,1)S(1)} %late.1), channel_id=1, source_target_pairs={{0,4},{4,0},{8,12},{12,8},{16,20},{20,16},{24,28},{28,24},{1,5},{5... | collective-permute-start | bytes 798728 | tf_op jit(solution)/shard_map/ppermute | solution.py:314
  47.2 0.6 %turn.1 = (bf16[256,1088]{1,0:T(8,128)(2,1)S(1)}, bf16[256,1088]{1,0:T(8,128)(2,1)S(1)}) custom-call(bf16[1088,128]{1,0:T(8,128)(2,1)S(1)} %get-tuple-element.22.refs_0_, bf16[640,128]{1,0:T(8,128)(2,1)S(1)} %collective-permute-done.2.refs_0_.refs_1_, bf16[640,128]{1,0:T(8,128)(2,1)S(1)} %collective-permute-done.3.refs_1_.refs_2_, ...), custom_call_target="tpu_custom_call" | custom-call | bytes 2228224 | tf_op jit(solution)/shard_map/turn/pallas_call | solution.py:409
  47.8 0.6 %grad_other_near.1 = bf16[256,640]{1,0:T(8,128)(2,1)S(1)} custom-call(bf16[256,1088]{1,0:T(8,128)(2,1)S(1)} %get-tuple-element.35.refs_0_, bf16[1040,128]{1,0:T(8,128)(2,1)S(1)} %get-tuple-element.32.refs_3_.refs_1_.refs_2_, bf16[1040,128]{1,0:T(8,128)(2,1)S(1)} %collective-permute-done.11.refs_2_.refs_0_.refs_3_, ...), custom_call_target="tpu_custom_call" | custom-call | flops 356515840 | bytes 655360 | tf_op jit(solution)/shard_map/grad_other_near/pallas_call | solution.py:419
  48.5 0.6 %grad_own_near.1.refs_4_.refs_0_ = f32[256,640]{1,0:T(8,128)S(1)} custom-call(bf16[256,1088]{1,0:T(8,128)(2,1)S(1)} %get-tuple-element.33.refs_0_, bf16[1040,128]{1,0:T(8,128)(2,1)S(1)} %get-tuple-element.32.refs_3_.refs_1_.refs_2_, bf16[1040,128]{1,0:T(8,128)(2,1)S(1)} %collective-permute-done.11.refs_2_.refs_0_.refs_3_, ...), custom_call_target="tpu_custom_call" | custom-call | flops 356515840 | bytes 1310720 | tf_op jit(solution)/shard_map/grad_own_near/pallas_call | solution.py:419
  49.1 3.0 %collective-permute-done.18.refs_3_.refs_6_ = bf16[1040,128]{1,0:T(8,128)(2,1)S(1)} collective-permute-done((bf16[1040,128]{1,0:T(8,128)(2,1)S(1)}, bf16[1040,128]{1,0:T(8,128)(2,1)S(1)}, u32[]{:S(2)}, u32[]{:S(2)}) %collective-permute-start.18) | collective-permute-done | bytes 266272 | tf_op jit(solution)/shard_map/ppermute | solution.py:314
  52.1 0.5 grad_other_far.1
  52.7 0.5 grad_own_far.1.refs_2_
  53.2 1.0 %near.1 = (bf16[256,1024]{1,0:T(8,128)(2,1)}, f32[256,1024]{1,0:T(8,128)}) custom-call(f32[256,640]{1,0:T(8,128)S(1)} %grad_own_near.1.refs_4_.refs_0_, bf16[256,640]{1,0:T(8,128)(2,1)S(1)} %collective-permute-done.15.refs_1_, bf16[1040,128]{1,0:T(8,128)(2,1)S(1)} %get-tuple-element.32.refs_3_.refs_1_.refs_2_, ...), custom_call_target="tpu_custom_call" | custom-call | bytes 3145728 | tf_op jit(solution)/shard_map/near/pallas_call | solution.py:435
  54.2 0.9 %last.1 = (bf16[256,1024]{1,0:T(8,128)(2,1)}, f32[256,1024]{1,0:T(8,128)}) custom-call(f32[256,640]{1,0:T(8,128)S(1)} %grad_own_near.1.refs_4_.refs_0_, bf16[256,640]{1,0:T(8,128)(2,1)S(1)} %collective-permute-done.15.refs_1_, f32[256,384]{1,0:T(8,128)S(1)} %grad_own_far.1.refs_2_, ...), custom_call_target="tpu_custom_call", output_to_operand_aliasing={{0}: (7, {}), {1}: (8, {})} | custom-call | bytes 3145728 | tf_op jit(solution)/shard_map/last/pallas_call | solution.py:444
  (29 shorter events, 0.7 us)
Async XLA Ops:
  2.5 14.1 %copy-start = (bf16[272,2048]{1,0:T(8,128)(2,1)S(1)}, bf16[272,2048]{1,0:T(8,128)(2,1)}, u32[]{:S(2)}) copy-start(bf16[272,2048]{1,0:T(8,128)(2,1)} %refs_1_.4) | copy-start | bytes 3342340
  2.5 14.1 %copy-start.1 = (s32[1,8]{1,0:T(1,128)S(1)}, s32[1,8]{1,0:T(1,128)}, u32[]{:S(2)}) copy-start(s32[1,8]{1,0:T(1,128)} %refs_0_.5) | copy-start | bytes 100
  2.5 10.0 %collective-permute-start = (bf16[784,128]{1,0:T(8,128)(2,1)}, bf16[784,128]{1,0:T(8,128)(2,1)S(1)}, u32[]{:S(2)}, u32[]{:S(2)}) collective-permute-start(bf16[784,128]{1,0:T(8,128)(2,1)} %get-tuple-element.20), channel_id=1, source_target_pairs={{0,24},{4,28},{8,16},{12,20},{16,8},{20,12},{24,0},{28,4},{1,25},{... | collective-permute-start | bytes 602120 | tf_op jit(solution)/shard_map/ppermute | solution.py:314
  6.5 10.1 %collective-permute-start.1 = (bf16[784,128]{1,0:T(8,128)(2,1)}, bf16[784,128]{1,0:T(8,128)(2,1)S(1)}, u32[]{:S(2)}, u32[]{:S(2)}) collective-permute-start(bf16[784,128]{1,0:T(8,128)(2,1)} %get-tuple-element.21), channel_id=1, source_target_pairs={{0,28},{4,24},{8,20},{12,16},{16,12},{20,8},{24,4},{28,0},{1,29},{... | collective-permute-start | bytes 602120 | tf_op jit(solution)/shard_map/ppermute | solution.py:314
  9.1 16.6 %copy-start.2 = (bf16[784,128]{1,0:T(8,128)(2,1)S(1)}, bf16[784,128]{1,0:T(8,128)(2,1)}, u32[]{:S(2)}) copy-start(bf16[784,128]{1,0:T(8,128)(2,1)} %get-tuple-element.26.refs_1_) | copy-start | bytes 602116
  9.1 16.6 %copy-start.3 = (s32[8]{0:T(128)S(1)}, s32[8]{0:T(128)}, u32[]{:S(2)}) copy-start(s32[8]{0:T(128)} %refs_0_.7) | copy-start | bytes 100
  9.1 12.6 %collective-permute-start.5 = (bf16[784,128]{1,0:T(8,128)(2,1)}, bf16[784,128]{1,0:T(8,128)(2,1)S(1)}, u32[]{:S(2)}, u32[]{:S(2)}) collective-permute-start(bf16[784,128]{1,0:T(8,128)(2,1)} %get-tuple-element.27), channel_id=1, source_target_pairs={{0,8},{4,12},{8,0},{12,4},{16,24},{20,28},{24,16},{28,20},{1,9},{5... | collective-permute-start | bytes 602120 | tf_op jit(solution)/shard_map/ppermute | solution.py:314
  10.3 12.9 %collective-permute-start.6 = (bf16[784,128]{1,0:T(8,128)(2,1)}, bf16[784,128]{1,0:T(8,128)(2,1)S(1)}, u32[]{:S(2)}, u32[]{:S(2)}) collective-permute-start(bf16[784,128]{1,0:T(8,128)(2,1)} %get-tuple-element.28), channel_id=1, source_target_pairs={{0,16},{4,20},{8,24},{12,28},{16,0},{20,4},{24,8},{28,12},{1,17},{... | collective-permute-start | bytes 602120 | tf_op jit(solution)/shard_map/ppermute | solution.py:314
  11.8 13.3 %collective-permute-start.7 = (bf16[784,128]{1,0:T(8,128)(2,1)}, bf16[784,128]{1,0:T(8,128)(2,1)S(1)}, u32[]{:S(2)}, u32[]{:S(2)}) collective-permute-start(bf16[784,128]{1,0:T(8,128)(2,1)} %get-tuple-element.29), channel_id=1, source_target_pairs={{0,12},{4,8},{8,4},{12,0},{16,28},{20,24},{24,20},{28,16},{1,13},{... | collective-permute-start | bytes 602120 | tf_op jit(solution)/shard_map/ppermute | solution.py:314
  12.5 13.1 %collective-permute-start.8 = (bf16[784,128]{1,0:T(8,128)(2,1)}, bf16[784,128]{1,0:T(8,128)(2,1)S(1)}, u32[]{:S(2)}, u32[]{:S(2)}) collective-permute-start(bf16[784,128]{1,0:T(8,128)(2,1)} %get-tuple-element.30), channel_id=1, source_target_pairs={{0,20},{4,16},{8,28},{12,24},{16,4},{20,0},{24,12},{28,8},{1,21},{... | collective-permute-start | bytes 602120 | tf_op jit(solution)/shard_map/ppermute | solution.py:314
  16.5 9.1 %collective-permute-start.9 = (bf16[784,128]{1,0:T(8,128)(2,1)}, bf16[784,128]{1,0:T(8,128)(2,1)S(1)}, u32[]{:S(2)}, u32[]{:S(2)}) collective-permute-start(bf16[784,128]{1,0:T(8,128)(2,1)} %get-tuple-element.31), channel_id=1, source_target_pairs={{0,4},{4,0},{8,12},{12,8},{16,20},{20,16},{24,28},{28,24},{1,5},{5... | collective-permute-start | bytes 602120 | tf_op jit(solution)/shard_map/ppermute | solution.py:314
  21.7 11.9 %collective-permute-start.2 = (bf16[640,128]{1,0:T(8,128)(2,1)S(1)}, bf16[640,128]{1,0:T(8,128)(2,1)S(1)}, u32[]{:S(2)}, u32[]{:S(2)}) collective-permute-start(bf16[640,128]{1,0:T(8,128)(2,1)S(1)} %get-tuple-element.23), channel_id=1, source_target_pairs={{0,24},{4,28},{8,16},{12,20},{16,8},{20,12},{24,0},{28,4},{1,25},{... | collective-permute-start | bytes 491528 | tf_op jit(solution)/shard_map/ppermute | solution.py:314
  23.2 10.6 %collective-permute-start.3 = (bf16[640,128]{1,0:T(8,128)(2,1)S(1)}, bf16[640,128]{1,0:T(8,128)(2,1)S(1)}, u32[]{:S(2)}, u32[]{:S(2)}) collective-permute-start(bf16[640,128]{1,0:T(8,128)(2,1)S(1)} %get-tuple-element.24), channel_id=1, source_target_pairs={{0,8},{4,12},{8,0},{12,4},{16,24},{20,28},{24,16},{28,20},{1,9},{5... | collective-permute-start | bytes 491528 | tf_op jit(solution)/shard_map/ppermute | solution.py:314
  25.1 9.3 %collective-permute-start.4 = (bf16[640,128]{1,0:T(8,128)(2,1)S(1)}, bf16[640,128]{1,0:T(8,128)(2,1)S(1)}, u32[]{:S(2)}, u32[]{:S(2)}) collective-permute-start(bf16[640,128]{1,0:T(8,128)(2,1)S(1)} %get-tuple-element.25), channel_id=1, source_target_pairs={{0,16},{4,20},{8,24},{12,28},{16,0},{20,4},{24,8},{28,12},{1,17},{... | collective-permute-start | bytes 491528 | tf_op jit(solution)/shard_map/ppermute | solution.py:314
  30.5 8.5 %collective-permute-start.14 = (bf16[1040,128]{1,0:T(8,128)(2,1)S(1)}, bf16[1040,128]{1,0:T(8,128)(2,1)S(1)}, u32[]{:S(2)}, u32[]{:S(2)}) collective-permute-start(bf16[1040,128]{1,0:T(8,128)(2,1)S(1)} %get-tuple-element.34.x_ref), channel_id=1, source_target_pairs={{0,20},{4,16},{8,28},{12,24},{16,4},{20,0},{24,12},{28,8},{1,21},{... | collective-permute-start | bytes 798728 | tf_op jit(solution)/shard_map/ppermute | solution.py:314
  32.1 9.2 %collective-permute-start.13 = (bf16[1040,128]{1,0:T(8,128)(2,1)S(1)}, bf16[1040,128]{1,0:T(8,128)(2,1)S(1)}, u32[]{:S(2)}, u32[]{:S(2)}) collective-permute-start(bf16[1040,128]{1,0:T(8,128)(2,1)S(1)} %get-tuple-element.32.refs_3_.refs_1_.refs_2_), channel_id=1, source_target_pairs={{0,8},{4,12},{8,0},{12,4},{16,24},{20,28},{24,16},{28,20},{1,9},{5... | collective-permute-start | bytes 798728 | tf_op jit(solution)/shard_map/ppermute | solution.py:314
  33.6 12.5 %collective-permute-start.11 = (bf16[1040,128]{1,0:T(8,128)(2,1)S(1)}, bf16[1040,128]{1,0:T(8,128)(2,1)S(1)}, u32[]{:S(2)}, u32[]{:S(2)}) collective-permute-start(bf16[1040,128]{1,0:T(8,128)(2,1)S(1)} %get-tuple-element.34.x_ref), channel_id=1, source_target_pairs={{0,12},{4,8},{8,4},{12,0},{16,28},{20,24},{24,20},{28,16},{1,13},{... | collective-permute-start | bytes 798728 | tf_op jit(solution)/shard_map/ppermute | solution.py:314
  33.7 12.3 %collective-permute-start.12 = (bf16[1040,128]{1,0:T(8,128)(2,1)S(1)}, bf16[1040,128]{1,0:T(8,128)(2,1)S(1)}, u32[]{:S(2)}, u32[]{:S(2)}) collective-permute-start(bf16[1040,128]{1,0:T(8,128)(2,1)S(1)} %get-tuple-element.32.refs_3_.refs_1_.refs_2_), channel_id=1, source_target_pairs={{0,16},{4,20},{8,24},{12,28},{16,0},{20,4},{24,8},{28,12},{1,17},{... | collective-permute-start | bytes 798728 | tf_op jit(solution)/shard_map/ppermute | solution.py:314
  34.5 12.7 %collective-permute-start.10 = (bf16[3,448,128]{2,1,0:T(8,128)(2,1)S(1)}, bf16[3,448,128]{2,1,0:T(8,128)(2,1)S(1)}, u32[]{:S(2)}, u32[]{:S(2)}) collective-permute-start(bf16[3,448,128]{2,1,0:T(8,128)(2,1)S(1)} %stack.1), channel_id=1, source_target_pairs={{0,1},{1,0},{2,3},{3,2},{4,5},{5,4},{6,7},{7,6},{8,9},{9,8},{10,11... | collective-permute-start | bytes 1032200 | tf_op jit(solution)/shard_map/ppermute | solution.py:320
  39.0 13.1 %collective-permute-start.18 = (bf16[1040,128]{1,0:T(8,128)(2,1)S(1)}, bf16[1040,128]{1,0:T(8,128)(2,1)S(1)}, u32[]{:S(2)}, u32[]{:S(2)}) collective-permute-start(bf16[1040,128]{1,0:T(8,128)(2,1)S(1)} %collective-permute-done.14.refs_5_.refs_6_), channel_id=1, source_target_pairs={{0,8},{4,12},{8,0},{12,4},{16,24},{20,28},{24,16},{28,20},{1,9},{5... | collective-permute-start | bytes 798728 | tf_op jit(solution)/shard_map/ppermute | solution.py:314
  41.3 10.8 %collective-permute-start.17 = (bf16[1040,128]{1,0:T(8,128)(2,1)S(1)}, bf16[1040,128]{1,0:T(8,128)(2,1)S(1)}, u32[]{:S(2)}, u32[]{:S(2)}) collective-permute-start(bf16[1040,128]{1,0:T(8,128)(2,1)S(1)} %collective-permute-done.13.refs_4_.refs_5_), channel_id=1, source_target_pairs={{0,16},{4,20},{8,24},{12,28},{16,0},{20,4},{24,8},{28,12},{1,17},{... | collective-permute-start | bytes 798728 | tf_op jit(solution)/shard_map/ppermute | solution.py:314
  46.1 6.0 %collective-permute-start.16 = (bf16[1040,128]{1,0:T(8,128)(2,1)S(1)}, bf16[1040,128]{1,0:T(8,128)(2,1)S(1)}, u32[]{:S(2)}, u32[]{:S(2)}) collective-permute-start(bf16[1040,128]{1,0:T(8,128)(2,1)S(1)} %late.1), channel_id=1, source_target_pairs={{0,4},{4,0},{8,12},{12,8},{16,20},{20,16},{24,28},{28,24},{1,5},{5... | collective-permute-start | bytes 798728 | tf_op jit(solution)/shard_map/ppermute | solution.py:314
  48.4 4.8 %collective-permute-start.15 = (bf16[256,640]{1,0:T(8,128)(2,1)S(1)}, bf16[256,640]{1,0:T(8,128)(2,1)S(1)}, u32[]{:S(2)}, u32[]{:S(2)}) collective-permute-start(bf16[256,640]{1,0:T(8,128)(2,1)S(1)} %grad_other_near.1), channel_id=1, source_target_pairs={{0,4},{4,0},{8,12},{12,8},{16,20},{20,16},{24,28},{28,24},{1,5},{5... | collective-permute-start | bytes 983048 | tf_op jit(solution)/shard_map/ppermute | solution.py:314
  52.6 1.6 %collective-permute-start.19 = (bf16[256,384]{1,0:T(8,128)(2,1)S(1)}, bf16[256,384]{1,0:T(8,128)(2,1)S(1)}, u32[]{:S(2)}, u32[]{:S(2)}) collective-permute-start(bf16[256,384]{1,0:T(8,128)(2,1)S(1)} %grad_other_far.1), channel_id=1, source_target_pairs={{0,4},{4,0},{8,12},{12,8},{16,20},{20,16},{24,28},{28,24},{1,5},{5... | collective-permute-start | bytes 589832 | tf_op jit(solution)/shard_map/ppermute | solution.py:314

commit v10 on v9

--- a/solution.py
+++ b/solution.py
@@ -391,7 +391,7 @@
         counts,
         2 * pairs,
     )(frame_counts, *by_head)
-    stack_order = [3, 1, 2]
+    stack_order = [1, 2, 3]
     (cot_rest,) = call(
         lambda *refs: stack_kernel(stack_order, lo, 2 * units, *refs),
         "stack",

time: 55.4 us -> 55.2 us (level)
  transfers between devices with their start and end apart: 20 -> 20, of which waited for: 8 -> 9; matrix products, arithmetic and copies ran while one was open for 0% -> 0% of each run, Pallas kernels for 22% -> 22%
where the time goes in v10:
time: 55.2 us; the launch traced here: 55 us
  waiting for transfers between devices  20.2 us (37%)
  starting transfers between devices  19.1 us (35%)
  Pallas kernels  14.9 us (27%)
  between operations  0.79 us (1%)
    ppermute x19, waiting for transfers between devices, swap(): return lax.ppermute(x, 'tm', [(i, i ^ bit) for i in range(n)])  20.2 us
    ppermute x19, starting transfers between devices, swap(): return lax.ppermute(x, 'tm', [(i, i ^ bit) for i in range(n)])  17.4 us
    pallas_call x1, Pallas kernels, head_body(): call(lambda *refs: attend_kernel(n, tok, [0] + order, *refs), 'attend', [...  4.81 us
    pallas_call x2, Pallas kernels, pack(): call(lambda *refs: pack_kernel(n, heads, *refs), name, [((length, HD), bf...  4.42 us
    pallas_call x4, Pallas kernels, grad(): call(lambda *refs: grad_kernel(rows, half, len(heads), *refs), name, [((c...  2.23 us
    ppermute x1, starting transfers between devices, swap_plane(): return lax.ppermute(x, ('tm', 'head'), pairs)  1.64 us
  transfers between devices with their start and end apart: 20, of which 9 were waited for; matrix products, arithmetic and copies ran while one was open for 0% of the time, Pallas kernels for 22%

profile of v10, /device:TPU:0, one launch (start us, length us, event | category | flops | bytes accessed | tf_op | source)
XLA Modules:
  0.0 55.0 jit_solution(17954492863059571379)
XLA Ops:
  0.6 1.9 %pack_first.1 = (bf16[784,128]{1,0:T(8,128)(2,1)}, bf16[784,128]{1,0:T(8,128)(2,1)}) custom-call(bf16[256,1024]{1,0:T(8,128)(2,1)} %refs_0_.6, bf16[256,1024]{1,0:T(8,128)(2,1)} %refs_1_.5, bf16[256,1024]{1,0:T(8,128)(2,1)} %refs_2_.3, bf16[2,1024]{1,0:T(2,128)(2,1)} %refs_3_.3), custom_call_target="tpu_custom_call" | custom-call | bytes 802816 | tf_op jit(solution)/shard_map/pack_first/pallas_call | solution.py:340
  2.5 4.0 %collective-permute-start = (bf16[784,128]{1,0:T(8,128)(2,1)}, bf16[784,128]{1,0:T(8,128)(2,1)S(1)}, u32[]{:S(2)}, u32[]{:S(2)}) collective-permute-start(bf16[784,128]{1,0:T(8,128)(2,1)} %get-tuple-element.20), channel_id=1, source_target_pairs={{0,24},{4,28},{8,16},{12,20},{16,8},{20,12},{24,0},{28,4},{1,25},{... | collective-permute-start | bytes 602120 | tf_op jit(solution)/shard_map/ppermute | solution.py:314
  6.5 2.6 %pack_rest.1 = (bf16[784,128]{1,0:T(8,128)(2,1)}, bf16[784,128]{1,0:T(8,128)(2,1)}, bf16[784,128]{1,0:T(8,128)(2,1)}, bf16[784,128]{1,0:T(8,128)(2,1)}, bf16[784...) custom-call(bf16[256,1024]{1,0:T(8,128)(2,1)} %refs_0_.6, bf16[256,1024]{1,0:T(8,128)(2,1)} %refs_1_.5, ...), custom_call_target="tpu_custom_call" | custom-call | bytes 2408448 | tf_op jit(solution)/shard_map/pack_rest/pallas_call | solution.py:340
  9.1 1.2 %collective-permute-start.5 = (bf16[784,128]{1,0:T(8,128)(2,1)}, bf16[784,128]{1,0:T(8,128)(2,1)S(1)}, u32[]{:S(2)}, u32[]{:S(2)}) collective-permute-start(bf16[784,128]{1,0:T(8,128)(2,1)} %get-tuple-element.27), channel_id=1, source_target_pairs={{0,8},{4,12},{8,0},{12,4},{16,24},{20,28},{24,16},{28,20},{1,9},{5... | collective-permute-start | bytes 602120 | tf_op jit(solution)/shard_map/ppermute | solution.py:314
  10.3 1.5 %collective-permute-start.6 = (bf16[784,128]{1,0:T(8,128)(2,1)}, bf16[784,128]{1,0:T(8,128)(2,1)S(1)}, u32[]{:S(2)}, u32[]{:S(2)}) collective-permute-start(bf16[784,128]{1,0:T(8,128)(2,1)} %get-tuple-element.28), channel_id=1, source_target_pairs={{0,16},{4,20},{8,24},{12,28},{16,0},{20,4},{24,8},{28,12},{1,17},{... | collective-permute-start | bytes 602120 | tf_op jit(solution)/shard_map/ppermute | solution.py:314
  11.8 0.6 %collective-permute-start.7 = (bf16[784,128]{1,0:T(8,128)(2,1)}, bf16[784,128]{1,0:T(8,128)(2,1)S(1)}, u32[]{:S(2)}, u32[]{:S(2)}) collective-permute-start(bf16[784,128]{1,0:T(8,128)(2,1)} %get-tuple-element.29), channel_id=1, source_target_pairs={{0,12},{4,8},{8,4},{12,0},{16,28},{20,24},{24,20},{28,16},{1,13},{... | collective-permute-start | bytes 602120 | tf_op jit(solution)/shard_map/ppermute | solution.py:314
  12.5 0.4 collective-permute-start.8
  12.9 3.6 %collective-permute-done.1.refs_3_ = bf16[784,128]{1,0:T(8,128)(2,1)S(1)} collective-permute-done((bf16[784,128]{1,0:T(8,128)(2,1)}, bf16[784,128]{1,0:T(8,128)(2,1)S(1)}, u32[]{:S(2)}, u32[]{:S(2)}) %collective-permute-start.1) | collective-permute-done | bytes 200736 | tf_op jit(solution)/shard_map/ppermute | solution.py:314
  16.6 0.9 %cot.1 = (bf16[1088,128]{1,0:T(8,128)(2,1)S(1)}, bf16[640,128]{1,0:T(8,128)(2,1)S(1)}, bf16[640,128]{1,0:T(8,128)(2,1)S(1)}, bf16[640,128]{1,0:T(8,128)(2,1)S(1)}) custom-call(s32[1,8]{1,0:T(1,128)S(1)} %copy-done.1, bf16[272,2048]{1,0:T(8,128)(2,1)S(1)} %copy-done, bf16[784,128]{1,0:T(8,128)(2,1)S(1)} %collective-permute-done.refs_2_, ...), custom_call_target="tpu_custom_call" | custom-call | bytes 1540096 | tf_op jit(solution)/shard_map/cot/pallas_call | solution.py:363
  17.6 4.1 %collective-permute-done.5.refs_4_ = bf16[784,128]{1,0:T(8,128)(2,1)S(1)} collective-permute-done((bf16[784,128]{1,0:T(8,128)(2,1)}, bf16[784,128]{1,0:T(8,128)(2,1)S(1)}, u32[]{:S(2)}, u32[]{:S(2)}) %collective-permute-start.5) | collective-permute-done | bytes 200736 | tf_op jit(solution)/shard_map/ppermute | solution.py:314
  21.7 1.5 %collective-permute-start.2 = (bf16[640,128]{1,0:T(8,128)(2,1)S(1)}, bf16[640,128]{1,0:T(8,128)(2,1)S(1)}, u32[]{:S(2)}, u32[]{:S(2)}) collective-permute-start(bf16[640,128]{1,0:T(8,128)(2,1)S(1)} %get-tuple-element.23), channel_id=1, source_target_pairs={{0,8},{4,12},{8,0},{12,4},{16,24},{20,28},{24,16},{28,20},{1,9},{5... | collective-permute-start | bytes 491528 | tf_op jit(solution)/shard_map/ppermute | solution.py:314
  23.2 0.5 collective-permute-start.3
  23.7 1.4 %collective-permute-done.7.refs_6_ = bf16[784,128]{1,0:T(8,128)(2,1)S(1)} collective-permute-done((bf16[784,128]{1,0:T(8,128)(2,1)}, bf16[784,128]{1,0:T(8,128)(2,1)S(1)}, u32[]{:S(2)}, u32[]{:S(2)}) %collective-permute-start.7) | collective-permute-done | bytes 200736 | tf_op jit(solution)/shard_map/ppermute | solution.py:314
  25.2 4.8 %attend.1 = (bf16[1040,128]{1,0:T(8,128)(2,1)S(1)}, bf16[1040,128]{1,0:T(8,128)(2,1)S(1)}) custom-call(s32[8]{0:T(128)S(1)} %copy-done.3, bf16[784,128]{1,0:T(8,128)(2,1)S(1)} %copy-done.2, bf16[784,128]{1,0:T(8,128)(2,1)S(1)} %collective-permute-done.refs_2_, bf16[784,128]{1,0:T(8,128)(2,1)S(1)} %collective-permute-done.1.refs_3_, ...), custom_call_target="tpu_custom_call" | custom-call | flops 1073741824 | bytes 1064960 | tf_op jit(solution)/shard_map/attend/pallas_call | solution.py:385
  30.0 3.3 %collective-permute-start.14 = (bf16[1040,128]{1,0:T(8,128)(2,1)S(1)}, bf16[1040,128]{1,0:T(8,128)(2,1)S(1)}, u32[]{:S(2)}, u32[]{:S(2)}) collective-permute-start(bf16[1040,128]{1,0:T(8,128)(2,1)S(1)} %get-tuple-element.34.x_ref), channel_id=1, source_target_pairs={{0,20},{4,16},{8,28},{12,24},{16,4},{20,0},{24,12},{28,8},{1,21},{... | collective-permute-start | bytes 798728 | tf_op jit(solution)/shard_map/ppermute | solution.py:314
  33.3 0.2 collective-permute-start.13
  33.6 1.5 %collective-permute-start.12 = (bf16[1040,128]{1,0:T(8,128)(2,1)S(1)}, bf16[1040,128]{1,0:T(8,128)(2,1)S(1)}, u32[]{:S(2)}, u32[]{:S(2)}) collective-permute-start(bf16[1040,128]{1,0:T(8,128)(2,1)S(1)} %get-tuple-element.32.refs_3_.refs_1_.refs_2_), channel_id=1, source_target_pairs={{0,16},{4,20},{8,24},{12,28},{16,0},{20,4},{24,8},{28,12},{1,17},{... | collective-permute-start | bytes 798728 | tf_op jit(solution)/shard_map/ppermute | solution.py:314
  35.2 1.6 %collective-permute-start.10 = (bf16[3,448,128]{2,1,0:T(8,128)(2,1)S(1)}, bf16[3,448,128]{2,1,0:T(8,128)(2,1)S(1)}, u32[]{:S(2)}, u32[]{:S(2)}) collective-permute-start(bf16[3,448,128]{2,1,0:T(8,128)(2,1)S(1)} %stack.1), channel_id=1, source_target_pairs={{0,1},{1,0},{2,3},{3,2},{4,5},{5,4},{6,7},{7,6},{8,9},{9,8},{10,11... | collective-permute-start | bytes 1032200 | tf_op jit(solution)/shard_map/ppermute | solution.py:320
  36.8 3.3 %collective-permute-done.14.refs_5_.refs_6_ = bf16[1040,128]{1,0:T(8,128)(2,1)S(1)} collective-permute-done((bf16[1040,128]{1,0:T(8,128)(2,1)S(1)}, bf16[1040,128]{1,0:T(8,128)(2,1)S(1)}, u32[]{:S(2)}, u32[]{:S(2)}) %collective-permute-start.14) | collective-permute-done | bytes 266272 | tf_op jit(solution)/shard_map/ppermute | solution.py:314
  40.2 2.4 %collective-permute-done.13.refs_4_.refs_5_ = bf16[1040,128]{1,0:T(8,128)(2,1)S(1)} collective-permute-done((bf16[1040,128]{1,0:T(8,128)(2,1)S(1)}, bf16[1040,128]{1,0:T(8,128)(2,1)S(1)}, u32[]{:S(2)}, u32[]{:S(2)}) %collective-permute-start.13) | collective-permute-done | bytes 266272 | tf_op jit(solution)/shard_map/ppermute | solution.py:314
  42.7 0.4 collective-permute-start.17
  43.1 2.9 %collective-permute-done.11.refs_2_.refs_0_.refs_3_ = bf16[1040,128]{1,0:T(8,128)(2,1)S(1)} collective-permute-done((bf16[1040,128]{1,0:T(8,128)(2,1)S(1)}, bf16[1040,128]{1,0:T(8,128)(2,1)S(1)}, u32[]{:S(2)}, u32[]{:S(2)}) %collective-permute-start.11) | collective-permute-done | bytes 266272 | tf_op jit(solution)/shard_map/ppermute | solution.py:314
  46.0 0.8 %collective-permute-done.12.refs_3_.refs_1_.refs_4_ = bf16[1040,128]{1,0:T(8,128)(2,1)S(1)} collective-permute-done((bf16[1040,128]{1,0:T(8,128)(2,1)S(1)}, bf16[1040,128]{1,0:T(8,128)(2,1)S(1)}, u32[]{:S(2)}, u32[]{:S(2)}) %collective-permute-start.12) | collective-permute-done | bytes 266272 | tf_op jit(solution)/shard_map/ppermute | solution.py:314
  46.8 1.8 %collective-permute-start.16 = (bf16[1040,128]{1,0:T(8,128)(2,1)S(1)}, bf16[1040,128]{1,0:T(8,128)(2,1)S(1)}, u32[]{:S(2)}, u32[]{:S(2)}) collective-permute-start(bf16[1040,128]{1,0:T(8,128)(2,1)S(1)} %late.1), channel_id=1, source_target_pairs={{0,4},{4,0},{8,12},{12,8},{16,20},{20,16},{24,28},{28,24},{1,5},{5... | collective-permute-start | bytes 798728 | tf_op jit(solution)/shard_map/ppermute | solution.py:314
  48.6 0.6 %turn.1 = (bf16[256,1088]{1,0:T(8,128)(2,1)S(1)}, bf16[256,1088]{1,0:T(8,128)(2,1)S(1)}) custom-call(bf16[1088,128]{1,0:T(8,128)(2,1)S(1)} %get-tuple-element.22.refs_0_, bf16[640,128]{1,0:T(8,128)(2,1)S(1)} %collective-permute-done.2.refs_0_.refs_1_, bf16[640,128]{1,0:T(8,128)(2,1)S(1)} %collective-permute-done.3.refs_1_.refs_2_, ...), custom_call_target="tpu_custom_call" | custom-call | bytes 2228224 | tf_op jit(solution)/shard_map/turn/pallas_call | solution.py:409
  49.1 0.6 %grad_other_near.1 = bf16[256,640]{1,0:T(8,128)(2,1)S(1)} custom-call(bf16[256,1088]{1,0:T(8,128)(2,1)S(1)} %get-tuple-element.35.refs_0_, bf16[1040,128]{1,0:T(8,128)(2,1)S(1)} %get-tuple-element.32.refs_3_.refs_1_.refs_2_, bf16[1040,128]{1,0:T(8,128)(2,1)S(1)} %collective-permute-done.11.refs_2_.refs_0_.refs_3_, ...), custom_call_target="tpu_custom_call" | custom-call | flops 356515840 | bytes 655360 | tf_op jit(solution)/shard_map/grad_other_near/pallas_call | solution.py:419
  49.9 0.6 %grad_own_near.1.refs_4_.refs_0_ = f32[256,640]{1,0:T(8,128)S(1)} custom-call(bf16[256,1088]{1,0:T(8,128)(2,1)S(1)} %get-tuple-element.33.refs_0_, bf16[1040,128]{1,0:T(8,128)(2,1)S(1)} %get-tuple-element.32.refs_3_.refs_1_.refs_2_, bf16[1040,128]{1,0:T(8,128)(2,1)S(1)} %collective-permute-done.11.refs_2_.refs_0_.refs_3_, ...), custom_call_target="tpu_custom_call" | custom-call | flops 356515840 | bytes 1310720 | tf_op jit(solution)/shard_map/grad_own_near/pallas_call | solution.py:419
  50.5 1.5 %collective-permute-done.18.refs_3_.refs_6_ = bf16[1040,128]{1,0:T(8,128)(2,1)S(1)} collective-permute-done((bf16[1040,128]{1,0:T(8,128)(2,1)S(1)}, bf16[1040,128]{1,0:T(8,128)(2,1)S(1)}, u32[]{:S(2)}, u32[]{:S(2)}) %collective-permute-start.18) | collective-permute-done | bytes 266272 | tf_op jit(solution)/shard_map/ppermute | solution.py:314
  52.0 0.5 grad_other_far.1
  52.6 0.5 grad_own_far.1.refs_2_
  53.1 1.0 %near.1 = (bf16[256,1024]{1,0:T(8,128)(2,1)}, f32[256,1024]{1,0:T(8,128)}) custom-call(f32[256,640]{1,0:T(8,128)S(1)} %grad_own_near.1.refs_4_.refs_0_, bf16[256,640]{1,0:T(8,128)(2,1)S(1)} %collective-permute-done.15.refs_1_, bf16[1040,128]{1,0:T(8,128)(2,1)S(1)} %get-tuple-element.32.refs_3_.refs_1_.refs_2_, ...), custom_call_target="tpu_custom_call" | custom-call | bytes 3145728 | tf_op jit(solution)/shard_map/near/pallas_call | solution.py:435
  54.1 0.9 %last.1 = (bf16[256,1024]{1,0:T(8,128)(2,1)}, f32[256,1024]{1,0:T(8,128)}) custom-call(f32[256,640]{1,0:T(8,128)S(1)} %grad_own_near.1.refs_4_.refs_0_, bf16[256,640]{1,0:T(8,128)(2,1)S(1)} %collective-permute-done.15.refs_1_, f32[256,384]{1,0:T(8,128)S(1)} %grad_own_far.1.refs_2_, ...), custom_call_target="tpu_custom_call", output_to_operand_aliasing={{0}: (7, {}), {1}: (8, {})} | custom-call | bytes 3145728 | tf_op jit(solution)/shard_map/last/pallas_call | solution.py:444
  (29 shorter events, 0.7 us)
Async XLA Ops:
  2.5 14.1 %copy-start = (bf16[272,2048]{1,0:T(8,128)(2,1)S(1)}, bf16[272,2048]{1,0:T(8,128)(2,1)}, u32[]{:S(2)}) copy-start(bf16[272,2048]{1,0:T(8,128)(2,1)} %refs_1_.4) | copy-start | bytes 3342340
  2.5 14.1 %copy-start.1 = (s32[1,8]{1,0:T(1,128)S(1)}, s32[1,8]{1,0:T(1,128)}, u32[]{:S(2)}) copy-start(s32[1,8]{1,0:T(1,128)} %refs_0_.5) | copy-start | bytes 100
  2.5 10.0 %collective-permute-start = (bf16[784,128]{1,0:T(8,128)(2,1)}, bf16[784,128]{1,0:T(8,128)(2,1)S(1)}, u32[]{:S(2)}, u32[]{:S(2)}) collective-permute-start(bf16[784,128]{1,0:T(8,128)(2,1)} %get-tuple-element.20), channel_id=1, source_target_pairs={{0,24},{4,28},{8,16},{12,20},{16,8},{20,12},{24,0},{28,4},{1,25},{... | collective-permute-start | bytes 602120 | tf_op jit(solution)/shard_map/ppermute | solution.py:314
  6.5 10.1 %collective-permute-start.1 = (bf16[784,128]{1,0:T(8,128)(2,1)}, bf16[784,128]{1,0:T(8,128)(2,1)S(1)}, u32[]{:S(2)}, u32[]{:S(2)}) collective-permute-start(bf16[784,128]{1,0:T(8,128)(2,1)} %get-tuple-element.21), channel_id=1, source_target_pairs={{0,28},{4,24},{8,20},{12,16},{16,12},{20,8},{24,4},{28,0},{1,29},{... | collective-permute-start | bytes 602120 | tf_op jit(solution)/shard_map/ppermute | solution.py:314
  9.1 16.1 %copy-start.2 = (bf16[784,128]{1,0:T(8,128)(2,1)S(1)}, bf16[784,128]{1,0:T(8,128)(2,1)}, u32[]{:S(2)}) copy-start(bf16[784,128]{1,0:T(8,128)(2,1)} %get-tuple-element.26.refs_1_) | copy-start | bytes 602116
  9.1 16.1 %copy-start.3 = (s32[8]{0:T(128)S(1)}, s32[8]{0:T(128)}, u32[]{:S(2)}) copy-start(s32[8]{0:T(128)} %refs_0_.7) | copy-start | bytes 100
  9.1 12.6 %collective-permute-start.5 = (bf16[784,128]{1,0:T(8,128)(2,1)}, bf16[784,128]{1,0:T(8,128)(2,1)S(1)}, u32[]{:S(2)}, u32[]{:S(2)}) collective-permute-start(bf16[784,128]{1,0:T(8,128)(2,1)} %get-tuple-element.27), channel_id=1, source_target_pairs={{0,8},{4,12},{8,0},{12,4},{16,24},{20,28},{24,16},{28,20},{1,9},{5... | collective-permute-start | bytes 602120 | tf_op jit(solution)/shard_map/ppermute | solution.py:314
  10.3 12.9 %collective-permute-start.6 = (bf16[784,128]{1,0:T(8,128)(2,1)}, bf16[784,128]{1,0:T(8,128)(2,1)S(1)}, u32[]{:S(2)}, u32[]{:S(2)}) collective-permute-start(bf16[784,128]{1,0:T(8,128)(2,1)} %get-tuple-element.28), channel_id=1, source_target_pairs={{0,16},{4,20},{8,24},{12,28},{16,0},{20,4},{24,8},{28,12},{1,17},{... | collective-permute-start | bytes 602120 | tf_op jit(solution)/shard_map/ppermute | solution.py:314
  11.8 13.3 %collective-permute-start.7 = (bf16[784,128]{1,0:T(8,128)(2,1)}, bf16[784,128]{1,0:T(8,128)(2,1)S(1)}, u32[]{:S(2)}, u32[]{:S(2)}) collective-permute-start(bf16[784,128]{1,0:T(8,128)(2,1)} %get-tuple-element.29), channel_id=1, source_target_pairs={{0,12},{4,8},{8,4},{12,0},{16,28},{20,24},{24,20},{28,16},{1,13},{... | collective-permute-start | bytes 602120 | tf_op jit(solution)/shard_map/ppermute | solution.py:314
  12.5 12.7 %collective-permute-start.8 = (bf16[784,128]{1,0:T(8,128)(2,1)}, bf16[784,128]{1,0:T(8,128)(2,1)S(1)}, u32[]{:S(2)}, u32[]{:S(2)}) collective-permute-start(bf16[784,128]{1,0:T(8,128)(2,1)} %get-tuple-element.30), channel_id=1, source_target_pairs={{0,20},{4,16},{8,28},{12,24},{16,4},{20,0},{24,12},{28,8},{1,21},{... | collective-permute-start | bytes 602120 | tf_op jit(solution)/shard_map/ppermute | solution.py:314
  16.5 8.6 %collective-permute-start.9 = (bf16[784,128]{1,0:T(8,128)(2,1)}, bf16[784,128]{1,0:T(8,128)(2,1)S(1)}, u32[]{:S(2)}, u32[]{:S(2)}) collective-permute-start(bf16[784,128]{1,0:T(8,128)(2,1)} %get-tuple-element.31), channel_id=1, source_target_pairs={{0,4},{4,0},{8,12},{12,8},{16,20},{20,16},{24,28},{28,24},{1,5},{5... | collective-permute-start | bytes 602120 | tf_op jit(solution)/shard_map/ppermute | solution.py:314
  21.7 11.8 %collective-permute-start.2 = (bf16[640,128]{1,0:T(8,128)(2,1)S(1)}, bf16[640,128]{1,0:T(8,128)(2,1)S(1)}, u32[]{:S(2)}, u32[]{:S(2)}) collective-permute-start(bf16[640,128]{1,0:T(8,128)(2,1)S(1)} %get-tuple-element.23), channel_id=1, source_target_pairs={{0,8},{4,12},{8,0},{12,4},{16,24},{20,28},{24,16},{28,20},{1,9},{5... | collective-permute-start | bytes 491528 | tf_op jit(solution)/shard_map/ppermute | solution.py:314
  23.2 10.4 %collective-permute-start.3 = (bf16[640,128]{1,0:T(8,128)(2,1)S(1)}, bf16[640,128]{1,0:T(8,128)(2,1)S(1)}, u32[]{:S(2)}, u32[]{:S(2)}) collective-permute-start(bf16[640,128]{1,0:T(8,128)(2,1)S(1)} %get-tuple-element.24), channel_id=1, source_target_pairs={{0,16},{4,20},{8,24},{12,28},{16,0},{20,4},{24,8},{28,12},{1,17},{... | collective-permute-start | bytes 491528 | tf_op jit(solution)/shard_map/ppermute | solution.py:314
  25.1 10.0 %collective-permute-start.4 = (bf16[640,128]{1,0:T(8,128)(2,1)S(1)}, bf16[640,128]{1,0:T(8,128)(2,1)S(1)}, u32[]{:S(2)}, u32[]{:S(2)}) collective-permute-start(bf16[640,128]{1,0:T(8,128)(2,1)S(1)} %get-tuple-element.25), channel_id=1, source_target_pairs={{0,24},{4,28},{8,16},{12,20},{16,8},{20,12},{24,0},{28,4},{1,25},{... | collective-permute-start | bytes 491528 | tf_op jit(solution)/shard_map/ppermute | solution.py:314
  30.0 10.2 %collective-permute-start.14 = (bf16[1040,128]{1,0:T(8,128)(2,1)S(1)}, bf16[1040,128]{1,0:T(8,128)(2,1)S(1)}, u32[]{:S(2)}, u32[]{:S(2)}) collective-permute-start(bf16[1040,128]{1,0:T(8,128)(2,1)S(1)} %get-tuple-element.34.x_ref), channel_id=1, source_target_pairs={{0,20},{4,16},{8,28},{12,24},{16,4},{20,0},{24,12},{28,8},{1,21},{... | collective-permute-start | bytes 798728 | tf_op jit(solution)/shard_map/ppermute | solution.py:314
  33.3 9.3 %collective-permute-start.13 = (bf16[1040,128]{1,0:T(8,128)(2,1)S(1)}, bf16[1040,128]{1,0:T(8,128)(2,1)S(1)}, u32[]{:S(2)}, u32[]{:S(2)}) collective-permute-start(bf16[1040,128]{1,0:T(8,128)(2,1)S(1)} %get-tuple-element.32.refs_3_.refs_1_.refs_2_), channel_id=1, source_target_pairs={{0,8},{4,12},{8,0},{12,4},{16,24},{20,28},{24,16},{28,20},{1,9},{5... | collective-permute-start | bytes 798728 | tf_op jit(solution)/shard_map/ppermute | solution.py:314
  33.5 12.5 %collective-permute-start.11 = (bf16[1040,128]{1,0:T(8,128)(2,1)S(1)}, bf16[1040,128]{1,0:T(8,128)(2,1)S(1)}, u32[]{:S(2)}, u32[]{:S(2)}) collective-permute-start(bf16[1040,128]{1,0:T(8,128)(2,1)S(1)} %get-tuple-element.34.x_ref), channel_id=1, source_target_pairs={{0,12},{4,8},{8,4},{12,0},{16,28},{20,24},{24,20},{28,16},{1,13},{... | collective-permute-start | bytes 798728 | tf_op jit(solution)/shard_map/ppermute | solution.py:314
  33.6 13.1 %collective-permute-start.12 = (bf16[1040,128]{1,0:T(8,128)(2,1)S(1)}, bf16[1040,128]{1,0:T(8,128)(2,1)S(1)}, u32[]{:S(2)}, u32[]{:S(2)}) collective-permute-start(bf16[1040,128]{1,0:T(8,128)(2,1)S(1)} %get-tuple-element.32.refs_3_.refs_1_.refs_2_), channel_id=1, source_target_pairs={{0,16},{4,20},{8,24},{12,28},{16,0},{20,4},{24,8},{28,12},{1,17},{... | collective-permute-start | bytes 798728 | tf_op jit(solution)/shard_map/ppermute | solution.py:314
  35.2 13.4 %collective-permute-start.10 = (bf16[3,448,128]{2,1,0:T(8,128)(2,1)S(1)}, bf16[3,448,128]{2,1,0:T(8,128)(2,1)S(1)}, u32[]{:S(2)}, u32[]{:S(2)}) collective-permute-start(bf16[3,448,128]{2,1,0:T(8,128)(2,1)S(1)} %stack.1), channel_id=1, source_target_pairs={{0,1},{1,0},{2,3},{3,2},{4,5},{5,4},{6,7},{7,6},{8,9},{9,8},{10,11... | collective-permute-start | bytes 1032200 | tf_op jit(solution)/shard_map/ppermute | solution.py:320
  40.2 11.8 %collective-permute-start.18 = (bf16[1040,128]{1,0:T(8,128)(2,1)S(1)}, bf16[1040,128]{1,0:T(8,128)(2,1)S(1)}, u32[]{:S(2)}, u32[]{:S(2)}) collective-permute-start(bf16[1040,128]{1,0:T(8,128)(2,1)S(1)} %collective-permute-done.14.refs_5_.refs_6_), channel_id=1, source_target_pairs={{0,8},{4,12},{8,0},{12,4},{16,24},{20,28},{24,16},{28,20},{1,9},{5... | collective-permute-start | bytes 798728 | tf_op jit(solution)/shard_map/ppermute | solution.py:314
  42.7 9.3 %collective-permute-start.17 = (bf16[1040,128]{1,0:T(8,128)(2,1)S(1)}, bf16[1040,128]{1,0:T(8,128)(2,1)S(1)}, u32[]{:S(2)}, u32[]{:S(2)}) collective-permute-start(bf16[1040,128]{1,0:T(8,128)(2,1)S(1)} %collective-permute-done.13.refs_4_.refs_5_), channel_id=1, source_target_pairs={{0,16},{4,20},{8,24},{12,28},{16,0},{20,4},{24,8},{28,12},{1,17},{... | collective-permute-start | bytes 798728 | tf_op jit(solution)/shard_map/ppermute | solution.py:314
  46.8 5.2 %collective-permute-start.16 = (bf16[1040,128]{1,0:T(8,128)(2,1)S(1)}, bf16[1040,128]{1,0:T(8,128)(2,1)S(1)}, u32[]{:S(2)}, u32[]{:S(2)}) collective-permute-start(bf16[1040,128]{1,0:T(8,128)(2,1)S(1)} %late.1), channel_id=1, source_target_pairs={{0,4},{4,0},{8,12},{12,8},{16,20},{20,16},{24,28},{28,24},{1,5},{5... | collective-permute-start | bytes 798728 | tf_op jit(solution)/shard_map/ppermute | solution.py:314
  49.8 3.3 %collective-permute-start.15 = (bf16[256,640]{1,0:T(8,128)(2,1)S(1)}, bf16[256,640]{1,0:T(8,128)(2,1)S(1)}, u32[]{:S(2)}, u32[]{:S(2)}) collective-permute-start(bf16[256,640]{1,0:T(8,128)(2,1)S(1)} %grad_other_near.1), channel_id=1, source_target_pairs={{0,4},{4,0},{8,12},{12,8},{16,20},{20,16},{24,28},{28,24},{1,5},{5... | collective-permute-start | bytes 983048 | tf_op jit(solution)/shard_map/ppermute | solution.py:314
  52.5 1.6 %collective-permute-start.19 = (bf16[256,384]{1,0:T(8,128)(2,1)S(1)}, bf16[256,384]{1,0:T(8,128)(2,1)S(1)}, u32[]{:S(2)}, u32[]{:S(2)}) collective-permute-start(bf16[256,384]{1,0:T(8,128)(2,1)S(1)} %grad_other_far.1), channel_id=1, source_target_pairs={{0,4},{4,0},{8,12},{12,8},{16,20},{20,16},{24,28},{28,24},{1,5},{5... | collective-permute-start | bytes 589832 | tf_op jit(solution)/shard_map/ppermute | solution.py:314

commit v11 on v9

--- a/solution.py
+++ b/solution.py
@@ -72,6 +72,10 @@
         tiled=True,
     )
     return (attended, disc_grad)
+
+
+def chip_bits(m, side):
+    return m if m in (0, 3) else jnp.where(side == 0, m, 3 - m)
 
 
 def cot_kernel(n, tile, lo, off_hbm, cot_hbm, *refs):
@@ -103,7 +107,8 @@
     units = cols // HD
     for m, out_ref in enumerate(outs):
         rows, first = (part, low) if m else (all_rows, 0)
-        for i, block in enumerate((2 * (chip ^ m) + side, 2 * (chip ^ m) + 1 - side)):
+        there = chip ^ chip_bits(m, side)
+        for i, block in enumerate((2 * there + side, 2 * there + 1 - side)):
             for u in range(units):
                 at = (i * units + u) * rows
                 lanes = pl.ds(pl.multiple_of(block * cols + u * HD, HD), HD)
@@ -210,18 +215,20 @@
 def turn_kernel(lo, clip_rows, order, own_in, *refs):
     pieces, (swapped_ref, own_ref, other_ref, whole) = refs[:-4], refs[-4:]
     plane = lax.rem(lax.axis_index("head"), 2)
-    chip = lax.axis_index("tm") // 2
+    own = lax.axis_index("tm")
+    chip, side = own // 2, lax.rem(own, 2)
     chips, all_rows, width = whole.shape
     part = all_rows - lo
     for u in range(width // HD):
         lanes = slice(u * HD, (u + 1) * HD)
         whole[0, :, lanes] = own_in[u * all_rows : (u + 1) * all_rows, :]
         for m, ref in zip(order, pieces):
+            at = chip_bits(m, side)
             a = ref[u * part : (u + 1) * part, :]
             b = swapped_ref[m - 1, u * lo : (u + 1) * lo, :]
-            whole[m, 0:lo, lanes] = jnp.where(plane == 0, a[:lo], b)
-            whole[m, lo:part, lanes] = jnp.where(plane == 0, a[lo:], a[: part - lo])
-            whole[m, part:all_rows, lanes] = jnp.where(plane == 0, b, a[part - lo :])
+            whole[at, 0:lo, lanes] = jnp.where(plane == 0, a[:lo], b)
+            whole[at, lo:part, lanes] = jnp.where(plane == 0, a[lo:], a[: part - lo])
+            whole[at, part:all_rows, lanes] = jnp.where(plane == 0, b, a[part - lo :])
     for i, out_ref in enumerate((own_ref, other_ref)):
         lanes = slice(i * width // 2, (i + 1) * width // 2)
         rows = [whole[chip ^ c, clip_rows:all_rows, lanes] for c in range(chips)]
@@ -246,8 +253,14 @@
     out_ref[...] = grad_part(turned_ref, refs[:heads], rows, copies).astype(out_ref.dtype)
 
 
+NEAR = ((0, 0), (3, 5), (4, 2), (2, 4), (5, 3))
+FAR = ((1, 1), (6, 6), (7, 7))
+THERE = (5, 2, 1, 4, 3, 0, 7, 6)
+
+
 def store_columns(tok, heads, sums, att_hbm, out_hbm, total, sems):
     own = lax.axis_index("tm")
+    side = lax.rem(own, 2)
     at = pl.multiple_of(own // 2 * tok, tok)
     moves = []
 
@@ -255,40 +268,39 @@
         moves.append(pltpu.make_async_copy(a, b, sems.at[len(moves)]))
         moves[-1].start()
 
-    def lanes(k):
-        return pl.ds(pl.multiple_of((own ^ k) * HD, HD), HD)
-
-    for k, ref in heads:
-        move(ref.at[pl.ds(at, tok), :], att_hbm.at[:, lanes(k)])
-    for i, (k, (mine, m), (got, g)) in enumerate(sums):
+    def lanes(bits):
+        return pl.ds(pl.multiple_of((own ^ jnp.where(side == 0, *bits)) * HD, HD), HD)
+
+    for bits, ref in heads:
+        move(ref.at[pl.ds(at, tok), :], att_hbm.at[:, lanes(bits)])
+    for i, (bits, (mine, m), (got, g)) in enumerate(sums):
         columns = got[:, g * HD : (g + 1) * HD].astype(jnp.float32)
         total[i] = mine[:, m * HD : (m + 1) * HD] + columns
-        move(total.at[i], out_hbm.at[:, lanes(k)])
+        move(total.at[i], out_hbm.at[:, lanes(bits)])
     for x in moves:
         x.wait()
 
 
-def near_kernel(tok, near, own_near, got_near, *refs):
-    heads, outs = refs[: len(near)], refs[len(near) :]
+def near_kernel(tok, own_near, got_near, *refs):
+    n = len(NEAR)
+    heads, outs = refs[:n], refs[n:]
+    sums = [(NEAR[i], (own_near, i), (got_near, THERE[i])) for i in range(n) if THERE[i] < n]
+    store_columns(tok, zip(NEAR, heads), sums, *outs)
+
+
+def last_kernel(tok, own_near, got_near, own_far, got_far, *refs):
+    n = len(NEAR)
+    heads, outs = refs[: len(FAR)], refs[len(FAR) + 2 :]
+
+    def column(near, far, i):
+        return (near, i) if i < n else (far, i - n)
+
     sums = [
-        (k, (own_near, i), (got_near, near.index(k ^ 1)))
-        for i, k in enumerate(near)
-        if k ^ 1 in near
+        (bits, column(own_near, own_far, i), column(got_near, got_far, THERE[i]))
+        for i, bits in enumerate(NEAR + FAR)
+        if i >= n or THERE[i] >= n
     ]
-    store_columns(tok, zip(near, heads), sums, *outs)
-
-
-def last_kernel(tok, near, far, own_near, got_near, own_far, got_far, *refs):
-    heads, outs = refs[: len(far)], refs[len(far) + 2 :]
-    sums = [
-        (k, (own_near, i), (got_far, far.index(k ^ 1)))
-        for i, k in enumerate(near)
-        if k ^ 1 in far
-    ]
-    for i, k in enumerate(far):
-        got = (got_far, far.index(k ^ 1)) if k ^ 1 in far else (got_near, near.index(k ^ 1))
-        sums.append((k, (own_far, i), got))
-    store_columns(tok, zip(far, heads), sums, *outs)
+    store_columns(tok, zip(FAR, heads), sums, *outs)
 
 
 def head_body(query_rows, key_rows, value_rows, frame_counts, history, offsets, cotangent):
@@ -310,8 +322,9 @@
     hbm = pl.BlockSpec(memory_space=pl.ANY)
     bf16 = jnp.bfloat16
 
-    def swap(x, bit):
-        return lax.ppermute(x, "tm", [(i, i ^ bit) for i in range(n)])
+    def swap(x, even, odd=None):
+        bits = (even, even if odd is None else odd)
+        return lax.ppermute(x, "tm", [(i, i ^ bits[i % 2]) for i in range(n)])
 
     def swap_plane(x, bit):
         pairs = [
@@ -372,8 +385,7 @@
             pltpu.SemaphoreType.DMA((2,)),
         ),
     )(offsets, cotangent, arrived[6], arrived[7])
-    moved = {m: swap(cots[m], 2 * m) for m in reversed(chips[1:])}
-    cots = [cots[0]] + [moved[m] for m in chips[1:]]
+    cots = [cots[0], swap(cots[1], 2, 4), swap(cots[2], 4, 2), swap(cots[3], 6)]
     counts = (
         pltpu.VMEM((n, length, HD), bf16),
         pltpu.VMEM((n, tok, HD), bf16),
@@ -400,10 +412,12 @@
         0,
     )(*[cots[m] for m in stack_order], same)
     cot_swapped = swap_plane(cot_rest, 0)
-    x_same, y_cross = swap(same, 2), swap(cross, 4 ^ 1)
-    y_same, x_cross = swap(same, 4), swap(cross, 2 ^ 1)
-    far_same, far_cross = swap(x_same, 4), swap(y_cross, 2)
-    (late_cross,) = call(late_kernel, "late", [head_shape], [vmem] + [hbm] * 2, 0)(cross, x_cross, y_same)
+    first_same, first_cross = swap(same, 2, 4), swap(cross, 3, 5)
+    second_same, second_cross = swap(same, 4, 2), swap(cross, 5, 3)
+    far_same, far_cross = swap(first_same, 4, 2), swap(first_cross, 2, 4)
+    (late_cross,) = call(late_kernel, "late", [head_shape], [vmem] + [hbm] * 2, 0)(
+        cross, second_cross, second_same
+    )
     c_cross = swap(late_cross, 1)
 
     turned_own, turned_other = call(
@@ -425,15 +439,15 @@
         )(turned, *heads, *behind)
         return out
 
-    near, near_bits = [same, x_cross, y_same, x_same, y_cross], [0, 3, 4, 2, 5]
-    far, far_bits = [c_cross, far_same, far_cross], [1, 6, 7]
+    near = [same, second_cross, second_same, first_same, first_cross]
+    far = [c_cross, far_same, far_cross]
     whole = [((tok, width), bf16), ((cols, width), jnp.float32)]
     got_near = swap(grad(turned_other, near, bf16, "grad_other_near"), 1)
     own_near = grad(turned_own, near, jnp.float32, "grad_own_near")
     got_far = swap(grad(turned_other, far, bf16, "grad_other_far", (own_near,)), 1)
     own_far = grad(turned_own, far, jnp.float32, "grad_own_far")
     halfway = call(
-        lambda *refs: near_kernel(tok, near_bits, *refs),
+        lambda *refs: near_kernel(tok, *refs),
         "near",
         whole,
         [vmem] * (2 + len(near)),
@@ -442,7 +456,7 @@
         out_spec=hbm,
     )(own_near, got_near, *near)
     return call(
-        lambda *refs: last_kernel(tok, near_bits, far_bits, *refs),
+        lambda *refs: last_kernel(tok, *refs),
         "last",
         whole,
         [vmem] * (4 + len(far)) + [hbm] * 2,

time: 55.4 us -> 55.3 us (level)
  waiting for transfers between devices: 20.6 us -> 20 us
    ppermute x19, waiting for transfers between devices: 20.6 us -> 20 us  [swap(): return lax.ppermute(x, 'tm', [(i, i ^ bits[i % 2]) for i in range(n)])]
  transfers between devices with their start and end apart: 20 -> 20, of which waited for: 8 -> 9; matrix products, arithmetic and copies ran while one was open for 0% -> 0% of each run, Pallas kernels for 22% -> 22%
where the time goes in v11:
time: 55.3 us; the launch traced here: 55.1 us
  waiting for transfers between devices  20 us (36%)
  starting transfers between devices  19.3 us (35%)
  Pallas kernels  14.9 us (27%)
  between operations  0.78 us (1%)
    ppermute x19, waiting for transfers between devices, swap(): return lax.ppermute(x, 'tm', [(i, i ^ bits[i % 2]) for i in range(n)])  20 us
    ppermute x19, starting transfers between devices, swap(): return lax.ppermute(x, 'tm', [(i, i ^ bits[i % 2]) for i in range(n)])  17.7 us
    pallas_call x1, Pallas kernels, head_body(): call(lambda *refs: attend_kernel(n, tok, [0] + order, *refs), 'attend', [...  4.81 us
    pallas_call x2, Pallas kernels, pack(): call(lambda *refs: pack_kernel(n, heads, *refs), name, [((length, HD), bf...  4.42 us
    pallas_call x4, Pallas kernels, grad(): call(lambda *refs: grad_kernel(rows, half, len(heads), *refs), name, [((c...  2.24 us
    ppermute x1, starting transfers between devices, swap_plane(): return lax.ppermute(x, ('tm', 'head'), pairs)  1.64 us
  transfers between devices with their start and end apart: 20, of which 9 were waited for; matrix products, arithmetic and copies ran while one was open for 0% of the time, Pallas kernels for 22%

profile of v11, /device:TPU:0, one launch (start us, length us, event | category | flops | bytes accessed | tf_op | source)
XLA Modules:
  0.0 55.1 jit_solution(14867102115441442494)
XLA Ops:
  0.6 1.9 %pack_first.1 = (bf16[784,128]{1,0:T(8,128)(2,1)}, bf16[784,128]{1,0:T(8,128)(2,1)}) custom-call(bf16[256,1024]{1,0:T(8,128)(2,1)} %refs_0_.6, bf16[256,1024]{1,0:T(8,128)(2,1)} %refs_1_.5, bf16[256,1024]{1,0:T(8,128)(2,1)} %refs_2_.3, bf16[2,1024]{1,0:T(2,128)(2,1)} %refs_3_.3), custom_call_target="tpu_custom_call" | custom-call | bytes 802816 | tf_op jit(solution)/shard_map/pack_first/pallas_call | solution.py:353
  2.5 4.0 %collective-permute-start = (bf16[784,128]{1,0:T(8,128)(2,1)}, bf16[784,128]{1,0:T(8,128)(2,1)S(1)}, u32[]{:S(2)}, u32[]{:S(2)}) collective-permute-start(bf16[784,128]{1,0:T(8,128)(2,1)} %get-tuple-element.20), channel_id=1, source_target_pairs={{0,24},{4,28},{8,16},{12,20},{16,8},{20,12},{24,0},{28,4},{1,25},{... | collective-permute-start | bytes 602120 | tf_op jit(solution)/shard_map/ppermute | solution.py:327
  6.5 2.6 %pack_rest.1 = (bf16[784,128]{1,0:T(8,128)(2,1)}, bf16[784,128]{1,0:T(8,128)(2,1)}, bf16[784,128]{1,0:T(8,128)(2,1)}, bf16[784,128]{1,0:T(8,128)(2,1)}, bf16[784...) custom-call(bf16[256,1024]{1,0:T(8,128)(2,1)} %refs_0_.6, bf16[256,1024]{1,0:T(8,128)(2,1)} %refs_1_.5, ...), custom_call_target="tpu_custom_call" | custom-call | bytes 2408448 | tf_op jit(solution)/shard_map/pack_rest/pallas_call | solution.py:353
  9.1 1.2 %collective-permute-start.5 = (bf16[784,128]{1,0:T(8,128)(2,1)}, bf16[784,128]{1,0:T(8,128)(2,1)S(1)}, u32[]{:S(2)}, u32[]{:S(2)}) collective-permute-start(bf16[784,128]{1,0:T(8,128)(2,1)} %get-tuple-element.27), channel_id=1, source_target_pairs={{0,8},{4,12},{8,0},{12,4},{16,24},{20,28},{24,16},{28,20},{1,9},{5... | collective-permute-start | bytes 602120 | tf_op jit(solution)/shard_map/ppermute | solution.py:327
  10.3 1.5 %collective-permute-start.6 = (bf16[784,128]{1,0:T(8,128)(2,1)}, bf16[784,128]{1,0:T(8,128)(2,1)S(1)}, u32[]{:S(2)}, u32[]{:S(2)}) collective-permute-start(bf16[784,128]{1,0:T(8,128)(2,1)} %get-tuple-element.28), channel_id=1, source_target_pairs={{0,16},{4,20},{8,24},{12,28},{16,0},{20,4},{24,8},{28,12},{1,17},{... | collective-permute-start | bytes 602120 | tf_op jit(solution)/shard_map/ppermute | solution.py:327
  11.8 0.6 %collective-permute-start.7 = (bf16[784,128]{1,0:T(8,128)(2,1)}, bf16[784,128]{1,0:T(8,128)(2,1)S(1)}, u32[]{:S(2)}, u32[]{:S(2)}) collective-permute-start(bf16[784,128]{1,0:T(8,128)(2,1)} %get-tuple-element.29), channel_id=1, source_target_pairs={{0,12},{4,8},{8,4},{12,0},{16,28},{20,24},{24,20},{28,16},{1,13},{... | collective-permute-start | bytes 602120 | tf_op jit(solution)/shard_map/ppermute | solution.py:327
  12.9 3.6 %collective-permute-done.1.refs_3_ = bf16[784,128]{1,0:T(8,128)(2,1)S(1)} collective-permute-done((bf16[784,128]{1,0:T(8,128)(2,1)}, bf16[784,128]{1,0:T(8,128)(2,1)S(1)}, u32[]{:S(2)}, u32[]{:S(2)}) %collective-permute-start.1) | collective-permute-done | bytes 200736 | tf_op jit(solution)/shard_map/ppermute | solution.py:327
  16.6 0.9 %cot.1 = (bf16[1088,128]{1,0:T(8,128)(2,1)S(1)}, bf16[640,128]{1,0:T(8,128)(2,1)S(1)}, bf16[640,128]{1,0:T(8,128)(2,1)S(1)}, bf16[640,128]{1,0:T(8,128)(2,1)S(1)}) custom-call(s32[1,8]{1,0:T(1,128)S(1)} %copy-done.1, bf16[272,2048]{1,0:T(8,128)(2,1)S(1)} %copy-done, bf16[784,128]{1,0:T(8,128)(2,1)S(1)} %collective-permute-done.refs_2_, ...), custom_call_target="tpu_custom_call" | custom-call | bytes 1540096 | tf_op jit(solution)/shard_map/cot/pallas_call | solution.py:376
  17.6 4.1 %collective-permute-done.5.refs_4_ = bf16[784,128]{1,0:T(8,128)(2,1)S(1)} collective-permute-done((bf16[784,128]{1,0:T(8,128)(2,1)}, bf16[784,128]{1,0:T(8,128)(2,1)S(1)}, u32[]{:S(2)}, u32[]{:S(2)}) %collective-permute-start.5) | collective-permute-done | bytes 200736 | tf_op jit(solution)/shard_map/ppermute | solution.py:327
  21.7 1.5 %collective-permute-start.2 = (bf16[640,128]{1,0:T(8,128)(2,1)S(1)}, bf16[640,128]{1,0:T(8,128)(2,1)S(1)}, u32[]{:S(2)}, u32[]{:S(2)}) collective-permute-start(bf16[640,128]{1,0:T(8,128)(2,1)S(1)} %get-tuple-element.23), channel_id=1, source_target_pairs={{0,24},{4,28},{8,16},{12,20},{16,8},{20,12},{24,0},{28,4},{1,25},{... | collective-permute-start | bytes 491528 | tf_op jit(solution)/shard_map/ppermute | solution.py:327
  23.2 1.9 %collective-permute-done.7.refs_6_ = bf16[784,128]{1,0:T(8,128)(2,1)S(1)} collective-permute-done((bf16[784,128]{1,0:T(8,128)(2,1)}, bf16[784,128]{1,0:T(8,128)(2,1)S(1)}, u32[]{:S(2)}, u32[]{:S(2)}) %collective-permute-start.7) | collective-permute-done | bytes 200736 | tf_op jit(solution)/shard_map/ppermute | solution.py:327
  25.1 0.5 collective-permute-start.4
  25.7 4.8 %attend.1 = (bf16[1040,128]{1,0:T(8,128)(2,1)S(1)}, bf16[1040,128]{1,0:T(8,128)(2,1)S(1)}) custom-call(s32[8]{0:T(128)S(1)} %copy-done.3, bf16[784,128]{1,0:T(8,128)(2,1)S(1)} %copy-done.2, bf16[784,128]{1,0:T(8,128)(2,1)S(1)} %collective-permute-done.refs_2_, bf16[784,128]{1,0:T(8,128)(2,1)S(1)} %collective-permute-done.1.refs_3_, ...), custom_call_target="tpu_custom_call" | custom-call | flops 1073741824 | bytes 1064960 | tf_op jit(solution)/shard_map/attend/pallas_call | solution.py:397
  30.5 1.6 %collective-permute-start.14 = (bf16[1040,128]{1,0:T(8,128)(2,1)S(1)}, bf16[1040,128]{1,0:T(8,128)(2,1)S(1)}, u32[]{:S(2)}, u32[]{:S(2)}) collective-permute-start(bf16[1040,128]{1,0:T(8,128)(2,1)S(1)} %get-tuple-element.34.x_ref), channel_id=1, source_target_pairs={{0,12},{4,16},{8,4},{12,24},{16,28},{20,0},{24,20},{28,8},{1,13},{... | collective-permute-start | bytes 798728 | tf_op jit(solution)/shard_map/ppermute | solution.py:327
  32.0 1.5 %collective-permute-start.13 = (bf16[1040,128]{1,0:T(8,128)(2,1)S(1)}, bf16[1040,128]{1,0:T(8,128)(2,1)S(1)}, u32[]{:S(2)}, u32[]{:S(2)}) collective-permute-start(bf16[1040,128]{1,0:T(8,128)(2,1)S(1)} %get-tuple-element.32.refs_3_.refs_1_.refs_2_), channel_id=1, source_target_pairs={{0,8},{4,20},{8,0},{12,28},{16,24},{20,4},{24,16},{28,12},{1,9},{5... | collective-permute-start | bytes 798728 | tf_op jit(solution)/shard_map/ppermute | solution.py:327
  33.7 0.7 %collective-permute-start.12 = (bf16[1040,128]{1,0:T(8,128)(2,1)S(1)}, bf16[1040,128]{1,0:T(8,128)(2,1)S(1)}, u32[]{:S(2)}, u32[]{:S(2)}) collective-permute-start(bf16[1040,128]{1,0:T(8,128)(2,1)S(1)} %get-tuple-element.32.refs_3_.refs_1_.refs_2_), channel_id=1, source_target_pairs={{0,16},{4,12},{8,24},{12,4},{16,0},{20,28},{24,8},{28,20},{1,17},{... | collective-permute-start | bytes 798728 | tf_op jit(solution)/shard_map/ppermute | solution.py:327
  34.5 1.6 %collective-permute-start.10 = (bf16[3,448,128]{2,1,0:T(8,128)(2,1)S(1)}, bf16[3,448,128]{2,1,0:T(8,128)(2,1)S(1)}, u32[]{:S(2)}, u32[]{:S(2)}) collective-permute-start(bf16[3,448,128]{2,1,0:T(8,128)(2,1)S(1)} %stack.1), channel_id=1, source_target_pairs={{0,1},{1,0},{2,3},{3,2},{4,5},{5,4},{6,7},{7,6},{8,9},{9,8},{10,11... | collective-permute-start | bytes 1032200 | tf_op jit(solution)/shard_map/ppermute | solution.py:333
  36.1 1.2 %collective-permute-done.14.refs_5_.refs_6_ = bf16[1040,128]{1,0:T(8,128)(2,1)S(1)} collective-permute-done((bf16[1040,128]{1,0:T(8,128)(2,1)S(1)}, bf16[1040,128]{1,0:T(8,128)(2,1)S(1)}, u32[]{:S(2)}, u32[]{:S(2)}) %collective-permute-start.14) | collective-permute-done | bytes 266272 | tf_op jit(solution)/shard_map/ppermute | solution.py:327
  37.3 1.5 %collective-permute-start.18 = (bf16[1040,128]{1,0:T(8,128)(2,1)S(1)}, bf16[1040,128]{1,0:T(8,128)(2,1)S(1)}, u32[]{:S(2)}, u32[]{:S(2)}) collective-permute-start(bf16[1040,128]{1,0:T(8,128)(2,1)S(1)} %collective-permute-done.14.refs_5_.refs_6_), channel_id=1, source_target_pairs={{0,8},{4,20},{8,0},{12,28},{16,24},{20,4},{24,16},{28,12},{1,9},{5... | collective-permute-start | bytes 798728 | tf_op jit(solution)/shard_map/ppermute | solution.py:327
  38.8 6.2 %collective-permute-done.13.refs_4_.refs_5_ = bf16[1040,128]{1,0:T(8,128)(2,1)S(1)} collective-permute-done((bf16[1040,128]{1,0:T(8,128)(2,1)S(1)}, bf16[1040,128]{1,0:T(8,128)(2,1)S(1)}, u32[]{:S(2)}, u32[]{:S(2)}) %collective-permute-start.13) | collective-permute-done | bytes 266272 | tf_op jit(solution)/shard_map/ppermute | solution.py:327
  45.0 0.8 %collective-permute-start.17 = (bf16[1040,128]{1,0:T(8,128)(2,1)S(1)}, bf16[1040,128]{1,0:T(8,128)(2,1)S(1)}, u32[]{:S(2)}, u32[]{:S(2)}) collective-permute-start(bf16[1040,128]{1,0:T(8,128)(2,1)S(1)} %collective-permute-done.13.refs_4_.refs_5_), channel_id=1, source_target_pairs={{0,16},{4,12},{8,24},{12,4},{16,0},{20,28},{24,8},{28,20},{1,17},{... | collective-permute-start | bytes 798728 | tf_op jit(solution)/shard_map/ppermute | solution.py:327
  45.8 1.6 %collective-permute-done.12.refs_3_.refs_1_.refs_4_ = bf16[1040,128]{1,0:T(8,128)(2,1)S(1)} collective-permute-done((bf16[1040,128]{1,0:T(8,128)(2,1)S(1)}, bf16[1040,128]{1,0:T(8,128)(2,1)S(1)}, u32[]{:S(2)}, u32[]{:S(2)}) %collective-permute-start.12) | collective-permute-done | bytes 266272 | tf_op jit(solution)/shard_map/ppermute | solution.py:327
  47.4 0.8 %collective-permute-start.16 = (bf16[1040,128]{1,0:T(8,128)(2,1)S(1)}, bf16[1040,128]{1,0:T(8,128)(2,1)S(1)}, u32[]{:S(2)}, u32[]{:S(2)}) collective-permute-start(bf16[1040,128]{1,0:T(8,128)(2,1)S(1)} %late.1), channel_id=1, source_target_pairs={{0,4},{4,0},{8,12},{12,8},{16,20},{20,16},{24,28},{28,24},{1,5},{5... | collective-permute-start | bytes 798728 | tf_op jit(solution)/shard_map/ppermute | solution.py:327
  48.2 0.6 %turn.1 = (bf16[256,1088]{1,0:T(8,128)(2,1)S(1)}, bf16[256,1088]{1,0:T(8,128)(2,1)S(1)}) custom-call(bf16[1088,128]{1,0:T(8,128)(2,1)S(1)} %get-tuple-element.22.refs_0_, bf16[640,128]{1,0:T(8,128)(2,1)S(1)} %collective-permute-done.2.refs_0_.refs_1_, bf16[640,128]{1,0:T(8,128)(2,1)S(1)} %collective-permute-done.3.refs_1_.refs_2_, ...), custom_call_target="tpu_custom_call" | custom-call | bytes 2228224 | tf_op jit(solution)/shard_map/turn/pallas_call | solution.py:423
  48.8 0.6 %grad_other_near.1 = bf16[256,640]{1,0:T(8,128)(2,1)S(1)} custom-call(bf16[256,1088]{1,0:T(8,128)(2,1)S(1)} %get-tuple-element.35.refs_0_, bf16[1040,128]{1,0:T(8,128)(2,1)S(1)} %get-tuple-element.32.refs_3_.refs_1_.refs_2_, bf16[1040,128]{1,0:T(8,128)(2,1)S(1)} %collective-permute-done.11.refs_2_.refs_0_.refs_3_, ...), custom_call_target="tpu_custom_call" | custom-call | flops 356515840 | bytes 655360 | tf_op jit(solution)/shard_map/grad_other_near/pallas_call | solution.py:433
  49.5 0.6 %grad_own_near.1.refs_4_.refs_0_ = f32[256,640]{1,0:T(8,128)S(1)} custom-call(bf16[256,1088]{1,0:T(8,128)(2,1)S(1)} %get-tuple-element.33.refs_0_, bf16[1040,128]{1,0:T(8,128)(2,1)S(1)} %get-tuple-element.32.refs_3_.refs_1_.refs_2_, bf16[1040,128]{1,0:T(8,128)(2,1)S(1)} %collective-permute-done.11.refs_2_.refs_0_.refs_3_, ...), custom_call_target="tpu_custom_call" | custom-call | flops 356515840 | bytes 1310720 | tf_op jit(solution)/shard_map/grad_own_near/pallas_call | solution.py:433
  50.2 0.5 collective-permute-done.18.refs_3_.refs_6_
  50.7 0.7 %collective-permute-done.17.refs_2_.refs_5_ = bf16[1040,128]{1,0:T(8,128)(2,1)S(1)} collective-permute-done((bf16[1040,128]{1,0:T(8,128)(2,1)S(1)}, bf16[1040,128]{1,0:T(8,128)(2,1)S(1)}, u32[]{:S(2)}, u32[]{:S(2)}) %collective-permute-start.17) | collective-permute-done | bytes 266272 | tf_op jit(solution)/shard_map/ppermute | solution.py:327
  51.9 0.7 %collective-permute-start.19 = (bf16[256,384]{1,0:T(8,128)(2,1)S(1)}, bf16[256,384]{1,0:T(8,128)(2,1)S(1)}, u32[]{:S(2)}, u32[]{:S(2)}) collective-permute-start(bf16[256,384]{1,0:T(8,128)(2,1)S(1)} %grad_other_far.1), channel_id=1, source_target_pairs={{0,4},{4,0},{8,12},{12,8},{16,20},{20,16},{24,28},{28,24},{1,5},{5... | collective-permute-start | bytes 589832 | tf_op jit(solution)/shard_map/ppermute | solution.py:327
  52.6 0.5 grad_own_far.1.refs_2_
  53.1 1.0 %near.1 = (bf16[256,1024]{1,0:T(8,128)(2,1)}, f32[256,1024]{1,0:T(8,128)}) custom-call(f32[256,640]{1,0:T(8,128)S(1)} %grad_own_near.1.refs_4_.refs_0_, bf16[256,640]{1,0:T(8,128)(2,1)S(1)} %collective-permute-done.15.refs_1_, bf16[1040,128]{1,0:T(8,128)(2,1)S(1)} %get-tuple-element.32.refs_3_.refs_1_.refs_2_, ...), custom_call_target="tpu_custom_call" | custom-call | bytes 3145728 | tf_op jit(solution)/shard_map/near/pallas_call | solution.py:449
  54.1 0.9 %last.1 = (bf16[256,1024]{1,0:T(8,128)(2,1)}, f32[256,1024]{1,0:T(8,128)}) custom-call(f32[256,640]{1,0:T(8,128)S(1)} %grad_own_near.1.refs_4_.refs_0_, bf16[256,640]{1,0:T(8,128)(2,1)S(1)} %collective-permute-done.15.refs_1_, f32[256,384]{1,0:T(8,128)S(1)} %grad_own_far.1.refs_2_, ...), custom_call_target="tpu_custom_call", output_to_operand_aliasing={{0}: (7, {}), {1}: (8, {})} | custom-call | bytes 3145728 | tf_op jit(solution)/shard_map/last/pallas_call | solution.py:458
  (29 shorter events, 1.5 us)
Async XLA Ops:
  2.5 14.1 %copy-start = (bf16[272,2048]{1,0:T(8,128)(2,1)S(1)}, bf16[272,2048]{1,0:T(8,128)(2,1)}, u32[]{:S(2)}) copy-start(bf16[272,2048]{1,0:T(8,128)(2,1)} %refs_1_.4) | copy-start | bytes 3342340
  2.5 14.1 %copy-start.1 = (s32[1,8]{1,0:T(1,128)S(1)}, s32[1,8]{1,0:T(1,128)}, u32[]{:S(2)}) copy-start(s32[1,8]{1,0:T(1,128)} %refs_0_.5) | copy-start | bytes 100
  2.5 10.0 %collective-permute-start = (bf16[784,128]{1,0:T(8,128)(2,1)}, bf16[784,128]{1,0:T(8,128)(2,1)S(1)}, u32[]{:S(2)}, u32[]{:S(2)}) collective-permute-start(bf16[784,128]{1,0:T(8,128)(2,1)} %get-tuple-element.20), channel_id=1, source_target_pairs={{0,24},{4,28},{8,16},{12,20},{16,8},{20,12},{24,0},{28,4},{1,25},{... | collective-permute-start | bytes 602120 | tf_op jit(solution)/shard_map/ppermute | solution.py:327
  6.5 10.1 %collective-permute-start.1 = (bf16[784,128]{1,0:T(8,128)(2,1)}, bf16[784,128]{1,0:T(8,128)(2,1)S(1)}, u32[]{:S(2)}, u32[]{:S(2)}) collective-permute-start(bf16[784,128]{1,0:T(8,128)(2,1)} %get-tuple-element.21), channel_id=1, source_target_pairs={{0,28},{4,24},{8,20},{12,16},{16,12},{20,8},{24,4},{28,0},{1,29},{... | collective-permute-start | bytes 602120 | tf_op jit(solution)/shard_map/ppermute | solution.py:327
  9.1 16.6 %copy-start.2 = (bf16[784,128]{1,0:T(8,128)(2,1)S(1)}, bf16[784,128]{1,0:T(8,128)(2,1)}, u32[]{:S(2)}) copy-start(bf16[784,128]{1,0:T(8,128)(2,1)} %get-tuple-element.26.refs_1_) | copy-start | bytes 602116
  9.1 16.6 %copy-start.3 = (s32[8]{0:T(128)S(1)}, s32[8]{0:T(128)}, u32[]{:S(2)}) copy-start(s32[8]{0:T(128)} %refs_0_.7) | copy-start | bytes 100
  9.1 12.6 %collective-permute-start.5 = (bf16[784,128]{1,0:T(8,128)(2,1)}, bf16[784,128]{1,0:T(8,128)(2,1)S(1)}, u32[]{:S(2)}, u32[]{:S(2)}) collective-permute-start(bf16[784,128]{1,0:T(8,128)(2,1)} %get-tuple-element.27), channel_id=1, source_target_pairs={{0,8},{4,12},{8,0},{12,4},{16,24},{20,28},{24,16},{28,20},{1,9},{5... | collective-permute-start | bytes 602120 | tf_op jit(solution)/shard_map/ppermute | solution.py:327
  10.3 12.9 %collective-permute-start.6 = (bf16[784,128]{1,0:T(8,128)(2,1)}, bf16[784,128]{1,0:T(8,128)(2,1)S(1)}, u32[]{:S(2)}, u32[]{:S(2)}) collective-permute-start(bf16[784,128]{1,0:T(8,128)(2,1)} %get-tuple-element.28), channel_id=1, source_target_pairs={{0,16},{4,20},{8,24},{12,28},{16,0},{20,4},{24,8},{28,12},{1,17},{... | collective-permute-start | bytes 602120 | tf_op jit(solution)/shard_map/ppermute | solution.py:327
  11.8 13.3 %collective-permute-start.7 = (bf16[784,128]{1,0:T(8,128)(2,1)}, bf16[784,128]{1,0:T(8,128)(2,1)S(1)}, u32[]{:S(2)}, u32[]{:S(2)}) collective-permute-start(bf16[784,128]{1,0:T(8,128)(2,1)} %get-tuple-element.29), channel_id=1, source_target_pairs={{0,12},{4,8},{8,4},{12,0},{16,28},{20,24},{24,20},{28,16},{1,13},{... | collective-permute-start | bytes 602120 | tf_op jit(solution)/shard_map/ppermute | solution.py:327
  12.5 13.1 %collective-permute-start.8 = (bf16[784,128]{1,0:T(8,128)(2,1)}, bf16[784,128]{1,0:T(8,128)(2,1)S(1)}, u32[]{:S(2)}, u32[]{:S(2)}) collective-permute-start(bf16[784,128]{1,0:T(8,128)(2,1)} %get-tuple-element.30), channel_id=1, source_target_pairs={{0,20},{4,16},{8,28},{12,24},{16,4},{20,0},{24,12},{28,8},{1,21},{... | collective-permute-start | bytes 602120 | tf_op jit(solution)/shard_map/ppermute | solution.py:327
  16.5 9.1 %collective-permute-start.9 = (bf16[784,128]{1,0:T(8,128)(2,1)}, bf16[784,128]{1,0:T(8,128)(2,1)S(1)}, u32[]{:S(2)}, u32[]{:S(2)}) collective-permute-start(bf16[784,128]{1,0:T(8,128)(2,1)} %get-tuple-element.31), channel_id=1, source_target_pairs={{0,4},{4,0},{8,12},{12,8},{16,20},{20,16},{24,28},{28,24},{1,5},{5... | collective-permute-start | bytes 602120 | tf_op jit(solution)/shard_map/ppermute | solution.py:327
  21.7 11.9 %collective-permute-start.2 = (bf16[640,128]{1,0:T(8,128)(2,1)S(1)}, bf16[640,128]{1,0:T(8,128)(2,1)S(1)}, u32[]{:S(2)}, u32[]{:S(2)}) collective-permute-start(bf16[640,128]{1,0:T(8,128)(2,1)S(1)} %get-tuple-element.23), channel_id=1, source_target_pairs={{0,24},{4,28},{8,16},{12,20},{16,8},{20,12},{24,0},{28,4},{1,25},{... | collective-permute-start | bytes 491528 | tf_op jit(solution)/shard_map/ppermute | solution.py:327
  23.2 10.6 %collective-permute-start.3 = (bf16[640,128]{1,0:T(8,128)(2,1)S(1)}, bf16[640,128]{1,0:T(8,128)(2,1)S(1)}, u32[]{:S(2)}, u32[]{:S(2)}) collective-permute-start(bf16[640,128]{1,0:T(8,128)(2,1)S(1)} %get-tuple-element.24), channel_id=1, source_target_pairs={{0,8},{4,20},{8,0},{12,28},{16,24},{20,4},{24,16},{28,12},{1,9},{5... | collective-permute-start | bytes 491528 | tf_op jit(solution)/shard_map/ppermute | solution.py:327
  25.1 9.3 %collective-permute-start.4 = (bf16[640,128]{1,0:T(8,128)(2,1)S(1)}, bf16[640,128]{1,0:T(8,128)(2,1)S(1)}, u32[]{:S(2)}, u32[]{:S(2)}) collective-permute-start(bf16[640,128]{1,0:T(8,128)(2,1)S(1)} %get-tuple-element.25), channel_id=1, source_target_pairs={{0,16},{4,12},{8,24},{12,4},{16,0},{20,28},{24,8},{28,20},{1,17},{... | collective-permute-start | bytes 491528 | tf_op jit(solution)/shard_map/ppermute | solution.py:327
  30.5 6.8 %collective-permute-start.14 = (bf16[1040,128]{1,0:T(8,128)(2,1)S(1)}, bf16[1040,128]{1,0:T(8,128)(2,1)S(1)}, u32[]{:S(2)}, u32[]{:S(2)}) collective-permute-start(bf16[1040,128]{1,0:T(8,128)(2,1)S(1)} %get-tuple-element.34.x_ref), channel_id=1, source_target_pairs={{0,12},{4,16},{8,4},{12,24},{16,28},{20,0},{24,20},{28,8},{1,13},{... | collective-permute-start | bytes 798728 | tf_op jit(solution)/shard_map/ppermute | solution.py:327
  32.0 13.0 %collective-permute-start.13 = (bf16[1040,128]{1,0:T(8,128)(2,1)S(1)}, bf16[1040,128]{1,0:T(8,128)(2,1)S(1)}, u32[]{:S(2)}, u32[]{:S(2)}) collective-permute-start(bf16[1040,128]{1,0:T(8,128)(2,1)S(1)} %get-tuple-element.32.refs_3_.refs_1_.refs_2_), channel_id=1, source_target_pairs={{0,8},{4,20},{8,0},{12,28},{16,24},{20,4},{24,16},{28,12},{1,9},{5... | collective-permute-start | bytes 798728 | tf_op jit(solution)/shard_map/ppermute | solution.py:327
  33.6 12.2 %collective-permute-start.11 = (bf16[1040,128]{1,0:T(8,128)(2,1)S(1)}, bf16[1040,128]{1,0:T(8,128)(2,1)S(1)}, u32[]{:S(2)}, u32[]{:S(2)}) collective-permute-start(bf16[1040,128]{1,0:T(8,128)(2,1)S(1)} %get-tuple-element.34.x_ref), channel_id=1, source_target_pairs={{0,20},{4,8},{8,28},{12,0},{16,4},{20,24},{24,12},{28,16},{1,21},{... | collective-permute-start | bytes 798728 | tf_op jit(solution)/shard_map/ppermute | solution.py:327
  33.7 13.7 %collective-permute-start.12 = (bf16[1040,128]{1,0:T(8,128)(2,1)S(1)}, bf16[1040,128]{1,0:T(8,128)(2,1)S(1)}, u32[]{:S(2)}, u32[]{:S(2)}) collective-permute-start(bf16[1040,128]{1,0:T(8,128)(2,1)S(1)} %get-tuple-element.32.refs_3_.refs_1_.refs_2_), channel_id=1, source_target_pairs={{0,16},{4,12},{8,24},{12,4},{16,0},{20,28},{24,8},{28,20},{1,17},{... | collective-permute-start | bytes 798728 | tf_op jit(solution)/shard_map/ppermute | solution.py:327
  34.5 13.8 %collective-permute-start.10 = (bf16[3,448,128]{2,1,0:T(8,128)(2,1)S(1)}, bf16[3,448,128]{2,1,0:T(8,128)(2,1)S(1)}, u32[]{:S(2)}, u32[]{:S(2)}) collective-permute-start(bf16[3,448,128]{2,1,0:T(8,128)(2,1)S(1)} %stack.1), channel_id=1, source_target_pairs={{0,1},{1,0},{2,3},{3,2},{4,5},{5,4},{6,7},{7,6},{8,9},{9,8},{10,11... | collective-permute-start | bytes 1032200 | tf_op jit(solution)/shard_map/ppermute | solution.py:333
  37.3 13.4 %collective-permute-start.18 = (bf16[1040,128]{1,0:T(8,128)(2,1)S(1)}, bf16[1040,128]{1,0:T(8,128)(2,1)S(1)}, u32[]{:S(2)}, u32[]{:S(2)}) collective-permute-start(bf16[1040,128]{1,0:T(8,128)(2,1)S(1)} %collective-permute-done.14.refs_5_.refs_6_), channel_id=1, source_target_pairs={{0,8},{4,20},{8,0},{12,28},{16,24},{20,4},{24,16},{28,12},{1,9},{5... | collective-permute-start | bytes 798728 | tf_op jit(solution)/shard_map/ppermute | solution.py:327
  45.0 6.4 %collective-permute-start.17 = (bf16[1040,128]{1,0:T(8,128)(2,1)S(1)}, bf16[1040,128]{1,0:T(8,128)(2,1)S(1)}, u32[]{:S(2)}, u32[]{:S(2)}) collective-permute-start(bf16[1040,128]{1,0:T(8,128)(2,1)S(1)} %collective-permute-done.13.refs_4_.refs_5_), channel_id=1, source_target_pairs={{0,16},{4,12},{8,24},{12,4},{16,0},{20,28},{24,8},{28,20},{1,17},{... | collective-permute-start | bytes 798728 | tf_op jit(solution)/shard_map/ppermute | solution.py:327
  47.4 4.0 %collective-permute-start.16 = (bf16[1040,128]{1,0:T(8,128)(2,1)S(1)}, bf16[1040,128]{1,0:T(8,128)(2,1)S(1)}, u32[]{:S(2)}, u32[]{:S(2)}) collective-permute-start(bf16[1040,128]{1,0:T(8,128)(2,1)S(1)} %late.1), channel_id=1, source_target_pairs={{0,4},{4,0},{8,12},{12,8},{16,20},{20,16},{24,28},{28,24},{1,5},{5... | collective-permute-start | bytes 798728 | tf_op jit(solution)/shard_map/ppermute | solution.py:327
  49.5 3.6 %collective-permute-start.15 = (bf16[256,640]{1,0:T(8,128)(2,1)S(1)}, bf16[256,640]{1,0:T(8,128)(2,1)S(1)}, u32[]{:S(2)}, u32[]{:S(2)}) collective-permute-start(bf16[256,640]{1,0:T(8,128)(2,1)S(1)} %grad_other_near.1), channel_id=1, source_target_pairs={{0,4},{4,0},{8,12},{12,8},{16,20},{20,16},{24,28},{28,24},{1,5},{5... | collective-permute-start | bytes 983048 | tf_op jit(solution)/shard_map/ppermute | solution.py:327
  51.9 2.2 %collective-permute-start.19 = (bf16[256,384]{1,0:T(8,128)(2,1)S(1)}, bf16[256,384]{1,0:T(8,128)(2,1)S(1)}, u32[]{:S(2)}, u32[]{:S(2)}) collective-permute-start(bf16[256,384]{1,0:T(8,128)(2,1)S(1)} %grad_other_far.1), channel_id=1, source_target_pairs={{0,4},{4,0},{8,12},{12,8},{16,20},{20,16},{24,28},{28,24},{1,5},{5... | collective-permute-start | bytes 589832 | tf_op jit(solution)/shard_map/ppermute | solution.py:327

commit v12 on v11

--- a/solution.py
+++ b/solution.py
@@ -169,21 +169,21 @@
                 (((1,), (1,)), ((), ())),
                 preferred_element_type=jnp.float32,
             )
+            * rate
             + bias[s]
             for s in sources
         ]
         top = jnp.max(scores[0], axis=0, keepdims=True)
         for s in scores[1:]:
             top = jnp.maximum(top, jnp.max(s, axis=0, keepdims=True))
-        weights = [jnp.exp2((s - top) * rate) for s in scores]
-        total = jnp.sum(weights[0], axis=0, keepdims=True)
-        for w in weights[1:]:
-            total = total + jnp.sum(w, axis=0, keepdims=True)
-        share = 1.0 / total
+        total = jnp.zeros((1, tok), jnp.float32)
+        for s in scores:
+            total = total + jnp.sum(jnp.exp2(s - top), axis=0, keepdims=True)
+        level = top + jnp.log2(total)
         mixed = jnp.zeros((HD, tok), jnp.float32)
-        for s, w in zip(sources, weights):
+        for i, s in zip(sources, scores):
             mixed = mixed + jnp.dot(
-                values[s], (w * share).astype(jnp.bfloat16), preferred_element_type=jnp.float32
+                values[i], jnp.exp2(s - level).astype(jnp.bfloat16), preferred_element_type=jnp.float32
             )
         mixed_ref[block] = mixed.astype(jnp.bfloat16).T
     rows = n // 2 * tok

time: 55.3 us -> 55.8 us (level)
  Pallas kernels: 14.9 us -> 15.5 us
  transfers between devices with their start and end apart: 20 -> 20, of which waited for: 9 -> 9; matrix products, arithmetic and copies ran while one was open for 0% -> 0% of each run, Pallas kernels for 22% -> 23%
where the time goes in v12:
time: 55.8 us; the launch traced here: 55.6 us
  waiting for transfers between devices  20 us (36%)
  starting transfers between devices  19.3 us (35%)
  Pallas kernels  15.5 us (28%)
  between operations  0.78 us (1%)
    ppermute x19, waiting for transfers between devices, swap(): return lax.ppermute(x, 'tm', [(i, i ^ bits[i % 2]) for i in range(n)])  20 us
    ppermute x19, starting transfers between devices, swap(): return lax.ppermute(x, 'tm', [(i, i ^ bits[i % 2]) for i in range(n)])  17.7 us
    pallas_call x1, Pallas kernels, head_body(): call(lambda *refs: attend_kernel(n, tok, [0] + order, *refs), 'attend', [...  5.33 us
    pallas_call x2, Pallas kernels, pack(): call(lambda *refs: pack_kernel(n, heads, *refs), name, [((length, HD), bf...  4.42 us
    pallas_call x4, Pallas kernels, grad(): call(lambda *refs: grad_kernel(rows, half, len(heads), *refs), name, [((c...  2.25 us
    ppermute x1, starting transfers between devices, swap_plane(): return lax.ppermute(x, ('tm', 'head'), pairs)  1.64 us
  transfers between devices with their start and end apart: 20, of which 9 were waited for; matrix products, arithmetic and copies ran while one was open for 0% of the time, Pallas kernels for 23%

profile of v12, /device:TPU:0, one launch (start us, length us, event | category | flops | bytes accessed | tf_op | source)
XLA Modules:
  0.0 55.6 jit_solution(9668092068212252289)
XLA Ops:
  0.6 1.9 %pack_first.1 = (bf16[784,128]{1,0:T(8,128)(2,1)}, bf16[784,128]{1,0:T(8,128)(2,1)}) custom-call(bf16[256,1024]{1,0:T(8,128)(2,1)} %refs_0_.6, bf16[256,1024]{1,0:T(8,128)(2,1)} %refs_1_.5, bf16[256,1024]{1,0:T(8,128)(2,1)} %refs_2_.3, bf16[2,1024]{1,0:T(2,128)(2,1)} %refs_3_.3), custom_call_target="tpu_custom_call" | custom-call | bytes 802816 | tf_op jit(solution)/shard_map/pack_first/pallas_call | solution.py:353
  2.5 4.0 %collective-permute-start = (bf16[784,128]{1,0:T(8,128)(2,1)}, bf16[784,128]{1,0:T(8,128)(2,1)S(1)}, u32[]{:S(2)}, u32[]{:S(2)}) collective-permute-start(bf16[784,128]{1,0:T(8,128)(2,1)} %get-tuple-element.20), channel_id=1, source_target_pairs={{0,24},{4,28},{8,16},{12,20},{16,8},{20,12},{24,0},{28,4},{1,25},{... | collective-permute-start | bytes 602120 | tf_op jit(solution)/shard_map/ppermute | solution.py:327
  6.5 2.6 %pack_rest.1 = (bf16[784,128]{1,0:T(8,128)(2,1)}, bf16[784,128]{1,0:T(8,128)(2,1)}, bf16[784,128]{1,0:T(8,128)(2,1)}, bf16[784,128]{1,0:T(8,128)(2,1)}, bf16[784...) custom-call(bf16[256,1024]{1,0:T(8,128)(2,1)} %refs_0_.6, bf16[256,1024]{1,0:T(8,128)(2,1)} %refs_1_.5, ...), custom_call_target="tpu_custom_call" | custom-call | bytes 2408448 | tf_op jit(solution)/shard_map/pack_rest/pallas_call | solution.py:353
  9.1 1.2 %collective-permute-start.5 = (bf16[784,128]{1,0:T(8,128)(2,1)}, bf16[784,128]{1,0:T(8,128)(2,1)S(1)}, u32[]{:S(2)}, u32[]{:S(2)}) collective-permute-start(bf16[784,128]{1,0:T(8,128)(2,1)} %get-tuple-element.27), channel_id=1, source_target_pairs={{0,8},{4,12},{8,0},{12,4},{16,24},{20,28},{24,16},{28,20},{1,9},{5... | collective-permute-start | bytes 602120 | tf_op jit(solution)/shard_map/ppermute | solution.py:327
  10.3 1.5 %collective-permute-start.6 = (bf16[784,128]{1,0:T(8,128)(2,1)}, bf16[784,128]{1,0:T(8,128)(2,1)S(1)}, u32[]{:S(2)}, u32[]{:S(2)}) collective-permute-start(bf16[784,128]{1,0:T(8,128)(2,1)} %get-tuple-element.28), channel_id=1, source_target_pairs={{0,16},{4,20},{8,24},{12,28},{16,0},{20,4},{24,8},{28,12},{1,17},{... | collective-permute-start | bytes 602120 | tf_op jit(solution)/shard_map/ppermute | solution.py:327
  11.8 0.6 %collective-permute-start.7 = (bf16[784,128]{1,0:T(8,128)(2,1)}, bf16[784,128]{1,0:T(8,128)(2,1)S(1)}, u32[]{:S(2)}, u32[]{:S(2)}) collective-permute-start(bf16[784,128]{1,0:T(8,128)(2,1)} %get-tuple-element.29), channel_id=1, source_target_pairs={{0,12},{4,8},{8,4},{12,0},{16,28},{20,24},{24,20},{28,16},{1,13},{... | collective-permute-start | bytes 602120 | tf_op jit(solution)/shard_map/ppermute | solution.py:327
  12.9 3.6 %collective-permute-done.1.refs_3_ = bf16[784,128]{1,0:T(8,128)(2,1)S(1)} collective-permute-done((bf16[784,128]{1,0:T(8,128)(2,1)}, bf16[784,128]{1,0:T(8,128)(2,1)S(1)}, u32[]{:S(2)}, u32[]{:S(2)}) %collective-permute-start.1) | collective-permute-done | bytes 200736 | tf_op jit(solution)/shard_map/ppermute | solution.py:327
  16.6 0.9 %cot.1 = (bf16[1088,128]{1,0:T(8,128)(2,1)S(1)}, bf16[640,128]{1,0:T(8,128)(2,1)S(1)}, bf16[640,128]{1,0:T(8,128)(2,1)S(1)}, bf16[640,128]{1,0:T(8,128)(2,1)S(1)}) custom-call(s32[1,8]{1,0:T(1,128)S(1)} %copy-done.1, bf16[272,2048]{1,0:T(8,128)(2,1)S(1)} %copy-done, bf16[784,128]{1,0:T(8,128)(2,1)S(1)} %collective-permute-done.refs_2_, ...), custom_call_target="tpu_custom_call" | custom-call | bytes 1540096 | tf_op jit(solution)/shard_map/cot/pallas_call | solution.py:376
  17.6 4.1 %collective-permute-done.5.refs_4_ = bf16[784,128]{1,0:T(8,128)(2,1)S(1)} collective-permute-done((bf16[784,128]{1,0:T(8,128)(2,1)}, bf16[784,128]{1,0:T(8,128)(2,1)S(1)}, u32[]{:S(2)}, u32[]{:S(2)}) %collective-permute-start.5) | collective-permute-done | bytes 200736 | tf_op jit(solution)/shard_map/ppermute | solution.py:327
  21.7 1.5 %collective-permute-start.2 = (bf16[640,128]{1,0:T(8,128)(2,1)S(1)}, bf16[640,128]{1,0:T(8,128)(2,1)S(1)}, u32[]{:S(2)}, u32[]{:S(2)}) collective-permute-start(bf16[640,128]{1,0:T(8,128)(2,1)S(1)} %get-tuple-element.23), channel_id=1, source_target_pairs={{0,24},{4,28},{8,16},{12,20},{16,8},{20,12},{24,0},{28,4},{1,25},{... | collective-permute-start | bytes 491528 | tf_op jit(solution)/shard_map/ppermute | solution.py:327
  23.2 1.9 %collective-permute-done.7.refs_6_ = bf16[784,128]{1,0:T(8,128)(2,1)S(1)} collective-permute-done((bf16[784,128]{1,0:T(8,128)(2,1)}, bf16[784,128]{1,0:T(8,128)(2,1)S(1)}, u32[]{:S(2)}, u32[]{:S(2)}) %collective-permute-start.7) | collective-permute-done | bytes 200736 | tf_op jit(solution)/shard_map/ppermute | solution.py:327
  25.1 0.5 collective-permute-start.4
  25.7 5.3 %attend.1 = (bf16[1040,128]{1,0:T(8,128)(2,1)S(1)}, bf16[1040,128]{1,0:T(8,128)(2,1)S(1)}) custom-call(s32[8]{0:T(128)S(1)} %copy-done.3, bf16[784,128]{1,0:T(8,128)(2,1)S(1)} %copy-done.2, bf16[784,128]{1,0:T(8,128)(2,1)S(1)} %collective-permute-done.refs_2_, bf16[784,128]{1,0:T(8,128)(2,1)S(1)} %collective-permute-done.1.refs_3_, ...), custom_call_target="tpu_custom_call" | custom-call | flops 1073741824 | bytes 1064960 | tf_op jit(solution)/shard_map/attend/pallas_call | solution.py:397
  31.0 1.6 %collective-permute-start.14 = (bf16[1040,128]{1,0:T(8,128)(2,1)S(1)}, bf16[1040,128]{1,0:T(8,128)(2,1)S(1)}, u32[]{:S(2)}, u32[]{:S(2)}) collective-permute-start(bf16[1040,128]{1,0:T(8,128)(2,1)S(1)} %get-tuple-element.34.x_ref), channel_id=1, source_target_pairs={{0,12},{4,16},{8,4},{12,24},{16,28},{20,0},{24,20},{28,8},{1,13},{... | collective-permute-start | bytes 798728 | tf_op jit(solution)/shard_map/ppermute | solution.py:327
  32.6 1.5 %collective-permute-start.13 = (bf16[1040,128]{1,0:T(8,128)(2,1)S(1)}, bf16[1040,128]{1,0:T(8,128)(2,1)S(1)}, u32[]{:S(2)}, u32[]{:S(2)}) collective-permute-start(bf16[1040,128]{1,0:T(8,128)(2,1)S(1)} %get-tuple-element.32.refs_3_.refs_1_.refs_2_), channel_id=1, source_target_pairs={{0,8},{4,20},{8,0},{12,28},{16,24},{20,4},{24,16},{28,12},{1,9},{5... | collective-permute-start | bytes 798728 | tf_op jit(solution)/shard_map/ppermute | solution.py:327
  34.3 0.7 %collective-permute-start.12 = (bf16[1040,128]{1,0:T(8,128)(2,1)S(1)}, bf16[1040,128]{1,0:T(8,128)(2,1)S(1)}, u32[]{:S(2)}, u32[]{:S(2)}) collective-permute-start(bf16[1040,128]{1,0:T(8,128)(2,1)S(1)} %get-tuple-element.32.refs_3_.refs_1_.refs_2_), channel_id=1, source_target_pairs={{0,16},{4,12},{8,24},{12,4},{16,0},{20,28},{24,8},{28,20},{1,17},{... | collective-permute-start | bytes 798728 | tf_op jit(solution)/shard_map/ppermute | solution.py:327
  35.0 1.6 %collective-permute-start.10 = (bf16[3,448,128]{2,1,0:T(8,128)(2,1)S(1)}, bf16[3,448,128]{2,1,0:T(8,128)(2,1)S(1)}, u32[]{:S(2)}, u32[]{:S(2)}) collective-permute-start(bf16[3,448,128]{2,1,0:T(8,128)(2,1)S(1)} %stack.1), channel_id=1, source_target_pairs={{0,1},{1,0},{2,3},{3,2},{4,5},{5,4},{6,7},{7,6},{8,9},{9,8},{10,11... | collective-permute-start | bytes 1032200 | tf_op jit(solution)/shard_map/ppermute | solution.py:333
  36.7 1.2 %collective-permute-done.14.refs_5_.refs_6_ = bf16[1040,128]{1,0:T(8,128)(2,1)S(1)} collective-permute-done((bf16[1040,128]{1,0:T(8,128)(2,1)S(1)}, bf16[1040,128]{1,0:T(8,128)(2,1)S(1)}, u32[]{:S(2)}, u32[]{:S(2)}) %collective-permute-start.14) | collective-permute-done | bytes 266272 | tf_op jit(solution)/shard_map/ppermute | solution.py:327
  37.8 1.5 %collective-permute-start.18 = (bf16[1040,128]{1,0:T(8,128)(2,1)S(1)}, bf16[1040,128]{1,0:T(8,128)(2,1)S(1)}, u32[]{:S(2)}, u32[]{:S(2)}) collective-permute-start(bf16[1040,128]{1,0:T(8,128)(2,1)S(1)} %collective-permute-done.14.refs_5_.refs_6_), channel_id=1, source_target_pairs={{0,8},{4,20},{8,0},{12,28},{16,24},{20,4},{24,16},{28,12},{1,9},{5... | collective-permute-start | bytes 798728 | tf_op jit(solution)/shard_map/ppermute | solution.py:327
  39.4 6.2 %collective-permute-done.13.refs_4_.refs_5_ = bf16[1040,128]{1,0:T(8,128)(2,1)S(1)} collective-permute-done((bf16[1040,128]{1,0:T(8,128)(2,1)S(1)}, bf16[1040,128]{1,0:T(8,128)(2,1)S(1)}, u32[]{:S(2)}, u32[]{:S(2)}) %collective-permute-start.13) | collective-permute-done | bytes 266272 | tf_op jit(solution)/shard_map/ppermute | solution.py:327
  45.5 0.8 %collective-permute-start.17 = (bf16[1040,128]{1,0:T(8,128)(2,1)S(1)}, bf16[1040,128]{1,0:T(8,128)(2,1)S(1)}, u32[]{:S(2)}, u32[]{:S(2)}) collective-permute-start(bf16[1040,128]{1,0:T(8,128)(2,1)S(1)} %collective-permute-done.13.refs_4_.refs_5_), channel_id=1, source_target_pairs={{0,16},{4,12},{8,24},{12,4},{16,0},{20,28},{24,8},{28,20},{1,17},{... | collective-permute-start | bytes 798728 | tf_op jit(solution)/shard_map/ppermute | solution.py:327
  46.3 1.6 %collective-permute-done.12.refs_3_.refs_1_.refs_4_ = bf16[1040,128]{1,0:T(8,128)(2,1)S(1)} collective-permute-done((bf16[1040,128]{1,0:T(8,128)(2,1)S(1)}, bf16[1040,128]{1,0:T(8,128)(2,1)S(1)}, u32[]{:S(2)}, u32[]{:S(2)}) %collective-permute-start.12) | collective-permute-done | bytes 266272 | tf_op jit(solution)/shard_map/ppermute | solution.py:327
  47.9 0.8 %collective-permute-start.16 = (bf16[1040,128]{1,0:T(8,128)(2,1)S(1)}, bf16[1040,128]{1,0:T(8,128)(2,1)S(1)}, u32[]{:S(2)}, u32[]{:S(2)}) collective-permute-start(bf16[1040,128]{1,0:T(8,128)(2,1)S(1)} %late.1), channel_id=1, source_target_pairs={{0,4},{4,0},{8,12},{12,8},{16,20},{20,16},{24,28},{28,24},{1,5},{5... | collective-permute-start | bytes 798728 | tf_op jit(solution)/shard_map/ppermute | solution.py:327
  48.8 0.6 turn.1
  49.3 0.6 %grad_other_near.1 = bf16[256,640]{1,0:T(8,128)(2,1)S(1)} custom-call(bf16[256,1088]{1,0:T(8,128)(2,1)S(1)} %get-tuple-element.35.refs_0_, bf16[1040,128]{1,0:T(8,128)(2,1)S(1)} %get-tuple-element.32.refs_3_.refs_1_.refs_2_, bf16[1040,128]{1,0:T(8,128)(2,1)S(1)} %collective-permute-done.11.refs_2_.refs_0_.refs_3_, ...), custom_call_target="tpu_custom_call" | custom-call | flops 356515840 | bytes 655360 | tf_op jit(solution)/shard_map/grad_other_near/pallas_call | solution.py:433
  50.1 0.6 %grad_own_near.1.refs_4_.refs_0_ = f32[256,640]{1,0:T(8,128)S(1)} custom-call(bf16[256,1088]{1,0:T(8,128)(2,1)S(1)} %get-tuple-element.33.refs_0_, bf16[1040,128]{1,0:T(8,128)(2,1)S(1)} %get-tuple-element.32.refs_3_.refs_1_.refs_2_, bf16[1040,128]{1,0:T(8,128)(2,1)S(1)} %collective-permute-done.11.refs_2_.refs_0_.refs_3_, ...), custom_call_target="tpu_custom_call" | custom-call | flops 356515840 | bytes 1310720 | tf_op jit(solution)/shard_map/grad_own_near/pallas_call | solution.py:433
  50.7 0.5 collective-permute-done.18.refs_3_.refs_6_
  51.2 0.7 %collective-permute-done.17.refs_2_.refs_5_ = bf16[1040,128]{1,0:T(8,128)(2,1)S(1)} collective-permute-done((bf16[1040,128]{1,0:T(8,128)(2,1)S(1)}, bf16[1040,128]{1,0:T(8,128)(2,1)S(1)}, u32[]{:S(2)}, u32[]{:S(2)}) %collective-permute-start.17) | collective-permute-done | bytes 266272 | tf_op jit(solution)/shard_map/ppermute | solution.py:327
  52.0 0.5 grad_other_far.1
  52.4 0.7 %collective-permute-start.19 = (bf16[256,384]{1,0:T(8,128)(2,1)S(1)}, bf16[256,384]{1,0:T(8,128)(2,1)S(1)}, u32[]{:S(2)}, u32[]{:S(2)}) collective-permute-start(bf16[256,384]{1,0:T(8,128)(2,1)S(1)} %grad_other_far.1), channel_id=1, source_target_pairs={{0,4},{4,0},{8,12},{12,8},{16,20},{20,16},{24,28},{28,24},{1,5},{5... | collective-permute-start | bytes 589832 | tf_op jit(solution)/shard_map/ppermute | solution.py:327
  53.6 1.0 %near.1 = (bf16[256,1024]{1,0:T(8,128)(2,1)}, f32[256,1024]{1,0:T(8,128)}) custom-call(f32[256,640]{1,0:T(8,128)S(1)} %grad_own_near.1.refs_4_.refs_0_, bf16[256,640]{1,0:T(8,128)(2,1)S(1)} %collective-permute-done.15.refs_1_, bf16[1040,128]{1,0:T(8,128)(2,1)S(1)} %get-tuple-element.32.refs_3_.refs_1_.refs_2_, ...), custom_call_target="tpu_custom_call" | custom-call | bytes 3145728 | tf_op jit(solution)/shard_map/near/pallas_call | solution.py:449
  54.7 0.9 %last.1 = (bf16[256,1024]{1,0:T(8,128)(2,1)}, f32[256,1024]{1,0:T(8,128)}) custom-call(f32[256,640]{1,0:T(8,128)S(1)} %grad_own_near.1.refs_4_.refs_0_, bf16[256,640]{1,0:T(8,128)(2,1)S(1)} %collective-permute-done.15.refs_1_, f32[256,384]{1,0:T(8,128)S(1)} %grad_own_far.1.refs_2_, ...), custom_call_target="tpu_custom_call", output_to_operand_aliasing={{0}: (7, {}), {1}: (8, {})} | custom-call | bytes 3145728 | tf_op jit(solution)/shard_map/last/pallas_call | solution.py:458
  (29 shorter events, 1.5 us)
Async XLA Ops:
  2.5 14.1 %copy-start = (bf16[272,2048]{1,0:T(8,128)(2,1)S(1)}, bf16[272,2048]{1,0:T(8,128)(2,1)}, u32[]{:S(2)}) copy-start(bf16[272,2048]{1,0:T(8,128)(2,1)} %refs_1_.4) | copy-start | bytes 3342340
  2.5 14.1 %copy-start.1 = (s32[1,8]{1,0:T(1,128)S(1)}, s32[1,8]{1,0:T(1,128)}, u32[]{:S(2)}) copy-start(s32[1,8]{1,0:T(1,128)} %refs_0_.5) | copy-start | bytes 100
  2.5 10.0 %collective-permute-start = (bf16[784,128]{1,0:T(8,128)(2,1)}, bf16[784,128]{1,0:T(8,128)(2,1)S(1)}, u32[]{:S(2)}, u32[]{:S(2)}) collective-permute-start(bf16[784,128]{1,0:T(8,128)(2,1)} %get-tuple-element.20), channel_id=1, source_target_pairs={{0,24},{4,28},{8,16},{12,20},{16,8},{20,12},{24,0},{28,4},{1,25},{... | collective-permute-start | bytes 602120 | tf_op jit(solution)/shard_map/ppermute | solution.py:327
  6.5 10.1 %collective-permute-start.1 = (bf16[784,128]{1,0:T(8,128)(2,1)}, bf16[784,128]{1,0:T(8,128)(2,1)S(1)}, u32[]{:S(2)}, u32[]{:S(2)}) collective-permute-start(bf16[784,128]{1,0:T(8,128)(2,1)} %get-tuple-element.21), channel_id=1, source_target_pairs={{0,28},{4,24},{8,20},{12,16},{16,12},{20,8},{24,4},{28,0},{1,29},{... | collective-permute-start | bytes 602120 | tf_op jit(solution)/shard_map/ppermute | solution.py:327
  9.1 16.6 %copy-start.2 = (bf16[784,128]{1,0:T(8,128)(2,1)S(1)}, bf16[784,128]{1,0:T(8,128)(2,1)}, u32[]{:S(2)}) copy-start(bf16[784,128]{1,0:T(8,128)(2,1)} %get-tuple-element.26.refs_1_) | copy-start | bytes 602116
  9.1 16.6 %copy-start.3 = (s32[8]{0:T(128)S(1)}, s32[8]{0:T(128)}, u32[]{:S(2)}) copy-start(s32[8]{0:T(128)} %refs_0_.7) | copy-start | bytes 100
  9.1 12.6 %collective-permute-start.5 = (bf16[784,128]{1,0:T(8,128)(2,1)}, bf16[784,128]{1,0:T(8,128)(2,1)S(1)}, u32[]{:S(2)}, u32[]{:S(2)}) collective-permute-start(bf16[784,128]{1,0:T(8,128)(2,1)} %get-tuple-element.27), channel_id=1, source_target_pairs={{0,8},{4,12},{8,0},{12,4},{16,24},{20,28},{24,16},{28,20},{1,9},{5... | collective-permute-start | bytes 602120 | tf_op jit(solution)/shard_map/ppermute | solution.py:327
  10.3 12.9 %collective-permute-start.6 = (bf16[784,128]{1,0:T(8,128)(2,1)}, bf16[784,128]{1,0:T(8,128)(2,1)S(1)}, u32[]{:S(2)}, u32[]{:S(2)}) collective-permute-start(bf16[784,128]{1,0:T(8,128)(2,1)} %get-tuple-element.28), channel_id=1, source_target_pairs={{0,16},{4,20},{8,24},{12,28},{16,0},{20,4},{24,8},{28,12},{1,17},{... | collective-permute-start | bytes 602120 | tf_op jit(solution)/shard_map/ppermute | solution.py:327
  11.8 13.3 %collective-permute-start.7 = (bf16[784,128]{1,0:T(8,128)(2,1)}, bf16[784,128]{1,0:T(8,128)(2,1)S(1)}, u32[]{:S(2)}, u32[]{:S(2)}) collective-permute-start(bf16[784,128]{1,0:T(8,128)(2,1)} %get-tuple-element.29), channel_id=1, source_target_pairs={{0,12},{4,8},{8,4},{12,0},{16,28},{20,24},{24,20},{28,16},{1,13},{... | collective-permute-start | bytes 602120 | tf_op jit(solution)/shard_map/ppermute | solution.py:327
  12.5 13.1 %collective-permute-start.8 = (bf16[784,128]{1,0:T(8,128)(2,1)}, bf16[784,128]{1,0:T(8,128)(2,1)S(1)}, u32[]{:S(2)}, u32[]{:S(2)}) collective-permute-start(bf16[784,128]{1,0:T(8,128)(2,1)} %get-tuple-element.30), channel_id=1, source_target_pairs={{0,20},{4,16},{8,28},{12,24},{16,4},{20,0},{24,12},{28,8},{1,21},{... | collective-permute-start | bytes 602120 | tf_op jit(solution)/shard_map/ppermute | solution.py:327
  16.5 9.1 %collective-permute-start.9 = (bf16[784,128]{1,0:T(8,128)(2,1)}, bf16[784,128]{1,0:T(8,128)(2,1)S(1)}, u32[]{:S(2)}, u32[]{:S(2)}) collective-permute-start(bf16[784,128]{1,0:T(8,128)(2,1)} %get-tuple-element.31), channel_id=1, source_target_pairs={{0,4},{4,0},{8,12},{12,8},{16,20},{20,16},{24,28},{28,24},{1,5},{5... | collective-permute-start | bytes 602120 | tf_op jit(solution)/shard_map/ppermute | solution.py:327
  21.7 12.4 %collective-permute-start.2 = (bf16[640,128]{1,0:T(8,128)(2,1)S(1)}, bf16[640,128]{1,0:T(8,128)(2,1)S(1)}, u32[]{:S(2)}, u32[]{:S(2)}) collective-permute-start(bf16[640,128]{1,0:T(8,128)(2,1)S(1)} %get-tuple-element.23), channel_id=1, source_target_pairs={{0,24},{4,28},{8,16},{12,20},{16,8},{20,12},{24,0},{28,4},{1,25},{... | collective-permute-start | bytes 491528 | tf_op jit(solution)/shard_map/ppermute | solution.py:327
  23.2 11.1 %collective-permute-start.3 = (bf16[640,128]{1,0:T(8,128)(2,1)S(1)}, bf16[640,128]{1,0:T(8,128)(2,1)S(1)}, u32[]{:S(2)}, u32[]{:S(2)}) collective-permute-start(bf16[640,128]{1,0:T(8,128)(2,1)S(1)} %get-tuple-element.24), channel_id=1, source_target_pairs={{0,8},{4,20},{8,0},{12,28},{16,24},{20,4},{24,16},{28,12},{1,9},{5... | collective-permute-start | bytes 491528 | tf_op jit(solution)/shard_map/ppermute | solution.py:327
  25.1 9.9 %collective-permute-start.4 = (bf16[640,128]{1,0:T(8,128)(2,1)S(1)}, bf16[640,128]{1,0:T(8,128)(2,1)S(1)}, u32[]{:S(2)}, u32[]{:S(2)}) collective-permute-start(bf16[640,128]{1,0:T(8,128)(2,1)S(1)} %get-tuple-element.25), channel_id=1, source_target_pairs={{0,16},{4,12},{8,24},{12,4},{16,0},{20,28},{24,8},{28,20},{1,17},{... | collective-permute-start | bytes 491528 | tf_op jit(solution)/shard_map/ppermute | solution.py:327
  31.0 6.8 %collective-permute-start.14 = (bf16[1040,128]{1,0:T(8,128)(2,1)S(1)}, bf16[1040,128]{1,0:T(8,128)(2,1)S(1)}, u32[]{:S(2)}, u32[]{:S(2)}) collective-permute-start(bf16[1040,128]{1,0:T(8,128)(2,1)S(1)} %get-tuple-element.34.x_ref), channel_id=1, source_target_pairs={{0,12},{4,16},{8,4},{12,24},{16,28},{20,0},{24,20},{28,8},{1,13},{... | collective-permute-start | bytes 798728 | tf_op jit(solution)/shard_map/ppermute | solution.py:327
  32.6 13.0 %collective-permute-start.13 = (bf16[1040,128]{1,0:T(8,128)(2,1)S(1)}, bf16[1040,128]{1,0:T(8,128)(2,1)S(1)}, u32[]{:S(2)}, u32[]{:S(2)}) collective-permute-start(bf16[1040,128]{1,0:T(8,128)(2,1)S(1)} %get-tuple-element.32.refs_3_.refs_1_.refs_2_), channel_id=1, source_target_pairs={{0,8},{4,20},{8,0},{12,28},{16,24},{20,4},{24,16},{28,12},{1,9},{5... | collective-permute-start | bytes 798728 | tf_op jit(solution)/shard_map/ppermute | solution.py:327
  34.1 12.2 %collective-permute-start.11 = (bf16[1040,128]{1,0:T(8,128)(2,1)S(1)}, bf16[1040,128]{1,0:T(8,128)(2,1)S(1)}, u32[]{:S(2)}, u32[]{:S(2)}) collective-permute-start(bf16[1040,128]{1,0:T(8,128)(2,1)S(1)} %get-tuple-element.34.x_ref), channel_id=1, source_target_pairs={{0,20},{4,8},{8,28},{12,0},{16,4},{20,24},{24,12},{28,16},{1,21},{... | collective-permute-start | bytes 798728 | tf_op jit(solution)/shard_map/ppermute | solution.py:327
  34.3 13.7 %collective-permute-start.12 = (bf16[1040,128]{1,0:T(8,128)(2,1)S(1)}, bf16[1040,128]{1,0:T(8,128)(2,1)S(1)}, u32[]{:S(2)}, u32[]{:S(2)}) collective-permute-start(bf16[1040,128]{1,0:T(8,128)(2,1)S(1)} %get-tuple-element.32.refs_3_.refs_1_.refs_2_), channel_id=1, source_target_pairs={{0,16},{4,12},{8,24},{12,4},{16,0},{20,28},{24,8},{28,20},{1,17},{... | collective-permute-start | bytes 798728 | tf_op jit(solution)/shard_map/ppermute | solution.py:327
  35.0 13.8 %collective-permute-start.10 = (bf16[3,448,128]{2,1,0:T(8,128)(2,1)S(1)}, bf16[3,448,128]{2,1,0:T(8,128)(2,1)S(1)}, u32[]{:S(2)}, u32[]{:S(2)}) collective-permute-start(bf16[3,448,128]{2,1,0:T(8,128)(2,1)S(1)} %stack.1), channel_id=1, source_target_pairs={{0,1},{1,0},{2,3},{3,2},{4,5},{5,4},{6,7},{7,6},{8,9},{9,8},{10,11... | collective-permute-start | bytes 1032200 | tf_op jit(solution)/shard_map/ppermute | solution.py:333
  37.8 13.4 %collective-permute-start.18 = (bf16[1040,128]{1,0:T(8,128)(2,1)S(1)}, bf16[1040,128]{1,0:T(8,128)(2,1)S(1)}, u32[]{:S(2)}, u32[]{:S(2)}) collective-permute-start(bf16[1040,128]{1,0:T(8,128)(2,1)S(1)} %collective-permute-done.14.refs_5_.refs_6_), channel_id=1, source_target_pairs={{0,8},{4,20},{8,0},{12,28},{16,24},{20,4},{24,16},{28,12},{1,9},{5... | collective-permute-start | bytes 798728 | tf_op jit(solution)/shard_map/ppermute | solution.py:327
  45.5 6.4 %collective-permute-start.17 = (bf16[1040,128]{1,0:T(8,128)(2,1)S(1)}, bf16[1040,128]{1,0:T(8,128)(2,1)S(1)}, u32[]{:S(2)}, u32[]{:S(2)}) collective-permute-start(bf16[1040,128]{1,0:T(8,128)(2,1)S(1)} %collective-permute-done.13.refs_4_.refs_5_), channel_id=1, source_target_pairs={{0,16},{4,12},{8,24},{12,4},{16,0},{20,28},{24,8},{28,20},{1,17},{... | collective-permute-start | bytes 798728 | tf_op jit(solution)/shard_map/ppermute | solution.py:327
  47.9 4.0 %collective-permute-start.16 = (bf16[1040,128]{1,0:T(8,128)(2,1)S(1)}, bf16[1040,128]{1,0:T(8,128)(2,1)S(1)}, u32[]{:S(2)}, u32[]{:S(2)}) collective-permute-start(bf16[1040,128]{1,0:T(8,128)(2,1)S(1)} %late.1), channel_id=1, source_target_pairs={{0,4},{4,0},{8,12},{12,8},{16,20},{20,16},{24,28},{28,24},{1,5},{5... | collective-permute-start | bytes 798728 | tf_op jit(solution)/shard_map/ppermute | solution.py:327
  50.0 3.6 %collective-permute-start.15 = (bf16[256,640]{1,0:T(8,128)(2,1)S(1)}, bf16[256,640]{1,0:T(8,128)(2,1)S(1)}, u32[]{:S(2)}, u32[]{:S(2)}) collective-permute-start(bf16[256,640]{1,0:T(8,128)(2,1)S(1)} %grad_other_near.1), channel_id=1, source_target_pairs={{0,4},{4,0},{8,12},{12,8},{16,20},{20,16},{24,28},{28,24},{1,5},{5... | collective-permute-start | bytes 983048 | tf_op jit(solution)/shard_map/ppermute | solution.py:327
  52.4 2.2 %collective-permute-start.19 = (bf16[256,384]{1,0:T(8,128)(2,1)S(1)}, bf16[256,384]{1,0:T(8,128)(2,1)S(1)}, u32[]{:S(2)}, u32[]{:S(2)}) collective-permute-start(bf16[256,384]{1,0:T(8,128)(2,1)S(1)} %grad_other_far.1), channel_id=1, source_target_pairs={{0,4},{4,0},{8,12},{12,8},{16,20},{20,16},{24,28},{28,24},{1,5},{5... | collective-permute-start | bytes 589832 | tf_op jit(solution)/shard_map/ppermute | solution.py:327

commit v13 on v11

--- a/solution.py
+++ b/solution.py
@@ -159,29 +159,33 @@
         jnp.where(token < counts[s] * TPF, 0.0, -jnp.inf).astype(jnp.float32) for s in range(n)
     ]
     values = [x_ref[s, 2 * tok : 3 * tok, :].T for s in range(n)]
-    for block in range(n):
-        sources = range(max(0, block - (WINB - 1)), block + 1)
+    def scores_of(block):
         q = x_ref[block, 0:tok, :]
-        scores = [
-            lax.dot_general(
+        return {
+            s: lax.dot_general(
                 x_ref[s, tok : 2 * tok, :],
                 q,
                 (((1,), (1,)), ((), ())),
                 preferred_element_type=jnp.float32,
             )
             + bias[s]
-            for s in sources
-        ]
-        top = jnp.max(scores[0], axis=0, keepdims=True)
-        for s in scores[1:]:
-            top = jnp.maximum(top, jnp.max(s, axis=0, keepdims=True))
-        weights = [jnp.exp2((s - top) * rate) for s in scores]
-        total = jnp.sum(weights[0], axis=0, keepdims=True)
-        for w in weights[1:]:
+            for s in range(max(0, block - (WINB - 1)), block + 1)
+        }
+
+    ahead = scores_of(0)
+    for block in range(n):
+        scores, ahead = ahead, scores_of(block + 1) if block + 1 < n else None
+        top = None
+        for x in scores.values():
+            high = jnp.max(x, axis=0, keepdims=True)
+            top = high if top is None else jnp.maximum(top, high)
+        weights = {s: jnp.exp2((x - top) * rate) for s, x in scores.items()}
+        total = jnp.zeros((1, tok), jnp.float32)
+        for w in weights.values():
             total = total + jnp.sum(w, axis=0, keepdims=True)
         share = 1.0 / total
         mixed = jnp.zeros((HD, tok), jnp.float32)
-        for s, w in zip(sources, weights):
+        for s, w in weights.items():
             mixed = mixed + jnp.dot(
                 values[s], (w * share).astype(jnp.bfloat16), preferred_element_type=jnp.float32
             )

time: 55.3 us -> 54 us (0.976)
  Pallas kernels: 14.9 us -> 13.7 us
    pallas_call x1, Pallas kernels: 4.81 us -> 3.55 us  [head_body(): call(lambda *refs: attend_kernel(n, tok, [0] + order, *refs), 'attend', [...]
  transfers between devices with their start and end apart: 20 -> 20, of which waited for: 9 -> 9; matrix products, arithmetic and copies ran while one was open for 0% -> 0% of each run, Pallas kernels for 22% -> 20%
where the time goes in v13:
time: 54 us; the launch traced here: 53.8 us
  waiting for transfers between devices  20 us (37%)
  starting transfers between devices  19.3 us (36%)
  Pallas kernels  13.7 us (25%)
  between operations  0.78 us (1%)
    ppermute x19, waiting for transfers between devices, swap(): return lax.ppermute(x, 'tm', [(i, i ^ bits[i % 2]) for i in range(n)])  20 us
    ppermute x19, starting transfers between devices, swap(): return lax.ppermute(x, 'tm', [(i, i ^ bits[i % 2]) for i in range(n)])  17.7 us
    pallas_call x2, Pallas kernels, pack(): call(lambda *refs: pack_kernel(n, heads, *refs), name, [((length, HD), bf...  4.42 us
    pallas_call x1, Pallas kernels, head_body(): call(lambda *refs: attend_kernel(n, tok, [0] + order, *refs), 'attend', [...  3.55 us
    pallas_call x4, Pallas kernels, grad(): call(lambda *refs: grad_kernel(rows, half, len(heads), *refs), name, [((c...  2.22 us
    ppermute x1, starting transfers between devices, swap_plane(): return lax.ppermute(x, ('tm', 'head'), pairs)  1.64 us
  transfers between devices with their start and end apart: 20, of which 9 were waited for; matrix products, arithmetic and copies ran while one was open for 0% of the time, Pallas kernels for 20%

profile of v13, /device:TPU:0, one launch (start us, length us, event | category | flops | bytes accessed | tf_op | source)
XLA Modules:
  0.0 53.8 jit_solution(4952452481814567987)
XLA Ops:
  0.6 1.9 %pack_first.1 = (bf16[784,128]{1,0:T(8,128)(2,1)}, bf16[784,128]{1,0:T(8,128)(2,1)}) custom-call(bf16[256,1024]{1,0:T(8,128)(2,1)} %refs_0_.6, bf16[256,1024]{1,0:T(8,128)(2,1)} %refs_1_.5, bf16[256,1024]{1,0:T(8,128)(2,1)} %refs_2_.3, bf16[2,1024]{1,0:T(2,128)(2,1)} %refs_3_.3), custom_call_target="tpu_custom_call" | custom-call | bytes 802816 | tf_op jit(solution)/shard_map/pack_first/pallas_call | solution.py:357
  2.5 4.0 %collective-permute-start = (bf16[784,128]{1,0:T(8,128)(2,1)}, bf16[784,128]{1,0:T(8,128)(2,1)S(1)}, u32[]{:S(2)}, u32[]{:S(2)}) collective-permute-start(bf16[784,128]{1,0:T(8,128)(2,1)} %get-tuple-element.20), channel_id=1, source_target_pairs={{0,24},{4,28},{8,16},{12,20},{16,8},{20,12},{24,0},{28,4},{1,25},{... | collective-permute-start | bytes 602120 | tf_op jit(solution)/shard_map/ppermute | solution.py:331
  6.5 2.6 %pack_rest.1 = (bf16[784,128]{1,0:T(8,128)(2,1)}, bf16[784,128]{1,0:T(8,128)(2,1)}, bf16[784,128]{1,0:T(8,128)(2,1)}, bf16[784,128]{1,0:T(8,128)(2,1)}, bf16[784...) custom-call(bf16[256,1024]{1,0:T(8,128)(2,1)} %refs_0_.6, bf16[256,1024]{1,0:T(8,128)(2,1)} %refs_1_.5, ...), custom_call_target="tpu_custom_call" | custom-call | bytes 2408448 | tf_op jit(solution)/shard_map/pack_rest/pallas_call | solution.py:357
  9.1 1.2 %collective-permute-start.5 = (bf16[784,128]{1,0:T(8,128)(2,1)}, bf16[784,128]{1,0:T(8,128)(2,1)S(1)}, u32[]{:S(2)}, u32[]{:S(2)}) collective-permute-start(bf16[784,128]{1,0:T(8,128)(2,1)} %get-tuple-element.27), channel_id=1, source_target_pairs={{0,8},{4,12},{8,0},{12,4},{16,24},{20,28},{24,16},{28,20},{1,9},{5... | collective-permute-start | bytes 602120 | tf_op jit(solution)/shard_map/ppermute | solution.py:331
  10.3 1.5 %collective-permute-start.6 = (bf16[784,128]{1,0:T(8,128)(2,1)}, bf16[784,128]{1,0:T(8,128)(2,1)S(1)}, u32[]{:S(2)}, u32[]{:S(2)}) collective-permute-start(bf16[784,128]{1,0:T(8,128)(2,1)} %get-tuple-element.28), channel_id=1, source_target_pairs={{0,16},{4,20},{8,24},{12,28},{16,0},{20,4},{24,8},{28,12},{1,17},{... | collective-permute-start | bytes 602120 | tf_op jit(solution)/shard_map/ppermute | solution.py:331
  11.8 0.6 %collective-permute-start.7 = (bf16[784,128]{1,0:T(8,128)(2,1)}, bf16[784,128]{1,0:T(8,128)(2,1)S(1)}, u32[]{:S(2)}, u32[]{:S(2)}) collective-permute-start(bf16[784,128]{1,0:T(8,128)(2,1)} %get-tuple-element.29), channel_id=1, source_target_pairs={{0,12},{4,8},{8,4},{12,0},{16,28},{20,24},{24,20},{28,16},{1,13},{... | collective-permute-start | bytes 602120 | tf_op jit(solution)/shard_map/ppermute | solution.py:331
  12.9 3.6 %collective-permute-done.1.refs_3_ = bf16[784,128]{1,0:T(8,128)(2,1)S(1)} collective-permute-done((bf16[784,128]{1,0:T(8,128)(2,1)}, bf16[784,128]{1,0:T(8,128)(2,1)S(1)}, u32[]{:S(2)}, u32[]{:S(2)}) %collective-permute-start.1) | collective-permute-done | bytes 200736 | tf_op jit(solution)/shard_map/ppermute | solution.py:331
  16.6 0.9 %cot.1 = (bf16[1088,128]{1,0:T(8,128)(2,1)S(1)}, bf16[640,128]{1,0:T(8,128)(2,1)S(1)}, bf16[640,128]{1,0:T(8,128)(2,1)S(1)}, bf16[640,128]{1,0:T(8,128)(2,1)S(1)}) custom-call(s32[1,8]{1,0:T(1,128)S(1)} %copy-done.1, bf16[272,2048]{1,0:T(8,128)(2,1)S(1)} %copy-done, bf16[784,128]{1,0:T(8,128)(2,1)S(1)} %collective-permute-done.refs_2_, ...), custom_call_target="tpu_custom_call" | custom-call | bytes 1540096 | tf_op jit(solution)/shard_map/cot/pallas_call | solution.py:380
  17.6 4.1 %collective-permute-done.5.refs_4_ = bf16[784,128]{1,0:T(8,128)(2,1)S(1)} collective-permute-done((bf16[784,128]{1,0:T(8,128)(2,1)}, bf16[784,128]{1,0:T(8,128)(2,1)S(1)}, u32[]{:S(2)}, u32[]{:S(2)}) %collective-permute-start.5) | collective-permute-done | bytes 200736 | tf_op jit(solution)/shard_map/ppermute | solution.py:331
  21.7 1.5 %collective-permute-start.2 = (bf16[640,128]{1,0:T(8,128)(2,1)S(1)}, bf16[640,128]{1,0:T(8,128)(2,1)S(1)}, u32[]{:S(2)}, u32[]{:S(2)}) collective-permute-start(bf16[640,128]{1,0:T(8,128)(2,1)S(1)} %get-tuple-element.23), channel_id=1, source_target_pairs={{0,24},{4,28},{8,16},{12,20},{16,8},{20,12},{24,0},{28,4},{1,25},{... | collective-permute-start | bytes 491528 | tf_op jit(solution)/shard_map/ppermute | solution.py:331
  23.2 1.9 %collective-permute-done.7.refs_6_ = bf16[784,128]{1,0:T(8,128)(2,1)S(1)} collective-permute-done((bf16[784,128]{1,0:T(8,128)(2,1)}, bf16[784,128]{1,0:T(8,128)(2,1)S(1)}, u32[]{:S(2)}, u32[]{:S(2)}) %collective-permute-start.7) | collective-permute-done | bytes 200736 | tf_op jit(solution)/shard_map/ppermute | solution.py:331
  25.1 0.5 collective-permute-start.4
  25.7 3.6 %attend.1 = (bf16[1040,128]{1,0:T(8,128)(2,1)S(1)}, bf16[1040,128]{1,0:T(8,128)(2,1)S(1)}) custom-call(s32[8]{0:T(128)S(1)} %copy-done.3, bf16[784,128]{1,0:T(8,128)(2,1)S(1)} %copy-done.2, bf16[784,128]{1,0:T(8,128)(2,1)S(1)} %collective-permute-done.refs_2_, bf16[784,128]{1,0:T(8,128)(2,1)S(1)} %collective-permute-done.1.refs_3_, ...), custom_call_target="tpu_custom_call" | custom-call | flops 1073741824 | bytes 1064960 | tf_op jit(solution)/shard_map/attend/pallas_call | solution.py:401
  29.2 1.6 %collective-permute-start.14 = (bf16[1040,128]{1,0:T(8,128)(2,1)S(1)}, bf16[1040,128]{1,0:T(8,128)(2,1)S(1)}, u32[]{:S(2)}, u32[]{:S(2)}) collective-permute-start(bf16[1040,128]{1,0:T(8,128)(2,1)S(1)} %get-tuple-element.34.x_ref), channel_id=1, source_target_pairs={{0,12},{4,16},{8,4},{12,24},{16,28},{20,0},{24,20},{28,8},{1,13},{... | collective-permute-start | bytes 798728 | tf_op jit(solution)/shard_map/ppermute | solution.py:331
  30.8 1.5 %collective-permute-start.13 = (bf16[1040,128]{1,0:T(8,128)(2,1)S(1)}, bf16[1040,128]{1,0:T(8,128)(2,1)S(1)}, u32[]{:S(2)}, u32[]{:S(2)}) collective-permute-start(bf16[1040,128]{1,0:T(8,128)(2,1)S(1)} %get-tuple-element.32.refs_3_.refs_1_.refs_2_), channel_id=1, source_target_pairs={{0,8},{4,20},{8,0},{12,28},{16,24},{20,4},{24,16},{28,12},{1,9},{5... | collective-permute-start | bytes 798728 | tf_op jit(solution)/shard_map/ppermute | solution.py:331
  32.5 0.7 %collective-permute-start.12 = (bf16[1040,128]{1,0:T(8,128)(2,1)S(1)}, bf16[1040,128]{1,0:T(8,128)(2,1)S(1)}, u32[]{:S(2)}, u32[]{:S(2)}) collective-permute-start(bf16[1040,128]{1,0:T(8,128)(2,1)S(1)} %get-tuple-element.32.refs_3_.refs_1_.refs_2_), channel_id=1, source_target_pairs={{0,16},{4,12},{8,24},{12,4},{16,0},{20,28},{24,8},{28,20},{1,17},{... | collective-permute-start | bytes 798728 | tf_op jit(solution)/shard_map/ppermute | solution.py:331
  33.2 1.6 %collective-permute-start.10 = (bf16[3,448,128]{2,1,0:T(8,128)(2,1)S(1)}, bf16[3,448,128]{2,1,0:T(8,128)(2,1)S(1)}, u32[]{:S(2)}, u32[]{:S(2)}) collective-permute-start(bf16[3,448,128]{2,1,0:T(8,128)(2,1)S(1)} %stack.1), channel_id=1, source_target_pairs={{0,1},{1,0},{2,3},{3,2},{4,5},{5,4},{6,7},{7,6},{8,9},{9,8},{10,11... | collective-permute-start | bytes 1032200 | tf_op jit(solution)/shard_map/ppermute | solution.py:337
  34.9 1.2 %collective-permute-done.14.refs_5_.refs_6_ = bf16[1040,128]{1,0:T(8,128)(2,1)S(1)} collective-permute-done((bf16[1040,128]{1,0:T(8,128)(2,1)S(1)}, bf16[1040,128]{1,0:T(8,128)(2,1)S(1)}, u32[]{:S(2)}, u32[]{:S(2)}) %collective-permute-start.14) | collective-permute-done | bytes 266272 | tf_op jit(solution)/shard_map/ppermute | solution.py:331
  36.1 1.5 %collective-permute-start.18 = (bf16[1040,128]{1,0:T(8,128)(2,1)S(1)}, bf16[1040,128]{1,0:T(8,128)(2,1)S(1)}, u32[]{:S(2)}, u32[]{:S(2)}) collective-permute-start(bf16[1040,128]{1,0:T(8,128)(2,1)S(1)} %collective-permute-done.14.refs_5_.refs_6_), channel_id=1, source_target_pairs={{0,8},{4,20},{8,0},{12,28},{16,24},{20,4},{24,16},{28,12},{1,9},{5... | collective-permute-start | bytes 798728 | tf_op jit(solution)/shard_map/ppermute | solution.py:331
  37.6 6.2 %collective-permute-done.13.refs_4_.refs_5_ = bf16[1040,128]{1,0:T(8,128)(2,1)S(1)} collective-permute-done((bf16[1040,128]{1,0:T(8,128)(2,1)S(1)}, bf16[1040,128]{1,0:T(8,128)(2,1)S(1)}, u32[]{:S(2)}, u32[]{:S(2)}) %collective-permute-start.13) | collective-permute-done | bytes 266272 | tf_op jit(solution)/shard_map/ppermute | solution.py:331
  43.8 0.8 %collective-permute-start.17 = (bf16[1040,128]{1,0:T(8,128)(2,1)S(1)}, bf16[1040,128]{1,0:T(8,128)(2,1)S(1)}, u32[]{:S(2)}, u32[]{:S(2)}) collective-permute-start(bf16[1040,128]{1,0:T(8,128)(2,1)S(1)} %collective-permute-done.13.refs_4_.refs_5_), channel_id=1, source_target_pairs={{0,16},{4,12},{8,24},{12,4},{16,0},{20,28},{24,8},{28,20},{1,17},{... | collective-permute-start | bytes 798728 | tf_op jit(solution)/shard_map/ppermute | solution.py:331
  44.6 1.6 %collective-permute-done.12.refs_3_.refs_1_.refs_4_ = bf16[1040,128]{1,0:T(8,128)(2,1)S(1)} collective-permute-done((bf16[1040,128]{1,0:T(8,128)(2,1)S(1)}, bf16[1040,128]{1,0:T(8,128)(2,1)S(1)}, u32[]{:S(2)}, u32[]{:S(2)}) %collective-permute-start.12) | collective-permute-done | bytes 266272 | tf_op jit(solution)/shard_map/ppermute | solution.py:331
  46.2 0.8 %collective-permute-start.16 = (bf16[1040,128]{1,0:T(8,128)(2,1)S(1)}, bf16[1040,128]{1,0:T(8,128)(2,1)S(1)}, u32[]{:S(2)}, u32[]{:S(2)}) collective-permute-start(bf16[1040,128]{1,0:T(8,128)(2,1)S(1)} %late.1), channel_id=1, source_target_pairs={{0,4},{4,0},{8,12},{12,8},{16,20},{20,16},{24,28},{28,24},{1,5},{5... | collective-permute-start | bytes 798728 | tf_op jit(solution)/shard_map/ppermute | solution.py:331
  47.0 0.6 %turn.1 = (bf16[256,1088]{1,0:T(8,128)(2,1)S(1)}, bf16[256,1088]{1,0:T(8,128)(2,1)S(1)}) custom-call(bf16[1088,128]{1,0:T(8,128)(2,1)S(1)} %get-tuple-element.22.refs_0_, bf16[640,128]{1,0:T(8,128)(2,1)S(1)} %collective-permute-done.2.refs_0_.refs_1_, bf16[640,128]{1,0:T(8,128)(2,1)S(1)} %collective-permute-done.3.refs_1_.refs_2_, ...), custom_call_target="tpu_custom_call" | custom-call | bytes 2228224 | tf_op jit(solution)/shard_map/turn/pallas_call | solution.py:427
  47.6 0.6 %grad_other_near.1 = bf16[256,640]{1,0:T(8,128)(2,1)S(1)} custom-call(bf16[256,1088]{1,0:T(8,128)(2,1)S(1)} %get-tuple-element.35.refs_0_, bf16[1040,128]{1,0:T(8,128)(2,1)S(1)} %get-tuple-element.32.refs_3_.refs_1_.refs_2_, bf16[1040,128]{1,0:T(8,128)(2,1)S(1)} %collective-permute-done.11.refs_2_.refs_0_.refs_3_, ...), custom_call_target="tpu_custom_call" | custom-call | flops 356515840 | bytes 655360 | tf_op jit(solution)/shard_map/grad_other_near/pallas_call | solution.py:437
  48.3 0.6 %grad_own_near.1.refs_4_.refs_0_ = f32[256,640]{1,0:T(8,128)S(1)} custom-call(bf16[256,1088]{1,0:T(8,128)(2,1)S(1)} %get-tuple-element.33.refs_0_, bf16[1040,128]{1,0:T(8,128)(2,1)S(1)} %get-tuple-element.32.refs_3_.refs_1_.refs_2_, bf16[1040,128]{1,0:T(8,128)(2,1)S(1)} %collective-permute-done.11.refs_2_.refs_0_.refs_3_, ...), custom_call_target="tpu_custom_call" | custom-call | flops 356515840 | bytes 1310720 | tf_op jit(solution)/shard_map/grad_own_near/pallas_call | solution.py:437
  48.9 0.5 %collective-permute-done.18.refs_3_.refs_6_ = bf16[1040,128]{1,0:T(8,128)(2,1)S(1)} collective-permute-done((bf16[1040,128]{1,0:T(8,128)(2,1)S(1)}, bf16[1040,128]{1,0:T(8,128)(2,1)S(1)}, u32[]{:S(2)}, u32[]{:S(2)}) %collective-permute-start.18) | collective-permute-done | bytes 266272 | tf_op jit(solution)/shard_map/ppermute | solution.py:331
  49.5 0.7 %collective-permute-done.17.refs_2_.refs_5_ = bf16[1040,128]{1,0:T(8,128)(2,1)S(1)} collective-permute-done((bf16[1040,128]{1,0:T(8,128)(2,1)S(1)}, bf16[1040,128]{1,0:T(8,128)(2,1)S(1)}, u32[]{:S(2)}, u32[]{:S(2)}) %collective-permute-start.17) | collective-permute-done | bytes 266272 | tf_op jit(solution)/shard_map/ppermute | solution.py:331
  50.2 0.5 grad_other_far.1
  50.7 0.7 %collective-permute-start.19 = (bf16[256,384]{1,0:T(8,128)(2,1)S(1)}, bf16[256,384]{1,0:T(8,128)(2,1)S(1)}, u32[]{:S(2)}, u32[]{:S(2)}) collective-permute-start(bf16[256,384]{1,0:T(8,128)(2,1)S(1)} %grad_other_far.1), channel_id=1, source_target_pairs={{0,4},{4,0},{8,12},{12,8},{16,20},{20,16},{24,28},{28,24},{1,5},{5... | collective-permute-start | bytes 589832 | tf_op jit(solution)/shard_map/ppermute | solution.py:331
  51.8 1.0 %near.1 = (bf16[256,1024]{1,0:T(8,128)(2,1)}, f32[256,1024]{1,0:T(8,128)}) custom-call(f32[256,640]{1,0:T(8,128)S(1)} %grad_own_near.1.refs_4_.refs_0_, bf16[256,640]{1,0:T(8,128)(2,1)S(1)} %collective-permute-done.15.refs_1_, bf16[1040,128]{1,0:T(8,128)(2,1)S(1)} %get-tuple-element.32.refs_3_.refs_1_.refs_2_, ...), custom_call_target="tpu_custom_call" | custom-call | bytes 3145728 | tf_op jit(solution)/shard_map/near/pallas_call | solution.py:453
  52.9 0.9 %last.1 = (bf16[256,1024]{1,0:T(8,128)(2,1)}, f32[256,1024]{1,0:T(8,128)}) custom-call(f32[256,640]{1,0:T(8,128)S(1)} %grad_own_near.1.refs_4_.refs_0_, bf16[256,640]{1,0:T(8,128)(2,1)S(1)} %collective-permute-done.15.refs_1_, f32[256,384]{1,0:T(8,128)S(1)} %grad_own_far.1.refs_2_, ...), custom_call_target="tpu_custom_call", output_to_operand_aliasing={{0}: (7, {}), {1}: (8, {})} | custom-call | bytes 3145728 | tf_op jit(solution)/shard_map/last/pallas_call | solution.py:462
  (29 shorter events, 1.5 us)
Async XLA Ops:
  2.5 14.1 %copy-start = (bf16[272,2048]{1,0:T(8,128)(2,1)S(1)}, bf16[272,2048]{1,0:T(8,128)(2,1)}, u32[]{:S(2)}) copy-start(bf16[272,2048]{1,0:T(8,128)(2,1)} %refs_1_.4) | copy-start | bytes 3342340
  2.5 14.1 %copy-start.1 = (s32[1,8]{1,0:T(1,128)S(1)}, s32[1,8]{1,0:T(1,128)}, u32[]{:S(2)}) copy-start(s32[1,8]{1,0:T(1,128)} %refs_0_.5) | copy-start | bytes 100
  2.5 10.0 %collective-permute-start = (bf16[784,128]{1,0:T(8,128)(2,1)}, bf16[784,128]{1,0:T(8,128)(2,1)S(1)}, u32[]{:S(2)}, u32[]{:S(2)}) collective-permute-start(bf16[784,128]{1,0:T(8,128)(2,1)} %get-tuple-element.20), channel_id=1, source_target_pairs={{0,24},{4,28},{8,16},{12,20},{16,8},{20,12},{24,0},{28,4},{1,25},{... | collective-permute-start | bytes 602120 | tf_op jit(solution)/shard_map/ppermute | solution.py:331
  6.5 10.1 %collective-permute-start.1 = (bf16[784,128]{1,0:T(8,128)(2,1)}, bf16[784,128]{1,0:T(8,128)(2,1)S(1)}, u32[]{:S(2)}, u32[]{:S(2)}) collective-permute-start(bf16[784,128]{1,0:T(8,128)(2,1)} %get-tuple-element.21), channel_id=1, source_target_pairs={{0,28},{4,24},{8,20},{12,16},{16,12},{20,8},{24,4},{28,0},{1,29},{... | collective-permute-start | bytes 602120 | tf_op jit(solution)/shard_map/ppermute | solution.py:331
  9.1 16.6 %copy-start.2 = (bf16[784,128]{1,0:T(8,128)(2,1)S(1)}, bf16[784,128]{1,0:T(8,128)(2,1)}, u32[]{:S(2)}) copy-start(bf16[784,128]{1,0:T(8,128)(2,1)} %get-tuple-element.26.refs_1_) | copy-start | bytes 602116
  9.1 16.6 %copy-start.3 = (s32[8]{0:T(128)S(1)}, s32[8]{0:T(128)}, u32[]{:S(2)}) copy-start(s32[8]{0:T(128)} %refs_0_.7) | copy-start | bytes 100
  9.1 12.6 %collective-permute-start.5 = (bf16[784,128]{1,0:T(8,128)(2,1)}, bf16[784,128]{1,0:T(8,128)(2,1)S(1)}, u32[]{:S(2)}, u32[]{:S(2)}) collective-permute-start(bf16[784,128]{1,0:T(8,128)(2,1)} %get-tuple-element.27), channel_id=1, source_target_pairs={{0,8},{4,12},{8,0},{12,4},{16,24},{20,28},{24,16},{28,20},{1,9},{5... | collective-permute-start | bytes 602120 | tf_op jit(solution)/shard_map/ppermute | solution.py:331
  10.3 12.9 %collective-permute-start.6 = (bf16[784,128]{1,0:T(8,128)(2,1)}, bf16[784,128]{1,0:T(8,128)(2,1)S(1)}, u32[]{:S(2)}, u32[]{:S(2)}) collective-permute-start(bf16[784,128]{1,0:T(8,128)(2,1)} %get-tuple-element.28), channel_id=1, source_target_pairs={{0,16},{4,20},{8,24},{12,28},{16,0},{20,4},{24,8},{28,12},{1,17},{... | collective-permute-start | bytes 602120 | tf_op jit(solution)/shard_map/ppermute | solution.py:331
  11.8 13.3 %collective-permute-start.7 = (bf16[784,128]{1,0:T(8,128)(2,1)}, bf16[784,128]{1,0:T(8,128)(2,1)S(1)}, u32[]{:S(2)}, u32[]{:S(2)}) collective-permute-start(bf16[784,128]{1,0:T(8,128)(2,1)} %get-tuple-element.29), channel_id=1, source_target_pairs={{0,12},{4,8},{8,4},{12,0},{16,28},{20,24},{24,20},{28,16},{1,13},{... | collective-permute-start | bytes 602120 | tf_op jit(solution)/shard_map/ppermute | solution.py:331
  12.5 13.1 %collective-permute-start.8 = (bf16[784,128]{1,0:T(8,128)(2,1)}, bf16[784,128]{1,0:T(8,128)(2,1)S(1)}, u32[]{:S(2)}, u32[]{:S(2)}) collective-permute-start(bf16[784,128]{1,0:T(8,128)(2,1)} %get-tuple-element.30), channel_id=1, source_target_pairs={{0,20},{4,16},{8,28},{12,24},{16,4},{20,0},{24,12},{28,8},{1,21},{... | collective-permute-start | bytes 602120 | tf_op jit(solution)/shard_map/ppermute | solution.py:331
  16.5 9.1 %collective-permute-start.9 = (bf16[784,128]{1,0:T(8,128)(2,1)}, bf16[784,128]{1,0:T(8,128)(2,1)S(1)}, u32[]{:S(2)}, u32[]{:S(2)}) collective-permute-start(bf16[784,128]{1,0:T(8,128)(2,1)} %get-tuple-element.31), channel_id=1, source_target_pairs={{0,4},{4,0},{8,12},{12,8},{16,20},{20,16},{24,28},{28,24},{1,5},{5... | collective-permute-start | bytes 602120 | tf_op jit(solution)/shard_map/ppermute | solution.py:331
  21.7 10.7 %collective-permute-start.2 = (bf16[640,128]{1,0:T(8,128)(2,1)S(1)}, bf16[640,128]{1,0:T(8,128)(2,1)S(1)}, u32[]{:S(2)}, u32[]{:S(2)}) collective-permute-start(bf16[640,128]{1,0:T(8,128)(2,1)S(1)} %get-tuple-element.23), channel_id=1, source_target_pairs={{0,24},{4,28},{8,16},{12,20},{16,8},{20,12},{24,0},{28,4},{1,25},{... | collective-permute-start | bytes 491528 | tf_op jit(solution)/shard_map/ppermute | solution.py:331
  23.2 9.3 %collective-permute-start.3 = (bf16[640,128]{1,0:T(8,128)(2,1)S(1)}, bf16[640,128]{1,0:T(8,128)(2,1)S(1)}, u32[]{:S(2)}, u32[]{:S(2)}) collective-permute-start(bf16[640,128]{1,0:T(8,128)(2,1)S(1)} %get-tuple-element.24), channel_id=1, source_target_pairs={{0,8},{4,20},{8,0},{12,28},{16,24},{20,4},{24,16},{28,12},{1,9},{5... | collective-permute-start | bytes 491528 | tf_op jit(solution)/shard_map/ppermute | solution.py:331
  25.1 8.1 %collective-permute-start.4 = (bf16[640,128]{1,0:T(8,128)(2,1)S(1)}, bf16[640,128]{1,0:T(8,128)(2,1)S(1)}, u32[]{:S(2)}, u32[]{:S(2)}) collective-permute-start(bf16[640,128]{1,0:T(8,128)(2,1)S(1)} %get-tuple-element.25), channel_id=1, source_target_pairs={{0,16},{4,12},{8,24},{12,4},{16,0},{20,28},{24,8},{28,20},{1,17},{... | collective-permute-start | bytes 491528 | tf_op jit(solution)/shard_map/ppermute | solution.py:331
  29.2 6.8 %collective-permute-start.14 = (bf16[1040,128]{1,0:T(8,128)(2,1)S(1)}, bf16[1040,128]{1,0:T(8,128)(2,1)S(1)}, u32[]{:S(2)}, u32[]{:S(2)}) collective-permute-start(bf16[1040,128]{1,0:T(8,128)(2,1)S(1)} %get-tuple-element.34.x_ref), channel_id=1, source_target_pairs={{0,12},{4,16},{8,4},{12,24},{16,28},{20,0},{24,20},{28,8},{1,13},{... | collective-permute-start | bytes 798728 | tf_op jit(solution)/shard_map/ppermute | solution.py:331
  30.8 13.0 %collective-permute-start.13 = (bf16[1040,128]{1,0:T(8,128)(2,1)S(1)}, bf16[1040,128]{1,0:T(8,128)(2,1)S(1)}, u32[]{:S(2)}, u32[]{:S(2)}) collective-permute-start(bf16[1040,128]{1,0:T(8,128)(2,1)S(1)} %get-tuple-element.32.refs_3_.refs_1_.refs_2_), channel_id=1, source_target_pairs={{0,8},{4,20},{8,0},{12,28},{16,24},{20,4},{24,16},{28,12},{1,9},{5... | collective-permute-start | bytes 798728 | tf_op jit(solution)/shard_map/ppermute | solution.py:331
  32.3 12.2 %collective-permute-start.11 = (bf16[1040,128]{1,0:T(8,128)(2,1)S(1)}, bf16[1040,128]{1,0:T(8,128)(2,1)S(1)}, u32[]{:S(2)}, u32[]{:S(2)}) collective-permute-start(bf16[1040,128]{1,0:T(8,128)(2,1)S(1)} %get-tuple-element.34.x_ref), channel_id=1, source_target_pairs={{0,20},{4,8},{8,28},{12,0},{16,4},{20,24},{24,12},{28,16},{1,21},{... | collective-permute-start | bytes 798728 | tf_op jit(solution)/shard_map/ppermute | solution.py:331
  32.5 13.7 %collective-permute-start.12 = (bf16[1040,128]{1,0:T(8,128)(2,1)S(1)}, bf16[1040,128]{1,0:T(8,128)(2,1)S(1)}, u32[]{:S(2)}, u32[]{:S(2)}) collective-permute-start(bf16[1040,128]{1,0:T(8,128)(2,1)S(1)} %get-tuple-element.32.refs_3_.refs_1_.refs_2_), channel_id=1, source_target_pairs={{0,16},{4,12},{8,24},{12,4},{16,0},{20,28},{24,8},{28,20},{1,17},{... | collective-permute-start | bytes 798728 | tf_op jit(solution)/shard_map/ppermute | solution.py:331
  33.2 13.8 %collective-permute-start.10 = (bf16[3,448,128]{2,1,0:T(8,128)(2,1)S(1)}, bf16[3,448,128]{2,1,0:T(8,128)(2,1)S(1)}, u32[]{:S(2)}, u32[]{:S(2)}) collective-permute-start(bf16[3,448,128]{2,1,0:T(8,128)(2,1)S(1)} %stack.1), channel_id=1, source_target_pairs={{0,1},{1,0},{2,3},{3,2},{4,5},{5,4},{6,7},{7,6},{8,9},{9,8},{10,11... | collective-permute-start | bytes 1032200 | tf_op jit(solution)/shard_map/ppermute | solution.py:337
  36.1 13.4 %collective-permute-start.18 = (bf16[1040,128]{1,0:T(8,128)(2,1)S(1)}, bf16[1040,128]{1,0:T(8,128)(2,1)S(1)}, u32[]{:S(2)}, u32[]{:S(2)}) collective-permute-start(bf16[1040,128]{1,0:T(8,128)(2,1)S(1)} %collective-permute-done.14.refs_5_.refs_6_), channel_id=1, source_target_pairs={{0,8},{4,20},{8,0},{12,28},{16,24},{20,4},{24,16},{28,12},{1,9},{5... | collective-permute-start | bytes 798728 | tf_op jit(solution)/shard_map/ppermute | solution.py:331
  43.8 6.4 %collective-permute-start.17 = (bf16[1040,128]{1,0:T(8,128)(2,1)S(1)}, bf16[1040,128]{1,0:T(8,128)(2,1)S(1)}, u32[]{:S(2)}, u32[]{:S(2)}) collective-permute-start(bf16[1040,128]{1,0:T(8,128)(2,1)S(1)} %collective-permute-done.13.refs_4_.refs_5_), channel_id=1, source_target_pairs={{0,16},{4,12},{8,24},{12,4},{16,0},{20,28},{24,8},{28,20},{1,17},{... | collective-permute-start | bytes 798728 | tf_op jit(solution)/shard_map/ppermute | solution.py:331
  46.2 4.0 %collective-permute-start.16 = (bf16[1040,128]{1,0:T(8,128)(2,1)S(1)}, bf16[1040,128]{1,0:T(8,128)(2,1)S(1)}, u32[]{:S(2)}, u32[]{:S(2)}) collective-permute-start(bf16[1040,128]{1,0:T(8,128)(2,1)S(1)} %late.1), channel_id=1, source_target_pairs={{0,4},{4,0},{8,12},{12,8},{16,20},{20,16},{24,28},{28,24},{1,5},{5... | collective-permute-start | bytes 798728 | tf_op jit(solution)/shard_map/ppermute | solution.py:331
  48.2 3.6 %collective-permute-start.15 = (bf16[256,640]{1,0:T(8,128)(2,1)S(1)}, bf16[256,640]{1,0:T(8,128)(2,1)S(1)}, u32[]{:S(2)}, u32[]{:S(2)}) collective-permute-start(bf16[256,640]{1,0:T(8,128)(2,1)S(1)} %grad_other_near.1), channel_id=1, source_target_pairs={{0,4},{4,0},{8,12},{12,8},{16,20},{20,16},{24,28},{28,24},{1,5},{5... | collective-permute-start | bytes 983048 | tf_op jit(solution)/shard_map/ppermute | solution.py:331
  50.7 2.2 %collective-permute-start.19 = (bf16[256,384]{1,0:T(8,128)(2,1)S(1)}, bf16[256,384]{1,0:T(8,128)(2,1)S(1)}, u32[]{:S(2)}, u32[]{:S(2)}) collective-permute-start(bf16[256,384]{1,0:T(8,128)(2,1)S(1)} %grad_other_far.1), channel_id=1, source_target_pairs={{0,4},{4,0},{8,12},{12,8},{16,20},{20,16},{24,28},{28,24},{1,5},{5... | collective-permute-start | bytes 589832 | tf_op jit(solution)/shard_map/ppermute | solution.py:331

commit v14 on v13

--- a/solution.py
+++ b/solution.py
@@ -172,9 +172,17 @@
             for s in range(max(0, block - (WINB - 1)), block + 1)
         }
 
-    ahead = scores_of(0)
+    def mix(block, probs):
+        mixed = jnp.zeros((HD, tok), jnp.float32)
+        for s, p in probs.items():
+            mixed = mixed + jnp.dot(values[s], p, preferred_element_type=jnp.float32)
+        mixed_ref[block] = mixed.astype(jnp.bfloat16).T
+
+    ahead, behind = scores_of(0), None
     for block in range(n):
         scores, ahead = ahead, scores_of(block + 1) if block + 1 < n else None
+        if behind is not None:
+            mix(block - 1, behind)
         top = None
         for x in scores.values():
             high = jnp.max(x, axis=0, keepdims=True)
@@ -184,12 +192,8 @@
         for w in weights.values():
             total = total + jnp.sum(w, axis=0, keepdims=True)
         share = 1.0 / total
-        mixed = jnp.zeros((HD, tok), jnp.float32)
-        for s, w in weights.items():
-            mixed = mixed + jnp.dot(
-                values[s], (w * share).astype(jnp.bfloat16), preferred_element_type=jnp.float32
-            )
-        mixed_ref[block] = mixed.astype(jnp.bfloat16).T
+        behind = {s: (w * share).astype(jnp.bfloat16) for s, w in weights.items()}
+    mix(n - 1, behind)
     rows = n // 2 * tok
     clip_rows = same_ref.shape[0] - rows
     hist = jnp.zeros((clip_rows, HD), jnp.float32)

time: 54 us -> 53.9 us (level)
  no operation moved by 1% of the time
where the time goes in v14:
time: 53.9 us; the launch traced here: 53.7 us
  waiting for transfers between devices  20 us (37%)
  starting transfers between devices  19.4 us (36%)
  Pallas kernels  13.6 us (25%)
  between operations  0.78 us (1%)
    ppermute x19, waiting for transfers between devices, swap(): return lax.ppermute(x, 'tm', [(i, i ^ bits[i % 2]) for i in range(n)])  20 us
    ppermute x19, starting transfers between devices, swap(): return lax.ppermute(x, 'tm', [(i, i ^ bits[i % 2]) for i in range(n)])  17.7 us
    pallas_call x2, Pallas kernels, pack(): call(lambda *refs: pack_kernel(n, heads, *refs), name, [((length, HD), bf...  4.42 us
    pallas_call x1, Pallas kernels, head_body(): call(lambda *refs: attend_kernel(n, tok, [0] + order, *refs), 'attend', [...  3.48 us
    pallas_call x4, Pallas kernels, grad(): call(lambda *refs: grad_kernel(rows, half, len(heads), *refs), name, [((c...  2.23 us
    ppermute x1, starting transfers between devices, swap_plane(): return lax.ppermute(x, ('tm', 'head'), pairs)  1.64 us
  transfers between devices with their start and end apart: 20, of which 9 were waited for; matrix products, arithmetic and copies ran while one was open for 0% of the time, Pallas kernels for 20%

profile of v14, /device:TPU:0, one launch (start us, length us, event | category | flops | bytes accessed | tf_op | source)
XLA Modules:
  0.0 53.7 jit_solution(12519039727107377504)
XLA Ops:
  0.6 1.9 %pack_first.1 = (bf16[784,128]{1,0:T(8,128)(2,1)}, bf16[784,128]{1,0:T(8,128)(2,1)}) custom-call(bf16[256,1024]{1,0:T(8,128)(2,1)} %refs_0_.6, bf16[256,1024]{1,0:T(8,128)(2,1)} %refs_1_.5, bf16[256,1024]{1,0:T(8,128)(2,1)} %refs_2_.3, bf16[2,1024]{1,0:T(2,128)(2,1)} %refs_3_.3), custom_call_target="tpu_custom_call" | custom-call | bytes 802816 | tf_op jit(solution)/shard_map/pack_first/pallas_call | solution.py:361
  2.5 4.0 %collective-permute-start = (bf16[784,128]{1,0:T(8,128)(2,1)}, bf16[784,128]{1,0:T(8,128)(2,1)S(1)}, u32[]{:S(2)}, u32[]{:S(2)}) collective-permute-start(bf16[784,128]{1,0:T(8,128)(2,1)} %get-tuple-element.20), channel_id=1, source_target_pairs={{0,24},{4,28},{8,16},{12,20},{16,8},{20,12},{24,0},{28,4},{1,25},{... | collective-permute-start | bytes 602120 | tf_op jit(solution)/shard_map/ppermute | solution.py:335
  6.5 2.6 %pack_rest.1 = (bf16[784,128]{1,0:T(8,128)(2,1)}, bf16[784,128]{1,0:T(8,128)(2,1)}, bf16[784,128]{1,0:T(8,128)(2,1)}, bf16[784,128]{1,0:T(8,128)(2,1)}, bf16[784...) custom-call(bf16[256,1024]{1,0:T(8,128)(2,1)} %refs_0_.6, bf16[256,1024]{1,0:T(8,128)(2,1)} %refs_1_.5, ...), custom_call_target="tpu_custom_call" | custom-call | bytes 2408448 | tf_op jit(solution)/shard_map/pack_rest/pallas_call | solution.py:361
  9.1 1.2 %collective-permute-start.5 = (bf16[784,128]{1,0:T(8,128)(2,1)}, bf16[784,128]{1,0:T(8,128)(2,1)S(1)}, u32[]{:S(2)}, u32[]{:S(2)}) collective-permute-start(bf16[784,128]{1,0:T(8,128)(2,1)} %get-tuple-element.27), channel_id=1, source_target_pairs={{0,8},{4,12},{8,0},{12,4},{16,24},{20,28},{24,16},{28,20},{1,9},{5... | collective-permute-start | bytes 602120 | tf_op jit(solution)/shard_map/ppermute | solution.py:335
  10.3 1.5 %collective-permute-start.6 = (bf16[784,128]{1,0:T(8,128)(2,1)}, bf16[784,128]{1,0:T(8,128)(2,1)S(1)}, u32[]{:S(2)}, u32[]{:S(2)}) collective-permute-start(bf16[784,128]{1,0:T(8,128)(2,1)} %get-tuple-element.28), channel_id=1, source_target_pairs={{0,16},{4,20},{8,24},{12,28},{16,0},{20,4},{24,8},{28,12},{1,17},{... | collective-permute-start | bytes 602120 | tf_op jit(solution)/shard_map/ppermute | solution.py:335
  11.8 0.6 %collective-permute-start.7 = (bf16[784,128]{1,0:T(8,128)(2,1)}, bf16[784,128]{1,0:T(8,128)(2,1)S(1)}, u32[]{:S(2)}, u32[]{:S(2)}) collective-permute-start(bf16[784,128]{1,0:T(8,128)(2,1)} %get-tuple-element.29), channel_id=1, source_target_pairs={{0,12},{4,8},{8,4},{12,0},{16,28},{20,24},{24,20},{28,16},{1,13},{... | collective-permute-start | bytes 602120 | tf_op jit(solution)/shard_map/ppermute | solution.py:335
  12.9 3.6 %collective-permute-done.1.refs_3_ = bf16[784,128]{1,0:T(8,128)(2,1)S(1)} collective-permute-done((bf16[784,128]{1,0:T(8,128)(2,1)}, bf16[784,128]{1,0:T(8,128)(2,1)S(1)}, u32[]{:S(2)}, u32[]{:S(2)}) %collective-permute-start.1) | collective-permute-done | bytes 200736 | tf_op jit(solution)/shard_map/ppermute | solution.py:335
  16.6 0.9 %cot.1 = (bf16[1088,128]{1,0:T(8,128)(2,1)S(1)}, bf16[640,128]{1,0:T(8,128)(2,1)S(1)}, bf16[640,128]{1,0:T(8,128)(2,1)S(1)}, bf16[640,128]{1,0:T(8,128)(2,1)S(1)}) custom-call(s32[1,8]{1,0:T(1,128)S(1)} %copy-done.1, bf16[272,2048]{1,0:T(8,128)(2,1)S(1)} %copy-done, bf16[784,128]{1,0:T(8,128)(2,1)S(1)} %collective-permute-done.refs_2_, ...), custom_call_target="tpu_custom_call" | custom-call | bytes 1540096 | tf_op jit(solution)/shard_map/cot/pallas_call | solution.py:384
  17.6 4.1 %collective-permute-done.5.refs_4_ = bf16[784,128]{1,0:T(8,128)(2,1)S(1)} collective-permute-done((bf16[784,128]{1,0:T(8,128)(2,1)}, bf16[784,128]{1,0:T(8,128)(2,1)S(1)}, u32[]{:S(2)}, u32[]{:S(2)}) %collective-permute-start.5) | collective-permute-done | bytes 200736 | tf_op jit(solution)/shard_map/ppermute | solution.py:335
  21.7 1.5 %collective-permute-start.2 = (bf16[640,128]{1,0:T(8,128)(2,1)S(1)}, bf16[640,128]{1,0:T(8,128)(2,1)S(1)}, u32[]{:S(2)}, u32[]{:S(2)}) collective-permute-start(bf16[640,128]{1,0:T(8,128)(2,1)S(1)} %get-tuple-element.23), channel_id=1, source_target_pairs={{0,24},{4,28},{8,16},{12,20},{16,8},{20,12},{24,0},{28,4},{1,25},{... | collective-permute-start | bytes 491528 | tf_op jit(solution)/shard_map/ppermute | solution.py:335
  23.2 1.9 %collective-permute-done.7.refs_6_ = bf16[784,128]{1,0:T(8,128)(2,1)S(1)} collective-permute-done((bf16[784,128]{1,0:T(8,128)(2,1)}, bf16[784,128]{1,0:T(8,128)(2,1)S(1)}, u32[]{:S(2)}, u32[]{:S(2)}) %collective-permute-start.7) | collective-permute-done | bytes 200736 | tf_op jit(solution)/shard_map/ppermute | solution.py:335
  25.1 0.5 collective-permute-start.4
  25.7 3.5 %attend.1 = (bf16[1040,128]{1,0:T(8,128)(2,1)S(1)}, bf16[1040,128]{1,0:T(8,128)(2,1)S(1)}) custom-call(s32[8]{0:T(128)S(1)} %copy-done.3, bf16[784,128]{1,0:T(8,128)(2,1)S(1)} %copy-done.2, bf16[784,128]{1,0:T(8,128)(2,1)S(1)} %collective-permute-done.refs_2_, bf16[784,128]{1,0:T(8,128)(2,1)S(1)} %collective-permute-done.1.refs_3_, ...), custom_call_target="tpu_custom_call" | custom-call | flops 1073741824 | bytes 1064960 | tf_op jit(solution)/shard_map/attend/pallas_call | solution.py:405
  29.1 1.6 %collective-permute-start.14 = (bf16[1040,128]{1,0:T(8,128)(2,1)S(1)}, bf16[1040,128]{1,0:T(8,128)(2,1)S(1)}, u32[]{:S(2)}, u32[]{:S(2)}) collective-permute-start(bf16[1040,128]{1,0:T(8,128)(2,1)S(1)} %get-tuple-element.34.x_ref), channel_id=1, source_target_pairs={{0,12},{4,16},{8,4},{12,24},{16,28},{20,0},{24,20},{28,8},{1,13},{... | collective-permute-start | bytes 798728 | tf_op jit(solution)/shard_map/ppermute | solution.py:335
  30.7 1.5 %collective-permute-start.13 = (bf16[1040,128]{1,0:T(8,128)(2,1)S(1)}, bf16[1040,128]{1,0:T(8,128)(2,1)S(1)}, u32[]{:S(2)}, u32[]{:S(2)}) collective-permute-start(bf16[1040,128]{1,0:T(8,128)(2,1)S(1)} %get-tuple-element.32.refs_3_.refs_1_.refs_2_), channel_id=1, source_target_pairs={{0,8},{4,20},{8,0},{12,28},{16,24},{20,4},{24,16},{28,12},{1,9},{5... | collective-permute-start | bytes 798728 | tf_op jit(solution)/shard_map/ppermute | solution.py:335
  32.4 0.7 %collective-permute-start.12 = (bf16[1040,128]{1,0:T(8,128)(2,1)S(1)}, bf16[1040,128]{1,0:T(8,128)(2,1)S(1)}, u32[]{:S(2)}, u32[]{:S(2)}) collective-permute-start(bf16[1040,128]{1,0:T(8,128)(2,1)S(1)} %get-tuple-element.32.refs_3_.refs_1_.refs_2_), channel_id=1, source_target_pairs={{0,16},{4,12},{8,24},{12,4},{16,0},{20,28},{24,8},{28,20},{1,17},{... | collective-permute-start | bytes 798728 | tf_op jit(solution)/shard_map/ppermute | solution.py:335
  33.2 1.6 %collective-permute-start.10 = (bf16[3,448,128]{2,1,0:T(8,128)(2,1)S(1)}, bf16[3,448,128]{2,1,0:T(8,128)(2,1)S(1)}, u32[]{:S(2)}, u32[]{:S(2)}) collective-permute-start(bf16[3,448,128]{2,1,0:T(8,128)(2,1)S(1)} %stack.1), channel_id=1, source_target_pairs={{0,1},{1,0},{2,3},{3,2},{4,5},{5,4},{6,7},{7,6},{8,9},{9,8},{10,11... | collective-permute-start | bytes 1032200 | tf_op jit(solution)/shard_map/ppermute | solution.py:341
  34.8 1.2 %collective-permute-done.14.refs_5_.refs_6_ = bf16[1040,128]{1,0:T(8,128)(2,1)S(1)} collective-permute-done((bf16[1040,128]{1,0:T(8,128)(2,1)S(1)}, bf16[1040,128]{1,0:T(8,128)(2,1)S(1)}, u32[]{:S(2)}, u32[]{:S(2)}) %collective-permute-start.14) | collective-permute-done | bytes 266272 | tf_op jit(solution)/shard_map/ppermute | solution.py:335
  36.0 1.5 %collective-permute-start.18 = (bf16[1040,128]{1,0:T(8,128)(2,1)S(1)}, bf16[1040,128]{1,0:T(8,128)(2,1)S(1)}, u32[]{:S(2)}, u32[]{:S(2)}) collective-permute-start(bf16[1040,128]{1,0:T(8,128)(2,1)S(1)} %collective-permute-done.14.refs_5_.refs_6_), channel_id=1, source_target_pairs={{0,8},{4,20},{8,0},{12,28},{16,24},{20,4},{24,16},{28,12},{1,9},{5... | collective-permute-start | bytes 798728 | tf_op jit(solution)/shard_map/ppermute | solution.py:335
  37.5 6.2 %collective-permute-done.13.refs_4_.refs_5_ = bf16[1040,128]{1,0:T(8,128)(2,1)S(1)} collective-permute-done((bf16[1040,128]{1,0:T(8,128)(2,1)S(1)}, bf16[1040,128]{1,0:T(8,128)(2,1)S(1)}, u32[]{:S(2)}, u32[]{:S(2)}) %collective-permute-start.13) | collective-permute-done | bytes 266272 | tf_op jit(solution)/shard_map/ppermute | solution.py:335
  43.7 0.8 %collective-permute-start.17 = (bf16[1040,128]{1,0:T(8,128)(2,1)S(1)}, bf16[1040,128]{1,0:T(8,128)(2,1)S(1)}, u32[]{:S(2)}, u32[]{:S(2)}) collective-permute-start(bf16[1040,128]{1,0:T(8,128)(2,1)S(1)} %collective-permute-done.13.refs_4_.refs_5_), channel_id=1, source_target_pairs={{0,16},{4,12},{8,24},{12,4},{16,0},{20,28},{24,8},{28,20},{1,17},{... | collective-permute-start | bytes 798728 | tf_op jit(solution)/shard_map/ppermute | solution.py:335
  44.5 1.6 %collective-permute-done.12.refs_3_.refs_1_.refs_4_ = bf16[1040,128]{1,0:T(8,128)(2,1)S(1)} collective-permute-done((bf16[1040,128]{1,0:T(8,128)(2,1)S(1)}, bf16[1040,128]{1,0:T(8,128)(2,1)S(1)}, u32[]{:S(2)}, u32[]{:S(2)}) %collective-permute-start.12) | collective-permute-done | bytes 266272 | tf_op jit(solution)/shard_map/ppermute | solution.py:335
  46.1 0.8 %collective-permute-start.16 = (bf16[1040,128]{1,0:T(8,128)(2,1)S(1)}, bf16[1040,128]{1,0:T(8,128)(2,1)S(1)}, u32[]{:S(2)}, u32[]{:S(2)}) collective-permute-start(bf16[1040,128]{1,0:T(8,128)(2,1)S(1)} %late.1), channel_id=1, source_target_pairs={{0,4},{4,0},{8,12},{12,8},{16,20},{20,16},{24,28},{28,24},{1,5},{5... | collective-permute-start | bytes 798728 | tf_op jit(solution)/shard_map/ppermute | solution.py:335
  46.9 0.6 %turn.1 = (bf16[256,1088]{1,0:T(8,128)(2,1)S(1)}, bf16[256,1088]{1,0:T(8,128)(2,1)S(1)}) custom-call(bf16[1088,128]{1,0:T(8,128)(2,1)S(1)} %get-tuple-element.22.refs_0_, bf16[640,128]{1,0:T(8,128)(2,1)S(1)} %collective-permute-done.2.refs_0_.refs_1_, bf16[640,128]{1,0:T(8,128)(2,1)S(1)} %collective-permute-done.3.refs_1_.refs_2_, ...), custom_call_target="tpu_custom_call" | custom-call | bytes 2228224 | tf_op jit(solution)/shard_map/turn/pallas_call | solution.py:431
  47.5 0.6 %grad_other_near.1 = bf16[256,640]{1,0:T(8,128)(2,1)S(1)} custom-call(bf16[256,1088]{1,0:T(8,128)(2,1)S(1)} %get-tuple-element.35.refs_0_, bf16[1040,128]{1,0:T(8,128)(2,1)S(1)} %get-tuple-element.32.refs_3_.refs_1_.refs_2_, bf16[1040,128]{1,0:T(8,128)(2,1)S(1)} %collective-permute-done.11.refs_2_.refs_0_.refs_3_, ...), custom_call_target="tpu_custom_call" | custom-call | flops 356515840 | bytes 655360 | tf_op jit(solution)/shard_map/grad_other_near/pallas_call | solution.py:441
  48.2 0.6 %grad_own_near.1.refs_4_.refs_0_ = f32[256,640]{1,0:T(8,128)S(1)} custom-call(bf16[256,1088]{1,0:T(8,128)(2,1)S(1)} %get-tuple-element.33.refs_0_, bf16[1040,128]{1,0:T(8,128)(2,1)S(1)} %get-tuple-element.32.refs_3_.refs_1_.refs_2_, bf16[1040,128]{1,0:T(8,128)(2,1)S(1)} %collective-permute-done.11.refs_2_.refs_0_.refs_3_, ...), custom_call_target="tpu_custom_call" | custom-call | flops 356515840 | bytes 1310720 | tf_op jit(solution)/shard_map/grad_own_near/pallas_call | solution.py:441
  48.9 0.5 collective-permute-done.18.refs_3_.refs_6_
  49.4 0.7 %collective-permute-done.17.refs_2_.refs_5_ = bf16[1040,128]{1,0:T(8,128)(2,1)S(1)} collective-permute-done((bf16[1040,128]{1,0:T(8,128)(2,1)S(1)}, bf16[1040,128]{1,0:T(8,128)(2,1)S(1)}, u32[]{:S(2)}, u32[]{:S(2)}) %collective-permute-start.17) | collective-permute-done | bytes 266272 | tf_op jit(solution)/shard_map/ppermute | solution.py:335
  50.1 0.5 grad_other_far.1
  50.6 0.7 %collective-permute-start.19 = (bf16[256,384]{1,0:T(8,128)(2,1)S(1)}, bf16[256,384]{1,0:T(8,128)(2,1)S(1)}, u32[]{:S(2)}, u32[]{:S(2)}) collective-permute-start(bf16[256,384]{1,0:T(8,128)(2,1)S(1)} %grad_other_far.1), channel_id=1, source_target_pairs={{0,4},{4,0},{8,12},{12,8},{16,20},{20,16},{24,28},{28,24},{1,5},{5... | collective-permute-start | bytes 589832 | tf_op jit(solution)/shard_map/ppermute | solution.py:335
  51.8 1.0 %near.1 = (bf16[256,1024]{1,0:T(8,128)(2,1)}, f32[256,1024]{1,0:T(8,128)}) custom-call(f32[256,640]{1,0:T(8,128)S(1)} %grad_own_near.1.refs_4_.refs_0_, bf16[256,640]{1,0:T(8,128)(2,1)S(1)} %collective-permute-done.15.refs_1_, bf16[1040,128]{1,0:T(8,128)(2,1)S(1)} %get-tuple-element.32.refs_3_.refs_1_.refs_2_, ...), custom_call_target="tpu_custom_call" | custom-call | bytes 3145728 | tf_op jit(solution)/shard_map/near/pallas_call | solution.py:457
  52.8 0.9 %last.1 = (bf16[256,1024]{1,0:T(8,128)(2,1)}, f32[256,1024]{1,0:T(8,128)}) custom-call(f32[256,640]{1,0:T(8,128)S(1)} %grad_own_near.1.refs_4_.refs_0_, bf16[256,640]{1,0:T(8,128)(2,1)S(1)} %collective-permute-done.15.refs_1_, f32[256,384]{1,0:T(8,128)S(1)} %grad_own_far.1.refs_2_, ...), custom_call_target="tpu_custom_call", output_to_operand_aliasing={{0}: (7, {}), {1}: (8, {})} | custom-call | bytes 3145728 | tf_op jit(solution)/shard_map/last/pallas_call | solution.py:466
  (29 shorter events, 1.5 us)
Async XLA Ops:
  2.5 14.1 %copy-start = (bf16[272,2048]{1,0:T(8,128)(2,1)S(1)}, bf16[272,2048]{1,0:T(8,128)(2,1)}, u32[]{:S(2)}) copy-start(bf16[272,2048]{1,0:T(8,128)(2,1)} %refs_1_.4) | copy-start | bytes 3342340
  2.5 14.1 %copy-start.1 = (s32[1,8]{1,0:T(1,128)S(1)}, s32[1,8]{1,0:T(1,128)}, u32[]{:S(2)}) copy-start(s32[1,8]{1,0:T(1,128)} %refs_0_.5) | copy-start | bytes 100
  2.5 10.0 %collective-permute-start = (bf16[784,128]{1,0:T(8,128)(2,1)}, bf16[784,128]{1,0:T(8,128)(2,1)S(1)}, u32[]{:S(2)}, u32[]{:S(2)}) collective-permute-start(bf16[784,128]{1,0:T(8,128)(2,1)} %get-tuple-element.20), channel_id=1, source_target_pairs={{0,24},{4,28},{8,16},{12,20},{16,8},{20,12},{24,0},{28,4},{1,25},{... | collective-permute-start | bytes 602120 | tf_op jit(solution)/shard_map/ppermute | solution.py:335
  6.5 10.1 %collective-permute-start.1 = (bf16[784,128]{1,0:T(8,128)(2,1)}, bf16[784,128]{1,0:T(8,128)(2,1)S(1)}, u32[]{:S(2)}, u32[]{:S(2)}) collective-permute-start(bf16[784,128]{1,0:T(8,128)(2,1)} %get-tuple-element.21), channel_id=1, source_target_pairs={{0,28},{4,24},{8,20},{12,16},{16,12},{20,8},{24,4},{28,0},{1,29},{... | collective-permute-start | bytes 602120 | tf_op jit(solution)/shard_map/ppermute | solution.py:335
  9.1 16.6 %copy-start.2 = (bf16[784,128]{1,0:T(8,128)(2,1)S(1)}, bf16[784,128]{1,0:T(8,128)(2,1)}, u32[]{:S(2)}) copy-start(bf16[784,128]{1,0:T(8,128)(2,1)} %get-tuple-element.26.refs_1_) | copy-start | bytes 602116
  9.1 16.6 %copy-start.3 = (s32[8]{0:T(128)S(1)}, s32[8]{0:T(128)}, u32[]{:S(2)}) copy-start(s32[8]{0:T(128)} %refs_0_.7) | copy-start | bytes 100
  9.1 12.6 %collective-permute-start.5 = (bf16[784,128]{1,0:T(8,128)(2,1)}, bf16[784,128]{1,0:T(8,128)(2,1)S(1)}, u32[]{:S(2)}, u32[]{:S(2)}) collective-permute-start(bf16[784,128]{1,0:T(8,128)(2,1)} %get-tuple-element.27), channel_id=1, source_target_pairs={{0,8},{4,12},{8,0},{12,4},{16,24},{20,28},{24,16},{28,20},{1,9},{5... | collective-permute-start | bytes 602120 | tf_op jit(solution)/shard_map/ppermute | solution.py:335
  10.3 12.9 %collective-permute-start.6 = (bf16[784,128]{1,0:T(8,128)(2,1)}, bf16[784,128]{1,0:T(8,128)(2,1)S(1)}, u32[]{:S(2)}, u32[]{:S(2)}) collective-permute-start(bf16[784,128]{1,0:T(8,128)(2,1)} %get-tuple-element.28), channel_id=1, source_target_pairs={{0,16},{4,20},{8,24},{12,28},{16,0},{20,4},{24,8},{28,12},{1,17},{... | collective-permute-start | bytes 602120 | tf_op jit(solution)/shard_map/ppermute | solution.py:335
  11.8 13.3 %collective-permute-start.7 = (bf16[784,128]{1,0:T(8,128)(2,1)}, bf16[784,128]{1,0:T(8,128)(2,1)S(1)}, u32[]{:S(2)}, u32[]{:S(2)}) collective-permute-start(bf16[784,128]{1,0:T(8,128)(2,1)} %get-tuple-element.29), channel_id=1, source_target_pairs={{0,12},{4,8},{8,4},{12,0},{16,28},{20,24},{24,20},{28,16},{1,13},{... | collective-permute-start | bytes 602120 | tf_op jit(solution)/shard_map/ppermute | solution.py:335
  12.5 13.1 %collective-permute-start.8 = (bf16[784,128]{1,0:T(8,128)(2,1)}, bf16[784,128]{1,0:T(8,128)(2,1)S(1)}, u32[]{:S(2)}, u32[]{:S(2)}) collective-permute-start(bf16[784,128]{1,0:T(8,128)(2,1)} %get-tuple-element.30), channel_id=1, source_target_pairs={{0,20},{4,16},{8,28},{12,24},{16,4},{20,0},{24,12},{28,8},{1,21},{... | collective-permute-start | bytes 602120 | tf_op jit(solution)/shard_map/ppermute | solution.py:335
  16.5 9.1 %collective-permute-start.9 = (bf16[784,128]{1,0:T(8,128)(2,1)}, bf16[784,128]{1,0:T(8,128)(2,1)S(1)}, u32[]{:S(2)}, u32[]{:S(2)}) collective-permute-start(bf16[784,128]{1,0:T(8,128)(2,1)} %get-tuple-element.31), channel_id=1, source_target_pairs={{0,4},{4,0},{8,12},{12,8},{16,20},{20,16},{24,28},{28,24},{1,5},{5... | collective-permute-start | bytes 602120 | tf_op jit(solution)/shard_map/ppermute | solution.py:335
  21.7 10.6 %collective-permute-start.2 = (bf16[640,128]{1,0:T(8,128)(2,1)S(1)}, bf16[640,128]{1,0:T(8,128)(2,1)S(1)}, u32[]{:S(2)}, u32[]{:S(2)}) collective-permute-start(bf16[640,128]{1,0:T(8,128)(2,1)S(1)} %get-tuple-element.23), channel_id=1, source_target_pairs={{0,24},{4,28},{8,16},{12,20},{16,8},{20,12},{24,0},{28,4},{1,25},{... | collective-permute-start | bytes 491528 | tf_op jit(solution)/shard_map/ppermute | solution.py:335
  23.2 9.3 %collective-permute-start.3 = (bf16[640,128]{1,0:T(8,128)(2,1)S(1)}, bf16[640,128]{1,0:T(8,128)(2,1)S(1)}, u32[]{:S(2)}, u32[]{:S(2)}) collective-permute-start(bf16[640,128]{1,0:T(8,128)(2,1)S(1)} %get-tuple-element.24), channel_id=1, source_target_pairs={{0,8},{4,20},{8,0},{12,28},{16,24},{20,4},{24,16},{28,12},{1,9},{5... | collective-permute-start | bytes 491528 | tf_op jit(solution)/shard_map/ppermute | solution.py:335
  25.1 8.0 %collective-permute-start.4 = (bf16[640,128]{1,0:T(8,128)(2,1)S(1)}, bf16[640,128]{1,0:T(8,128)(2,1)S(1)}, u32[]{:S(2)}, u32[]{:S(2)}) collective-permute-start(bf16[640,128]{1,0:T(8,128)(2,1)S(1)} %get-tuple-element.25), channel_id=1, source_target_pairs={{0,16},{4,12},{8,24},{12,4},{16,0},{20,28},{24,8},{28,20},{1,17},{... | collective-permute-start | bytes 491528 | tf_op jit(solution)/shard_map/ppermute | solution.py:335
  29.1 6.8 %collective-permute-start.14 = (bf16[1040,128]{1,0:T(8,128)(2,1)S(1)}, bf16[1040,128]{1,0:T(8,128)(2,1)S(1)}, u32[]{:S(2)}, u32[]{:S(2)}) collective-permute-start(bf16[1040,128]{1,0:T(8,128)(2,1)S(1)} %get-tuple-element.34.x_ref), channel_id=1, source_target_pairs={{0,12},{4,16},{8,4},{12,24},{16,28},{20,0},{24,20},{28,8},{1,13},{... | collective-permute-start | bytes 798728 | tf_op jit(solution)/shard_map/ppermute | solution.py:335
  30.7 13.0 %collective-permute-start.13 = (bf16[1040,128]{1,0:T(8,128)(2,1)S(1)}, bf16[1040,128]{1,0:T(8,128)(2,1)S(1)}, u32[]{:S(2)}, u32[]{:S(2)}) collective-permute-start(bf16[1040,128]{1,0:T(8,128)(2,1)S(1)} %get-tuple-element.32.refs_3_.refs_1_.refs_2_), channel_id=1, source_target_pairs={{0,8},{4,20},{8,0},{12,28},{16,24},{20,4},{24,16},{28,12},{1,9},{5... | collective-permute-start | bytes 798728 | tf_op jit(solution)/shard_map/ppermute | solution.py:335
  32.2 12.2 %collective-permute-start.11 = (bf16[1040,128]{1,0:T(8,128)(2,1)S(1)}, bf16[1040,128]{1,0:T(8,128)(2,1)S(1)}, u32[]{:S(2)}, u32[]{:S(2)}) collective-permute-start(bf16[1040,128]{1,0:T(8,128)(2,1)S(1)} %get-tuple-element.34.x_ref), channel_id=1, source_target_pairs={{0,20},{4,8},{8,28},{12,0},{16,4},{20,24},{24,12},{28,16},{1,21},{... | collective-permute-start | bytes 798728 | tf_op jit(solution)/shard_map/ppermute | solution.py:335
  32.4 13.7 %collective-permute-start.12 = (bf16[1040,128]{1,0:T(8,128)(2,1)S(1)}, bf16[1040,128]{1,0:T(8,128)(2,1)S(1)}, u32[]{:S(2)}, u32[]{:S(2)}) collective-permute-start(bf16[1040,128]{1,0:T(8,128)(2,1)S(1)} %get-tuple-element.32.refs_3_.refs_1_.refs_2_), channel_id=1, source_target_pairs={{0,16},{4,12},{8,24},{12,4},{16,0},{20,28},{24,8},{28,20},{1,17},{... | collective-permute-start | bytes 798728 | tf_op jit(solution)/shard_map/ppermute | solution.py:335
  33.2 13.8 %collective-permute-start.10 = (bf16[3,448,128]{2,1,0:T(8,128)(2,1)S(1)}, bf16[3,448,128]{2,1,0:T(8,128)(2,1)S(1)}, u32[]{:S(2)}, u32[]{:S(2)}) collective-permute-start(bf16[3,448,128]{2,1,0:T(8,128)(2,1)S(1)} %stack.1), channel_id=1, source_target_pairs={{0,1},{1,0},{2,3},{3,2},{4,5},{5,4},{6,7},{7,6},{8,9},{9,8},{10,11... | collective-permute-start | bytes 1032200 | tf_op jit(solution)/shard_map/ppermute | solution.py:341
  36.0 13.4 %collective-permute-start.18 = (bf16[1040,128]{1,0:T(8,128)(2,1)S(1)}, bf16[1040,128]{1,0:T(8,128)(2,1)S(1)}, u32[]{:S(2)}, u32[]{:S(2)}) collective-permute-start(bf16[1040,128]{1,0:T(8,128)(2,1)S(1)} %collective-permute-done.14.refs_5_.refs_6_), channel_id=1, source_target_pairs={{0,8},{4,20},{8,0},{12,28},{16,24},{20,4},{24,16},{28,12},{1,9},{5... | collective-permute-start | bytes 798728 | tf_op jit(solution)/shard_map/ppermute | solution.py:335
  43.7 6.4 %collective-permute-start.17 = (bf16[1040,128]{1,0:T(8,128)(2,1)S(1)}, bf16[1040,128]{1,0:T(8,128)(2,1)S(1)}, u32[]{:S(2)}, u32[]{:S(2)}) collective-permute-start(bf16[1040,128]{1,0:T(8,128)(2,1)S(1)} %collective-permute-done.13.refs_4_.refs_5_), channel_id=1, source_target_pairs={{0,16},{4,12},{8,24},{12,4},{16,0},{20,28},{24,8},{28,20},{1,17},{... | collective-permute-start | bytes 798728 | tf_op jit(solution)/shard_map/ppermute | solution.py:335
  46.1 4.0 %collective-permute-start.16 = (bf16[1040,128]{1,0:T(8,128)(2,1)S(1)}, bf16[1040,128]{1,0:T(8,128)(2,1)S(1)}, u32[]{:S(2)}, u32[]{:S(2)}) collective-permute-start(bf16[1040,128]{1,0:T(8,128)(2,1)S(1)} %late.1), channel_id=1, source_target_pairs={{0,4},{4,0},{8,12},{12,8},{16,20},{20,16},{24,28},{28,24},{1,5},{5... | collective-permute-start | bytes 798728 | tf_op jit(solution)/shard_map/ppermute | solution.py:335
  48.1 3.6 %collective-permute-start.15 = (bf16[256,640]{1,0:T(8,128)(2,1)S(1)}, bf16[256,640]{1,0:T(8,128)(2,1)S(1)}, u32[]{:S(2)}, u32[]{:S(2)}) collective-permute-start(bf16[256,640]{1,0:T(8,128)(2,1)S(1)} %grad_other_near.1), channel_id=1, source_target_pairs={{0,4},{4,0},{8,12},{12,8},{16,20},{20,16},{24,28},{28,24},{1,5},{5... | collective-permute-start | bytes 983048 | tf_op jit(solution)/shard_map/ppermute | solution.py:335
  50.6 2.2 %collective-permute-start.19 = (bf16[256,384]{1,0:T(8,128)(2,1)S(1)}, bf16[256,384]{1,0:T(8,128)(2,1)S(1)}, u32[]{:S(2)}, u32[]{:S(2)}) collective-permute-start(bf16[256,384]{1,0:T(8,128)(2,1)S(1)} %grad_other_far.1), channel_id=1, source_target_pairs={{0,4},{4,0},{8,12},{12,8},{16,20},{20,16},{24,28},{28,24},{1,5},{5... | collective-permute-start | bytes 589832 | tf_op jit(solution)/shard_map/ppermute | solution.py:335

commit v15 on v14

--- a/solution.py
+++ b/solution.py
@@ -78,7 +78,7 @@
     return m if m in (0, 3) else jnp.where(side == 0, m, 3 - m)
 
 
-def cot_kernel(n, tile, lo, off_hbm, cot_hbm, *refs):
+def cot_kernel(n, tile, cuts, off_hbm, cot_hbm, *refs):
     outs, (off, cot, sems) = refs[-3 - n // 2 : -3], refs[-3:]
     own = lax.axis_index("tm")
     chip, side = own // 2, lax.rem(own, 2)
@@ -86,8 +86,6 @@
     clip_rows = n * tile
     all_rows, all_cols = cot.shape
     cols = all_cols // n
-    part = all_rows - lo
-    low = pl.multiple_of(plane * lo, 16)
     fetch_off = pltpu.make_async_copy(off_hbm, off, sems.at[0])
     fetch_cot = pltpu.make_async_copy(cot_hbm, cot, sems.at[1])
     fetch_off.start()
@@ -106,7 +104,7 @@
     ).astype(jnp.bfloat16)
     units = cols // HD
     for m, out_ref in enumerate(outs):
-        rows, first = (part, low) if m else (all_rows, 0)
+        rows, first = all_rows - cuts[m], pl.multiple_of(plane * cuts[m], 16)
         there = chip ^ chip_bits(m, side)
         for i, block in enumerate((2 * there + side, 2 * there + 1 - side)):
             for u in range(units):
@@ -206,34 +204,39 @@
         out_ref[rows:, :] = hist
 
 
-def stack_kernel(order, lo, tiles, *refs):
+def stack_kernel(order, cuts, tiles, *refs):
     out_ref = refs[-1]
     plane = lax.rem(lax.axis_index("head"), 2)
+    at = 0
     for m, ref in zip(order, refs):
         part = ref.shape[0] // tiles
         for u in range(tiles):
-            first = pl.multiple_of(u * part + plane * (part - lo), 16)
-            out_ref[m - 1, u * lo : (u + 1) * lo, :] = ref[pl.ds(first, lo), :]
+            first = pl.multiple_of(u * part + plane * (part - cuts[m]), 16)
+            out_ref[at : at + cuts[m], :] = ref[pl.ds(first, cuts[m]), :]
+            at += cuts[m]
 
 
 def late_kernel(x_ref, *refs):
     refs[-1][...] = x_ref[...]
 
 
-def turn_kernel(lo, clip_rows, order, own_in, *refs):
+def turn_kernel(cuts, clip_rows, order, own_in, *refs):
     pieces, (swapped_ref, own_ref, other_ref, whole) = refs[:-4], refs[-4:]
     plane = lax.rem(lax.axis_index("head"), 2)
     own = lax.axis_index("tm")
     chip, side = own // 2, lax.rem(own, 2)
     chips, all_rows, width = whole.shape
-    part = all_rows - lo
-    for u in range(width // HD):
+    tiles = width // HD
+    for u in range(tiles):
         lanes = slice(u * HD, (u + 1) * HD)
         whole[0, :, lanes] = own_in[u * all_rows : (u + 1) * all_rows, :]
+        start = 0
         for m, ref in zip(order, pieces):
-            at = chip_bits(m, side)
+            at, lo = chip_bits(m, side), cuts[m]
+            part = all_rows - lo
             a = ref[u * part : (u + 1) * part, :]
-            b = swapped_ref[m - 1, u * lo : (u + 1) * lo, :]
+            b = swapped_ref[start + u * lo : start + (u + 1) * lo, :]
+            start += tiles * lo
             whole[at, 0:lo, lanes] = jnp.where(plane == 0, a[:lo], b)
             whole[at, lo:part, lanes] = jnp.where(plane == 0, a[lo:], a[: part - lo])
             whole[at, part:all_rows, lanes] = jnp.where(plane == 0, b, a[part - lo :])
@@ -321,8 +324,7 @@
     cot_rows, all_cols = cotangent.shape
     cols = all_cols // n
     units = cols // HD
-    lo = cot_rows * 7 // 17 // 16 * 16
-    part = cot_rows - lo
+    cuts = [0, cot_rows * 7 // 17 // 16 * 16] + [cot_rows // 32 * 16] * 2
     base = 3 * tok + clip_rows
     length = base
     rows = half * tok
@@ -382,9 +384,9 @@
     by_head = [packed[0]] + [arrived[k] for k in order]
     chips = range(half)
     cots = call(
-        lambda *refs: cot_kernel(n, tile, lo, *refs),
+        lambda *refs: cot_kernel(n, tile, cuts, *refs),
         "cot",
-        [((2 * units * cot_rows, HD), bf16)] + [((2 * units * part, HD), bf16)] * (half - 1),
+        [((2 * units * (cot_rows - cut), HD), bf16) for cut in cuts],
         [hbm] * 4,
         0,
         (
@@ -413,9 +415,9 @@
     )(frame_counts, *by_head)
     stack_order = [3, 1, 2]
     (cot_rest,) = call(
-        lambda *refs: stack_kernel(stack_order, lo, 2 * units, *refs),
+        lambda *refs: stack_kernel(stack_order, cuts, 2 * units, *refs),
         "stack",
-        [((half - 1, 2 * units * lo, HD), bf16)],
+        [((2 * units * sum(cuts), HD), bf16)],
         [vmem] * (half - 1) + [hbm],
         0,
     )(*[cots[m] for m in stack_order], same)
@@ -429,7 +431,7 @@
     c_cross = swap(late_cross, 1)
 
     turned_own, turned_other = call(
-        lambda *refs: turn_kernel(lo, clip_rows, stack_order, *refs),
+        lambda *refs: turn_kernel(cuts, clip_rows, stack_order, *refs),
         "turn",
         [((cols, half * cot_rows), bf16)] * 2,
         [vmem] * (half + 1),

time: 53.9 us -> 53.5 us (level)
  no operation moved by 1% of the time
where the time goes in v15:
time: 53.5 us; the launch traced here: 53.3 us
  waiting for transfers between devices  19.6 us (37%)
  starting transfers between devices  19.3 us (36%)
  Pallas kernels  13.6 us (25%)
  between operations  0.78 us (1%)
    ppermute x19, waiting for transfers between devices, swap(): return lax.ppermute(x, 'tm', [(i, i ^ bits[i % 2]) for i in range(n)])  19.6 us
    ppermute x19, starting transfers between devices, swap(): return lax.ppermute(x, 'tm', [(i, i ^ bits[i % 2]) for i in range(n)])  17.7 us
    pallas_call x2, Pallas kernels, pack(): call(lambda *refs: pack_kernel(n, heads, *refs), name, [((length, HD), bf...  4.42 us
    pallas_call x1, Pallas kernels, head_body(): call(lambda *refs: attend_kernel(n, tok, [0] + order, *refs), 'attend', [...  3.48 us
    pallas_call x4, Pallas kernels, grad(): call(lambda *refs: grad_kernel(rows, half, len(heads), *refs), name, [((c...  2.24 us
    ppermute x1, starting transfers between devices, swap_plane(): return lax.ppermute(x, ('tm', 'head'), pairs)  1.64 us
  transfers between devices with their start and end apart: 20, of which 9 were waited for; matrix products, arithmetic and copies ran while one was open for 0% of the time, Pallas kernels for 20%

profile of v15, /device:TPU:0, one launch (start us, length us, event | category | flops | bytes accessed | tf_op | source)
XLA Modules:
  0.0 53.3 jit_solution(16123660402853887225)
XLA Ops:
  0.6 1.9 %pack_first.1 = (bf16[784,128]{1,0:T(8,128)(2,1)}, bf16[784,128]{1,0:T(8,128)(2,1)}) custom-call(bf16[256,1024]{1,0:T(8,128)(2,1)} %refs_0_.6, bf16[256,1024]{1,0:T(8,128)(2,1)} %refs_1_.5, bf16[256,1024]{1,0:T(8,128)(2,1)} %refs_2_.3, bf16[2,1024]{1,0:T(2,128)(2,1)} %refs_3_.3), custom_call_target="tpu_custom_call" | custom-call | bytes 802816 | tf_op jit(solution)/shard_map/pack_first/pallas_call | solution.py:363
  2.5 4.0 %collective-permute-start = (bf16[784,128]{1,0:T(8,128)(2,1)}, bf16[784,128]{1,0:T(8,128)(2,1)S(1)}, u32[]{:S(2)}, u32[]{:S(2)}) collective-permute-start(bf16[784,128]{1,0:T(8,128)(2,1)} %get-tuple-element.20), channel_id=1, source_target_pairs={{0,24},{4,28},{8,16},{12,20},{16,8},{20,12},{24,0},{28,4},{1,25},{... | collective-permute-start | bytes 602120 | tf_op jit(solution)/shard_map/ppermute | solution.py:337
  6.5 2.6 %pack_rest.1 = (bf16[784,128]{1,0:T(8,128)(2,1)}, bf16[784,128]{1,0:T(8,128)(2,1)}, bf16[784,128]{1,0:T(8,128)(2,1)}, bf16[784,128]{1,0:T(8,128)(2,1)}, bf16[784...) custom-call(bf16[256,1024]{1,0:T(8,128)(2,1)} %refs_0_.6, bf16[256,1024]{1,0:T(8,128)(2,1)} %refs_1_.5, ...), custom_call_target="tpu_custom_call" | custom-call | bytes 2408448 | tf_op jit(solution)/shard_map/pack_rest/pallas_call | solution.py:363
  9.1 1.2 %collective-permute-start.5 = (bf16[784,128]{1,0:T(8,128)(2,1)}, bf16[784,128]{1,0:T(8,128)(2,1)S(1)}, u32[]{:S(2)}, u32[]{:S(2)}) collective-permute-start(bf16[784,128]{1,0:T(8,128)(2,1)} %get-tuple-element.27), channel_id=1, source_target_pairs={{0,8},{4,12},{8,0},{12,4},{16,24},{20,28},{24,16},{28,20},{1,9},{5... | collective-permute-start | bytes 602120 | tf_op jit(solution)/shard_map/ppermute | solution.py:337
  10.3 1.5 %collective-permute-start.6 = (bf16[784,128]{1,0:T(8,128)(2,1)}, bf16[784,128]{1,0:T(8,128)(2,1)S(1)}, u32[]{:S(2)}, u32[]{:S(2)}) collective-permute-start(bf16[784,128]{1,0:T(8,128)(2,1)} %get-tuple-element.28), channel_id=1, source_target_pairs={{0,16},{4,20},{8,24},{12,28},{16,0},{20,4},{24,8},{28,12},{1,17},{... | collective-permute-start | bytes 602120 | tf_op jit(solution)/shard_map/ppermute | solution.py:337
  11.8 0.6 %collective-permute-start.7 = (bf16[784,128]{1,0:T(8,128)(2,1)}, bf16[784,128]{1,0:T(8,128)(2,1)S(1)}, u32[]{:S(2)}, u32[]{:S(2)}) collective-permute-start(bf16[784,128]{1,0:T(8,128)(2,1)} %get-tuple-element.29), channel_id=1, source_target_pairs={{0,12},{4,8},{8,4},{12,0},{16,28},{20,24},{24,20},{28,16},{1,13},{... | collective-permute-start | bytes 602120 | tf_op jit(solution)/shard_map/ppermute | solution.py:337
  12.9 3.6 %collective-permute-done.1.refs_3_ = bf16[784,128]{1,0:T(8,128)(2,1)S(1)} collective-permute-done((bf16[784,128]{1,0:T(8,128)(2,1)}, bf16[784,128]{1,0:T(8,128)(2,1)S(1)}, u32[]{:S(2)}, u32[]{:S(2)}) %collective-permute-start.1) | collective-permute-done | bytes 200736 | tf_op jit(solution)/shard_map/ppermute | solution.py:337
  16.6 0.9 %cot.1 = (bf16[1088,128]{1,0:T(8,128)(2,1)S(1)}, bf16[640,128]{1,0:T(8,128)(2,1)S(1)}, bf16[576,128]{1,0:T(8,128)(2,1)S(1)}, bf16[576,128]{1,0:T(8,128)(2,1)S(1)}) custom-call(s32[1,8]{1,0:T(1,128)S(1)} %copy-done.1, bf16[272,2048]{1,0:T(8,128)(2,1)S(1)} %copy-done, bf16[784,128]{1,0:T(8,128)(2,1)S(1)} %collective-permute-done.refs_2_, ...), custom_call_target="tpu_custom_call" | custom-call | bytes 1474560 | tf_op jit(solution)/shard_map/cot/pallas_call | solution.py:386
  17.6 4.1 %collective-permute-done.5.refs_4_ = bf16[784,128]{1,0:T(8,128)(2,1)S(1)} collective-permute-done((bf16[784,128]{1,0:T(8,128)(2,1)}, bf16[784,128]{1,0:T(8,128)(2,1)S(1)}, u32[]{:S(2)}, u32[]{:S(2)}) %collective-permute-start.5) | collective-permute-done | bytes 200736 | tf_op jit(solution)/shard_map/ppermute | solution.py:337
  21.7 1.5 %collective-permute-start.3 = (bf16[640,128]{1,0:T(8,128)(2,1)S(1)}, bf16[640,128]{1,0:T(8,128)(2,1)S(1)}, u32[]{:S(2)}, u32[]{:S(2)}) collective-permute-start(bf16[640,128]{1,0:T(8,128)(2,1)S(1)} %get-tuple-element.24), channel_id=1, source_target_pairs={{0,8},{4,20},{8,0},{12,28},{16,24},{20,4},{24,16},{28,12},{1,9},{5... | collective-permute-start | bytes 491528 | tf_op jit(solution)/shard_map/ppermute | solution.py:337
  23.2 1.5 %collective-permute-done.7.refs_6_ = bf16[784,128]{1,0:T(8,128)(2,1)S(1)} collective-permute-done((bf16[784,128]{1,0:T(8,128)(2,1)}, bf16[784,128]{1,0:T(8,128)(2,1)S(1)}, u32[]{:S(2)}, u32[]{:S(2)}) %collective-permute-start.7) | collective-permute-done | bytes 200736 | tf_op jit(solution)/shard_map/ppermute | solution.py:337
  24.7 0.6 %collective-permute-start.4 = (bf16[576,128]{1,0:T(8,128)(2,1)S(1)}, bf16[576,128]{1,0:T(8,128)(2,1)S(1)}, u32[]{:S(2)}, u32[]{:S(2)}) collective-permute-start(bf16[576,128]{1,0:T(8,128)(2,1)S(1)} %get-tuple-element.25), channel_id=1, source_target_pairs={{0,16},{4,12},{8,24},{12,4},{16,0},{20,28},{24,8},{28,20},{1,17},{... | collective-permute-start | bytes 442376 | tf_op jit(solution)/shard_map/ppermute | solution.py:337
  25.3 3.5 %attend.1 = (bf16[1040,128]{1,0:T(8,128)(2,1)S(1)}, bf16[1040,128]{1,0:T(8,128)(2,1)S(1)}) custom-call(s32[8]{0:T(128)S(1)} %copy-done.3, bf16[784,128]{1,0:T(8,128)(2,1)S(1)} %copy-done.2, bf16[784,128]{1,0:T(8,128)(2,1)S(1)} %collective-permute-done.refs_2_, bf16[784,128]{1,0:T(8,128)(2,1)S(1)} %collective-permute-done.1.refs_3_, ...), custom_call_target="tpu_custom_call" | custom-call | flops 1073741824 | bytes 1064960 | tf_op jit(solution)/shard_map/attend/pallas_call | solution.py:407
  28.7 1.7 %collective-permute-start.14 = (bf16[1040,128]{1,0:T(8,128)(2,1)S(1)}, bf16[1040,128]{1,0:T(8,128)(2,1)S(1)}, u32[]{:S(2)}, u32[]{:S(2)}) collective-permute-start(bf16[1040,128]{1,0:T(8,128)(2,1)S(1)} %get-tuple-element.34.x_ref), channel_id=1, source_target_pairs={{0,12},{4,16},{8,4},{12,24},{16,28},{20,0},{24,20},{28,8},{1,13},{... | collective-permute-start | bytes 798728 | tf_op jit(solution)/shard_map/ppermute | solution.py:337
  30.4 1.4 %collective-permute-start.13 = (bf16[1040,128]{1,0:T(8,128)(2,1)S(1)}, bf16[1040,128]{1,0:T(8,128)(2,1)S(1)}, u32[]{:S(2)}, u32[]{:S(2)}) collective-permute-start(bf16[1040,128]{1,0:T(8,128)(2,1)S(1)} %get-tuple-element.32.refs_3_.refs_1_.refs_2_), channel_id=1, source_target_pairs={{0,8},{4,20},{8,0},{12,28},{16,24},{20,4},{24,16},{28,12},{1,9},{5... | collective-permute-start | bytes 798728 | tf_op jit(solution)/shard_map/ppermute | solution.py:337
  31.9 0.9 %collective-permute-start.12 = (bf16[1040,128]{1,0:T(8,128)(2,1)S(1)}, bf16[1040,128]{1,0:T(8,128)(2,1)S(1)}, u32[]{:S(2)}, u32[]{:S(2)}) collective-permute-start(bf16[1040,128]{1,0:T(8,128)(2,1)S(1)} %get-tuple-element.32.refs_3_.refs_1_.refs_2_), channel_id=1, source_target_pairs={{0,16},{4,12},{8,24},{12,4},{16,0},{20,28},{24,8},{28,20},{1,17},{... | collective-permute-start | bytes 798728 | tf_op jit(solution)/shard_map/ppermute | solution.py:337
  32.8 1.6 %collective-permute-start.10 = (bf16[1472,128]{1,0:T(8,128)(2,1)S(1)}, bf16[1472,128]{1,0:T(8,128)(2,1)S(1)}, u32[]{:S(2)}, u32[]{:S(2)}) collective-permute-start(bf16[1472,128]{1,0:T(8,128)(2,1)S(1)} %stack.1), channel_id=1, source_target_pairs={{0,1},{1,0},{2,3},{3,2},{4,5},{5,4},{6,7},{7,6},{8,9},{9,8},{10,11... | collective-permute-start | bytes 1130504 | tf_op jit(solution)/shard_map/ppermute | solution.py:343
  34.5 1.0 %collective-permute-done.14.refs_5_.refs_6_ = bf16[1040,128]{1,0:T(8,128)(2,1)S(1)} collective-permute-done((bf16[1040,128]{1,0:T(8,128)(2,1)S(1)}, bf16[1040,128]{1,0:T(8,128)(2,1)S(1)}, u32[]{:S(2)}, u32[]{:S(2)}) %collective-permute-start.14) | collective-permute-done | bytes 266272 | tf_op jit(solution)/shard_map/ppermute | solution.py:337
  35.5 1.6 %collective-permute-start.18 = (bf16[1040,128]{1,0:T(8,128)(2,1)S(1)}, bf16[1040,128]{1,0:T(8,128)(2,1)S(1)}, u32[]{:S(2)}, u32[]{:S(2)}) collective-permute-start(bf16[1040,128]{1,0:T(8,128)(2,1)S(1)} %collective-permute-done.14.refs_5_.refs_6_), channel_id=1, source_target_pairs={{0,8},{4,20},{8,0},{12,28},{16,24},{20,4},{24,16},{28,12},{1,9},{5... | collective-permute-start | bytes 798728 | tf_op jit(solution)/shard_map/ppermute | solution.py:337
  37.1 6.2 %collective-permute-done.13.refs_4_.refs_5_ = bf16[1040,128]{1,0:T(8,128)(2,1)S(1)} collective-permute-done((bf16[1040,128]{1,0:T(8,128)(2,1)S(1)}, bf16[1040,128]{1,0:T(8,128)(2,1)S(1)}, u32[]{:S(2)}, u32[]{:S(2)}) %collective-permute-start.13) | collective-permute-done | bytes 266272 | tf_op jit(solution)/shard_map/ppermute | solution.py:337
  43.3 0.7 %collective-permute-start.17 = (bf16[1040,128]{1,0:T(8,128)(2,1)S(1)}, bf16[1040,128]{1,0:T(8,128)(2,1)S(1)}, u32[]{:S(2)}, u32[]{:S(2)}) collective-permute-start(bf16[1040,128]{1,0:T(8,128)(2,1)S(1)} %collective-permute-done.13.refs_4_.refs_5_), channel_id=1, source_target_pairs={{0,16},{4,12},{8,24},{12,4},{16,0},{20,28},{24,8},{28,20},{1,17},{... | collective-permute-start | bytes 798728 | tf_op jit(solution)/shard_map/ppermute | solution.py:337
  44.0 1.8 %collective-permute-done.12.refs_3_.refs_1_.refs_4_ = bf16[1040,128]{1,0:T(8,128)(2,1)S(1)} collective-permute-done((bf16[1040,128]{1,0:T(8,128)(2,1)S(1)}, bf16[1040,128]{1,0:T(8,128)(2,1)S(1)}, u32[]{:S(2)}, u32[]{:S(2)}) %collective-permute-start.12) | collective-permute-done | bytes 266272 | tf_op jit(solution)/shard_map/ppermute | solution.py:337
  45.8 0.7 %collective-permute-start.16 = (bf16[1040,128]{1,0:T(8,128)(2,1)S(1)}, bf16[1040,128]{1,0:T(8,128)(2,1)S(1)}, u32[]{:S(2)}, u32[]{:S(2)}) collective-permute-start(bf16[1040,128]{1,0:T(8,128)(2,1)S(1)} %late.1), channel_id=1, source_target_pairs={{0,4},{4,0},{8,12},{12,8},{16,20},{20,16},{24,28},{28,24},{1,5},{5... | collective-permute-start | bytes 798728 | tf_op jit(solution)/shard_map/ppermute | solution.py:337
  46.5 0.6 %turn.1 = (bf16[256,1088]{1,0:T(8,128)(2,1)S(1)}, bf16[256,1088]{1,0:T(8,128)(2,1)S(1)}) custom-call(bf16[1088,128]{1,0:T(8,128)(2,1)S(1)} %get-tuple-element.22.refs_0_, bf16[576,128]{1,0:T(8,128)(2,1)S(1)} %collective-permute-done.2.refs_0_.refs_1_, bf16[640,128]{1,0:T(8,128)(2,1)S(1)} %collective-permute-done.3.refs_1_.refs_2_, ...), custom_call_target="tpu_custom_call" | custom-call | bytes 2228224 | tf_op jit(solution)/shard_map/turn/pallas_call | solution.py:433
  47.1 0.6 %grad_other_near.1 = bf16[256,640]{1,0:T(8,128)(2,1)S(1)} custom-call(bf16[256,1088]{1,0:T(8,128)(2,1)S(1)} %get-tuple-element.35.refs_0_, bf16[1040,128]{1,0:T(8,128)(2,1)S(1)} %get-tuple-element.32.refs_3_.refs_1_.refs_2_, bf16[1040,128]{1,0:T(8,128)(2,1)S(1)} %collective-permute-done.11.refs_2_.refs_0_.refs_3_, ...), custom_call_target="tpu_custom_call" | custom-call | flops 356515840 | bytes 655360 | tf_op jit(solution)/shard_map/grad_other_near/pallas_call | solution.py:443
  47.8 0.6 %grad_own_near.1.refs_4_.refs_0_ = f32[256,640]{1,0:T(8,128)S(1)} custom-call(bf16[256,1088]{1,0:T(8,128)(2,1)S(1)} %get-tuple-element.33.refs_0_, bf16[1040,128]{1,0:T(8,128)(2,1)S(1)} %get-tuple-element.32.refs_3_.refs_1_.refs_2_, bf16[1040,128]{1,0:T(8,128)(2,1)S(1)} %collective-permute-done.11.refs_2_.refs_0_.refs_3_, ...), custom_call_target="tpu_custom_call" | custom-call | flops 356515840 | bytes 1310720 | tf_op jit(solution)/shard_map/grad_own_near/pallas_call | solution.py:443
  48.5 0.5 collective-permute-done.18.refs_3_.refs_6_
  49.0 0.7 %collective-permute-done.17.refs_2_.refs_5_ = bf16[1040,128]{1,0:T(8,128)(2,1)S(1)} collective-permute-done((bf16[1040,128]{1,0:T(8,128)(2,1)S(1)}, bf16[1040,128]{1,0:T(8,128)(2,1)S(1)}, u32[]{:S(2)}, u32[]{:S(2)}) %collective-permute-start.17) | collective-permute-done | bytes 266272 | tf_op jit(solution)/shard_map/ppermute | solution.py:337
  49.7 0.5 grad_other_far.1
  50.2 0.7 %collective-permute-start.19 = (bf16[256,384]{1,0:T(8,128)(2,1)S(1)}, bf16[256,384]{1,0:T(8,128)(2,1)S(1)}, u32[]{:S(2)}, u32[]{:S(2)}) collective-permute-start(bf16[256,384]{1,0:T(8,128)(2,1)S(1)} %grad_other_far.1), channel_id=1, source_target_pairs={{0,4},{4,0},{8,12},{12,8},{16,20},{20,16},{24,28},{28,24},{1,5},{5... | collective-permute-start | bytes 589832 | tf_op jit(solution)/shard_map/ppermute | solution.py:337
  51.4 1.0 %near.1 = (bf16[256,1024]{1,0:T(8,128)(2,1)}, f32[256,1024]{1,0:T(8,128)}) custom-call(f32[256,640]{1,0:T(8,128)S(1)} %grad_own_near.1.refs_4_.refs_0_, bf16[256,640]{1,0:T(8,128)(2,1)S(1)} %collective-permute-done.15.refs_1_, bf16[1040,128]{1,0:T(8,128)(2,1)S(1)} %get-tuple-element.32.refs_3_.refs_1_.refs_2_, ...), custom_call_target="tpu_custom_call" | custom-call | bytes 3145728 | tf_op jit(solution)/shard_map/near/pallas_call | solution.py:459
  52.4 0.9 %last.1 = (bf16[256,1024]{1,0:T(8,128)(2,1)}, f32[256,1024]{1,0:T(8,128)}) custom-call(f32[256,640]{1,0:T(8,128)S(1)} %grad_own_near.1.refs_4_.refs_0_, bf16[256,640]{1,0:T(8,128)(2,1)S(1)} %collective-permute-done.15.refs_1_, f32[256,384]{1,0:T(8,128)S(1)} %grad_own_far.1.refs_2_, ...), custom_call_target="tpu_custom_call", output_to_operand_aliasing={{0}: (7, {}), {1}: (8, {})} | custom-call | bytes 3145728 | tf_op jit(solution)/shard_map/last/pallas_call | solution.py:468
  (29 shorter events, 1.4 us)
Async XLA Ops:
  2.5 14.1 %copy-start = (bf16[272,2048]{1,0:T(8,128)(2,1)S(1)}, bf16[272,2048]{1,0:T(8,128)(2,1)}, u32[]{:S(2)}) copy-start(bf16[272,2048]{1,0:T(8,128)(2,1)} %refs_1_.4) | copy-start | bytes 3342340
  2.5 14.1 %copy-start.1 = (s32[1,8]{1,0:T(1,128)S(1)}, s32[1,8]{1,0:T(1,128)}, u32[]{:S(2)}) copy-start(s32[1,8]{1,0:T(1,128)} %refs_0_.5) | copy-start | bytes 100
  2.5 10.0 %collective-permute-start = (bf16[784,128]{1,0:T(8,128)(2,1)}, bf16[784,128]{1,0:T(8,128)(2,1)S(1)}, u32[]{:S(2)}, u32[]{:S(2)}) collective-permute-start(bf16[784,128]{1,0:T(8,128)(2,1)} %get-tuple-element.20), channel_id=1, source_target_pairs={{0,24},{4,28},{8,16},{12,20},{16,8},{20,12},{24,0},{28,4},{1,25},{... | collective-permute-start | bytes 602120 | tf_op jit(solution)/shard_map/ppermute | solution.py:337
  6.5 10.1 %collective-permute-start.1 = (bf16[784,128]{1,0:T(8,128)(2,1)}, bf16[784,128]{1,0:T(8,128)(2,1)S(1)}, u32[]{:S(2)}, u32[]{:S(2)}) collective-permute-start(bf16[784,128]{1,0:T(8,128)(2,1)} %get-tuple-element.21), channel_id=1, source_target_pairs={{0,28},{4,24},{8,20},{12,16},{16,12},{20,8},{24,4},{28,0},{1,29},{... | collective-permute-start | bytes 602120 | tf_op jit(solution)/shard_map/ppermute | solution.py:337
  9.1 16.2 %copy-start.2 = (bf16[784,128]{1,0:T(8,128)(2,1)S(1)}, bf16[784,128]{1,0:T(8,128)(2,1)}, u32[]{:S(2)}) copy-start(bf16[784,128]{1,0:T(8,128)(2,1)} %get-tuple-element.26.refs_1_) | copy-start | bytes 602116
  9.1 16.2 %copy-start.3 = (s32[8]{0:T(128)S(1)}, s32[8]{0:T(128)}, u32[]{:S(2)}) copy-start(s32[8]{0:T(128)} %refs_0_.7) | copy-start | bytes 100
  9.1 12.6 %collective-permute-start.5 = (bf16[784,128]{1,0:T(8,128)(2,1)}, bf16[784,128]{1,0:T(8,128)(2,1)S(1)}, u32[]{:S(2)}, u32[]{:S(2)}) collective-permute-start(bf16[784,128]{1,0:T(8,128)(2,1)} %get-tuple-element.27), channel_id=1, source_target_pairs={{0,8},{4,12},{8,0},{12,4},{16,24},{20,28},{24,16},{28,20},{1,9},{5... | collective-permute-start | bytes 602120 | tf_op jit(solution)/shard_map/ppermute | solution.py:337
  10.3 12.9 %collective-permute-start.6 = (bf16[784,128]{1,0:T(8,128)(2,1)}, bf16[784,128]{1,0:T(8,128)(2,1)S(1)}, u32[]{:S(2)}, u32[]{:S(2)}) collective-permute-start(bf16[784,128]{1,0:T(8,128)(2,1)} %get-tuple-element.28), channel_id=1, source_target_pairs={{0,16},{4,20},{8,24},{12,28},{16,0},{20,4},{24,8},{28,12},{1,17},{... | collective-permute-start | bytes 602120 | tf_op jit(solution)/shard_map/ppermute | solution.py:337
  11.8 12.9 %collective-permute-start.7 = (bf16[784,128]{1,0:T(8,128)(2,1)}, bf16[784,128]{1,0:T(8,128)(2,1)S(1)}, u32[]{:S(2)}, u32[]{:S(2)}) collective-permute-start(bf16[784,128]{1,0:T(8,128)(2,1)} %get-tuple-element.29), channel_id=1, source_target_pairs={{0,12},{4,8},{8,4},{12,0},{16,28},{20,24},{24,20},{28,16},{1,13},{... | collective-permute-start | bytes 602120 | tf_op jit(solution)/shard_map/ppermute | solution.py:337
  12.5 12.7 %collective-permute-start.8 = (bf16[784,128]{1,0:T(8,128)(2,1)}, bf16[784,128]{1,0:T(8,128)(2,1)S(1)}, u32[]{:S(2)}, u32[]{:S(2)}) collective-permute-start(bf16[784,128]{1,0:T(8,128)(2,1)} %get-tuple-element.30), channel_id=1, source_target_pairs={{0,20},{4,16},{8,28},{12,24},{16,4},{20,0},{24,12},{28,8},{1,21},{... | collective-permute-start | bytes 602120 | tf_op jit(solution)/shard_map/ppermute | solution.py:337
  16.5 8.7 %collective-permute-start.9 = (bf16[784,128]{1,0:T(8,128)(2,1)}, bf16[784,128]{1,0:T(8,128)(2,1)S(1)}, u32[]{:S(2)}, u32[]{:S(2)}) collective-permute-start(bf16[784,128]{1,0:T(8,128)(2,1)} %get-tuple-element.31), channel_id=1, source_target_pairs={{0,4},{4,0},{8,12},{12,8},{16,20},{20,16},{24,28},{28,24},{1,5},{5... | collective-permute-start | bytes 602120 | tf_op jit(solution)/shard_map/ppermute | solution.py:337
  21.7 11.1 %collective-permute-start.3 = (bf16[640,128]{1,0:T(8,128)(2,1)S(1)}, bf16[640,128]{1,0:T(8,128)(2,1)S(1)}, u32[]{:S(2)}, u32[]{:S(2)}) collective-permute-start(bf16[640,128]{1,0:T(8,128)(2,1)S(1)} %get-tuple-element.24), channel_id=1, source_target_pairs={{0,8},{4,20},{8,0},{12,28},{16,24},{20,4},{24,16},{28,12},{1,9},{5... | collective-permute-start | bytes 491528 | tf_op jit(solution)/shard_map/ppermute | solution.py:337
  23.2 8.6 %collective-permute-start.2 = (bf16[576,128]{1,0:T(8,128)(2,1)S(1)}, bf16[576,128]{1,0:T(8,128)(2,1)S(1)}, u32[]{:S(2)}, u32[]{:S(2)}) collective-permute-start(bf16[576,128]{1,0:T(8,128)(2,1)S(1)} %get-tuple-element.23), channel_id=1, source_target_pairs={{0,24},{4,28},{8,16},{12,20},{16,8},{20,12},{24,0},{28,4},{1,25},{... | collective-permute-start | bytes 442376 | tf_op jit(solution)/shard_map/ppermute | solution.py:337
  24.7 7.2 %collective-permute-start.4 = (bf16[576,128]{1,0:T(8,128)(2,1)S(1)}, bf16[576,128]{1,0:T(8,128)(2,1)S(1)}, u32[]{:S(2)}, u32[]{:S(2)}) collective-permute-start(bf16[576,128]{1,0:T(8,128)(2,1)S(1)} %get-tuple-element.25), channel_id=1, source_target_pairs={{0,16},{4,12},{8,24},{12,4},{16,0},{20,28},{24,8},{28,20},{1,17},{... | collective-permute-start | bytes 442376 | tf_op jit(solution)/shard_map/ppermute | solution.py:337
  28.7 6.7 %collective-permute-start.14 = (bf16[1040,128]{1,0:T(8,128)(2,1)S(1)}, bf16[1040,128]{1,0:T(8,128)(2,1)S(1)}, u32[]{:S(2)}, u32[]{:S(2)}) collective-permute-start(bf16[1040,128]{1,0:T(8,128)(2,1)S(1)} %get-tuple-element.34.x_ref), channel_id=1, source_target_pairs={{0,12},{4,16},{8,4},{12,24},{16,28},{20,0},{24,20},{28,8},{1,13},{... | collective-permute-start | bytes 798728 | tf_op jit(solution)/shard_map/ppermute | solution.py:337
  30.4 12.9 %collective-permute-start.13 = (bf16[1040,128]{1,0:T(8,128)(2,1)S(1)}, bf16[1040,128]{1,0:T(8,128)(2,1)S(1)}, u32[]{:S(2)}, u32[]{:S(2)}) collective-permute-start(bf16[1040,128]{1,0:T(8,128)(2,1)S(1)} %get-tuple-element.32.refs_3_.refs_1_.refs_2_), channel_id=1, source_target_pairs={{0,8},{4,20},{8,0},{12,28},{16,24},{20,4},{24,16},{28,12},{1,9},{5... | collective-permute-start | bytes 798728 | tf_op jit(solution)/shard_map/ppermute | solution.py:337
  31.8 12.1 %collective-permute-start.11 = (bf16[1040,128]{1,0:T(8,128)(2,1)S(1)}, bf16[1040,128]{1,0:T(8,128)(2,1)S(1)}, u32[]{:S(2)}, u32[]{:S(2)}) collective-permute-start(bf16[1040,128]{1,0:T(8,128)(2,1)S(1)} %get-tuple-element.34.x_ref), channel_id=1, source_target_pairs={{0,20},{4,8},{8,28},{12,0},{16,4},{20,24},{24,12},{28,16},{1,21},{... | collective-permute-start | bytes 798728 | tf_op jit(solution)/shard_map/ppermute | solution.py:337
  31.9 13.9 %collective-permute-start.12 = (bf16[1040,128]{1,0:T(8,128)(2,1)S(1)}, bf16[1040,128]{1,0:T(8,128)(2,1)S(1)}, u32[]{:S(2)}, u32[]{:S(2)}) collective-permute-start(bf16[1040,128]{1,0:T(8,128)(2,1)S(1)} %get-tuple-element.32.refs_3_.refs_1_.refs_2_), channel_id=1, source_target_pairs={{0,16},{4,12},{8,24},{12,4},{16,0},{20,28},{24,8},{28,20},{1,17},{... | collective-permute-start | bytes 798728 | tf_op jit(solution)/shard_map/ppermute | solution.py:337
  32.8 13.7 %collective-permute-start.10 = (bf16[1472,128]{1,0:T(8,128)(2,1)S(1)}, bf16[1472,128]{1,0:T(8,128)(2,1)S(1)}, u32[]{:S(2)}, u32[]{:S(2)}) collective-permute-start(bf16[1472,128]{1,0:T(8,128)(2,1)S(1)} %stack.1), channel_id=1, source_target_pairs={{0,1},{1,0},{2,3},{3,2},{4,5},{5,4},{6,7},{7,6},{8,9},{9,8},{10,11... | collective-permute-start | bytes 1130504 | tf_op jit(solution)/shard_map/ppermute | solution.py:343
  35.5 13.5 %collective-permute-start.18 = (bf16[1040,128]{1,0:T(8,128)(2,1)S(1)}, bf16[1040,128]{1,0:T(8,128)(2,1)S(1)}, u32[]{:S(2)}, u32[]{:S(2)}) collective-permute-start(bf16[1040,128]{1,0:T(8,128)(2,1)S(1)} %collective-permute-done.14.refs_5_.refs_6_), channel_id=1, source_target_pairs={{0,8},{4,20},{8,0},{12,28},{16,24},{20,4},{24,16},{28,12},{1,9},{5... | collective-permute-start | bytes 798728 | tf_op jit(solution)/shard_map/ppermute | solution.py:337
  43.3 6.4 %collective-permute-start.17 = (bf16[1040,128]{1,0:T(8,128)(2,1)S(1)}, bf16[1040,128]{1,0:T(8,128)(2,1)S(1)}, u32[]{:S(2)}, u32[]{:S(2)}) collective-permute-start(bf16[1040,128]{1,0:T(8,128)(2,1)S(1)} %collective-permute-done.13.refs_4_.refs_5_), channel_id=1, source_target_pairs={{0,16},{4,12},{8,24},{12,4},{16,0},{20,28},{24,8},{28,20},{1,17},{... | collective-permute-start | bytes 798728 | tf_op jit(solution)/shard_map/ppermute | solution.py:337
  45.8 3.9 %collective-permute-start.16 = (bf16[1040,128]{1,0:T(8,128)(2,1)S(1)}, bf16[1040,128]{1,0:T(8,128)(2,1)S(1)}, u32[]{:S(2)}, u32[]{:S(2)}) collective-permute-start(bf16[1040,128]{1,0:T(8,128)(2,1)S(1)} %late.1), channel_id=1, source_target_pairs={{0,4},{4,0},{8,12},{12,8},{16,20},{20,16},{24,28},{28,24},{1,5},{5... | collective-permute-start | bytes 798728 | tf_op jit(solution)/shard_map/ppermute | solution.py:337
  47.7 3.6 %collective-permute-start.15 = (bf16[256,640]{1,0:T(8,128)(2,1)S(1)}, bf16[256,640]{1,0:T(8,128)(2,1)S(1)}, u32[]{:S(2)}, u32[]{:S(2)}) collective-permute-start(bf16[256,640]{1,0:T(8,128)(2,1)S(1)} %grad_other_near.1), channel_id=1, source_target_pairs={{0,4},{4,0},{8,12},{12,8},{16,20},{20,16},{24,28},{28,24},{1,5},{5... | collective-permute-start | bytes 983048 | tf_op jit(solution)/shard_map/ppermute | solution.py:337
  50.2 2.2 %collective-permute-start.19 = (bf16[256,384]{1,0:T(8,128)(2,1)S(1)}, bf16[256,384]{1,0:T(8,128)(2,1)S(1)}, u32[]{:S(2)}, u32[]{:S(2)}) collective-permute-start(bf16[256,384]{1,0:T(8,128)(2,1)S(1)} %grad_other_far.1), channel_id=1, source_target_pairs={{0,4},{4,0},{8,12},{12,8},{16,20},{20,16},{24,28},{28,24},{1,5},{5... | collective-permute-start | bytes 589832 | tf_op jit(solution)/shard_map/ppermute | solution.py:337

commit v16 on v15

--- a/solution.py
+++ b/solution.py
@@ -292,11 +292,28 @@
         x.wait()
 
 
+def own_near_kernel(rows, copies, tok, turned_ref, *refs):
+    n = len(NEAR)
+    heads, (out_ref, att_hbm, sems) = refs[:n], refs[n:]
+    own = lax.axis_index("tm")
+    side = lax.rem(own, 2)
+    at = pl.multiple_of(own // 2 * tok, tok)
+    moves = []
+    for i, (bits, ref) in enumerate(zip(NEAR, heads)):
+        lanes = pl.ds(pl.multiple_of((own ^ jnp.where(side == 0, *bits)) * HD, HD), HD)
+        moves.append(
+            pltpu.make_async_copy(ref.at[pl.ds(at, tok), :], att_hbm.at[:, lanes], sems.at[i])
+        )
+        moves[-1].start()
+    out_ref[...] = grad_part(turned_ref, heads, rows, copies)
+    for x in moves:
+        x.wait()
+
+
 def near_kernel(tok, own_near, got_near, *refs):
     n = len(NEAR)
-    heads, outs = refs[:n], refs[n:]
     sums = [(NEAR[i], (own_near, i), (got_near, THERE[i])) for i in range(n) if THERE[i] < n]
-    store_columns(tok, zip(NEAR, heads), sums, *outs)
+    store_columns(tok, [], sums, None, *refs)
 
 
 def last_kernel(tok, own_near, got_near, own_far, got_far, *refs):
@@ -351,7 +368,7 @@
             kernel,
             out_shape=tuple(shapes),
             in_specs=specs,
-            out_specs=tuple([out_spec] * len(shapes)),
+            out_specs=out_spec if isinstance(out_spec, tuple) else (out_spec,) * len(shapes),
             scratch_shapes=scratch,
             input_output_aliases=aliases,
             compiler_params=pltpu.CompilerParams(vmem_limit_bytes=limit),
@@ -453,18 +470,26 @@
     far = [c_cross, far_same, far_cross]
     whole = [((tok, width), bf16), ((cols, width), jnp.float32)]
     got_near = swap(grad(turned_other, near, bf16, "grad_other_near"), 1)
-    own_near = grad(turned_own, near, jnp.float32, "grad_own_near")
+    own_near, attended = call(
+        lambda *refs: own_near_kernel(rows, half, tok, *refs),
+        "grad_own_near",
+        [((cols, len(near) * HD), jnp.float32), whole[0]],
+        [vmem] * (1 + len(near)),
+        2 * cols * half * cot_rows * len(near) * HD,
+        (pltpu.SemaphoreType.DMA((len(near),)),),
+        out_spec=(vmem, hbm),
+    )(turned_own, *near)
     got_far = swap(grad(turned_other, far, bf16, "grad_other_far", (own_near,)), 1)
     own_far = grad(turned_own, far, jnp.float32, "grad_own_far")
-    halfway = call(
+    (grads,) = call(
         lambda *refs: near_kernel(tok, *refs),
         "near",
-        whole,
-        [vmem] * (2 + len(near)),
+        whole[1:],
+        [vmem] * 2,
         0,
-        (pltpu.VMEM((4, cols, HD), jnp.float32), pltpu.SemaphoreType.DMA((9,))),
+        (pltpu.VMEM((4, cols, HD), jnp.float32), pltpu.SemaphoreType.DMA((4,))),
         out_spec=hbm,
-    )(own_near, got_near, *near)
+    )(own_near, got_near)
     return call(
         lambda *refs: last_kernel(tok, *refs),
         "last",
@@ -474,7 +499,7 @@
         (pltpu.VMEM((4, cols, HD), jnp.float32), pltpu.SemaphoreType.DMA((7,))),
         out_spec=hbm,
         aliases={4 + len(far): 0, 5 + len(far): 1},
-    )(own_near, got_near, own_far, got_far, *far, *halfway)
+    )(own_near, got_near, own_far, got_far, *far, attended, grads)
 
 
 def body(query_rows, key_rows, value_rows, frame_counts, history, offsets, cotangent):

time: 53.5 us -> 53.3 us (level)
  waiting for transfers between devices: 19.6 us -> 19 us
    pallas_call x1 -> x2, Pallas kernels: 1.01 us -> 2.14 us  [the longest x1 1.29 us: head_body(): call(lambda *refs: own_near_kernel(rows, half, tok, *refs), 'grad_own_nea...]
    ppermute x19, waiting for transfers between devices: 19.6 us -> 19 us  [swap(): return lax.ppermute(x, 'tm', [(i, i ^ bits[i % 2]) for i in range(n)])]
    pallas_call x4 -> x3, Pallas kernels: 2.24 us -> 1.59 us  [grad(): call(lambda *refs: grad_kernel(rows, half, len(heads), *refs), name, [((c...]
  transfers between devices with their start and end apart: 20 -> 20, of which waited for: 9 -> 8; matrix products, arithmetic and copies ran while one was open for 0% -> 0% of each run, Pallas kernels for 20% -> 21%
where the time goes in v16:
time: 53.3 us; the launch traced here: 53.2 us
  starting transfers between devices  19.3 us (36%)
  waiting for transfers between devices  19 us (36%)
  Pallas kernels  14.1 us (26%)
  between operations  0.8 us (2%)
    ppermute x19, waiting for transfers between devices, swap(): return lax.ppermute(x, 'tm', [(i, i ^ bits[i % 2]) for i in range(n)])  19 us
    ppermute x19, starting transfers between devices, swap(): return lax.ppermute(x, 'tm', [(i, i ^ bits[i % 2]) for i in range(n)])  17.7 us
    pallas_call x2, Pallas kernels, pack(): call(lambda *refs: pack_kernel(n, heads, *refs), name, [((length, HD), bf...  4.42 us
    pallas_call x1, Pallas kernels, head_body(): call(lambda *refs: attend_kernel(n, tok, [0] + order, *refs), 'attend', [...  3.48 us
    ppermute x1, starting transfers between devices, swap_plane(): return lax.ppermute(x, ('tm', 'head'), pairs)  1.64 us
    pallas_call x3, Pallas kernels, grad(): call(lambda *refs: grad_kernel(rows, half, len(heads), *refs), name, [((c...  1.59 us
    pallas_call x1, Pallas kernels, head_body(): call(lambda *refs: own_near_kernel(rows, half, tok, *refs), 'grad_own_nea...  1.29 us
  transfers between devices with their start and end apart: 20, of which 8 were waited for; matrix products, arithmetic and copies ran while one was open for 0% of the time, Pallas kernels for 21%

profile of v16, /device:TPU:0, one launch (start us, length us, event | category | flops | bytes accessed | tf_op | source)
XLA Modules:
  0.0 53.2 jit_solution(17393965696606600774)
XLA Ops:
  0.6 1.9 %pack_first.1 = (bf16[784,128]{1,0:T(8,128)(2,1)}, bf16[784,128]{1,0:T(8,128)(2,1)}) custom-call(bf16[256,1024]{1,0:T(8,128)(2,1)} %refs_0_.6, bf16[256,1024]{1,0:T(8,128)(2,1)} %refs_1_.5, bf16[256,1024]{1,0:T(8,128)(2,1)} %refs_2_.3, bf16[2,1024]{1,0:T(2,128)(2,1)} %refs_3_.3), custom_call_target="tpu_custom_call" | custom-call | bytes 802816 | tf_op jit(solution)/shard_map/pack_first/pallas_call | solution.py:380
  2.5 4.0 %collective-permute-start = (bf16[784,128]{1,0:T(8,128)(2,1)}, bf16[784,128]{1,0:T(8,128)(2,1)S(1)}, u32[]{:S(2)}, u32[]{:S(2)}) collective-permute-start(bf16[784,128]{1,0:T(8,128)(2,1)} %get-tuple-element.20), channel_id=1, source_target_pairs={{0,24},{4,28},{8,16},{12,20},{16,8},{20,12},{24,0},{28,4},{1,25},{... | collective-permute-start | bytes 602120 | tf_op jit(solution)/shard_map/ppermute | solution.py:354
  6.5 2.6 %pack_rest.1 = (bf16[784,128]{1,0:T(8,128)(2,1)}, bf16[784,128]{1,0:T(8,128)(2,1)}, bf16[784,128]{1,0:T(8,128)(2,1)}, bf16[784,128]{1,0:T(8,128)(2,1)}, bf16[784...) custom-call(bf16[256,1024]{1,0:T(8,128)(2,1)} %refs_0_.6, bf16[256,1024]{1,0:T(8,128)(2,1)} %refs_1_.5, ...), custom_call_target="tpu_custom_call" | custom-call | bytes 2408448 | tf_op jit(solution)/shard_map/pack_rest/pallas_call | solution.py:380
  9.1 1.2 %collective-permute-start.5 = (bf16[784,128]{1,0:T(8,128)(2,1)}, bf16[784,128]{1,0:T(8,128)(2,1)S(1)}, u32[]{:S(2)}, u32[]{:S(2)}) collective-permute-start(bf16[784,128]{1,0:T(8,128)(2,1)} %get-tuple-element.27), channel_id=1, source_target_pairs={{0,8},{4,12},{8,0},{12,4},{16,24},{20,28},{24,16},{28,20},{1,9},{5... | collective-permute-start | bytes 602120 | tf_op jit(solution)/shard_map/ppermute | solution.py:354
  10.3 1.5 %collective-permute-start.6 = (bf16[784,128]{1,0:T(8,128)(2,1)}, bf16[784,128]{1,0:T(8,128)(2,1)S(1)}, u32[]{:S(2)}, u32[]{:S(2)}) collective-permute-start(bf16[784,128]{1,0:T(8,128)(2,1)} %get-tuple-element.28), channel_id=1, source_target_pairs={{0,16},{4,20},{8,24},{12,28},{16,0},{20,4},{24,8},{28,12},{1,17},{... | collective-permute-start | bytes 602120 | tf_op jit(solution)/shard_map/ppermute | solution.py:354
  11.8 0.6 %collective-permute-start.7 = (bf16[784,128]{1,0:T(8,128)(2,1)}, bf16[784,128]{1,0:T(8,128)(2,1)S(1)}, u32[]{:S(2)}, u32[]{:S(2)}) collective-permute-start(bf16[784,128]{1,0:T(8,128)(2,1)} %get-tuple-element.29), channel_id=1, source_target_pairs={{0,12},{4,8},{8,4},{12,0},{16,28},{20,24},{24,20},{28,16},{1,13},{... | collective-permute-start | bytes 602120 | tf_op jit(solution)/shard_map/ppermute | solution.py:354
  12.9 3.6 %collective-permute-done.1.refs_3_ = bf16[784,128]{1,0:T(8,128)(2,1)S(1)} collective-permute-done((bf16[784,128]{1,0:T(8,128)(2,1)}, bf16[784,128]{1,0:T(8,128)(2,1)S(1)}, u32[]{:S(2)}, u32[]{:S(2)}) %collective-permute-start.1) | collective-permute-done | bytes 200736 | tf_op jit(solution)/shard_map/ppermute | solution.py:354
  16.6 0.9 %cot.1 = (bf16[1088,128]{1,0:T(8,128)(2,1)S(1)}, bf16[640,128]{1,0:T(8,128)(2,1)S(1)}, bf16[576,128]{1,0:T(8,128)(2,1)S(1)}, bf16[576,128]{1,0:T(8,128)(2,1)S(1)}) custom-call(s32[1,8]{1,0:T(1,128)S(1)} %copy-done.1, bf16[272,2048]{1,0:T(8,128)(2,1)S(1)} %copy-done, bf16[784,128]{1,0:T(8,128)(2,1)S(1)} %collective-permute-done.refs_2_, ...), custom_call_target="tpu_custom_call" | custom-call | bytes 1474560 | tf_op jit(solution)/shard_map/cot/pallas_call | solution.py:403
  17.6 4.1 %collective-permute-done.5.refs_4_ = bf16[784,128]{1,0:T(8,128)(2,1)S(1)} collective-permute-done((bf16[784,128]{1,0:T(8,128)(2,1)}, bf16[784,128]{1,0:T(8,128)(2,1)S(1)}, u32[]{:S(2)}, u32[]{:S(2)}) %collective-permute-start.5) | collective-permute-done | bytes 200736 | tf_op jit(solution)/shard_map/ppermute | solution.py:354
  21.7 1.5 %collective-permute-start.3 = (bf16[640,128]{1,0:T(8,128)(2,1)S(1)}, bf16[640,128]{1,0:T(8,128)(2,1)S(1)}, u32[]{:S(2)}, u32[]{:S(2)}) collective-permute-start(bf16[640,128]{1,0:T(8,128)(2,1)S(1)} %get-tuple-element.24), channel_id=1, source_target_pairs={{0,8},{4,20},{8,0},{12,28},{16,24},{20,4},{24,16},{28,12},{1,9},{5... | collective-permute-start | bytes 491528 | tf_op jit(solution)/shard_map/ppermute | solution.py:354
  23.2 1.5 %collective-permute-done.7.refs_6_ = bf16[784,128]{1,0:T(8,128)(2,1)S(1)} collective-permute-done((bf16[784,128]{1,0:T(8,128)(2,1)}, bf16[784,128]{1,0:T(8,128)(2,1)S(1)}, u32[]{:S(2)}, u32[]{:S(2)}) %collective-permute-start.7) | collective-permute-done | bytes 200736 | tf_op jit(solution)/shard_map/ppermute | solution.py:354
  24.7 0.6 %collective-permute-start.4 = (bf16[576,128]{1,0:T(8,128)(2,1)S(1)}, bf16[576,128]{1,0:T(8,128)(2,1)S(1)}, u32[]{:S(2)}, u32[]{:S(2)}) collective-permute-start(bf16[576,128]{1,0:T(8,128)(2,1)S(1)} %get-tuple-element.25), channel_id=1, source_target_pairs={{0,16},{4,12},{8,24},{12,4},{16,0},{20,28},{24,8},{28,20},{1,17},{... | collective-permute-start | bytes 442376 | tf_op jit(solution)/shard_map/ppermute | solution.py:354
  25.3 3.5 %attend.1 = (bf16[1040,128]{1,0:T(8,128)(2,1)S(1)}, bf16[1040,128]{1,0:T(8,128)(2,1)S(1)}) custom-call(s32[8]{0:T(128)S(1)} %copy-done.3, bf16[784,128]{1,0:T(8,128)(2,1)S(1)} %copy-done.2, bf16[784,128]{1,0:T(8,128)(2,1)S(1)} %collective-permute-done.refs_2_, bf16[784,128]{1,0:T(8,128)(2,1)S(1)} %collective-permute-done.1.refs_3_, ...), custom_call_target="tpu_custom_call" | custom-call | flops 1073741824 | bytes 1064960 | tf_op jit(solution)/shard_map/attend/pallas_call | solution.py:424
  28.7 1.7 %collective-permute-start.14 = (bf16[1040,128]{1,0:T(8,128)(2,1)S(1)}, bf16[1040,128]{1,0:T(8,128)(2,1)S(1)}, u32[]{:S(2)}, u32[]{:S(2)}) collective-permute-start(bf16[1040,128]{1,0:T(8,128)(2,1)S(1)} %get-tuple-element.34.x_ref), channel_id=1, source_target_pairs={{0,12},{4,16},{8,4},{12,24},{16,28},{20,0},{24,20},{28,8},{1,13},{... | collective-permute-start | bytes 798728 | tf_op jit(solution)/shard_map/ppermute | solution.py:354
  30.4 1.4 %collective-permute-start.13 = (bf16[1040,128]{1,0:T(8,128)(2,1)S(1)}, bf16[1040,128]{1,0:T(8,128)(2,1)S(1)}, u32[]{:S(2)}, u32[]{:S(2)}) collective-permute-start(bf16[1040,128]{1,0:T(8,128)(2,1)S(1)} %get-tuple-element.32.refs_3_.refs_1_), channel_id=1, source_target_pairs={{0,8},{4,20},{8,0},{12,28},{16,24},{20,4},{24,16},{28,12},{1,9},{5... | collective-permute-start | bytes 798728 | tf_op jit(solution)/shard_map/ppermute | solution.py:354
  31.9 0.9 %collective-permute-start.12 = (bf16[1040,128]{1,0:T(8,128)(2,1)S(1)}, bf16[1040,128]{1,0:T(8,128)(2,1)S(1)}, u32[]{:S(2)}, u32[]{:S(2)}) collective-permute-start(bf16[1040,128]{1,0:T(8,128)(2,1)S(1)} %get-tuple-element.32.refs_3_.refs_1_), channel_id=1, source_target_pairs={{0,16},{4,12},{8,24},{12,4},{16,0},{20,28},{24,8},{28,20},{1,17},{... | collective-permute-start | bytes 798728 | tf_op jit(solution)/shard_map/ppermute | solution.py:354
  32.8 1.6 %collective-permute-start.10 = (bf16[1472,128]{1,0:T(8,128)(2,1)S(1)}, bf16[1472,128]{1,0:T(8,128)(2,1)S(1)}, u32[]{:S(2)}, u32[]{:S(2)}) collective-permute-start(bf16[1472,128]{1,0:T(8,128)(2,1)S(1)} %stack.1), channel_id=1, source_target_pairs={{0,1},{1,0},{2,3},{3,2},{4,5},{5,4},{6,7},{7,6},{8,9},{9,8},{10,11... | collective-permute-start | bytes 1130504 | tf_op jit(solution)/shard_map/ppermute | solution.py:360
  34.5 1.0 %collective-permute-done.14.refs_5_ = bf16[1040,128]{1,0:T(8,128)(2,1)S(1)} collective-permute-done((bf16[1040,128]{1,0:T(8,128)(2,1)S(1)}, bf16[1040,128]{1,0:T(8,128)(2,1)S(1)}, u32[]{:S(2)}, u32[]{:S(2)}) %collective-permute-start.14) | collective-permute-done | bytes 266272 | tf_op jit(solution)/shard_map/ppermute | solution.py:354
  35.5 1.6 %collective-permute-start.18 = (bf16[1040,128]{1,0:T(8,128)(2,1)S(1)}, bf16[1040,128]{1,0:T(8,128)(2,1)S(1)}, u32[]{:S(2)}, u32[]{:S(2)}) collective-permute-start(bf16[1040,128]{1,0:T(8,128)(2,1)S(1)} %collective-permute-done.14.refs_5_), channel_id=1, source_target_pairs={{0,8},{4,20},{8,0},{12,28},{16,24},{20,4},{24,16},{28,12},{1,9},{5... | collective-permute-start | bytes 798728 | tf_op jit(solution)/shard_map/ppermute | solution.py:354
  37.1 6.2 %collective-permute-done.13.refs_4_ = bf16[1040,128]{1,0:T(8,128)(2,1)S(1)} collective-permute-done((bf16[1040,128]{1,0:T(8,128)(2,1)S(1)}, bf16[1040,128]{1,0:T(8,128)(2,1)S(1)}, u32[]{:S(2)}, u32[]{:S(2)}) %collective-permute-start.13) | collective-permute-done | bytes 266272 | tf_op jit(solution)/shard_map/ppermute | solution.py:354
  43.3 0.7 %collective-permute-start.17 = (bf16[1040,128]{1,0:T(8,128)(2,1)S(1)}, bf16[1040,128]{1,0:T(8,128)(2,1)S(1)}, u32[]{:S(2)}, u32[]{:S(2)}) collective-permute-start(bf16[1040,128]{1,0:T(8,128)(2,1)S(1)} %collective-permute-done.13.refs_4_), channel_id=1, source_target_pairs={{0,16},{4,12},{8,24},{12,4},{16,0},{20,28},{24,8},{28,20},{1,17},{... | collective-permute-start | bytes 798728 | tf_op jit(solution)/shard_map/ppermute | solution.py:354
  44.0 1.8 %collective-permute-done.12.refs_3_.refs_1_ = bf16[1040,128]{1,0:T(8,128)(2,1)S(1)} collective-permute-done((bf16[1040,128]{1,0:T(8,128)(2,1)S(1)}, bf16[1040,128]{1,0:T(8,128)(2,1)S(1)}, u32[]{:S(2)}, u32[]{:S(2)}) %collective-permute-start.12) | collective-permute-done | bytes 266272 | tf_op jit(solution)/shard_map/ppermute | solution.py:354
  45.8 0.7 %collective-permute-start.16 = (bf16[1040,128]{1,0:T(8,128)(2,1)S(1)}, bf16[1040,128]{1,0:T(8,128)(2,1)S(1)}, u32[]{:S(2)}, u32[]{:S(2)}) collective-permute-start(bf16[1040,128]{1,0:T(8,128)(2,1)S(1)} %late.1), channel_id=1, source_target_pairs={{0,4},{4,0},{8,12},{12,8},{16,20},{20,16},{24,28},{28,24},{1,5},{5... | collective-permute-start | bytes 798728 | tf_op jit(solution)/shard_map/ppermute | solution.py:354
  46.5 0.6 %turn.1 = (bf16[256,1088]{1,0:T(8,128)(2,1)S(1)}, bf16[256,1088]{1,0:T(8,128)(2,1)S(1)}) custom-call(bf16[1088,128]{1,0:T(8,128)(2,1)S(1)} %get-tuple-element.22.refs_0_, bf16[576,128]{1,0:T(8,128)(2,1)S(1)} %collective-permute-done.2.refs_0_.refs_1_, bf16[640,128]{1,0:T(8,128)(2,1)S(1)} %collective-permute-done.3.refs_1_.refs_2_, ...), custom_call_target="tpu_custom_call" | custom-call | bytes 2228224 | tf_op jit(solution)/shard_map/turn/pallas_call | solution.py:450
  47.1 0.6 %grad_other_near.1 = bf16[256,640]{1,0:T(8,128)(2,1)S(1)} custom-call(bf16[256,1088]{1,0:T(8,128)(2,1)S(1)} %get-tuple-element.36.refs_0_, bf16[1040,128]{1,0:T(8,128)(2,1)S(1)} %get-tuple-element.32.refs_3_.refs_1_, bf16[1040,128]{1,0:T(8,128)(2,1)S(1)} %collective-permute-done.11.refs_2_.refs_0_, ...), custom_call_target="tpu_custom_call" | custom-call | flops 356515840 | bytes 655360 | tf_op jit(solution)/shard_map/grad_other_near/pallas_call | solution.py:460
  47.8 1.3 %grad_own_near.1 = (f32[256,640]{1,0:T(8,128)S(1)}, bf16[256,1024]{1,0:T(8,128)(2,1)}) custom-call(bf16[256,1088]{1,0:T(8,128)(2,1)S(1)} %get-tuple-element.33.refs_0_, bf16[1040,128]{1,0:T(8,128)(2,1)S(1)} %get-tuple-element.32.refs_3_.refs_1_, bf16[1040,128]{1,0:T(8,128)(2,1)S(1)} %collective-permute-done.11.refs_2_.refs_0_, ...), custom_call_target="tpu_custom_call" | custom-call | flops 356515840 | bytes 2359296 | tf_op jit(solution)/shard_map/grad_own_near/pallas_call | solution.py:473
  49.1 0.6 %collective-permute-done.17.refs_2_.refs_5_ = bf16[1040,128]{1,0:T(8,128)(2,1)S(1)} collective-permute-done((bf16[1040,128]{1,0:T(8,128)(2,1)S(1)}, bf16[1040,128]{1,0:T(8,128)(2,1)S(1)}, u32[]{:S(2)}, u32[]{:S(2)}) %collective-permute-start.17) | collective-permute-done | bytes 266272 | tf_op jit(solution)/shard_map/ppermute | solution.py:354
  49.7 0.5 grad_other_far.1
  50.2 0.7 %collective-permute-start.19 = (bf16[256,384]{1,0:T(8,128)(2,1)S(1)}, bf16[256,384]{1,0:T(8,128)(2,1)S(1)}, u32[]{:S(2)}, u32[]{:S(2)}) collective-permute-start(bf16[256,384]{1,0:T(8,128)(2,1)S(1)} %grad_other_far.1), channel_id=1, source_target_pairs={{0,4},{4,0},{8,12},{12,8},{16,20},{20,16},{24,28},{28,24},{1,5},{5... | collective-permute-start | bytes 589832 | tf_op jit(solution)/shard_map/ppermute | solution.py:354
  50.9 0.5 grad_own_far.1.refs_2_
  51.4 0.9 %near.1.refs_8_ = f32[256,1024]{1,0:T(8,128)} custom-call(f32[256,640]{1,0:T(8,128)S(1)} %get-tuple-element.35.refs_4_.refs_0_, bf16[256,640]{1,0:T(8,128)(2,1)S(1)} %collective-permute-done.15.refs_1_), custom_call_target="tpu_custom_call" | custom-call | bytes 2097152 | tf_op jit(solution)/shard_map/near/pallas_call | solution.py:484
  52.2 0.9 %last.1 = (bf16[256,1024]{1,0:T(8,128)(2,1)}, f32[256,1024]{1,0:T(8,128)}) custom-call(f32[256,640]{1,0:T(8,128)S(1)} %get-tuple-element.35.refs_4_.refs_0_, bf16[256,640]{1,0:T(8,128)(2,1)S(1)} %collective-permute-done.15.refs_1_, f32[256,384]{1,0:T(8,128)S(1)} %grad_own_far.1.refs_2_, ...), custom_call_target="tpu_custom_call", output_to_operand_aliasing={{0}: (7, {}), {1}: (8, {})} | custom-call | bytes 3145728 | tf_op jit(solution)/shard_map/last/pallas_call | solution.py:493
  (29 shorter events, 0.9 us)
Async XLA Ops:
  2.5 14.1 %copy-start = (bf16[272,2048]{1,0:T(8,128)(2,1)S(1)}, bf16[272,2048]{1,0:T(8,128)(2,1)}, u32[]{:S(2)}) copy-start(bf16[272,2048]{1,0:T(8,128)(2,1)} %refs_1_.4) | copy-start | bytes 3342340
  2.5 14.1 %copy-start.1 = (s32[1,8]{1,0:T(1,128)S(1)}, s32[1,8]{1,0:T(1,128)}, u32[]{:S(2)}) copy-start(s32[1,8]{1,0:T(1,128)} %refs_0_.5) | copy-start | bytes 100
  2.5 10.0 %collective-permute-start = (bf16[784,128]{1,0:T(8,128)(2,1)}, bf16[784,128]{1,0:T(8,128)(2,1)S(1)}, u32[]{:S(2)}, u32[]{:S(2)}) collective-permute-start(bf16[784,128]{1,0:T(8,128)(2,1)} %get-tuple-element.20), channel_id=1, source_target_pairs={{0,24},{4,28},{8,16},{12,20},{16,8},{20,12},{24,0},{28,4},{1,25},{... | collective-permute-start | bytes 602120 | tf_op jit(solution)/shard_map/ppermute | solution.py:354
  6.5 10.1 %collective-permute-start.1 = (bf16[784,128]{1,0:T(8,128)(2,1)}, bf16[784,128]{1,0:T(8,128)(2,1)S(1)}, u32[]{:S(2)}, u32[]{:S(2)}) collective-permute-start(bf16[784,128]{1,0:T(8,128)(2,1)} %get-tuple-element.21), channel_id=1, source_target_pairs={{0,28},{4,24},{8,20},{12,16},{16,12},{20,8},{24,4},{28,0},{1,29},{... | collective-permute-start | bytes 602120 | tf_op jit(solution)/shard_map/ppermute | solution.py:354
  9.1 16.2 %copy-start.2 = (bf16[784,128]{1,0:T(8,128)(2,1)S(1)}, bf16[784,128]{1,0:T(8,128)(2,1)}, u32[]{:S(2)}) copy-start(bf16[784,128]{1,0:T(8,128)(2,1)} %get-tuple-element.26.refs_1_) | copy-start | bytes 602116
  9.1 16.2 %copy-start.3 = (s32[8]{0:T(128)S(1)}, s32[8]{0:T(128)}, u32[]{:S(2)}) copy-start(s32[8]{0:T(128)} %refs_0_.7) | copy-start | bytes 100
  9.1 12.6 %collective-permute-start.5 = (bf16[784,128]{1,0:T(8,128)(2,1)}, bf16[784,128]{1,0:T(8,128)(2,1)S(1)}, u32[]{:S(2)}, u32[]{:S(2)}) collective-permute-start(bf16[784,128]{1,0:T(8,128)(2,1)} %get-tuple-element.27), channel_id=1, source_target_pairs={{0,8},{4,12},{8,0},{12,4},{16,24},{20,28},{24,16},{28,20},{1,9},{5... | collective-permute-start | bytes 602120 | tf_op jit(solution)/shard_map/ppermute | solution.py:354
  10.3 12.9 %collective-permute-start.6 = (bf16[784,128]{1,0:T(8,128)(2,1)}, bf16[784,128]{1,0:T(8,128)(2,1)S(1)}, u32[]{:S(2)}, u32[]{:S(2)}) collective-permute-start(bf16[784,128]{1,0:T(8,128)(2,1)} %get-tuple-element.28), channel_id=1, source_target_pairs={{0,16},{4,20},{8,24},{12,28},{16,0},{20,4},{24,8},{28,12},{1,17},{... | collective-permute-start | bytes 602120 | tf_op jit(solution)/shard_map/ppermute | solution.py:354
  11.8 12.9 %collective-permute-start.7 = (bf16[784,128]{1,0:T(8,128)(2,1)}, bf16[784,128]{1,0:T(8,128)(2,1)S(1)}, u32[]{:S(2)}, u32[]{:S(2)}) collective-permute-start(bf16[784,128]{1,0:T(8,128)(2,1)} %get-tuple-element.29), channel_id=1, source_target_pairs={{0,12},{4,8},{8,4},{12,0},{16,28},{20,24},{24,20},{28,16},{1,13},{... | collective-permute-start | bytes 602120 | tf_op jit(solution)/shard_map/ppermute | solution.py:354
  12.5 12.7 %collective-permute-start.8 = (bf16[784,128]{1,0:T(8,128)(2,1)}, bf16[784,128]{1,0:T(8,128)(2,1)S(1)}, u32[]{:S(2)}, u32[]{:S(2)}) collective-permute-start(bf16[784,128]{1,0:T(8,128)(2,1)} %get-tuple-element.30), channel_id=1, source_target_pairs={{0,20},{4,16},{8,28},{12,24},{16,4},{20,0},{24,12},{28,8},{1,21},{... | collective-permute-start | bytes 602120 | tf_op jit(solution)/shard_map/ppermute | solution.py:354
  16.5 8.7 %collective-permute-start.9 = (bf16[784,128]{1,0:T(8,128)(2,1)}, bf16[784,128]{1,0:T(8,128)(2,1)S(1)}, u32[]{:S(2)}, u32[]{:S(2)}) collective-permute-start(bf16[784,128]{1,0:T(8,128)(2,1)} %get-tuple-element.31), channel_id=1, source_target_pairs={{0,4},{4,0},{8,12},{12,8},{16,20},{20,16},{24,28},{28,24},{1,5},{5... | collective-permute-start | bytes 602120 | tf_op jit(solution)/shard_map/ppermute | solution.py:354
  21.7 11.1 %collective-permute-start.3 = (bf16[640,128]{1,0:T(8,128)(2,1)S(1)}, bf16[640,128]{1,0:T(8,128)(2,1)S(1)}, u32[]{:S(2)}, u32[]{:S(2)}) collective-permute-start(bf16[640,128]{1,0:T(8,128)(2,1)S(1)} %get-tuple-element.24), channel_id=1, source_target_pairs={{0,8},{4,20},{8,0},{12,28},{16,24},{20,4},{24,16},{28,12},{1,9},{5... | collective-permute-start | bytes 491528 | tf_op jit(solution)/shard_map/ppermute | solution.py:354
  23.2 8.6 %collective-permute-start.2 = (bf16[576,128]{1,0:T(8,128)(2,1)S(1)}, bf16[576,128]{1,0:T(8,128)(2,1)S(1)}, u32[]{:S(2)}, u32[]{:S(2)}) collective-permute-start(bf16[576,128]{1,0:T(8,128)(2,1)S(1)} %get-tuple-element.23), channel_id=1, source_target_pairs={{0,24},{4,28},{8,16},{12,20},{16,8},{20,12},{24,0},{28,4},{1,25},{... | collective-permute-start | bytes 442376 | tf_op jit(solution)/shard_map/ppermute | solution.py:354
  24.7 7.2 %collective-permute-start.4 = (bf16[576,128]{1,0:T(8,128)(2,1)S(1)}, bf16[576,128]{1,0:T(8,128)(2,1)S(1)}, u32[]{:S(2)}, u32[]{:S(2)}) collective-permute-start(bf16[576,128]{1,0:T(8,128)(2,1)S(1)} %get-tuple-element.25), channel_id=1, source_target_pairs={{0,16},{4,12},{8,24},{12,4},{16,0},{20,28},{24,8},{28,20},{1,17},{... | collective-permute-start | bytes 442376 | tf_op jit(solution)/shard_map/ppermute | solution.py:354
  28.7 6.7 %collective-permute-start.14 = (bf16[1040,128]{1,0:T(8,128)(2,1)S(1)}, bf16[1040,128]{1,0:T(8,128)(2,1)S(1)}, u32[]{:S(2)}, u32[]{:S(2)}) collective-permute-start(bf16[1040,128]{1,0:T(8,128)(2,1)S(1)} %get-tuple-element.34.x_ref), channel_id=1, source_target_pairs={{0,12},{4,16},{8,4},{12,24},{16,28},{20,0},{24,20},{28,8},{1,13},{... | collective-permute-start | bytes 798728 | tf_op jit(solution)/shard_map/ppermute | solution.py:354
  30.4 12.9 %collective-permute-start.13 = (bf16[1040,128]{1,0:T(8,128)(2,1)S(1)}, bf16[1040,128]{1,0:T(8,128)(2,1)S(1)}, u32[]{:S(2)}, u32[]{:S(2)}) collective-permute-start(bf16[1040,128]{1,0:T(8,128)(2,1)S(1)} %get-tuple-element.32.refs_3_.refs_1_), channel_id=1, source_target_pairs={{0,8},{4,20},{8,0},{12,28},{16,24},{20,4},{24,16},{28,12},{1,9},{5... | collective-permute-start | bytes 798728 | tf_op jit(solution)/shard_map/ppermute | solution.py:354
  31.8 12.1 %collective-permute-start.11 = (bf16[1040,128]{1,0:T(8,128)(2,1)S(1)}, bf16[1040,128]{1,0:T(8,128)(2,1)S(1)}, u32[]{:S(2)}, u32[]{:S(2)}) collective-permute-start(bf16[1040,128]{1,0:T(8,128)(2,1)S(1)} %get-tuple-element.34.x_ref), channel_id=1, source_target_pairs={{0,20},{4,8},{8,28},{12,0},{16,4},{20,24},{24,12},{28,16},{1,21},{... | collective-permute-start | bytes 798728 | tf_op jit(solution)/shard_map/ppermute | solution.py:354
  31.9 13.9 %collective-permute-start.12 = (bf16[1040,128]{1,0:T(8,128)(2,1)S(1)}, bf16[1040,128]{1,0:T(8,128)(2,1)S(1)}, u32[]{:S(2)}, u32[]{:S(2)}) collective-permute-start(bf16[1040,128]{1,0:T(8,128)(2,1)S(1)} %get-tuple-element.32.refs_3_.refs_1_), channel_id=1, source_target_pairs={{0,16},{4,12},{8,24},{12,4},{16,0},{20,28},{24,8},{28,20},{1,17},{... | collective-permute-start | bytes 798728 | tf_op jit(solution)/shard_map/ppermute | solution.py:354
  32.8 13.7 %collective-permute-start.10 = (bf16[1472,128]{1,0:T(8,128)(2,1)S(1)}, bf16[1472,128]{1,0:T(8,128)(2,1)S(1)}, u32[]{:S(2)}, u32[]{:S(2)}) collective-permute-start(bf16[1472,128]{1,0:T(8,128)(2,1)S(1)} %stack.1), channel_id=1, source_target_pairs={{0,1},{1,0},{2,3},{3,2},{4,5},{5,4},{6,7},{7,6},{8,9},{9,8},{10,11... | collective-permute-start | bytes 1130504 | tf_op jit(solution)/shard_map/ppermute | solution.py:360
  35.5 13.6 %collective-permute-start.18 = (bf16[1040,128]{1,0:T(8,128)(2,1)S(1)}, bf16[1040,128]{1,0:T(8,128)(2,1)S(1)}, u32[]{:S(2)}, u32[]{:S(2)}) collective-permute-start(bf16[1040,128]{1,0:T(8,128)(2,1)S(1)} %collective-permute-done.14.refs_5_), channel_id=1, source_target_pairs={{0,8},{4,20},{8,0},{12,28},{16,24},{20,4},{24,16},{28,12},{1,9},{5... | collective-permute-start | bytes 798728 | tf_op jit(solution)/shard_map/ppermute | solution.py:354
  43.3 6.4 %collective-permute-start.17 = (bf16[1040,128]{1,0:T(8,128)(2,1)S(1)}, bf16[1040,128]{1,0:T(8,128)(2,1)S(1)}, u32[]{:S(2)}, u32[]{:S(2)}) collective-permute-start(bf16[1040,128]{1,0:T(8,128)(2,1)S(1)} %collective-permute-done.13.refs_4_), channel_id=1, source_target_pairs={{0,16},{4,12},{8,24},{12,4},{16,0},{20,28},{24,8},{28,20},{1,17},{... | collective-permute-start | bytes 798728 | tf_op jit(solution)/shard_map/ppermute | solution.py:354
  45.8 3.9 %collective-permute-start.16 = (bf16[1040,128]{1,0:T(8,128)(2,1)S(1)}, bf16[1040,128]{1,0:T(8,128)(2,1)S(1)}, u32[]{:S(2)}, u32[]{:S(2)}) collective-permute-start(bf16[1040,128]{1,0:T(8,128)(2,1)S(1)} %late.1), channel_id=1, source_target_pairs={{0,4},{4,0},{8,12},{12,8},{16,20},{20,16},{24,28},{28,24},{1,5},{5... | collective-permute-start | bytes 798728 | tf_op jit(solution)/shard_map/ppermute | solution.py:354
  47.7 3.6 %collective-permute-start.15 = (bf16[256,640]{1,0:T(8,128)(2,1)S(1)}, bf16[256,640]{1,0:T(8,128)(2,1)S(1)}, u32[]{:S(2)}, u32[]{:S(2)}) collective-permute-start(bf16[256,640]{1,0:T(8,128)(2,1)S(1)} %grad_other_near.1), channel_id=1, source_target_pairs={{0,4},{4,0},{8,12},{12,8},{16,20},{20,16},{24,28},{28,24},{1,5},{5... | collective-permute-start | bytes 983048 | tf_op jit(solution)/shard_map/ppermute | solution.py:354
  50.2 2.0 %collective-permute-start.19 = (bf16[256,384]{1,0:T(8,128)(2,1)S(1)}, bf16[256,384]{1,0:T(8,128)(2,1)S(1)}, u32[]{:S(2)}, u32[]{:S(2)}) collective-permute-start(bf16[256,384]{1,0:T(8,128)(2,1)S(1)} %grad_other_far.1), channel_id=1, source_target_pairs={{0,4},{4,0},{8,12},{12,8},{16,20},{20,16},{24,28},{28,24},{1,5},{5... | collective-permute-start | bytes 589832 | tf_op jit(solution)/shard_map/ppermute | solution.py:354

commit v17 on v16

--- a/solution.py
+++ b/solution.py
@@ -156,7 +156,7 @@
     bias = [
         jnp.where(token < counts[s] * TPF, 0.0, -jnp.inf).astype(jnp.float32) for s in range(n)
     ]
-    values = [x_ref[s, 2 * tok : 3 * tok, :].T for s in range(n)]
+    values = []
     def scores_of(block):
         q = x_ref[block, 0:tok, :]
         return {
@@ -181,6 +181,7 @@
         scores, ahead = ahead, scores_of(block + 1) if block + 1 < n else None
         if behind is not None:
             mix(block - 1, behind)
+        values.append(x_ref[block, 2 * tok : 3 * tok, :].T)
         top = None
         for x in scores.values():
             high = jnp.max(x, axis=0, keepdims=True)

time: 53.3 us -> 53.3 us (level)
  no operation moved by 1% of the time
where the time goes in v17:
time: 53.3 us; the launch traced here: 53.2 us
  starting transfers between devices  19.3 us (36%)
  waiting for transfers between devices  18.9 us (35%)
  Pallas kernels  14.1 us (26%)
  between operations  0.8 us (2%)
    ppermute x19, waiting for transfers between devices, swap(): return lax.ppermute(x, 'tm', [(i, i ^ bits[i % 2]) for i in range(n)])  18.9 us
    ppermute x19, starting transfers between devices, swap(): return lax.ppermute(x, 'tm', [(i, i ^ bits[i % 2]) for i in range(n)])  17.7 us
    pallas_call x2, Pallas kernels, pack(): call(lambda *refs: pack_kernel(n, heads, *refs), name, [((length, HD), bf...  4.42 us
    pallas_call x1, Pallas kernels, head_body(): call(lambda *refs: attend_kernel(n, tok, [0] + order, *refs), 'attend', [...  3.48 us
    ppermute x1, starting transfers between devices, swap_plane(): return lax.ppermute(x, ('tm', 'head'), pairs)  1.64 us
    pallas_call x3, Pallas kernels, grad(): call(lambda *refs: grad_kernel(rows, half, len(heads), *refs), name, [((c...  1.59 us
    pallas_call x1, Pallas kernels, head_body(): call(lambda *refs: own_near_kernel(rows, half, tok, *refs), 'grad_own_nea...  1.3 us
  transfers between devices with their start and end apart: 20, of which 8 were waited for; matrix products, arithmetic and copies ran while one was open for 0% of the time, Pallas kernels for 21%

profile of v17, /device:TPU:0, one launch (start us, length us, event | category | flops | bytes accessed | tf_op | source)
XLA Modules:
  0.0 53.2 jit_solution(17935911089723907261)
XLA Ops:
  0.6 1.9 %pack_first.1 = (bf16[784,128]{1,0:T(8,128)(2,1)}, bf16[784,128]{1,0:T(8,128)(2,1)}) custom-call(bf16[256,1024]{1,0:T(8,128)(2,1)} %refs_0_.6, bf16[256,1024]{1,0:T(8,128)(2,1)} %refs_1_.5, bf16[256,1024]{1,0:T(8,128)(2,1)} %refs_2_.3, bf16[2,1024]{1,0:T(2,128)(2,1)} %refs_3_.3), custom_call_target="tpu_custom_call" | custom-call | bytes 802816 | tf_op jit(solution)/shard_map/pack_first/pallas_call | solution.py:381
  2.5 4.0 %collective-permute-start = (bf16[784,128]{1,0:T(8,128)(2,1)}, bf16[784,128]{1,0:T(8,128)(2,1)S(1)}, u32[]{:S(2)}, u32[]{:S(2)}) collective-permute-start(bf16[784,128]{1,0:T(8,128)(2,1)} %get-tuple-element.20), channel_id=1, source_target_pairs={{0,24},{4,28},{8,16},{12,20},{16,8},{20,12},{24,0},{28,4},{1,25},{... | collective-permute-start | bytes 602120 | tf_op jit(solution)/shard_map/ppermute | solution.py:355
  6.5 2.6 %pack_rest.1 = (bf16[784,128]{1,0:T(8,128)(2,1)}, bf16[784,128]{1,0:T(8,128)(2,1)}, bf16[784,128]{1,0:T(8,128)(2,1)}, bf16[784,128]{1,0:T(8,128)(2,1)}, bf16[784...) custom-call(bf16[256,1024]{1,0:T(8,128)(2,1)} %refs_0_.6, bf16[256,1024]{1,0:T(8,128)(2,1)} %refs_1_.5, ...), custom_call_target="tpu_custom_call" | custom-call | bytes 2408448 | tf_op jit(solution)/shard_map/pack_rest/pallas_call | solution.py:381
  9.1 1.2 %collective-permute-start.5 = (bf16[784,128]{1,0:T(8,128)(2,1)}, bf16[784,128]{1,0:T(8,128)(2,1)S(1)}, u32[]{:S(2)}, u32[]{:S(2)}) collective-permute-start(bf16[784,128]{1,0:T(8,128)(2,1)} %get-tuple-element.27), channel_id=1, source_target_pairs={{0,8},{4,12},{8,0},{12,4},{16,24},{20,28},{24,16},{28,20},{1,9},{5... | collective-permute-start | bytes 602120 | tf_op jit(solution)/shard_map/ppermute | solution.py:355
  10.3 1.5 %collective-permute-start.6 = (bf16[784,128]{1,0:T(8,128)(2,1)}, bf16[784,128]{1,0:T(8,128)(2,1)S(1)}, u32[]{:S(2)}, u32[]{:S(2)}) collective-permute-start(bf16[784,128]{1,0:T(8,128)(2,1)} %get-tuple-element.28), channel_id=1, source_target_pairs={{0,16},{4,20},{8,24},{12,28},{16,0},{20,4},{24,8},{28,12},{1,17},{... | collective-permute-start | bytes 602120 | tf_op jit(solution)/shard_map/ppermute | solution.py:355
  11.8 0.6 %collective-permute-start.7 = (bf16[784,128]{1,0:T(8,128)(2,1)}, bf16[784,128]{1,0:T(8,128)(2,1)S(1)}, u32[]{:S(2)}, u32[]{:S(2)}) collective-permute-start(bf16[784,128]{1,0:T(8,128)(2,1)} %get-tuple-element.29), channel_id=1, source_target_pairs={{0,12},{4,8},{8,4},{12,0},{16,28},{20,24},{24,20},{28,16},{1,13},{... | collective-permute-start | bytes 602120 | tf_op jit(solution)/shard_map/ppermute | solution.py:355
  12.9 3.6 %collective-permute-done.1.refs_3_ = bf16[784,128]{1,0:T(8,128)(2,1)S(1)} collective-permute-done((bf16[784,128]{1,0:T(8,128)(2,1)}, bf16[784,128]{1,0:T(8,128)(2,1)S(1)}, u32[]{:S(2)}, u32[]{:S(2)}) %collective-permute-start.1) | collective-permute-done | bytes 200736 | tf_op jit(solution)/shard_map/ppermute | solution.py:355
  16.6 0.9 %cot.1 = (bf16[1088,128]{1,0:T(8,128)(2,1)S(1)}, bf16[640,128]{1,0:T(8,128)(2,1)S(1)}, bf16[576,128]{1,0:T(8,128)(2,1)S(1)}, bf16[576,128]{1,0:T(8,128)(2,1)S(1)}) custom-call(s32[1,8]{1,0:T(1,128)S(1)} %copy-done.1, bf16[272,2048]{1,0:T(8,128)(2,1)S(1)} %copy-done, bf16[784,128]{1,0:T(8,128)(2,1)S(1)} %collective-permute-done.refs_2_, ...), custom_call_target="tpu_custom_call" | custom-call | bytes 1474560 | tf_op jit(solution)/shard_map/cot/pallas_call | solution.py:404
  17.6 4.1 %collective-permute-done.5.refs_4_ = bf16[784,128]{1,0:T(8,128)(2,1)S(1)} collective-permute-done((bf16[784,128]{1,0:T(8,128)(2,1)}, bf16[784,128]{1,0:T(8,128)(2,1)S(1)}, u32[]{:S(2)}, u32[]{:S(2)}) %collective-permute-start.5) | collective-permute-done | bytes 200736 | tf_op jit(solution)/shard_map/ppermute | solution.py:355
  21.7 1.5 %collective-permute-start.3 = (bf16[640,128]{1,0:T(8,128)(2,1)S(1)}, bf16[640,128]{1,0:T(8,128)(2,1)S(1)}, u32[]{:S(2)}, u32[]{:S(2)}) collective-permute-start(bf16[640,128]{1,0:T(8,128)(2,1)S(1)} %get-tuple-element.24), channel_id=1, source_target_pairs={{0,8},{4,20},{8,0},{12,28},{16,24},{20,4},{24,16},{28,12},{1,9},{5... | collective-permute-start | bytes 491528 | tf_op jit(solution)/shard_map/ppermute | solution.py:355
  23.2 1.5 %collective-permute-done.7.refs_6_ = bf16[784,128]{1,0:T(8,128)(2,1)S(1)} collective-permute-done((bf16[784,128]{1,0:T(8,128)(2,1)}, bf16[784,128]{1,0:T(8,128)(2,1)S(1)}, u32[]{:S(2)}, u32[]{:S(2)}) %collective-permute-start.7) | collective-permute-done | bytes 200736 | tf_op jit(solution)/shard_map/ppermute | solution.py:355
  24.7 0.6 %collective-permute-start.4 = (bf16[576,128]{1,0:T(8,128)(2,1)S(1)}, bf16[576,128]{1,0:T(8,128)(2,1)S(1)}, u32[]{:S(2)}, u32[]{:S(2)}) collective-permute-start(bf16[576,128]{1,0:T(8,128)(2,1)S(1)} %get-tuple-element.25), channel_id=1, source_target_pairs={{0,16},{4,12},{8,24},{12,4},{16,0},{20,28},{24,8},{28,20},{1,17},{... | collective-permute-start | bytes 442376 | tf_op jit(solution)/shard_map/ppermute | solution.py:355
  25.3 3.5 %attend.1 = (bf16[1040,128]{1,0:T(8,128)(2,1)S(1)}, bf16[1040,128]{1,0:T(8,128)(2,1)S(1)}) custom-call(s32[8]{0:T(128)S(1)} %copy-done.3, bf16[784,128]{1,0:T(8,128)(2,1)S(1)} %copy-done.2, bf16[784,128]{1,0:T(8,128)(2,1)S(1)} %collective-permute-done.refs_2_, bf16[784,128]{1,0:T(8,128)(2,1)S(1)} %collective-permute-done.1.refs_3_, ...), custom_call_target="tpu_custom_call" | custom-call | flops 1073741824 | bytes 1064960 | tf_op jit(solution)/shard_map/attend/pallas_call | solution.py:425
  28.7 1.6 %collective-permute-start.14 = (bf16[1040,128]{1,0:T(8,128)(2,1)S(1)}, bf16[1040,128]{1,0:T(8,128)(2,1)S(1)}, u32[]{:S(2)}, u32[]{:S(2)}) collective-permute-start(bf16[1040,128]{1,0:T(8,128)(2,1)S(1)} %get-tuple-element.34.x_ref), channel_id=1, source_target_pairs={{0,12},{4,16},{8,4},{12,24},{16,28},{20,0},{24,20},{28,8},{1,13},{... | collective-permute-start | bytes 798728 | tf_op jit(solution)/shard_map/ppermute | solution.py:355
  30.4 1.4 %collective-permute-start.13 = (bf16[1040,128]{1,0:T(8,128)(2,1)S(1)}, bf16[1040,128]{1,0:T(8,128)(2,1)S(1)}, u32[]{:S(2)}, u32[]{:S(2)}) collective-permute-start(bf16[1040,128]{1,0:T(8,128)(2,1)S(1)} %get-tuple-element.32.refs_3_.refs_1_), channel_id=1, source_target_pairs={{0,8},{4,20},{8,0},{12,28},{16,24},{20,4},{24,16},{28,12},{1,9},{5... | collective-permute-start | bytes 798728 | tf_op jit(solution)/shard_map/ppermute | solution.py:355
  31.9 0.9 %collective-permute-start.12 = (bf16[1040,128]{1,0:T(8,128)(2,1)S(1)}, bf16[1040,128]{1,0:T(8,128)(2,1)S(1)}, u32[]{:S(2)}, u32[]{:S(2)}) collective-permute-start(bf16[1040,128]{1,0:T(8,128)(2,1)S(1)} %get-tuple-element.32.refs_3_.refs_1_), channel_id=1, source_target_pairs={{0,16},{4,12},{8,24},{12,4},{16,0},{20,28},{24,8},{28,20},{1,17},{... | collective-permute-start | bytes 798728 | tf_op jit(solution)/shard_map/ppermute | solution.py:355
  32.8 1.6 %collective-permute-start.10 = (bf16[1472,128]{1,0:T(8,128)(2,1)S(1)}, bf16[1472,128]{1,0:T(8,128)(2,1)S(1)}, u32[]{:S(2)}, u32[]{:S(2)}) collective-permute-start(bf16[1472,128]{1,0:T(8,128)(2,1)S(1)} %stack.1), channel_id=1, source_target_pairs={{0,1},{1,0},{2,3},{3,2},{4,5},{5,4},{6,7},{7,6},{8,9},{9,8},{10,11... | collective-permute-start | bytes 1130504 | tf_op jit(solution)/shard_map/ppermute | solution.py:361
  34.5 1.0 %collective-permute-done.14.refs_5_ = bf16[1040,128]{1,0:T(8,128)(2,1)S(1)} collective-permute-done((bf16[1040,128]{1,0:T(8,128)(2,1)S(1)}, bf16[1040,128]{1,0:T(8,128)(2,1)S(1)}, u32[]{:S(2)}, u32[]{:S(2)}) %collective-permute-start.14) | collective-permute-done | bytes 266272 | tf_op jit(solution)/shard_map/ppermute | solution.py:355
  35.5 1.6 %collective-permute-start.18 = (bf16[1040,128]{1,0:T(8,128)(2,1)S(1)}, bf16[1040,128]{1,0:T(8,128)(2,1)S(1)}, u32[]{:S(2)}, u32[]{:S(2)}) collective-permute-start(bf16[1040,128]{1,0:T(8,128)(2,1)S(1)} %collective-permute-done.14.refs_5_), channel_id=1, source_target_pairs={{0,8},{4,20},{8,0},{12,28},{16,24},{20,4},{24,16},{28,12},{1,9},{5... | collective-permute-start | bytes 798728 | tf_op jit(solution)/shard_map/ppermute | solution.py:355
  37.1 6.2 %collective-permute-done.13.refs_4_ = bf16[1040,128]{1,0:T(8,128)(2,1)S(1)} collective-permute-done((bf16[1040,128]{1,0:T(8,128)(2,1)S(1)}, bf16[1040,128]{1,0:T(8,128)(2,1)S(1)}, u32[]{:S(2)}, u32[]{:S(2)}) %collective-permute-start.13) | collective-permute-done | bytes 266272 | tf_op jit(solution)/shard_map/ppermute | solution.py:355
  43.3 0.7 %collective-permute-start.17 = (bf16[1040,128]{1,0:T(8,128)(2,1)S(1)}, bf16[1040,128]{1,0:T(8,128)(2,1)S(1)}, u32[]{:S(2)}, u32[]{:S(2)}) collective-permute-start(bf16[1040,128]{1,0:T(8,128)(2,1)S(1)} %collective-permute-done.13.refs_4_), channel_id=1, source_target_pairs={{0,16},{4,12},{8,24},{12,4},{16,0},{20,28},{24,8},{28,20},{1,17},{... | collective-permute-start | bytes 798728 | tf_op jit(solution)/shard_map/ppermute | solution.py:355
  44.0 1.8 %collective-permute-done.12.refs_3_.refs_1_ = bf16[1040,128]{1,0:T(8,128)(2,1)S(1)} collective-permute-done((bf16[1040,128]{1,0:T(8,128)(2,1)S(1)}, bf16[1040,128]{1,0:T(8,128)(2,1)S(1)}, u32[]{:S(2)}, u32[]{:S(2)}) %collective-permute-start.12) | collective-permute-done | bytes 266272 | tf_op jit(solution)/shard_map/ppermute | solution.py:355
  45.8 0.7 %collective-permute-start.16 = (bf16[1040,128]{1,0:T(8,128)(2,1)S(1)}, bf16[1040,128]{1,0:T(8,128)(2,1)S(1)}, u32[]{:S(2)}, u32[]{:S(2)}) collective-permute-start(bf16[1040,128]{1,0:T(8,128)(2,1)S(1)} %late.1), channel_id=1, source_target_pairs={{0,4},{4,0},{8,12},{12,8},{16,20},{20,16},{24,28},{28,24},{1,5},{5... | collective-permute-start | bytes 798728 | tf_op jit(solution)/shard_map/ppermute | solution.py:355
  46.5 0.6 %turn.1 = (bf16[256,1088]{1,0:T(8,128)(2,1)S(1)}, bf16[256,1088]{1,0:T(8,128)(2,1)S(1)}) custom-call(bf16[1088,128]{1,0:T(8,128)(2,1)S(1)} %get-tuple-element.22.refs_0_, bf16[576,128]{1,0:T(8,128)(2,1)S(1)} %collective-permute-done.2.refs_0_.refs_1_, bf16[640,128]{1,0:T(8,128)(2,1)S(1)} %collective-permute-done.3.refs_1_.refs_2_, ...), custom_call_target="tpu_custom_call" | custom-call | bytes 2228224 | tf_op jit(solution)/shard_map/turn/pallas_call | solution.py:451
  47.1 0.6 %grad_other_near.1 = bf16[256,640]{1,0:T(8,128)(2,1)S(1)} custom-call(bf16[256,1088]{1,0:T(8,128)(2,1)S(1)} %get-tuple-element.36.refs_0_, bf16[1040,128]{1,0:T(8,128)(2,1)S(1)} %get-tuple-element.32.refs_3_.refs_1_, bf16[1040,128]{1,0:T(8,128)(2,1)S(1)} %collective-permute-done.11.refs_2_.refs_0_, ...), custom_call_target="tpu_custom_call" | custom-call | flops 356515840 | bytes 655360 | tf_op jit(solution)/shard_map/grad_other_near/pallas_call | solution.py:461
  47.8 1.3 %grad_own_near.1 = (f32[256,640]{1,0:T(8,128)S(1)}, bf16[256,1024]{1,0:T(8,128)(2,1)}) custom-call(bf16[256,1088]{1,0:T(8,128)(2,1)S(1)} %get-tuple-element.33.refs_0_, bf16[1040,128]{1,0:T(8,128)(2,1)S(1)} %get-tuple-element.32.refs_3_.refs_1_, bf16[1040,128]{1,0:T(8,128)(2,1)S(1)} %collective-permute-done.11.refs_2_.refs_0_, ...), custom_call_target="tpu_custom_call" | custom-call | flops 356515840 | bytes 2359296 | tf_op jit(solution)/shard_map/grad_own_near/pallas_call | solution.py:474
  49.1 0.6 %collective-permute-done.17.refs_2_.refs_5_ = bf16[1040,128]{1,0:T(8,128)(2,1)S(1)} collective-permute-done((bf16[1040,128]{1,0:T(8,128)(2,1)S(1)}, bf16[1040,128]{1,0:T(8,128)(2,1)S(1)}, u32[]{:S(2)}, u32[]{:S(2)}) %collective-permute-start.17) | collective-permute-done | bytes 266272 | tf_op jit(solution)/shard_map/ppermute | solution.py:355
  49.7 0.5 grad_other_far.1
  50.2 0.7 %collective-permute-start.19 = (bf16[256,384]{1,0:T(8,128)(2,1)S(1)}, bf16[256,384]{1,0:T(8,128)(2,1)S(1)}, u32[]{:S(2)}, u32[]{:S(2)}) collective-permute-start(bf16[256,384]{1,0:T(8,128)(2,1)S(1)} %grad_other_far.1), channel_id=1, source_target_pairs={{0,4},{4,0},{8,12},{12,8},{16,20},{20,16},{24,28},{28,24},{1,5},{5... | collective-permute-start | bytes 589832 | tf_op jit(solution)/shard_map/ppermute | solution.py:355
  50.9 0.5 grad_own_far.1.refs_2_
  51.3 0.9 %near.1.refs_8_ = f32[256,1024]{1,0:T(8,128)} custom-call(f32[256,640]{1,0:T(8,128)S(1)} %get-tuple-element.35.refs_4_.refs_0_, bf16[256,640]{1,0:T(8,128)(2,1)S(1)} %collective-permute-done.15.refs_1_), custom_call_target="tpu_custom_call" | custom-call | bytes 2097152 | tf_op jit(solution)/shard_map/near/pallas_call | solution.py:485
  52.2 0.9 %last.1 = (bf16[256,1024]{1,0:T(8,128)(2,1)}, f32[256,1024]{1,0:T(8,128)}) custom-call(f32[256,640]{1,0:T(8,128)S(1)} %get-tuple-element.35.refs_4_.refs_0_, bf16[256,640]{1,0:T(8,128)(2,1)S(1)} %collective-permute-done.15.refs_1_, f32[256,384]{1,0:T(8,128)S(1)} %grad_own_far.1.refs_2_, ...), custom_call_target="tpu_custom_call", output_to_operand_aliasing={{0}: (7, {}), {1}: (8, {})} | custom-call | bytes 3145728 | tf_op jit(solution)/shard_map/last/pallas_call | solution.py:494
  (29 shorter events, 0.9 us)
Async XLA Ops:
  2.5 14.1 %copy-start = (bf16[272,2048]{1,0:T(8,128)(2,1)S(1)}, bf16[272,2048]{1,0:T(8,128)(2,1)}, u32[]{:S(2)}) copy-start(bf16[272,2048]{1,0:T(8,128)(2,1)} %refs_1_.4) | copy-start | bytes 3342340
  2.5 14.1 %copy-start.1 = (s32[1,8]{1,0:T(1,128)S(1)}, s32[1,8]{1,0:T(1,128)}, u32[]{:S(2)}) copy-start(s32[1,8]{1,0:T(1,128)} %refs_0_.5) | copy-start | bytes 100
  2.5 10.0 %collective-permute-start = (bf16[784,128]{1,0:T(8,128)(2,1)}, bf16[784,128]{1,0:T(8,128)(2,1)S(1)}, u32[]{:S(2)}, u32[]{:S(2)}) collective-permute-start(bf16[784,128]{1,0:T(8,128)(2,1)} %get-tuple-element.20), channel_id=1, source_target_pairs={{0,24},{4,28},{8,16},{12,20},{16,8},{20,12},{24,0},{28,4},{1,25},{... | collective-permute-start | bytes 602120 | tf_op jit(solution)/shard_map/ppermute | solution.py:355
  6.5 10.1 %collective-permute-start.1 = (bf16[784,128]{1,0:T(8,128)(2,1)}, bf16[784,128]{1,0:T(8,128)(2,1)S(1)}, u32[]{:S(2)}, u32[]{:S(2)}) collective-permute-start(bf16[784,128]{1,0:T(8,128)(2,1)} %get-tuple-element.21), channel_id=1, source_target_pairs={{0,28},{4,24},{8,20},{12,16},{16,12},{20,8},{24,4},{28,0},{1,29},{... | collective-permute-start | bytes 602120 | tf_op jit(solution)/shard_map/ppermute | solution.py:355
  9.1 16.2 %copy-start.2 = (bf16[784,128]{1,0:T(8,128)(2,1)S(1)}, bf16[784,128]{1,0:T(8,128)(2,1)}, u32[]{:S(2)}) copy-start(bf16[784,128]{1,0:T(8,128)(2,1)} %get-tuple-element.26.refs_1_) | copy-start | bytes 602116
  9.1 16.2 %copy-start.3 = (s32[8]{0:T(128)S(1)}, s32[8]{0:T(128)}, u32[]{:S(2)}) copy-start(s32[8]{0:T(128)} %refs_0_.7) | copy-start | bytes 100
  9.1 12.6 %collective-permute-start.5 = (bf16[784,128]{1,0:T(8,128)(2,1)}, bf16[784,128]{1,0:T(8,128)(2,1)S(1)}, u32[]{:S(2)}, u32[]{:S(2)}) collective-permute-start(bf16[784,128]{1,0:T(8,128)(2,1)} %get-tuple-element.27), channel_id=1, source_target_pairs={{0,8},{4,12},{8,0},{12,4},{16,24},{20,28},{24,16},{28,20},{1,9},{5... | collective-permute-start | bytes 602120 | tf_op jit(solution)/shard_map/ppermute | solution.py:355
  10.3 12.9 %collective-permute-start.6 = (bf16[784,128]{1,0:T(8,128)(2,1)}, bf16[784,128]{1,0:T(8,128)(2,1)S(1)}, u32[]{:S(2)}, u32[]{:S(2)}) collective-permute-start(bf16[784,128]{1,0:T(8,128)(2,1)} %get-tuple-element.28), channel_id=1, source_target_pairs={{0,16},{4,20},{8,24},{12,28},{16,0},{20,4},{24,8},{28,12},{1,17},{... | collective-permute-start | bytes 602120 | tf_op jit(solution)/shard_map/ppermute | solution.py:355
  11.8 12.9 %collective-permute-start.7 = (bf16[784,128]{1,0:T(8,128)(2,1)}, bf16[784,128]{1,0:T(8,128)(2,1)S(1)}, u32[]{:S(2)}, u32[]{:S(2)}) collective-permute-start(bf16[784,128]{1,0:T(8,128)(2,1)} %get-tuple-element.29), channel_id=1, source_target_pairs={{0,12},{4,8},{8,4},{12,0},{16,28},{20,24},{24,20},{28,16},{1,13},{... | collective-permute-start | bytes 602120 | tf_op jit(solution)/shard_map/ppermute | solution.py:355
  12.5 12.7 %collective-permute-start.8 = (bf16[784,128]{1,0:T(8,128)(2,1)}, bf16[784,128]{1,0:T(8,128)(2,1)S(1)}, u32[]{:S(2)}, u32[]{:S(2)}) collective-permute-start(bf16[784,128]{1,0:T(8,128)(2,1)} %get-tuple-element.30), channel_id=1, source_target_pairs={{0,20},{4,16},{8,28},{12,24},{16,4},{20,0},{24,12},{28,8},{1,21},{... | collective-permute-start | bytes 602120 | tf_op jit(solution)/shard_map/ppermute | solution.py:355
  16.5 8.7 %collective-permute-start.9 = (bf16[784,128]{1,0:T(8,128)(2,1)}, bf16[784,128]{1,0:T(8,128)(2,1)S(1)}, u32[]{:S(2)}, u32[]{:S(2)}) collective-permute-start(bf16[784,128]{1,0:T(8,128)(2,1)} %get-tuple-element.31), channel_id=1, source_target_pairs={{0,4},{4,0},{8,12},{12,8},{16,20},{20,16},{24,28},{28,24},{1,5},{5... | collective-permute-start | bytes 602120 | tf_op jit(solution)/shard_map/ppermute | solution.py:355
  21.7 11.1 %collective-permute-start.3 = (bf16[640,128]{1,0:T(8,128)(2,1)S(1)}, bf16[640,128]{1,0:T(8,128)(2,1)S(1)}, u32[]{:S(2)}, u32[]{:S(2)}) collective-permute-start(bf16[640,128]{1,0:T(8,128)(2,1)S(1)} %get-tuple-element.24), channel_id=1, source_target_pairs={{0,8},{4,20},{8,0},{12,28},{16,24},{20,4},{24,16},{28,12},{1,9},{5... | collective-permute-start | bytes 491528 | tf_op jit(solution)/shard_map/ppermute | solution.py:355
  23.2 8.6 %collective-permute-start.2 = (bf16[576,128]{1,0:T(8,128)(2,1)S(1)}, bf16[576,128]{1,0:T(8,128)(2,1)S(1)}, u32[]{:S(2)}, u32[]{:S(2)}) collective-permute-start(bf16[576,128]{1,0:T(8,128)(2,1)S(1)} %get-tuple-element.23), channel_id=1, source_target_pairs={{0,24},{4,28},{8,16},{12,20},{16,8},{20,12},{24,0},{28,4},{1,25},{... | collective-permute-start | bytes 442376 | tf_op jit(solution)/shard_map/ppermute | solution.py:355
  24.7 7.2 %collective-permute-start.4 = (bf16[576,128]{1,0:T(8,128)(2,1)S(1)}, bf16[576,128]{1,0:T(8,128)(2,1)S(1)}, u32[]{:S(2)}, u32[]{:S(2)}) collective-permute-start(bf16[576,128]{1,0:T(8,128)(2,1)S(1)} %get-tuple-element.25), channel_id=1, source_target_pairs={{0,16},{4,12},{8,24},{12,4},{16,0},{20,28},{24,8},{28,20},{1,17},{... | collective-permute-start | bytes 442376 | tf_op jit(solution)/shard_map/ppermute | solution.py:355
  28.7 6.7 %collective-permute-start.14 = (bf16[1040,128]{1,0:T(8,128)(2,1)S(1)}, bf16[1040,128]{1,0:T(8,128)(2,1)S(1)}, u32[]{:S(2)}, u32[]{:S(2)}) collective-permute-start(bf16[1040,128]{1,0:T(8,128)(2,1)S(1)} %get-tuple-element.34.x_ref), channel_id=1, source_target_pairs={{0,12},{4,16},{8,4},{12,24},{16,28},{20,0},{24,20},{28,8},{1,13},{... | collective-permute-start | bytes 798728 | tf_op jit(solution)/shard_map/ppermute | solution.py:355
  30.4 12.9 %collective-permute-start.13 = (bf16[1040,128]{1,0:T(8,128)(2,1)S(1)}, bf16[1040,128]{1,0:T(8,128)(2,1)S(1)}, u32[]{:S(2)}, u32[]{:S(2)}) collective-permute-start(bf16[1040,128]{1,0:T(8,128)(2,1)S(1)} %get-tuple-element.32.refs_3_.refs_1_), channel_id=1, source_target_pairs={{0,8},{4,20},{8,0},{12,28},{16,24},{20,4},{24,16},{28,12},{1,9},{5... | collective-permute-start | bytes 798728 | tf_op jit(solution)/shard_map/ppermute | solution.py:355
  31.8 12.1 %collective-permute-start.11 = (bf16[1040,128]{1,0:T(8,128)(2,1)S(1)}, bf16[1040,128]{1,0:T(8,128)(2,1)S(1)}, u32[]{:S(2)}, u32[]{:S(2)}) collective-permute-start(bf16[1040,128]{1,0:T(8,128)(2,1)S(1)} %get-tuple-element.34.x_ref), channel_id=1, source_target_pairs={{0,20},{4,8},{8,28},{12,0},{16,4},{20,24},{24,12},{28,16},{1,21},{... | collective-permute-start | bytes 798728 | tf_op jit(solution)/shard_map/ppermute | solution.py:355
  31.9 13.9 %collective-permute-start.12 = (bf16[1040,128]{1,0:T(8,128)(2,1)S(1)}, bf16[1040,128]{1,0:T(8,128)(2,1)S(1)}, u32[]{:S(2)}, u32[]{:S(2)}) collective-permute-start(bf16[1040,128]{1,0:T(8,128)(2,1)S(1)} %get-tuple-element.32.refs_3_.refs_1_), channel_id=1, source_target_pairs={{0,16},{4,12},{8,24},{12,4},{16,0},{20,28},{24,8},{28,20},{1,17},{... | collective-permute-start | bytes 798728 | tf_op jit(solution)/shard_map/ppermute | solution.py:355
  32.8 13.7 %collective-permute-start.10 = (bf16[1472,128]{1,0:T(8,128)(2,1)S(1)}, bf16[1472,128]{1,0:T(8,128)(2,1)S(1)}, u32[]{:S(2)}, u32[]{:S(2)}) collective-permute-start(bf16[1472,128]{1,0:T(8,128)(2,1)S(1)} %stack.1), channel_id=1, source_target_pairs={{0,1},{1,0},{2,3},{3,2},{4,5},{5,4},{6,7},{7,6},{8,9},{9,8},{10,11... | collective-permute-start | bytes 1130504 | tf_op jit(solution)/shard_map/ppermute | solution.py:361
  35.5 13.6 %collective-permute-start.18 = (bf16[1040,128]{1,0:T(8,128)(2,1)S(1)}, bf16[1040,128]{1,0:T(8,128)(2,1)S(1)}, u32[]{:S(2)}, u32[]{:S(2)}) collective-permute-start(bf16[1040,128]{1,0:T(8,128)(2,1)S(1)} %collective-permute-done.14.refs_5_), channel_id=1, source_target_pairs={{0,8},{4,20},{8,0},{12,28},{16,24},{20,4},{24,16},{28,12},{1,9},{5... | collective-permute-start | bytes 798728 | tf_op jit(solution)/shard_map/ppermute | solution.py:355
  43.3 6.4 %collective-permute-start.17 = (bf16[1040,128]{1,0:T(8,128)(2,1)S(1)}, bf16[1040,128]{1,0:T(8,128)(2,1)S(1)}, u32[]{:S(2)}, u32[]{:S(2)}) collective-permute-start(bf16[1040,128]{1,0:T(8,128)(2,1)S(1)} %collective-permute-done.13.refs_4_), channel_id=1, source_target_pairs={{0,16},{4,12},{8,24},{12,4},{16,0},{20,28},{24,8},{28,20},{1,17},{... | collective-permute-start | bytes 798728 | tf_op jit(solution)/shard_map/ppermute | solution.py:355
  45.8 3.9 %collective-permute-start.16 = (bf16[1040,128]{1,0:T(8,128)(2,1)S(1)}, bf16[1040,128]{1,0:T(8,128)(2,1)S(1)}, u32[]{:S(2)}, u32[]{:S(2)}) collective-permute-start(bf16[1040,128]{1,0:T(8,128)(2,1)S(1)} %late.1), channel_id=1, source_target_pairs={{0,4},{4,0},{8,12},{12,8},{16,20},{20,16},{24,28},{28,24},{1,5},{5... | collective-permute-start | bytes 798728 | tf_op jit(solution)/shard_map/ppermute | solution.py:355
  47.7 3.6 %collective-permute-start.15 = (bf16[256,640]{1,0:T(8,128)(2,1)S(1)}, bf16[256,640]{1,0:T(8,128)(2,1)S(1)}, u32[]{:S(2)}, u32[]{:S(2)}) collective-permute-start(bf16[256,640]{1,0:T(8,128)(2,1)S(1)} %grad_other_near.1), channel_id=1, source_target_pairs={{0,4},{4,0},{8,12},{12,8},{16,20},{20,16},{24,28},{28,24},{1,5},{5... | collective-permute-start | bytes 983048 | tf_op jit(solution)/shard_map/ppermute | solution.py:355
  50.2 2.0 %collective-permute-start.19 = (bf16[256,384]{1,0:T(8,128)(2,1)S(1)}, bf16[256,384]{1,0:T(8,128)(2,1)S(1)}, u32[]{:S(2)}, u32[]{:S(2)}) collective-permute-start(bf16[256,384]{1,0:T(8,128)(2,1)S(1)} %grad_other_far.1), channel_id=1, source_target_pairs={{0,4},{4,0},{8,12},{12,8},{16,20},{20,16},{24,28},{28,24},{1,5},{5... | collective-permute-start | bytes 589832 | tf_op jit(solution)/shard_map/ppermute | solution.py:355

commit v18 on v16

--- a/solution.py
+++ b/solution.py
@@ -442,8 +442,8 @@
     first_same, first_cross = swap(same, 2, 4), swap(cross, 3, 5)
     second_same, second_cross = swap(same, 4, 2), swap(cross, 5, 3)
     far_same, far_cross = swap(first_same, 4, 2), swap(first_cross, 2, 4)
-    (late_cross,) = call(late_kernel, "late", [head_shape], [vmem] + [hbm] * 2, 0)(
-        cross, second_cross, second_same
+    (late_cross,) = call(late_kernel, "late", [head_shape], [vmem, hbm], 0)(
+        cross, second_same
     )
     c_cross = swap(late_cross, 1)
 

time: 53.3 us -> 54.3 us (1.019)
  waiting for transfers between devices: 19 us -> 20.5 us
  starting transfers between devices: 19.3 us -> 18.7 us
    ppermute x19, waiting for transfers between devices: 19 us -> 20.5 us  [swap(): return lax.ppermute(x, 'tm', [(i, i ^ bits[i % 2]) for i in range(n)])]
    ppermute x19, starting transfers between devices: 17.7 us -> 17 us  [swap(): return lax.ppermute(x, 'tm', [(i, i ^ bits[i % 2]) for i in range(n)])]
  transfers between devices with their start and end apart: 20 -> 20, of which waited for: 8 -> 9; matrix products, arithmetic and copies ran while one was open for 0% -> 0% of each run, Pallas kernels for 21% -> 21%
where the time goes in v18:
time: 54.3 us; the launch traced here: 54.1 us
  waiting for transfers between devices  20.5 us (38%)
  starting transfers between devices  18.7 us (34%)
  Pallas kernels  14.1 us (26%)
  between operations  0.81 us (1%)
    ppermute x19, waiting for transfers between devices, swap(): return lax.ppermute(x, 'tm', [(i, i ^ bits[i % 2]) for i in range(n)])  20.5 us
    ppermute x19, starting transfers between devices, swap(): return lax.ppermute(x, 'tm', [(i, i ^ bits[i % 2]) for i in range(n)])  17 us
    pallas_call x2, Pallas kernels, pack(): call(lambda *refs: pack_kernel(n, heads, *refs), name, [((length, HD), bf...  4.42 us
    pallas_call x1, Pallas kernels, head_body(): call(lambda *refs: attend_kernel(n, tok, [0] + order, *refs), 'attend', [...  3.48 us
    ppermute x1, starting transfers between devices, swap_plane(): return lax.ppermute(x, ('tm', 'head'), pairs)  1.64 us
    pallas_call x3, Pallas kernels, grad(): call(lambda *refs: grad_kernel(rows, half, len(heads), *refs), name, [((c...  1.59 us
    pallas_call x1, Pallas kernels, head_body(): call(lambda *refs: own_near_kernel(rows, half, tok, *refs), 'grad_own_nea...  1.29 us
  transfers between devices with their start and end apart: 20, of which 9 were waited for; matrix products, arithmetic and copies ran while one was open for 0% of the time, Pallas kernels for 21%

profile of v18, /device:TPU:0, one launch (start us, length us, event | category | flops | bytes accessed | tf_op | source)
XLA Modules:
  0.0 54.1 jit_solution(3396311712539786104)
XLA Ops:
  0.6 1.9 %pack_first.1 = (bf16[784,128]{1,0:T(8,128)(2,1)}, bf16[784,128]{1,0:T(8,128)(2,1)}) custom-call(bf16[256,1024]{1,0:T(8,128)(2,1)} %refs_0_.6, bf16[256,1024]{1,0:T(8,128)(2,1)} %refs_1_.5, bf16[256,1024]{1,0:T(8,128)(2,1)} %refs_2_.3, bf16[2,1024]{1,0:T(2,128)(2,1)} %refs_3_.3), custom_call_target="tpu_custom_call" | custom-call | bytes 802816 | tf_op jit(solution)/shard_map/pack_first/pallas_call | solution.py:380
  2.5 4.0 %collective-permute-start = (bf16[784,128]{1,0:T(8,128)(2,1)}, bf16[784,128]{1,0:T(8,128)(2,1)S(1)}, u32[]{:S(2)}, u32[]{:S(2)}) collective-permute-start(bf16[784,128]{1,0:T(8,128)(2,1)} %get-tuple-element.20), channel_id=1, source_target_pairs={{0,24},{4,28},{8,16},{12,20},{16,8},{20,12},{24,0},{28,4},{1,25},{... | collective-permute-start | bytes 602120 | tf_op jit(solution)/shard_map/ppermute | solution.py:354
  6.5 2.6 %pack_rest.1 = (bf16[784,128]{1,0:T(8,128)(2,1)}, bf16[784,128]{1,0:T(8,128)(2,1)}, bf16[784,128]{1,0:T(8,128)(2,1)}, bf16[784,128]{1,0:T(8,128)(2,1)}, bf16[784...) custom-call(bf16[256,1024]{1,0:T(8,128)(2,1)} %refs_0_.6, bf16[256,1024]{1,0:T(8,128)(2,1)} %refs_1_.5, ...), custom_call_target="tpu_custom_call" | custom-call | bytes 2408448 | tf_op jit(solution)/shard_map/pack_rest/pallas_call | solution.py:380
  9.1 1.2 %collective-permute-start.5 = (bf16[784,128]{1,0:T(8,128)(2,1)}, bf16[784,128]{1,0:T(8,128)(2,1)S(1)}, u32[]{:S(2)}, u32[]{:S(2)}) collective-permute-start(bf16[784,128]{1,0:T(8,128)(2,1)} %get-tuple-element.27), channel_id=1, source_target_pairs={{0,8},{4,12},{8,0},{12,4},{16,24},{20,28},{24,16},{28,20},{1,9},{5... | collective-permute-start | bytes 602120 | tf_op jit(solution)/shard_map/ppermute | solution.py:354
  10.3 1.5 %collective-permute-start.6 = (bf16[784,128]{1,0:T(8,128)(2,1)}, bf16[784,128]{1,0:T(8,128)(2,1)S(1)}, u32[]{:S(2)}, u32[]{:S(2)}) collective-permute-start(bf16[784,128]{1,0:T(8,128)(2,1)} %get-tuple-element.28), channel_id=1, source_target_pairs={{0,16},{4,20},{8,24},{12,28},{16,0},{20,4},{24,8},{28,12},{1,17},{... | collective-permute-start | bytes 602120 | tf_op jit(solution)/shard_map/ppermute | solution.py:354
  11.8 0.6 %collective-permute-start.7 = (bf16[784,128]{1,0:T(8,128)(2,1)}, bf16[784,128]{1,0:T(8,128)(2,1)S(1)}, u32[]{:S(2)}, u32[]{:S(2)}) collective-permute-start(bf16[784,128]{1,0:T(8,128)(2,1)} %get-tuple-element.29), channel_id=1, source_target_pairs={{0,12},{4,8},{8,4},{12,0},{16,28},{20,24},{24,20},{28,16},{1,13},{... | collective-permute-start | bytes 602120 | tf_op jit(solution)/shard_map/ppermute | solution.py:354
  12.5 0.4 collective-permute-start.8
  12.9 3.6 %collective-permute-done.1.refs_3_ = bf16[784,128]{1,0:T(8,128)(2,1)S(1)} collective-permute-done((bf16[784,128]{1,0:T(8,128)(2,1)}, bf16[784,128]{1,0:T(8,128)(2,1)S(1)}, u32[]{:S(2)}, u32[]{:S(2)}) %collective-permute-start.1) | collective-permute-done | bytes 200736 | tf_op jit(solution)/shard_map/ppermute | solution.py:354
  16.6 0.9 %cot.1 = (bf16[1088,128]{1,0:T(8,128)(2,1)S(1)}, bf16[640,128]{1,0:T(8,128)(2,1)S(1)}, bf16[576,128]{1,0:T(8,128)(2,1)S(1)}, bf16[576,128]{1,0:T(8,128)(2,1)S(1)}) custom-call(s32[1,8]{1,0:T(1,128)S(1)} %copy-done.1, bf16[272,2048]{1,0:T(8,128)(2,1)S(1)} %copy-done, bf16[784,128]{1,0:T(8,128)(2,1)S(1)} %collective-permute-done.refs_2_, ...), custom_call_target="tpu_custom_call" | custom-call | bytes 1474560 | tf_op jit(solution)/shard_map/cot/pallas_call | solution.py:403
  17.6 4.1 %collective-permute-done.5.refs_4_ = bf16[784,128]{1,0:T(8,128)(2,1)S(1)} collective-permute-done((bf16[784,128]{1,0:T(8,128)(2,1)}, bf16[784,128]{1,0:T(8,128)(2,1)S(1)}, u32[]{:S(2)}, u32[]{:S(2)}) %collective-permute-start.5) | collective-permute-done | bytes 200736 | tf_op jit(solution)/shard_map/ppermute | solution.py:354
  21.7 1.5 %collective-permute-start.3 = (bf16[640,128]{1,0:T(8,128)(2,1)S(1)}, bf16[640,128]{1,0:T(8,128)(2,1)S(1)}, u32[]{:S(2)}, u32[]{:S(2)}) collective-permute-start(bf16[640,128]{1,0:T(8,128)(2,1)S(1)} %get-tuple-element.24), channel_id=1, source_target_pairs={{0,8},{4,20},{8,0},{12,28},{16,24},{20,4},{24,16},{28,12},{1,9},{5... | collective-permute-start | bytes 491528 | tf_op jit(solution)/shard_map/ppermute | solution.py:354
  23.2 1.5 %collective-permute-done.7.refs_6_ = bf16[784,128]{1,0:T(8,128)(2,1)S(1)} collective-permute-done((bf16[784,128]{1,0:T(8,128)(2,1)}, bf16[784,128]{1,0:T(8,128)(2,1)S(1)}, u32[]{:S(2)}, u32[]{:S(2)}) %collective-permute-start.7) | collective-permute-done | bytes 200736 | tf_op jit(solution)/shard_map/ppermute | solution.py:354
  24.7 0.6 %collective-permute-start.4 = (bf16[576,128]{1,0:T(8,128)(2,1)S(1)}, bf16[576,128]{1,0:T(8,128)(2,1)S(1)}, u32[]{:S(2)}, u32[]{:S(2)}) collective-permute-start(bf16[576,128]{1,0:T(8,128)(2,1)S(1)} %get-tuple-element.25), channel_id=1, source_target_pairs={{0,16},{4,12},{8,24},{12,4},{16,0},{20,28},{24,8},{28,20},{1,17},{... | collective-permute-start | bytes 442376 | tf_op jit(solution)/shard_map/ppermute | solution.py:354
  25.3 3.5 %attend.1 = (bf16[1040,128]{1,0:T(8,128)(2,1)S(1)}, bf16[1040,128]{1,0:T(8,128)(2,1)S(1)}) custom-call(s32[8]{0:T(128)S(1)} %copy-done.3, bf16[784,128]{1,0:T(8,128)(2,1)S(1)} %copy-done.2, bf16[784,128]{1,0:T(8,128)(2,1)S(1)} %collective-permute-done.refs_2_, bf16[784,128]{1,0:T(8,128)(2,1)S(1)} %collective-permute-done.1.refs_3_, ...), custom_call_target="tpu_custom_call" | custom-call | flops 1073741824 | bytes 1064960 | tf_op jit(solution)/shard_map/attend/pallas_call | solution.py:424
  28.7 1.7 %collective-permute-start.14 = (bf16[1040,128]{1,0:T(8,128)(2,1)S(1)}, bf16[1040,128]{1,0:T(8,128)(2,1)S(1)}, u32[]{:S(2)}, u32[]{:S(2)}) collective-permute-start(bf16[1040,128]{1,0:T(8,128)(2,1)S(1)} %get-tuple-element.34.x_ref), channel_id=1, source_target_pairs={{0,12},{4,16},{8,4},{12,24},{16,28},{20,0},{24,20},{28,8},{1,13},{... | collective-permute-start | bytes 798728 | tf_op jit(solution)/shard_map/ppermute | solution.py:354
  30.4 1.5 %collective-permute-start.13 = (bf16[1040,128]{1,0:T(8,128)(2,1)S(1)}, bf16[1040,128]{1,0:T(8,128)(2,1)S(1)}, u32[]{:S(2)}, u32[]{:S(2)}) collective-permute-start(bf16[1040,128]{1,0:T(8,128)(2,1)S(1)} %get-tuple-element.32.refs_3_.refs_1_), channel_id=1, source_target_pairs={{0,8},{4,20},{8,0},{12,28},{16,24},{20,4},{24,16},{28,12},{1,9},{5... | collective-permute-start | bytes 798728 | tf_op jit(solution)/shard_map/ppermute | solution.py:354
  31.9 0.9 %collective-permute-start.12 = (bf16[1040,128]{1,0:T(8,128)(2,1)S(1)}, bf16[1040,128]{1,0:T(8,128)(2,1)S(1)}, u32[]{:S(2)}, u32[]{:S(2)}) collective-permute-start(bf16[1040,128]{1,0:T(8,128)(2,1)S(1)} %get-tuple-element.32.refs_3_.refs_1_), channel_id=1, source_target_pairs={{0,16},{4,12},{8,24},{12,4},{16,0},{20,28},{24,8},{28,20},{1,17},{... | collective-permute-start | bytes 798728 | tf_op jit(solution)/shard_map/ppermute | solution.py:354
  32.8 1.6 %collective-permute-start.10 = (bf16[1472,128]{1,0:T(8,128)(2,1)S(1)}, bf16[1472,128]{1,0:T(8,128)(2,1)S(1)}, u32[]{:S(2)}, u32[]{:S(2)}) collective-permute-start(bf16[1472,128]{1,0:T(8,128)(2,1)S(1)} %stack.1), channel_id=1, source_target_pairs={{0,1},{1,0},{2,3},{3,2},{4,5},{5,4},{6,7},{7,6},{8,9},{9,8},{10,11... | collective-permute-start | bytes 1130504 | tf_op jit(solution)/shard_map/ppermute | solution.py:360
  34.5 1.8 %collective-permute-done.14.refs_5_ = bf16[1040,128]{1,0:T(8,128)(2,1)S(1)} collective-permute-done((bf16[1040,128]{1,0:T(8,128)(2,1)S(1)}, bf16[1040,128]{1,0:T(8,128)(2,1)S(1)}, u32[]{:S(2)}, u32[]{:S(2)}) %collective-permute-start.14) | collective-permute-done | bytes 266272 | tf_op jit(solution)/shard_map/ppermute | solution.py:354
  36.4 2.2 %collective-permute-start.18 = (bf16[1040,128]{1,0:T(8,128)(2,1)S(1)}, bf16[1040,128]{1,0:T(8,128)(2,1)S(1)}, u32[]{:S(2)}, u32[]{:S(2)}) collective-permute-start(bf16[1040,128]{1,0:T(8,128)(2,1)S(1)} %collective-permute-done.14.refs_5_), channel_id=1, source_target_pairs={{0,8},{4,20},{8,0},{12,28},{16,24},{20,4},{24,16},{28,12},{1,9},{5... | collective-permute-start | bytes 798728 | tf_op jit(solution)/shard_map/ppermute | solution.py:354
  38.6 6.2 %collective-permute-done.13.refs_4_ = bf16[1040,128]{1,0:T(8,128)(2,1)S(1)} collective-permute-done((bf16[1040,128]{1,0:T(8,128)(2,1)S(1)}, bf16[1040,128]{1,0:T(8,128)(2,1)S(1)}, u32[]{:S(2)}, u32[]{:S(2)}) %collective-permute-start.13) | collective-permute-done | bytes 266272 | tf_op jit(solution)/shard_map/ppermute | solution.py:354
  44.7 0.2 collective-permute-start.17
  45.1 0.6 %turn.1 = (bf16[256,1088]{1,0:T(8,128)(2,1)S(1)}, bf16[256,1088]{1,0:T(8,128)(2,1)S(1)}) custom-call(bf16[1088,128]{1,0:T(8,128)(2,1)S(1)} %get-tuple-element.22.refs_0_, bf16[576,128]{1,0:T(8,128)(2,1)S(1)} %collective-permute-done.2.refs_0_.refs_1_, bf16[640,128]{1,0:T(8,128)(2,1)S(1)} %collective-permute-done.3.refs_1_.refs_2_, ...), custom_call_target="tpu_custom_call" | custom-call | bytes 2228224 | tf_op jit(solution)/shard_map/turn/pallas_call | solution.py:450
  45.6 0.6 %grad_other_near.1 = bf16[256,640]{1,0:T(8,128)(2,1)S(1)} custom-call(bf16[256,1088]{1,0:T(8,128)(2,1)S(1)} %get-tuple-element.36.refs_0_, bf16[1040,128]{1,0:T(8,128)(2,1)S(1)} %get-tuple-element.32.refs_3_.refs_1_, bf16[1040,128]{1,0:T(8,128)(2,1)S(1)} %collective-permute-done.11.refs_2_, bf16[1040,128]{1,0:T(8,128)(2,1)S(1)} %collective-permute-done.12.refs_3_.refs_0_, ...), custom_call_target="tpu_custom_call" | custom-call | flops 356515840 | bytes 655360 | tf_op jit(solution)/shard_map/grad_other_near/pallas_call | solution.py:460
  46.3 0.5 %collective-permute-start.15 = (bf16[256,640]{1,0:T(8,128)(2,1)S(1)}, bf16[256,640]{1,0:T(8,128)(2,1)S(1)}, u32[]{:S(2)}, u32[]{:S(2)}) collective-permute-start(bf16[256,640]{1,0:T(8,128)(2,1)S(1)} %grad_other_near.1), channel_id=1, source_target_pairs={{0,4},{4,0},{8,12},{12,8},{16,20},{20,16},{24,28},{28,24},{1,5},{5... | collective-permute-start | bytes 983048 | tf_op jit(solution)/shard_map/ppermute | solution.py:354
  46.8 1.3 %grad_own_near.1 = (f32[256,640]{1,0:T(8,128)S(1)}, bf16[256,1024]{1,0:T(8,128)(2,1)}) custom-call(bf16[256,1088]{1,0:T(8,128)(2,1)S(1)} %get-tuple-element.33.refs_0_, bf16[1040,128]{1,0:T(8,128)(2,1)S(1)} %get-tuple-element.32.refs_3_.refs_1_, bf16[1040,128]{1,0:T(8,128)(2,1)S(1)} %collective-permute-done.11.refs_2_, ...), custom_call_target="tpu_custom_call" | custom-call | flops 356515840 | bytes 2359296 | tf_op jit(solution)/shard_map/grad_own_near/pallas_call | solution.py:473
  48.1 2.3 %collective-permute-done.18.refs_3_.refs_6_ = bf16[1040,128]{1,0:T(8,128)(2,1)S(1)} collective-permute-done((bf16[1040,128]{1,0:T(8,128)(2,1)S(1)}, bf16[1040,128]{1,0:T(8,128)(2,1)S(1)}, u32[]{:S(2)}, u32[]{:S(2)}) %collective-permute-start.18) | collective-permute-done | bytes 266272 | tf_op jit(solution)/shard_map/ppermute | solution.py:354
  50.4 0.7 %collective-permute-done.17.refs_2_.refs_5_ = bf16[1040,128]{1,0:T(8,128)(2,1)S(1)} collective-permute-done((bf16[1040,128]{1,0:T(8,128)(2,1)S(1)}, bf16[1040,128]{1,0:T(8,128)(2,1)S(1)}, u32[]{:S(2)}, u32[]{:S(2)}) %collective-permute-start.17) | collective-permute-done | bytes 266272 | tf_op jit(solution)/shard_map/ppermute | solution.py:354
  51.1 0.5 grad_other_far.1
  51.7 0.5 grad_own_far.1.refs_2_
  52.2 0.9 %near.1.refs_8_ = f32[256,1024]{1,0:T(8,128)} custom-call(f32[256,640]{1,0:T(8,128)S(1)} %get-tuple-element.35.refs_4_.refs_0_, bf16[256,640]{1,0:T(8,128)(2,1)S(1)} %collective-permute-done.15.refs_1_), custom_call_target="tpu_custom_call" | custom-call | bytes 2097152 | tf_op jit(solution)/shard_map/near/pallas_call | solution.py:484
  53.1 0.9 %last.1 = (bf16[256,1024]{1,0:T(8,128)(2,1)}, f32[256,1024]{1,0:T(8,128)}) custom-call(f32[256,640]{1,0:T(8,128)S(1)} %get-tuple-element.35.refs_4_.refs_0_, bf16[256,640]{1,0:T(8,128)(2,1)S(1)} %collective-permute-done.15.refs_1_, f32[256,384]{1,0:T(8,128)S(1)} %grad_own_far.1.refs_2_, ...), custom_call_target="tpu_custom_call", output_to_operand_aliasing={{0}: (7, {}), {1}: (8, {})} | custom-call | bytes 3145728 | tf_op jit(solution)/shard_map/last/pallas_call | solution.py:493
  (29 shorter events, 0.6 us)
Async XLA Ops:
  2.5 14.1 %copy-start = (bf16[272,2048]{1,0:T(8,128)(2,1)S(1)}, bf16[272,2048]{1,0:T(8,128)(2,1)}, u32[]{:S(2)}) copy-start(bf16[272,2048]{1,0:T(8,128)(2,1)} %refs_1_.4) | copy-start | bytes 3342340
  2.5 14.1 %copy-start.1 = (s32[1,8]{1,0:T(1,128)S(1)}, s32[1,8]{1,0:T(1,128)}, u32[]{:S(2)}) copy-start(s32[1,8]{1,0:T(1,128)} %refs_0_.5) | copy-start | bytes 100
  2.5 10.0 %collective-permute-start = (bf16[784,128]{1,0:T(8,128)(2,1)}, bf16[784,128]{1,0:T(8,128)(2,1)S(1)}, u32[]{:S(2)}, u32[]{:S(2)}) collective-permute-start(bf16[784,128]{1,0:T(8,128)(2,1)} %get-tuple-element.20), channel_id=1, source_target_pairs={{0,24},{4,28},{8,16},{12,20},{16,8},{20,12},{24,0},{28,4},{1,25},{... | collective-permute-start | bytes 602120 | tf_op jit(solution)/shard_map/ppermute | solution.py:354
  6.5 10.1 %collective-permute-start.1 = (bf16[784,128]{1,0:T(8,128)(2,1)}, bf16[784,128]{1,0:T(8,128)(2,1)S(1)}, u32[]{:S(2)}, u32[]{:S(2)}) collective-permute-start(bf16[784,128]{1,0:T(8,128)(2,1)} %get-tuple-element.21), channel_id=1, source_target_pairs={{0,28},{4,24},{8,20},{12,16},{16,12},{20,8},{24,4},{28,0},{1,29},{... | collective-permute-start | bytes 602120 | tf_op jit(solution)/shard_map/ppermute | solution.py:354
  9.1 16.2 %copy-start.2 = (bf16[784,128]{1,0:T(8,128)(2,1)S(1)}, bf16[784,128]{1,0:T(8,128)(2,1)}, u32[]{:S(2)}) copy-start(bf16[784,128]{1,0:T(8,128)(2,1)} %get-tuple-element.26.refs_1_) | copy-start | bytes 602116
  9.1 16.2 %copy-start.3 = (s32[8]{0:T(128)S(1)}, s32[8]{0:T(128)}, u32[]{:S(2)}) copy-start(s32[8]{0:T(128)} %refs_0_.7) | copy-start | bytes 100
  9.1 12.6 %collective-permute-start.5 = (bf16[784,128]{1,0:T(8,128)(2,1)}, bf16[784,128]{1,0:T(8,128)(2,1)S(1)}, u32[]{:S(2)}, u32[]{:S(2)}) collective-permute-start(bf16[784,128]{1,0:T(8,128)(2,1)} %get-tuple-element.27), channel_id=1, source_target_pairs={{0,8},{4,12},{8,0},{12,4},{16,24},{20,28},{24,16},{28,20},{1,9},{5... | collective-permute-start | bytes 602120 | tf_op jit(solution)/shard_map/ppermute | solution.py:354
  10.3 12.9 %collective-permute-start.6 = (bf16[784,128]{1,0:T(8,128)(2,1)}, bf16[784,128]{1,0:T(8,128)(2,1)S(1)}, u32[]{:S(2)}, u32[]{:S(2)}) collective-permute-start(bf16[784,128]{1,0:T(8,128)(2,1)} %get-tuple-element.28), channel_id=1, source_target_pairs={{0,16},{4,20},{8,24},{12,28},{16,0},{20,4},{24,8},{28,12},{1,17},{... | collective-permute-start | bytes 602120 | tf_op jit(solution)/shard_map/ppermute | solution.py:354
  11.8 12.9 %collective-permute-start.7 = (bf16[784,128]{1,0:T(8,128)(2,1)}, bf16[784,128]{1,0:T(8,128)(2,1)S(1)}, u32[]{:S(2)}, u32[]{:S(2)}) collective-permute-start(bf16[784,128]{1,0:T(8,128)(2,1)} %get-tuple-element.29), channel_id=1, source_target_pairs={{0,12},{4,8},{8,4},{12,0},{16,28},{20,24},{24,20},{28,16},{1,13},{... | collective-permute-start | bytes 602120 | tf_op jit(solution)/shard_map/ppermute | solution.py:354
  12.5 12.7 %collective-permute-start.8 = (bf16[784,128]{1,0:T(8,128)(2,1)}, bf16[784,128]{1,0:T(8,128)(2,1)S(1)}, u32[]{:S(2)}, u32[]{:S(2)}) collective-permute-start(bf16[784,128]{1,0:T(8,128)(2,1)} %get-tuple-element.30), channel_id=1, source_target_pairs={{0,20},{4,16},{8,28},{12,24},{16,4},{20,0},{24,12},{28,8},{1,21},{... | collective-permute-start | bytes 602120 | tf_op jit(solution)/shard_map/ppermute | solution.py:354
  16.5 8.7 %collective-permute-start.9 = (bf16[784,128]{1,0:T(8,128)(2,1)}, bf16[784,128]{1,0:T(8,128)(2,1)S(1)}, u32[]{:S(2)}, u32[]{:S(2)}) collective-permute-start(bf16[784,128]{1,0:T(8,128)(2,1)} %get-tuple-element.31), channel_id=1, source_target_pairs={{0,4},{4,0},{8,12},{12,8},{16,20},{20,16},{24,28},{28,24},{1,5},{5... | collective-permute-start | bytes 602120 | tf_op jit(solution)/shard_map/ppermute | solution.py:354
  21.7 11.1 %collective-permute-start.3 = (bf16[640,128]{1,0:T(8,128)(2,1)S(1)}, bf16[640,128]{1,0:T(8,128)(2,1)S(1)}, u32[]{:S(2)}, u32[]{:S(2)}) collective-permute-start(bf16[640,128]{1,0:T(8,128)(2,1)S(1)} %get-tuple-element.24), channel_id=1, source_target_pairs={{0,8},{4,20},{8,0},{12,28},{16,24},{20,4},{24,16},{28,12},{1,9},{5... | collective-permute-start | bytes 491528 | tf_op jit(solution)/shard_map/ppermute | solution.py:354
  23.2 8.7 %collective-permute-start.2 = (bf16[576,128]{1,0:T(8,128)(2,1)S(1)}, bf16[576,128]{1,0:T(8,128)(2,1)S(1)}, u32[]{:S(2)}, u32[]{:S(2)}) collective-permute-start(bf16[576,128]{1,0:T(8,128)(2,1)S(1)} %get-tuple-element.23), channel_id=1, source_target_pairs={{0,24},{4,28},{8,16},{12,20},{16,8},{20,12},{24,0},{28,4},{1,25},{... | collective-permute-start | bytes 442376 | tf_op jit(solution)/shard_map/ppermute | solution.py:354
  24.7 8.1 %collective-permute-start.4 = (bf16[576,128]{1,0:T(8,128)(2,1)S(1)}, bf16[576,128]{1,0:T(8,128)(2,1)S(1)}, u32[]{:S(2)}, u32[]{:S(2)}) collective-permute-start(bf16[576,128]{1,0:T(8,128)(2,1)S(1)} %get-tuple-element.25), channel_id=1, source_target_pairs={{0,16},{4,12},{8,24},{12,4},{16,0},{20,28},{24,8},{28,20},{1,17},{... | collective-permute-start | bytes 442376 | tf_op jit(solution)/shard_map/ppermute | solution.py:354
  28.7 7.6 %collective-permute-start.14 = (bf16[1040,128]{1,0:T(8,128)(2,1)S(1)}, bf16[1040,128]{1,0:T(8,128)(2,1)S(1)}, u32[]{:S(2)}, u32[]{:S(2)}) collective-permute-start(bf16[1040,128]{1,0:T(8,128)(2,1)S(1)} %get-tuple-element.34.x_ref), channel_id=1, source_target_pairs={{0,12},{4,16},{8,4},{12,24},{16,28},{20,0},{24,20},{28,8},{1,13},{... | collective-permute-start | bytes 798728 | tf_op jit(solution)/shard_map/ppermute | solution.py:354
  30.4 14.3 %collective-permute-start.13 = (bf16[1040,128]{1,0:T(8,128)(2,1)S(1)}, bf16[1040,128]{1,0:T(8,128)(2,1)S(1)}, u32[]{:S(2)}, u32[]{:S(2)}) collective-permute-start(bf16[1040,128]{1,0:T(8,128)(2,1)S(1)} %get-tuple-element.32.refs_3_.refs_1_), channel_id=1, source_target_pairs={{0,8},{4,20},{8,0},{12,28},{16,24},{20,4},{24,16},{28,12},{1,9},{5... | collective-permute-start | bytes 798728 | tf_op jit(solution)/shard_map/ppermute | solution.py:354
  31.9 13.1 %collective-permute-start.12 = (bf16[1040,128]{1,0:T(8,128)(2,1)S(1)}, bf16[1040,128]{1,0:T(8,128)(2,1)S(1)}, u32[]{:S(2)}, u32[]{:S(2)}) collective-permute-start(bf16[1040,128]{1,0:T(8,128)(2,1)S(1)} %get-tuple-element.32.refs_3_.refs_1_), channel_id=1, source_target_pairs={{0,16},{4,12},{8,24},{12,4},{16,0},{20,28},{24,8},{28,20},{1,17},{... | collective-permute-start | bytes 798728 | tf_op jit(solution)/shard_map/ppermute | solution.py:354
  32.8 12.2 %collective-permute-start.10 = (bf16[1472,128]{1,0:T(8,128)(2,1)S(1)}, bf16[1472,128]{1,0:T(8,128)(2,1)S(1)}, u32[]{:S(2)}, u32[]{:S(2)}) collective-permute-start(bf16[1472,128]{1,0:T(8,128)(2,1)S(1)} %stack.1), channel_id=1, source_target_pairs={{0,1},{1,0},{2,3},{3,2},{4,5},{5,4},{6,7},{7,6},{8,9},{9,8},{10,11... | collective-permute-start | bytes 1130504 | tf_op jit(solution)/shard_map/ppermute | solution.py:360
  34.5 11.2 %collective-permute-start.11 = (bf16[1040,128]{1,0:T(8,128)(2,1)S(1)}, bf16[1040,128]{1,0:T(8,128)(2,1)S(1)}, u32[]{:S(2)}, u32[]{:S(2)}) collective-permute-start(bf16[1040,128]{1,0:T(8,128)(2,1)S(1)} %get-tuple-element.34.x_ref), channel_id=1, source_target_pairs={{0,20},{4,8},{8,28},{12,0},{16,4},{20,24},{24,12},{28,16},{1,21},{... | collective-permute-start | bytes 798728 | tf_op jit(solution)/shard_map/ppermute | solution.py:354
  36.4 14.1 %collective-permute-start.18 = (bf16[1040,128]{1,0:T(8,128)(2,1)S(1)}, bf16[1040,128]{1,0:T(8,128)(2,1)S(1)}, u32[]{:S(2)}, u32[]{:S(2)}) collective-permute-start(bf16[1040,128]{1,0:T(8,128)(2,1)S(1)} %collective-permute-done.14.refs_5_), channel_id=1, source_target_pairs={{0,8},{4,20},{8,0},{12,28},{16,24},{20,4},{24,16},{28,12},{1,9},{5... | collective-permute-start | bytes 798728 | tf_op jit(solution)/shard_map/ppermute | solution.py:354
  44.7 6.4 %collective-permute-start.17 = (bf16[1040,128]{1,0:T(8,128)(2,1)S(1)}, bf16[1040,128]{1,0:T(8,128)(2,1)S(1)}, u32[]{:S(2)}, u32[]{:S(2)}) collective-permute-start(bf16[1040,128]{1,0:T(8,128)(2,1)S(1)} %collective-permute-done.13.refs_4_), channel_id=1, source_target_pairs={{0,16},{4,12},{8,24},{12,4},{16,0},{20,28},{24,8},{28,20},{1,17},{... | collective-permute-start | bytes 798728 | tf_op jit(solution)/shard_map/ppermute | solution.py:354
  45.0 6.2 %collective-permute-start.16 = (bf16[1040,128]{1,0:T(8,128)(2,1)S(1)}, bf16[1040,128]{1,0:T(8,128)(2,1)S(1)}, u32[]{:S(2)}, u32[]{:S(2)}) collective-permute-start(bf16[1040,128]{1,0:T(8,128)(2,1)S(1)} %late.1), channel_id=1, source_target_pairs={{0,4},{4,0},{8,12},{12,8},{16,20},{20,16},{24,28},{28,24},{1,5},{5... | collective-permute-start | bytes 798728 | tf_op jit(solution)/shard_map/ppermute | solution.py:354
  46.3 5.9 %collective-permute-start.15 = (bf16[256,640]{1,0:T(8,128)(2,1)S(1)}, bf16[256,640]{1,0:T(8,128)(2,1)S(1)}, u32[]{:S(2)}, u32[]{:S(2)}) collective-permute-start(bf16[256,640]{1,0:T(8,128)(2,1)S(1)} %grad_other_near.1), channel_id=1, source_target_pairs={{0,4},{4,0},{8,12},{12,8},{16,20},{20,16},{24,28},{28,24},{1,5},{5... | collective-permute-start | bytes 983048 | tf_op jit(solution)/shard_map/ppermute | solution.py:354
  51.6 1.5 %collective-permute-start.19 = (bf16[256,384]{1,0:T(8,128)(2,1)S(1)}, bf16[256,384]{1,0:T(8,128)(2,1)S(1)}, u32[]{:S(2)}, u32[]{:S(2)}) collective-permute-start(bf16[256,384]{1,0:T(8,128)(2,1)S(1)} %grad_other_far.1), channel_id=1, source_target_pairs={{0,4},{4,0},{8,12},{12,8},{16,20},{20,16},{24,28},{28,24},{1,5},{5... | collective-permute-start | bytes 589832 | tf_op jit(solution)/shard_map/ppermute | solution.py:354
